TPU v7x, 32 devices: a whole 2x2x4 slice. The times are simulated.
32 devices in a mesh: row: 2 (over y), col: 16 (over z, x, core).
Axes of the slice: x: 2, y: 2, z: 4, core: 2. Of those that a mesh axis runs over, the one named last changes fastest.
Arguments:
- grad_output: bfloat16 [256, 8192], P('col', 'row'), may hold values from -6 to 6
- inputs: bfloat16 [256, 28672], P('row', 'col'), may hold values from -0.375 to 0.375
- weight: bfloat16 [28672, 8192], P('col', 'row'), may hold values from -0.125 to 0.125
- block_mask: int32 [224, 64], P('col'), may hold values from 0 to 1, as said below
Outputs:
- grad_input: bfloat16 [256, 28672], P('row', 'col')
- grad_weight: bfloat16 [28672, 8192], P('col', 'row')
Inputs may be any that keep to these rules, and one draw needn't show every extreme that they name: `block_mask`: 1 where the 128 x 128 block of weight is kept, 0 where it is zero; the share of kept blocks differs widely from block row to block row.
All inputs are finite; a program needn't handle non-finite values.
Results may differ from a plain program's by a relative error of at most 0.001.
Values may be sent and summed in bfloat16 or wider, within the bound.
No kernel may reach another device: no remote copies, remote signals or barrier semaphores. Data moves between devices by JAX's collectives and lax.ppermute only.
A program may use at most 128 MiB of HBM per device.

v0:
```python
import jax
import jax.numpy as jnp
from jax import lax
from jax.sharding import PartitionSpec as P

BLOCK = 128


def masked_tile(weight_tile, mask_tile):
    rows = weight_tile.shape[0]
    cols = weight_tile.shape[1]
    shaped = weight_tile.reshape(rows // BLOCK, BLOCK, cols // BLOCK, BLOCK)
    factor = mask_tile.astype(jnp.bfloat16)[:, None, :, None]
    return (shaped * factor).reshape(rows, cols)


def per_device(grad_output, inputs, weight, block_mask):
    grads_all = lax.all_gather(grad_output, "col", axis=0, tiled=True)
    inputs_all = lax.all_gather(inputs, "row", axis=0, tiled=True)
    tile_cols = weight.shape[1] // BLOCK
    mask_tile = lax.dynamic_slice_in_dim(
        block_mask, lax.axis_index("row") * tile_cols, tile_cols, 1
    )
    kept_tile = masked_tile(weight, mask_tile)
    partial_value = lax.dot_general(
        grads_all, kept_tile, (((1,), (1,)), ((), ())), preferred_element_type=jnp.float32
    )
    grad_input = lax.psum_scatter(partial_value, "row", scatter_dimension=0, tiled=True).astype(
        jnp.bfloat16
    )
    product = lax.dot_general(
        inputs_all, grads_all, (((0,), (0,)), ((), ())), preferred_element_type=jnp.float32
    )
    rows = product.shape[0]
    cols = product.shape[1]
    factor = mask_tile.astype(jnp.float32)[:, None, :, None]
    grad_weight = (
        (product.reshape(rows // BLOCK, BLOCK, cols // BLOCK, BLOCK) * factor)
        .reshape(rows, cols)
        .astype(jnp.bfloat16)
    )
    return (grad_input, grad_weight)


def solution(mesh):
    return jax.shard_map(
        per_device,
        mesh=mesh,
        in_specs=(P("col", "row"), P("row", "col"), P("col", "row"), P("col", None)),
        out_specs=(P("row", "col"), P("col", "row")),
        check_vma=False,
    )
```

profile of v0, /device:TPU:0, one launch (start us, length us, event | category | flops | bytes accessed | tf_op | source)
XLA Modules:
  0.0 143.6 jit_solution(4401833558534503993)
XLA Ops:
  7.2 0.0 all-gather.2.cloned.1.call-start
  7.2 0.7 all-gather.2.cloned.1.call-update
  7.9 0.0 reduce-scatter.2.cloned.1.call-start
  7.9 0.8 dynamic-slice_convert_fusion
  8.7 45.6 %all-gather.2.cloned.1.call-done = bf16[256,4096]{1,0:T(8,128)(2,1)} async-done(((bf16[16,4096]{1,0:T(8,128)(2,1)}), bf16[256,4096]{1,0:T(8,128)(2,1)}) %all-gather.2.cloned.1.call-update) | async-done | bytes 2097168 | tf_op jit(solution)/shard_map/all_gather | solution.py:18
  54.3 0.0 copy-start
  54.3 7.4 %mul.26 = bf16[14,128,32,128]{3,2,1,0:T(8,128)(2,1)} broadcast(bf16[14,32]{1,0:T(8,128)(2,1)S(1)} %get-tuple-element.5), dimensions={0,2} | broadcast | bytes 14680960 | tf_op jit(solution)/shard_map/mul | solution.py:14
  61.7 0.0 copy-done
  61.7 0.0 copy-start.1
  61.7 14.3 %fusion.3 = f32[256,1792]{0,1:T(8,128)} fusion(bf16[256,4096]{1,0:T(8,128)(2,1)S(1)} %copy-done, bf16[1792,4096]{1,0:T(8,128)(2,1)} %param.6, bf16[224,8,32,128]{3,2,1,0:T(8,128)(2,1)} %bitcast.19), kind=kOutput, calls=%fused_computation.5 | convolution fusion | flops 3765436416 | bytes 33292288 | tf_op jit(solution)/shard_map/dot_general | solution.py:25
  76.0 0.0 reduce-scatter.2.cloned.1.call-update
  76.0 0.0 copy-done.1
  76.0 20.9 %all_gather.7 = bf16[256,1792]{1,0:T(8,128)(2,1)S(1)} all-gather(bf16[128,1792]{1,0:T(8,128)(2,1)S(1)} %copy-done.1), channel_id=1, replica_groups=mesh['row'=2,'col'=16] {'row'}, dimensions={0}, use_global_device_ids=true | all-gather | bytes 1376256 | tf_op jit(solution)/shard_map/all_gather | solution.py:19
  97.0 13.7 %mul.29 = f32[14,128,32,128]{3,2,1,0:T(8,128)} broadcast(f32[14,32]{1,0:T(8,128)S(1)} %get-tuple-element.4), dimensions={0,2} | broadcast | bytes 29361920 | tf_op jit(solution)/shard_map/mul | solution.py:38
  110.7 23.8 %fusion = bf16[1792,4096]{1,0:T(8,128)(2,1)} fusion(f32[224,8,32,128]{3,2,1,0:T(8,128)} %bitcast.18, bf16[256,1792]{1,0:T(8,128)(2,1)S(1)} %all_gather.7, bf16[256,4096]{1,0:T(8,128)(2,1)S(1)} %copy-done), kind=kOutput, calls=%fused_computation.1 | convolution fusion | flops 3772776448 | bytes 47054848 | tf_op jit(solution)/shard_map/dot_general | solution.py:31
  134.5 0.0 reduce-scatter.2.cloned.1.call-done
  134.5 1.2 convert_element_type.13
  135.7 1.0 copy.6
Async XLA Ops:
  7.2 47.1 %all-gather.2.cloned.1.call-start = ((), (), s32[]{:S(2)}) async-start(), calls=%async_computation.1 | async-start | bytes 2228224 | tf_op jit(solution)/shard_map/all_gather | solution.py:18
  7.9 126.6 %reduce-scatter.2.cloned.1.call-start = ((), (), s32[]{:S(2)}) async-start(), calls=%async_computation.2 | async-start | bytes 2752512 | tf_op jit(solution)/shard_map/reduce_scatter | solution.py:28
  54.3 7.4 %copy-start = (bf16[256,4096]{1,0:T(8,128)(2,1)S(1)}, bf16[256,4096]{1,0:T(8,128)(2,1)}, u32[]{:S(2)}) copy-start(bf16[256,4096]{1,0:T(8,128)(2,1)} %all-gather.2.cloned.1.call-done) | copy-start | bytes 6291460
  61.7 14.3 %copy-start.1 = (bf16[128,1792]{1,0:T(8,128)(2,1)S(1)}, bf16[128,1792]{1,0:T(8,128)(2,1)}, u32[]{:S(2)}) copy-start(bf16[128,1792]{1,0:T(8,128)(2,1)} %param.5) | copy-start | bytes 1376260
Sparse Core Ops, SparseCore 0:
  10.2 44.0 all-gather.1
  76.1 34.3 reduce-scatter.1
where the time goes:
time: 144 us
  waiting for transfers between devices  46.3 us (32%)
  matrix products  38.1 us (26%)
  local copies, waits for them, and re-layouts  22.1 us (15%)
  blocking collectives  20.9 us (15%)
  between operations  14.1 us (10%)
  other arithmetic  2 us (1%)
    all_gather x1, waiting for transfers between devices, per_device(): grads_all = lax.all_gather(grad_output, 'col', axis=0, tiled=True)  45.6 us
    dot_general x1, matrix products, per_device(): lax.dot_general(inputs_all, grads_all, (((0,), (0,)), ((), ())), preferre...  23.8 us
    all_gather x1, blocking collectives, per_device(): inputs_all = lax.all_gather(inputs, 'row', axis=0, tiled=True)  20.9 us
    dot_general x1, matrix products, per_device(): lax.dot_general(grads_all, kept_tile, (((1,), (1,)), ((), ())), preferred...  14.3 us
    mul x1, local copies, waits for them, and re-layouts, per_device(): product.reshape(rows // BLOCK, BLOCK, cols // BLOCK, BLOCK) * factor  13.7 us
    mul x1, local copies, waits for them, and re-layouts, masked_tile(): return (shaped * factor).reshape(rows, cols)  7.42 us
  transfers between devices with their start and end apart: 2, of which 1 were waited for; matrix products, arithmetic and copies ran while one was open for 27% of the time, Pallas kernels for 0%

commit v1 on v0

v1 whole, which is shorter than its diff:
```python
import functools

import jax
import jax.numpy as jnp
from jax import lax
from jax.experimental import pallas as pl
from jax.experimental.pallas import tpu as pltpu
from jax.sharding import PartitionSpec as P

BLOCK = 128
CODE = 32700.0
STEPS = 64.0
VMEM_LIMIT = 56 * 1024 * 1024


def pair_of(blocks):
    return 2 if blocks % 2 == 0 else 1


def grid_of(cols):
    half, fast = cols // 2, 1
    while half % (fast * 2) == 0 and fast * 2 * fast * 2 <= half:
        fast *= 2
    return half // fast, fast


def encode(part):
    top = jnp.max(jnp.abs(part), axis=0, keepdims=True)
    code = jnp.ceil(STEPS * jnp.log2(jnp.maximum(top, 1e-30)))
    scaled = part * (jnp.exp2(code * (-1.0 / STEPS)) * CODE)
    whole = jnp.clip(jnp.round(scaled), -32767.0, 32767.0)
    return whole.astype(jnp.int32), code.astype(jnp.int32)


def fill_tokens(src_cols, shards, full):
    rows = shards[0].shape[0]
    for n, shard in enumerate(shards):
        at = pl.multiple_of(src_cols[n] * rows, rows)
        full[pl.ds(at, rows), :] = shard[...]


def remote_kernel(n_shards, n_parts, blocks, pair, idx, *refs):
    shards = refs[:n_shards]
    weight, mask = refs[n_shards : n_shards + 2]
    full = refs[n_shards + 2]
    outs = refs[n_shards + 3 : n_shards + 3 + n_parts]
    codes = refs[n_shards + 3 + n_parts]
    step = pl.program_id(0)
    tokens = full.shape[0] // (n_parts + 1)

    @pl.when(step == 0)
    def _():
        fill_tokens(idx, shards, full)
        codes[...] = jnp.zeros_like(codes)

    kept = []
    for b in range(pair):
        factor = mask[pl.ds(step * pair + b, 1), :].astype(jnp.bfloat16)
        kept.append(weight[b * BLOCK : (b + 1) * BLOCK, :] * factor)
    kept = kept[0] if pair == 1 else jnp.concatenate(kept, axis=0)
    row_of_code = lax.broadcasted_iota(jnp.int32, codes.shape[1:], 0)
    for k in range(n_parts):
        at = pl.multiple_of(idx[n_shards + 1 + k] * tokens, tokens)
        part = lax.dot_general(
            full[pl.ds(at, tokens), :],
            kept,
            (((1,), (1,)), ((), ())),
            preferred_element_type=jnp.float32,
        )
        for b in range(pair):
            block = step * pair + b
            whole, code = encode(part[:, b * BLOCK : (b + 1) * BLOCK])
            rows = pl.ds(pl.multiple_of(block * tokens, tokens), tokens)
            outs[k][rows, :] = whole.astype(jnp.int16)
            codes[k] = jnp.where(row_of_code == block, code, codes[k])

    @pl.when(step == blocks // pair - 1)
    def _():
        for k in range(n_parts):
            outs[k][blocks * tokens :, :] = codes[k].astype(jnp.int16)


def own_kernel(pair, idx, full, weight, mask, out):
    step = pl.program_id(0)
    tokens = out.shape[0]
    kept = []
    for b in range(pair):
        factor = mask[pl.ds(step * pair + b, 1), :].astype(jnp.bfloat16)
        kept.append(weight[b * BLOCK : (b + 1) * BLOCK, :] * factor)
    kept = kept[0] if pair == 1 else jnp.concatenate(kept, axis=0)
    at = pl.multiple_of(idx[0] * tokens, tokens)
    out[...] = lax.dot_general(
        full[pl.ds(at, tokens), :],
        kept,
        (((1,), (1,)), ((), ())),
        preferred_element_type=jnp.float32,
    )


def weight_grad_kernel(n_parts, pair, chunk, idx, *refs):
    acts = refs[:n_parts]
    full, mask, out = refs[n_parts : n_parts + 3]
    held = refs[n_parts + 3]
    step = pl.program_id(0)
    tokens = acts[0].shape[0]
    for k in range(n_parts):
        held[pl.ds(pl.multiple_of(idx[k] * tokens, tokens), tokens), :] = acts[k][...]

    def columns(c, _):
        at = pl.ds(pl.multiple_of(c * chunk, chunk), chunk)
        product = lax.dot_general(
            held[...],
            full[:, at],
            (((0,), (0,)), ((), ())),
            preferred_element_type=jnp.float32,
        )
        for b in range(pair):
            factor = mask[pl.ds(step * pair + b, 1), at]
            rows = slice(b * BLOCK, (b + 1) * BLOCK)
            out[rows, at] = (product[rows, :] * factor).astype(out.dtype)
        return 0

    lax.fori_loop(0, out.shape[1] // chunk, columns, 0, unroll=True)


def finish_kernel(n_parts, blocks, own, *refs):
    parts = refs[:n_parts]
    out = refs[n_parts]
    tokens = own.shape[0]
    scales = []
    for part in parts:
        code = part[blocks * tokens :, :].astype(jnp.int32).astype(jnp.float32)
        scales.append(jnp.exp2(code * (1.0 / STEPS)) * (1.0 / CODE))
    for i in range(blocks):
        cols = slice(i * BLOCK, (i + 1) * BLOCK)
        total = own[:, cols]
        for part, scale in zip(parts, scales, strict=True):
            got = part[i * tokens : (i + 1) * tokens, :].astype(jnp.int32)
            total = total + got.astype(jnp.float32) * scale[i : i + 1, :]
        out[:, cols] = total.astype(out.dtype)


def in_vmem():
    return pl.BlockSpec(memory_space=pltpu.VMEM)


def in_smem():
    return pl.BlockSpec(memory_space=pltpu.SMEM)


def params():
    return pltpu.CompilerParams(vmem_limit_bytes=VMEM_LIMIT)


def per_device(n_rows, n_cols, grad_output, inputs, weight, block_mask):
    slow, fast = grid_of(n_cols)
    row, col = lax.axis_index("row"), lax.axis_index("col")
    my_slow, my_fast, my_core = col // (2 * fast), (col // 2) % fast, col % 2
    hidden, width = weight.shape
    blocks = hidden // BLOCK
    pair = pair_of(blocks)
    n_parts = n_rows - 1
    tokens = inputs.shape[0]

    def col_index(s, f, c):
        return (s * fast + f) * 2 + c

    def send_col(x, by_slow, by_fast, by_core):
        perm = [
            (
                col_index(s, f, c),
                col_index((s + by_slow) % slow, (f + by_fast) % fast, (c + by_core) % 2),
            )
            for s in range(slow)
            for f in range(fast)
            for c in range(2)
        ]
        return lax.ppermute(x, "col", perm)

    def send_row(x, by):
        return lax.ppermute(x, "row", [(r, (r + by) % n_rows) for r in range(n_rows)])

    acts = [inputs] + [send_row(inputs, k) for k in range(1, n_rows)]

    held = {(0, 0): grad_output}
    for s in range(1, slow):
        held[s, 0] = send_col(grad_output, s, 0, 0)
    for f in range(1, fast):
        for s in range(slow):
            held[s, f] = send_col(held[s, 0], 0, f, 0)
    shards, sources = [], []
    for (s, f), shard in held.items():
        for c in range(2):
            shards.append(shard if c == 0 else send_col(shard, 0, 0, 1))
            sources.append(
                col_index(
                    (my_slow + slow - s) % slow,
                    (my_fast + fast - f) % fast,
                    (my_core + c) % 2,
                )
            )

    tile_cols = width // BLOCK
    mask_tile = lax.dynamic_slice_in_dim(block_mask, row * tile_cols, tile_cols, 1)
    wide_mask = jnp.repeat(mask_tile.astype(jnp.float32), BLOCK, axis=1)

    all_tokens = tokens * n_rows
    n_shards = len(shards)
    code_rows = -(-blocks // 16) * 16
    idx = jnp.stack(
        [jnp.asarray(s, jnp.int32) for s in sources]
        + [((row + k) % n_rows).astype(jnp.int32) for k in range(n_rows)]
    )
    sent_shape = jax.ShapeDtypeStruct((blocks * tokens + code_rows, BLOCK), jnp.int16)
    weight_spec = pl.BlockSpec((pair * BLOCK, width), lambda i: (i, 0))
    remote = pl.pallas_call(
        functools.partial(remote_kernel, n_shards, n_parts, blocks, pair),
        grid=(blocks // pair,),
        in_specs=[in_smem()] + [in_vmem()] * n_shards + [weight_spec, in_vmem()],
        out_specs=[in_vmem()] * (n_parts + 1),
        out_shape=[jax.ShapeDtypeStruct((all_tokens, width), jnp.bfloat16)]
        + [sent_shape] * n_parts,
        scratch_shapes=[pltpu.VMEM((n_parts, code_rows, BLOCK), jnp.int32)],
        compiler_params=params(),
        cost_estimate=pl.CostEstimate(
            flops=2 * tokens * n_parts * hidden * width,
            bytes_accessed=2 * hidden * width,
            transcendentals=0,
        ),
        name="remote_terms",
    )(idx, *shards, weight, wide_mask)
    full = remote[0]
    parts = [send_row(remote[k], k) for k in range(1, n_rows)]

    own_idx = row.astype(jnp.int32).reshape(1)
    own = pl.pallas_call(
        functools.partial(own_kernel, pair),
        grid=(blocks // pair,),
        in_specs=[in_smem(), in_vmem(), weight_spec, in_vmem()],
        out_specs=pl.BlockSpec((tokens, pair * BLOCK), lambda i: (0, i)),
        out_shape=jax.ShapeDtypeStruct((tokens, hidden), jnp.float32),
        compiler_params=params(),
        cost_estimate=pl.CostEstimate(
            flops=2 * tokens * hidden * width,
            bytes_accessed=2 * hidden * width,
            transcendentals=0,
        ),
        name="own_terms",
    )(own_idx, full, weight, wide_mask)

    act_idx = jnp.stack([((row + n_rows - k) % n_rows).astype(jnp.int32) for k in range(n_rows)])
    grad_weight = pl.pallas_call(
        functools.partial(weight_grad_kernel, n_rows, pair, min(512, width)),
        grid=(blocks // pair,),
        in_specs=[in_smem()]
        + [pl.BlockSpec((tokens, pair * BLOCK), lambda i: (0, i))] * n_rows
        + [in_vmem(), in_vmem()],
        out_specs=weight_spec,
        out_shape=jax.ShapeDtypeStruct((hidden, width), jnp.bfloat16),
        scratch_shapes=[pltpu.VMEM((all_tokens, pair * BLOCK), jnp.bfloat16)],
        compiler_params=params(),
        cost_estimate=pl.CostEstimate(
            flops=2 * all_tokens * hidden * width,
            bytes_accessed=2 * hidden * width,
            transcendentals=0,
        ),
        name="weight_grad",
    )(act_idx, *acts, full, wide_mask)

    grad_input = pl.pallas_call(
        functools.partial(finish_kernel, n_parts, blocks),
        in_specs=[in_vmem()] * (1 + n_parts),
        out_specs=in_vmem(),
        out_shape=jax.ShapeDtypeStruct((tokens, hidden), jnp.bfloat16),
        compiler_params=params(),
        name="add_terms",
    )(own, *parts)
    return (grad_input, grad_weight)


def solution(mesh):
    return jax.shard_map(
        functools.partial(per_device, mesh.shape["row"], mesh.shape["col"]),
        mesh=mesh,
        in_specs=(P("col", "row"), P("row", "col"), P("col", "row"), P("col", None)),
        out_specs=(P("row", "col"), P("col", "row")),
        check_vma=False,
    )
```

time: 144 us -> 70.1 us (0.49)
  matrix products: 38.1 us -> 0 us
  Pallas kernels: 0 us -> 36.1 us
  waiting for transfers between devices: 46.3 us -> 12.9 us
  blocking collectives: 20.9 us -> 0 us
  local copies, waits for them, and re-layouts: 22.1 us -> 3.89 us
  starting transfers between devices: 0.08 us -> 14.4 us
  between operations: 14.1 us -> 0.83 us
    all_gather x1 -> x0, waiting for transfers between devices: 45.6 us -> none  [per_device(): grads_all = lax.all_gather(grad_output, 'col', axis=0, tiled=True)]
    dot_general x2 -> x0, matrix products: 38.1 us -> none  [the longest x1 23.8 us: per_device(): lax.dot_general(inputs_all, grads_all, (((0,), (0,)), ((), ())), preferre...]
    pallas_call x0 -> x4, Pallas kernels: none -> 36.1 us  [the longest x1 12.4 us: per_device(): pl.pallas_call(functools.partial(remote_kernel, n_shards, n_parts, blocks...]
    mul x2 -> x0, local copies, waits for them, and re-layouts: 21.1 us -> none  [the longest x1 13.7 us: per_device(): product.reshape(rows // BLOCK, BLOCK, cols // BLOCK, BLOCK) * factor]
    all_gather x1 -> x0, blocking collectives: 20.9 us -> none  [per_device(): inputs_all = lax.all_gather(inputs, 'row', axis=0, tiled=True)]
    ppermute x0 -> x17, starting transfers between devices: none -> 14.4 us  [the longest x15 12.4 us: send_col(): return lax.ppermute(x, 'col', perm)]
    ppermute x0 -> x17, waiting for transfers between devices: none -> 12.9 us  [the longest x15 12.9 us: send_col(): return lax.ppermute(x, 'col', perm)]
    unnamed x5 -> x36, local copies, waits for them, and re-layouts: 0.99 us -> 3.1 us
  transfers between devices with their start and end apart: 2 -> 17, of which waited for: 1 -> 4; matrix products, arithmetic and copies ran while one was open for 27% -> 4% of each run, Pallas kernels for 0% -> 49%
where the time goes in v1:
time: 70.1 us; the launch traced here: 69.5 us
  Pallas kernels  36.1 us (51%)
  starting transfers between devices  14.4 us (21%)
  waiting for transfers between devices  12.9 us (18%)
  local copies, waits for them, and re-layouts  3.89 us (6%)
  other arithmetic  1.42 us (2%)
  between operations  0.83 us (1%)
    ppermute x15, waiting for transfers between devices, send_col(): return lax.ppermute(x, 'col', perm)  12.9 us
    pallas_call x1, Pallas kernels, per_device(): pl.pallas_call(functools.partial(remote_kernel, n_shards, n_parts, blocks...  12.4 us
    ppermute x15, starting transfers between devices, send_col(): return lax.ppermute(x, 'col', perm)  12.4 us
    pallas_call x1, Pallas kernels, per_device(): pl.pallas_call(functools.partial(own_kernel, pair), grid=(blocks // pair,...  11.3 us
    pallas_call x1, Pallas kernels, per_device(): pl.pallas_call(functools.partial(weight_grad_kernel, n_rows, pair, min(51...  10.1 us
    unnamed x36, local copies, waits for them, and re-layouts  3.1 us
    pallas_call x1, Pallas kernels, per_device(): pl.pallas_call(functools.partial(finish_kernel, n_parts, blocks), in_spec...  2.22 us
    ppermute x2, starting transfers between devices, send_row(): lax.ppermute(x, 'row', [(r, (r + by) % n_rows) for r in range(n_rows)])  2.03 us
  transfers between devices with their start and end apart: 17, of which 4 were waited for; matrix products, arithmetic and copies ran while one was open for 4% of the time, Pallas kernels for 49%

profile of v1, /device:TPU:0, one launch (start us, length us, event | category | flops | bytes accessed | tf_op | source)
XLA Modules:
  0.0 69.5 jit_solution(443225607362206543)
XLA Ops:
  0.6 5.1 %collective-permute-start.5 = (bf16[16,4096]{1,0:T(8,128)(2,1)}, bf16[16,4096]{1,0:T(8,128)(2,1)S(1)}, u32[]{:S(2)}, u32[]{:S(2)}) collective-permute-start(bf16[16,4096]{1,0:T(8,128)(2,1)} %refs_0_.2), channel_id=1, source_target_pairs={{0,12},{1,13},{2,14},{3,15},{4,0},{5,1},{6,2},{7,3},{8,4},{9,5},{1... | collective-permute-start | bytes 393224 | tf_op jit(solution)/shard_map/ppermute | solution.py:178
  5.7 0.0 collective-permute-start.3
  5.7 1.0 %collective-permute-start.1 = (bf16[16,4096]{1,0:T(8,128)(2,1)}, bf16[16,4096]{1,0:T(8,128)(2,1)S(1)}, u32[]{:S(2)}, u32[]{:S(2)}) collective-permute-start(bf16[16,4096]{1,0:T(8,128)(2,1)} %refs_0_.2), channel_id=1, source_target_pairs={{0,4},{1,5},{2,6},{3,7},{4,8},{5,9},{6,10},{7,11},{8,12},{9,13},{1... | collective-permute-start | bytes 393224 | tf_op jit(solution)/shard_map/ppermute | solution.py:178
  6.7 0.0 collective-permute-start
  6.7 1.5 %collective-permute-start.7 = (bf16[16,4096]{1,0:T(8,128)(2,1)}, bf16[16,4096]{1,0:T(8,128)(2,1)S(1)}, u32[]{:S(2)}, u32[]{:S(2)}) collective-permute-start(bf16[16,4096]{1,0:T(8,128)(2,1)} %refs_0_.2), channel_id=1, source_target_pairs={{0,2},{1,3},{2,0},{3,1},{4,6},{5,7},{6,4},{7,5},{8,10},{9,11},{10,... | collective-permute-start | bytes 393224 | tf_op jit(solution)/shard_map/ppermute | solution.py:178
  8.2 1.7 %collective-permute-done.5.refs_6_ = bf16[16,4096]{1,0:T(8,128)(2,1)S(1)} collective-permute-done((bf16[16,4096]{1,0:T(8,128)(2,1)}, bf16[16,4096]{1,0:T(8,128)(2,1)S(1)}, u32[]{:S(2)}, u32[]{:S(2)}) %collective-permute-start.5) | collective-permute-done | bytes 131104 | tf_op jit(solution)/shard_map/ppermute | solution.py:178
  10.0 1.5 %collective-permute-start.13 = (bf16[16,4096]{1,0:T(8,128)(2,1)S(1)}, bf16[16,4096]{1,0:T(8,128)(2,1)S(1)}, u32[]{:S(2)}, u32[]{:S(2)}) collective-permute-start(bf16[16,4096]{1,0:T(8,128)(2,1)S(1)} %collective-permute-done.5.refs_6_), channel_id=1, source_target_pairs={{0,2},{1,3},{2,0},{3,1},{4,6},{5,7},{6,4},{7,5},{8,10},{9,11},{10,... | collective-permute-start | bytes 393224 | tf_op jit(solution)/shard_map/ppermute | solution.py:178
  11.4 5.7 %collective-permute-done.3.refs_4_ = bf16[16,4096]{1,0:T(8,128)(2,1)S(1)} collective-permute-done((bf16[16,4096]{1,0:T(8,128)(2,1)}, bf16[16,4096]{1,0:T(8,128)(2,1)S(1)}, u32[]{:S(2)}, u32[]{:S(2)}) %collective-permute-start.3) | collective-permute-done | bytes 131104 | tf_op jit(solution)/shard_map/ppermute | solution.py:178
  17.1 0.0 collective-permute-start.6
  17.2 0.0 collective-permute-done.1.refs_2_
  17.2 0.0 copy-start.4
  17.2 1.6 %collective-permute-start.11 = (bf16[16,4096]{1,0:T(8,128)(2,1)S(1)}, bf16[16,4096]{1,0:T(8,128)(2,1)S(1)}, u32[]{:S(2)}, u32[]{:S(2)}) collective-permute-start(bf16[16,4096]{1,0:T(8,128)(2,1)S(1)} %collective-permute-done.3.refs_4_), channel_id=1, source_target_pairs={{0,2},{1,3},{2,0},{3,1},{4,6},{5,7},{6,4},{7,5},{8,10},{9,11},{10,... | collective-permute-start | bytes 393224 | tf_op jit(solution)/shard_map/ppermute | solution.py:178
  18.7 0.0 collective-permute-done.refs_1_
  18.7 0.2 collective-permute-start.4
  18.9 0.0 collective-permute-done.7.refs_8_
  18.9 0.5 collective-permute-start.9
  19.4 0.0 collective-permute-done.13.refs_14_
  19.4 0.1 collective-permute-start.2
  19.5 0.0 collective-permute-done.6.refs_7_
  19.5 0.4 collective-permute-start.8
  20.0 3.6 %collective-permute-done.11.refs_12_ = bf16[16,4096]{1,0:T(8,128)(2,1)S(1)} collective-permute-done((bf16[16,4096]{1,0:T(8,128)(2,1)S(1)}, bf16[16,4096]{1,0:T(8,128)(2,1)S(1)}, u32[]{:S(2)}, u32[]{:S(2)}) %collective-permute-start.11) | collective-permute-done | bytes 131104 | tf_op jit(solution)/shard_map/ppermute | solution.py:178
  23.5 0.0 collective-permute-start.14
  23.5 0.0 collective-permute-done.4.refs_5_
  23.5 0.0 copy-start.10
  23.6 0.5 collective-permute-start.12
  24.1 1.8 %collective-permute-done.9.refs_10_ = bf16[16,4096]{1,0:T(8,128)(2,1)S(1)} collective-permute-done((bf16[16,4096]{1,0:T(8,128)(2,1)S(1)}, bf16[16,4096]{1,0:T(8,128)(2,1)S(1)}, u32[]{:S(2)}, u32[]{:S(2)}) %collective-permute-start.9) | collective-permute-done | bytes 131104 | tf_op jit(solution)/shard_map/ppermute | solution.py:178
  25.9 0.0 collective-permute-start.10
  25.9 0.8 %dynamic-slice_convert_fusion = f32[14,32]{1,0:T(8,128)S(1)} fusion(s32[14,64]{1,0:T(8,128)} %param.7, s32[]{:T(128)S(6)} %select_n.161), kind=kLoop, calls=%fused_computation | loop fusion | flops 448 | bytes 3588 | tf_op jit(solution)/shard_map/convert_element_type | solution.py:205
  26.7 0.1 broadcast_in_dim.3
  26.8 0.8 %copy.6 = f32[2,8,32,128]{3,1,2,0:T(8,128)} copy(f32[2,8,32,128]{3,2,1,0:T(8,128)S(1)} %bitcast.26) | data formatting | bytes 524288
  27.7 0.7 stack.82.idx
  28.3 0.0 collective-permute-done.2.refs_3_
  28.3 1.5 %collective-permute-start.16 = (bf16[128,1792]{1,0:T(8,128)(2,1)}, bf16[128,1792]{1,0:T(8,128)(2,1)S(1)}, u32[]{:S(2)}, u32[]{:S(2)}) collective-permute-start(bf16[128,1792]{1,0:T(8,128)(2,1)} %refs_0_.3), channel_id=1, source_target_pairs={{0,16},{16,0},{1,17},{17,1},{2,18},{18,2},{3,19},{19,3},{4,20},{20... | collective-permute-start | bytes 1376264 | tf_op jit(solution)/shard_map/ppermute | solution.py:181
  29.9 0.6 pad_add_fusion.idx
  30.5 0.0 collective-permute-done.8.refs_9_
  30.5 0.0 collective-permute-done.14.refs_15_
  30.5 0.0 copy-start.14
  30.5 0.0 collective-permute-done.12.refs_13_
  30.6 0.0 collective-permute-done.10.refs_11_
  30.6 0.0 copy-start.16
  30.6 0.0 copy-done.2
  30.6 0.0 copy-done.3
  30.6 0.0 copy-done.4
  30.6 0.0 copy-done.5
  30.6 0.0 copy-done.6
  30.6 0.0 copy-done.7
  30.6 0.0 copy-done.8
  30.6 0.0 copy-done.9
  30.7 0.0 copy-done.10
  30.7 0.0 copy-done.11
  30.7 0.0 copy-done.12
  30.7 0.5 copy-done.13
  31.2 0.0 copy-done.14
  31.2 0.1 copy-done.15
  31.3 0.0 copy-done.16
  31.3 12.4 %remote_terms.1 = (bf16[256,4096]{1,0:T(8,128)(2,1)}, s16[1808,128]{1,0:T(8,128)(2,1)}) custom-call(s32[18]{0:T(128)} %stack.82.idx, bf16[16,4096]{1,0:T(8,128)(2,1)} %refs_0_.2, bf16[16,4096]{1,0:T(8,128)(2,1)} %copy-done.5, bf16[16,4096]{1,0:T(8,128)(2,1)} %copy-done.4, bf16[16,4096]{1,0:T(8,128)(2,1)} %copy-done.12, bf16[16,4096]{1,0:T(8,128)(2,1)} %copy-done.3, ...), custom_call_target="tpu_custom_call" | custom-call | flops 1879048192 | bytes 14680064 | tf_op jit(solution)/shard_map/remote_terms/pallas_call | solution.py:216
  43.7 0.5 collective-permute-start.15
  44.2 11.3 %own_terms.1.own = f32[128,1792]{1,0:T(8,128)} custom-call(s32[1]{0:T(128)} %bitcast.idx, bf16[256,4096]{1,0:T(8,128)(2,1)} %get-tuple-element.4.full.refs_2_, bf16[1792,4096]{1,0:T(8,128)(2,1)} %weight.1, f32[14,4096]{1,0:T(8,128)} %bitcast.24), custom_call_target="tpu_custom_call" | custom-call | flops 1879048192 | bytes 14680064 | tf_op jit(solution)/shard_map/own_terms/pallas_call | solution.py:236
  55.5 0.0 collective-permute-done.16.refs_1_
  55.6 0.8 %copy-done.1 = bf16[128,1792]{1,0:T(8,128)(2,1)} copy-done((bf16[128,1792]{1,0:T(8,128)(2,1)}, bf16[128,1792]{1,0:T(8,128)(2,1)S(1)}, u32[]{:S(2)}) %copy-start.1) | copy-done | bytes 458776
  56.3 10.1 %weight_grad.1 = bf16[1792,4096]{1,0:T(8,128)(2,1)} custom-call(s32[2]{0:T(128)} %pad_add_fusion.idx, bf16[128,1792]{1,0:T(8,128)(2,1)} %refs_0_.3, bf16[128,1792]{1,0:T(8,128)(2,1)} %copy-done.1, bf16[256,4096]{1,0:T(8,128)(2,1)} %get-tuple-element.4.full.refs_2_, f32[14,4096]{1,0:T(8,128)} %bitcast.25), custom_call_target="tpu_custom_call" | custom-call | flops 3758096384 | bytes 14680064 | tf_op jit(solution)/shard_map/weight_grad/pallas_call | solution.py:252
  66.4 0.0 collective-permute-done.15.refs_0_
  66.5 0.8 %copy-done = s16[1808,128]{1,0:T(8,128)(2,1)} copy-done((s16[1808,128]{1,0:T(8,128)(2,1)}, s16[1808,128]{1,0:T(8,128)(2,1)S(1)}, u32[]{:S(2)}) %copy-start) | copy-done | bytes 462872
  67.2 2.2 %add_terms.1 = bf16[128,1792]{1,0:T(8,128)(2,1)} custom-call(f32[128,1792]{1,0:T(8,128)} %own_terms.1.own, s16[1808,128]{1,0:T(8,128)(2,1)} %copy-done), custom_call_target="tpu_custom_call" | custom-call | tf_op jit(solution)/shard_map/add_terms/pallas_call | solution.py:270
  (14 shorter events, 0.0 us)
Async XLA Ops:
  0.6 9.3 %collective-permute-start.5 = (bf16[16,4096]{1,0:T(8,128)(2,1)}, bf16[16,4096]{1,0:T(8,128)(2,1)S(1)}, u32[]{:S(2)}, u32[]{:S(2)}) collective-permute-start(bf16[16,4096]{1,0:T(8,128)(2,1)} %refs_0_.2), channel_id=1, source_target_pairs={{0,12},{1,13},{2,14},{3,15},{4,0},{5,1},{6,2},{7,3},{8,4},{9,5},{1... | collective-permute-start | bytes 393224 | tf_op jit(solution)/shard_map/ppermute | solution.py:178
  5.7 11.4 %collective-permute-start.3 = (bf16[16,4096]{1,0:T(8,128)(2,1)}, bf16[16,4096]{1,0:T(8,128)(2,1)S(1)}, u32[]{:S(2)}, u32[]{:S(2)}) collective-permute-start(bf16[16,4096]{1,0:T(8,128)(2,1)} %refs_0_.2), channel_id=1, source_target_pairs={{0,8},{1,9},{2,10},{3,11},{4,12},{5,13},{6,14},{7,15},{8,0},{9,1},... | collective-permute-start | bytes 393224 | tf_op jit(solution)/shard_map/ppermute | solution.py:178
  5.7 11.4 %collective-permute-start.1 = (bf16[16,4096]{1,0:T(8,128)(2,1)}, bf16[16,4096]{1,0:T(8,128)(2,1)S(1)}, u32[]{:S(2)}, u32[]{:S(2)}) collective-permute-start(bf16[16,4096]{1,0:T(8,128)(2,1)} %refs_0_.2), channel_id=1, source_target_pairs={{0,4},{1,5},{2,6},{3,7},{4,8},{5,9},{6,10},{7,11},{8,12},{9,13},{1... | collective-permute-start | bytes 393224 | tf_op jit(solution)/shard_map/ppermute | solution.py:178
  6.7 12.0 %collective-permute-start = (bf16[16,4096]{1,0:T(8,128)(2,1)}, bf16[16,4096]{1,0:T(8,128)(2,1)S(1)}, u32[]{:S(2)}, u32[]{:S(2)}) collective-permute-start(bf16[16,4096]{1,0:T(8,128)(2,1)} %refs_0_.2), channel_id=1, source_target_pairs={{0,1},{1,0},{2,3},{3,2},{4,5},{5,4},{6,7},{7,6},{8,9},{9,8},{10,11... | collective-permute-start | bytes 393224 | tf_op jit(solution)/shard_map/ppermute | solution.py:178
  6.7 12.2 %collective-permute-start.7 = (bf16[16,4096]{1,0:T(8,128)(2,1)}, bf16[16,4096]{1,0:T(8,128)(2,1)S(1)}, u32[]{:S(2)}, u32[]{:S(2)}) collective-permute-start(bf16[16,4096]{1,0:T(8,128)(2,1)} %refs_0_.2), channel_id=1, source_target_pairs={{0,2},{1,3},{2,0},{3,1},{4,6},{5,7},{6,4},{7,5},{8,10},{9,11},{10,... | collective-permute-start | bytes 393224 | tf_op jit(solution)/shard_map/ppermute | solution.py:178
  9.9 20.6 %copy-start.2 = (bf16[16,4096]{1,0:T(8,128)(2,1)}, bf16[16,4096]{1,0:T(8,128)(2,1)S(1)}, u32[]{:S(2)}) copy-start(bf16[16,4096]{1,0:T(8,128)(2,1)S(1)} %collective-permute-done.5.refs_6_) | copy-start | bytes 393220
  10.0 9.5 %collective-permute-start.13 = (bf16[16,4096]{1,0:T(8,128)(2,1)S(1)}, bf16[16,4096]{1,0:T(8,128)(2,1)S(1)}, u32[]{:S(2)}, u32[]{:S(2)}) collective-permute-start(bf16[16,4096]{1,0:T(8,128)(2,1)S(1)} %collective-permute-done.5.refs_6_), channel_id=1, source_target_pairs={{0,2},{1,3},{2,0},{3,1},{4,6},{5,7},{6,4},{7,5},{8,10},{9,11},{10,... | collective-permute-start | bytes 393224 | tf_op jit(solution)/shard_map/ppermute | solution.py:178
  17.1 13.4 %copy-start.3 = (bf16[16,4096]{1,0:T(8,128)(2,1)}, bf16[16,4096]{1,0:T(8,128)(2,1)S(1)}, u32[]{:S(2)}) copy-start(bf16[16,4096]{1,0:T(8,128)(2,1)S(1)} %collective-permute-done.3.refs_4_) | copy-start | bytes 393220
  17.1 2.4 %collective-permute-start.6 = (bf16[16,4096]{1,0:T(8,128)(2,1)S(1)}, bf16[16,4096]{1,0:T(8,128)(2,1)S(1)}, u32[]{:S(2)}, u32[]{:S(2)}) collective-permute-start(bf16[16,4096]{1,0:T(8,128)(2,1)S(1)} %collective-permute-done.5.refs_6_), channel_id=1, source_target_pairs={{0,1},{1,0},{2,3},{3,2},{4,5},{5,4},{6,7},{7,6},{8,9},{9,8},{10,11... | collective-permute-start | bytes 393224 | tf_op jit(solution)/shard_map/ppermute | solution.py:178
  17.2 13.4 %copy-start.4 = (bf16[16,4096]{1,0:T(8,128)(2,1)}, bf16[16,4096]{1,0:T(8,128)(2,1)S(1)}, u32[]{:S(2)}) copy-start(bf16[16,4096]{1,0:T(8,128)(2,1)S(1)} %collective-permute-done.1.refs_2_) | copy-start | bytes 393220
  17.2 6.4 %collective-permute-start.11 = (bf16[16,4096]{1,0:T(8,128)(2,1)S(1)}, bf16[16,4096]{1,0:T(8,128)(2,1)S(1)}, u32[]{:S(2)}, u32[]{:S(2)}) collective-permute-start(bf16[16,4096]{1,0:T(8,128)(2,1)S(1)} %collective-permute-done.3.refs_4_), channel_id=1, source_target_pairs={{0,2},{1,3},{2,0},{3,1},{4,6},{5,7},{6,4},{7,5},{8,10},{9,11},{10,... | collective-permute-start | bytes 393224 | tf_op jit(solution)/shard_map/ppermute | solution.py:178
  18.7 11.9 %copy-start.5 = (bf16[16,4096]{1,0:T(8,128)(2,1)}, bf16[16,4096]{1,0:T(8,128)(2,1)S(1)}, u32[]{:S(2)}) copy-start(bf16[16,4096]{1,0:T(8,128)(2,1)S(1)} %collective-permute-done.refs_1_) | copy-start | bytes 393220
  18.7 4.8 %collective-permute-start.4 = (bf16[16,4096]{1,0:T(8,128)(2,1)S(1)}, bf16[16,4096]{1,0:T(8,128)(2,1)S(1)}, u32[]{:S(2)}, u32[]{:S(2)}) collective-permute-start(bf16[16,4096]{1,0:T(8,128)(2,1)S(1)} %collective-permute-done.3.refs_4_), channel_id=1, source_target_pairs={{0,1},{1,0},{2,3},{3,2},{4,5},{5,4},{6,7},{7,6},{8,9},{9,8},{10,11... | collective-permute-start | bytes 393224 | tf_op jit(solution)/shard_map/ppermute | solution.py:178
  18.9 11.7 %copy-start.6 = (bf16[16,4096]{1,0:T(8,128)(2,1)}, bf16[16,4096]{1,0:T(8,128)(2,1)S(1)}, u32[]{:S(2)}) copy-start(bf16[16,4096]{1,0:T(8,128)(2,1)S(1)} %collective-permute-done.7.refs_8_) | copy-start | bytes 393220
  18.9 7.0 %collective-permute-start.9 = (bf16[16,4096]{1,0:T(8,128)(2,1)S(1)}, bf16[16,4096]{1,0:T(8,128)(2,1)S(1)}, u32[]{:S(2)}, u32[]{:S(2)}) collective-permute-start(bf16[16,4096]{1,0:T(8,128)(2,1)S(1)} %collective-permute-done.1.refs_2_), channel_id=1, source_target_pairs={{0,2},{1,3},{2,0},{3,1},{4,6},{5,7},{6,4},{7,5},{8,10},{9,11},{10,... | collective-permute-start | bytes 393224 | tf_op jit(solution)/shard_map/ppermute | solution.py:178
  19.4 11.2 %copy-start.7 = (bf16[16,4096]{1,0:T(8,128)(2,1)}, bf16[16,4096]{1,0:T(8,128)(2,1)S(1)}, u32[]{:S(2)}) copy-start(bf16[16,4096]{1,0:T(8,128)(2,1)S(1)} %collective-permute-done.13.refs_14_) | copy-start | bytes 393220
  19.4 8.9 %collective-permute-start.2 = (bf16[16,4096]{1,0:T(8,128)(2,1)S(1)}, bf16[16,4096]{1,0:T(8,128)(2,1)S(1)}, u32[]{:S(2)}, u32[]{:S(2)}) collective-permute-start(bf16[16,4096]{1,0:T(8,128)(2,1)S(1)} %collective-permute-done.1.refs_2_), channel_id=1, source_target_pairs={{0,1},{1,0},{2,3},{3,2},{4,5},{5,4},{6,7},{7,6},{8,9},{9,8},{10,11... | collective-permute-start | bytes 393224 | tf_op jit(solution)/shard_map/ppermute | solution.py:178
  19.5 11.1 %copy-start.8 = (bf16[16,4096]{1,0:T(8,128)(2,1)}, bf16[16,4096]{1,0:T(8,128)(2,1)S(1)}, u32[]{:S(2)}) copy-start(bf16[16,4096]{1,0:T(8,128)(2,1)S(1)} %collective-permute-done.6.refs_7_) | copy-start | bytes 393220
  19.5 11.0 %collective-permute-start.8 = (bf16[16,4096]{1,0:T(8,128)(2,1)S(1)}, bf16[16,4096]{1,0:T(8,128)(2,1)S(1)}, u32[]{:S(2)}, u32[]{:S(2)}) collective-permute-start(bf16[16,4096]{1,0:T(8,128)(2,1)S(1)} %collective-permute-done.7.refs_8_), channel_id=1, source_target_pairs={{0,1},{1,0},{2,3},{3,2},{4,5},{5,4},{6,7},{7,6},{8,9},{9,8},{10,11... | collective-permute-start | bytes 393224 | tf_op jit(solution)/shard_map/ppermute | solution.py:178
  23.5 7.1 %copy-start.9 = (bf16[16,4096]{1,0:T(8,128)(2,1)}, bf16[16,4096]{1,0:T(8,128)(2,1)S(1)}, u32[]{:S(2)}) copy-start(bf16[16,4096]{1,0:T(8,128)(2,1)S(1)} %collective-permute-done.11.refs_12_) | copy-start | bytes 393220
  23.5 7.0 %collective-permute-start.14 = (bf16[16,4096]{1,0:T(8,128)(2,1)S(1)}, bf16[16,4096]{1,0:T(8,128)(2,1)S(1)}, u32[]{:S(2)}, u32[]{:S(2)}) collective-permute-start(bf16[16,4096]{1,0:T(8,128)(2,1)S(1)} %collective-permute-done.13.refs_14_), channel_id=1, source_target_pairs={{0,1},{1,0},{2,3},{3,2},{4,5},{5,4},{6,7},{7,6},{8,9},{9,8},{10,11... | collective-permute-start | bytes 393224 | tf_op jit(solution)/shard_map/ppermute | solution.py:178
  23.5 7.1 %copy-start.10 = (bf16[16,4096]{1,0:T(8,128)(2,1)}, bf16[16,4096]{1,0:T(8,128)(2,1)S(1)}, u32[]{:S(2)}) copy-start(bf16[16,4096]{1,0:T(8,128)(2,1)S(1)} %collective-permute-done.4.refs_5_) | copy-start | bytes 393220
  23.6 7.0 %collective-permute-start.12 = (bf16[16,4096]{1,0:T(8,128)(2,1)S(1)}, bf16[16,4096]{1,0:T(8,128)(2,1)S(1)}, u32[]{:S(2)}, u32[]{:S(2)}) collective-permute-start(bf16[16,4096]{1,0:T(8,128)(2,1)S(1)} %collective-permute-done.11.refs_12_), channel_id=1, source_target_pairs={{0,1},{1,0},{2,3},{3,2},{4,5},{5,4},{6,7},{7,6},{8,9},{9,8},{10,11... | collective-permute-start | bytes 393224 | tf_op jit(solution)/shard_map/ppermute | solution.py:178
  25.9 4.8 %copy-start.11 = (bf16[16,4096]{1,0:T(8,128)(2,1)}, bf16[16,4096]{1,0:T(8,128)(2,1)S(1)}, u32[]{:S(2)}) copy-start(bf16[16,4096]{1,0:T(8,128)(2,1)S(1)} %collective-permute-done.9.refs_10_) | copy-start | bytes 393220
  25.9 4.7 %collective-permute-start.10 = (bf16[16,4096]{1,0:T(8,128)(2,1)S(1)}, bf16[16,4096]{1,0:T(8,128)(2,1)S(1)}, u32[]{:S(2)}, u32[]{:S(2)}) collective-permute-start(bf16[16,4096]{1,0:T(8,128)(2,1)S(1)} %collective-permute-done.9.refs_10_), channel_id=1, source_target_pairs={{0,1},{1,0},{2,3},{3,2},{4,5},{5,4},{6,7},{7,6},{8,9},{9,8},{10,11... | collective-permute-start | bytes 393224 | tf_op jit(solution)/shard_map/ppermute | solution.py:178
  28.3 2.3 %copy-start.12 = (bf16[16,4096]{1,0:T(8,128)(2,1)}, bf16[16,4096]{1,0:T(8,128)(2,1)S(1)}, u32[]{:S(2)}) copy-start(bf16[16,4096]{1,0:T(8,128)(2,1)S(1)} %collective-permute-done.2.refs_3_) | copy-start | bytes 393220
  28.3 27.2 %collective-permute-start.16 = (bf16[128,1792]{1,0:T(8,128)(2,1)}, bf16[128,1792]{1,0:T(8,128)(2,1)S(1)}, u32[]{:S(2)}, u32[]{:S(2)}) collective-permute-start(bf16[128,1792]{1,0:T(8,128)(2,1)} %refs_0_.3), channel_id=1, source_target_pairs={{0,16},{16,0},{1,17},{17,1},{2,18},{18,2},{3,19},{19,3},{4,20},{20... | collective-permute-start | bytes 1376264 | tf_op jit(solution)/shard_map/ppermute | solution.py:181
  30.5 0.7 copy-start.13
  30.5 0.7 copy-start.14
  30.5 0.7 %copy-start.15 = (bf16[16,4096]{1,0:T(8,128)(2,1)}, bf16[16,4096]{1,0:T(8,128)(2,1)S(1)}, u32[]{:S(2)}) copy-start(bf16[16,4096]{1,0:T(8,128)(2,1)S(1)} %collective-permute-done.12.refs_13_) | copy-start | bytes 393220
  30.6 0.8 %copy-start.16 = (bf16[16,4096]{1,0:T(8,128)(2,1)}, bf16[16,4096]{1,0:T(8,128)(2,1)S(1)}, u32[]{:S(2)}) copy-start(bf16[16,4096]{1,0:T(8,128)(2,1)S(1)} %collective-permute-done.10.refs_11_) | copy-start | bytes 393220
  43.7 22.7 %collective-permute-start.15 = (s16[1808,128]{1,0:T(8,128)(2,1)}, s16[1808,128]{1,0:T(8,128)(2,1)S(1)}, u32[]{:S(2)}, u32[]{:S(2)}) collective-permute-start(s16[1808,128]{1,0:T(8,128)(2,1)} %get-tuple-element.5), channel_id=1, source_target_pairs={{0,16},{16,0},{1,17},{17,1},{2,18},{18,2},{3,19},{19,3},{4,20},{20... | collective-permute-start | bytes 1388552 | tf_op jit(solution)/shard_map/ppermute | solution.py:181
  55.6 0.8 %copy-start.1 = (bf16[128,1792]{1,0:T(8,128)(2,1)}, bf16[128,1792]{1,0:T(8,128)(2,1)S(1)}, u32[]{:S(2)}) copy-start(bf16[128,1792]{1,0:T(8,128)(2,1)S(1)} %collective-permute-done.16.refs_1_) | copy-start | bytes 1376260
  66.4 0.8 %copy-start = (s16[1808,128]{1,0:T(8,128)(2,1)}, s16[1808,128]{1,0:T(8,128)(2,1)S(1)}, u32[]{:S(2)}) copy-start(s16[1808,128]{1,0:T(8,128)(2,1)S(1)} %collective-permute-done.15.refs_0_) | copy-start | bytes 1388548

commit v2 on v0

v2 whole, which is shorter than its diff:
```python
import functools

import jax
import jax.numpy as jnp
from jax import lax
from jax.experimental import pallas as pl
from jax.experimental.pallas import tpu as pltpu
from jax.sharding import PartitionSpec as P

BLOCK = 128
CODE = 32700.0
STEPS = 64.0
VMEM_LIMIT = 32 * 1024 * 1024


def pair_of(blocks):
    return 2 if blocks % 2 == 0 else 1


def chip_ring(cols):
    half, fast = cols // 2, 1
    while half % (fast * 2) == 0 and fast * 2 * fast * 2 <= half:
        fast *= 2
    slow = half // fast
    ring = []
    for s in range(slow):
        along = range(1, fast) if s % 2 == 0 else range(fast - 1, 0, -1)
        ring += [s * fast + f for f in along]
    ring += [s * fast for s in range(slow - 1, -1, -1)]
    return ring


def encode(part):
    top = jnp.max(jnp.abs(part), axis=0, keepdims=True)
    code = jnp.ceil(STEPS * jnp.log2(jnp.maximum(top, 1e-30)))
    scaled = part * (jnp.exp2(code * (-1.0 / STEPS)) * CODE)
    whole = jnp.clip(jnp.round(scaled), -32767.0, 32767.0)
    return whole.astype(jnp.int32), code.astype(jnp.int32)


def wide_mask(mask, first, width):
    cols = mask.shape[1]
    of_column = first + lax.broadcasted_iota(jnp.int32, (cols, width), 1) // BLOCK
    spread = of_column == lax.broadcasted_iota(jnp.int32, (cols, width), 0)
    return jnp.dot(
        mask.astype(jnp.float32).astype(jnp.bfloat16),
        spread.astype(jnp.float32).astype(jnp.bfloat16),
        preferred_element_type=jnp.float32,
    )


def terms_kernel(n_shards, n_parts, pair, chunk, idx, *refs):
    shards = refs[:n_shards]
    weight, mask, full, own = refs[n_shards : n_shards + 4]
    outs = refs[n_shards + 4 : n_shards + 4 + n_parts]
    turned, spread, codes = refs[n_shards + 4 + n_parts :]
    step = pl.program_id(0)
    tokens = own.shape[1]
    hidden = outs[0].shape[0] - codes.shape[1]
    width = full.shape[1]

    @pl.when(step == 0)
    def _():
        rows = shards[0].shape[0]
        for n, shard in enumerate(shards):
            full[pl.ds(pl.multiple_of(idx[n + 1] * rows, rows), rows), :] = shard[...]
        for c in range(0, width, chunk):
            turned[c : c + chunk, :] = full[:, c : c + chunk].T
        spread[...] = wide_mask(mask[...], idx[0] * (width // BLOCK), width)
        codes[...] = jnp.zeros_like(codes)

    kept = []
    for b in range(pair):
        factor = spread[pl.ds(step * pair + b, 1), :].astype(jnp.bfloat16)
        kept.append(weight[b * BLOCK : (b + 1) * BLOCK, :] * factor)
    kept = kept[0] if pair == 1 else jnp.concatenate(kept, axis=0)
    terms = jnp.dot(kept, turned[...], preferred_element_type=jnp.float32)
    own[...] = terms[:, :tokens]
    row_of_code = lax.broadcasted_iota(jnp.int32, codes.shape[1:], 0)
    for k in range(n_parts):
        for b in range(pair):
            block = step * pair + b
            whole, code = encode(
                terms[b * BLOCK : (b + 1) * BLOCK, (k + 1) * tokens : (k + 2) * tokens]
            )
            rows = pl.ds(pl.multiple_of(block * BLOCK, BLOCK), BLOCK)
            outs[k][rows, :] = whole.astype(jnp.int16)
            codes[k] = jnp.where(row_of_code == block, code, codes[k])

    @pl.when(step == pl.num_programs(0) - 1)
    def _():
        for k in range(n_parts):
            outs[k][hidden:, :] = codes[k].astype(jnp.int16)


def weight_grad_kernel(n_parts, idx, *refs):
    acts = refs[:n_parts]
    full, mask, out, turned = refs[n_parts:]
    step = pl.program_id(0)
    tokens, hidden = acts[0].shape
    width = full.shape[1]

    @pl.when(step == 0)
    def _():
        for k in range(n_parts):
            place = (n_parts - k) % n_parts
            for c in range(0, hidden, BLOCK):
                turned[c : c + BLOCK, place * tokens : (place + 1) * tokens] = (
                    acts[k][:, c : c + BLOCK].T
                )

    first = idx[0] * (pl.num_programs(0) * (width // BLOCK)) + step * (width // BLOCK)
    spread = wide_mask(mask[...], first, width)
    product = jnp.dot(turned[...], full[...], preferred_element_type=jnp.float32)
    for b in range(hidden // BLOCK):
        rows = slice(b * BLOCK, (b + 1) * BLOCK)
        out[rows, :] = (product[rows, :] * spread[b : b + 1, :]).astype(out.dtype)


def finish_kernel(n_parts, own, *refs):
    parts = refs[:n_parts]
    out = refs[n_parts]
    hidden = own.shape[0]
    scales = []
    for part in parts:
        code = part[hidden:, :].astype(jnp.int32).astype(jnp.float32)
        scales.append(jnp.exp2(code * (1.0 / STEPS)) * (1.0 / CODE))
    for i in range(hidden // BLOCK):
        rows = slice(i * BLOCK, (i + 1) * BLOCK)
        total = own[rows, :]
        for part, scale in zip(parts, scales, strict=True):
            got = part[rows, :].astype(jnp.int32).astype(jnp.float32)
            total = total + got * scale[i : i + 1, :]
        out[:, rows] = total.T.astype(out.dtype)


def in_vmem():
    return pl.BlockSpec(memory_space=pltpu.VMEM)


def in_smem():
    return pl.BlockSpec(memory_space=pltpu.SMEM)


def params():
    return pltpu.CompilerParams(vmem_limit_bytes=VMEM_LIMIT)


def per_device(n_rows, n_cols, grad_output, inputs, weight, block_mask):
    row, col = lax.axis_index("row"), lax.axis_index("col")
    hidden, width = weight.shape
    blocks = hidden // BLOCK
    pair = pair_of(blocks)
    n_parts = n_rows - 1
    tokens = inputs.shape[0]
    shard_rows = grad_output.shape[0]
    all_tokens = tokens * n_rows

    ring = chip_ring(n_cols)
    n_chips = len(ring)

    def send_ring(x, by):
        perm = []
        for p in range(n_chips):
            for core in range(2):
                q = (p + (by if core == 0 else -by)) % n_chips
                perm.append((ring[p] * 2 + core, ring[q] * 2 + core))
        return lax.ppermute(x, "col", perm)

    def send_core(x):
        return lax.ppermute(x, "col", [(c, c ^ 1) for c in range(n_cols)])

    def send_row(x, by):
        return lax.ppermute(x, "row", [(r, (r + by) % n_rows) for r in range(n_rows)])

    held = {0: grad_output}
    there, back = grad_output, grad_output
    for j in range(1, n_chips // 2 + 1):
        there = send_ring(there, 1)
        held[j] = there
        if 2 * j < n_chips:
            back = send_ring(back, -1)
            held[-j] = back
    acts = [inputs] + [send_row(inputs, k) for k in range(1, n_rows)]
    shards, steps = [], []
    for j, shard in held.items():
        shards += [shard, send_core(shard)]
        steps += [(j, 0), (j, 1)]

    table = []
    for c in range(n_cols):
        p, core = ring.index(c // 2), c % 2
        line = []
        for j, other in steps:
            of_core = core ^ other
            q = (p - j if of_core == 0 else p + j) % n_chips
            line.append(ring[q] * 2 + of_core)
        table.append(line)
    sources = lax.dynamic_index_in_dim(jnp.array(table, jnp.int32), col, 0, keepdims=False)
    places = (sources - row * (tokens // shard_rows)) % n_cols
    idx = jnp.concatenate([row.astype(jnp.int32).reshape(1), places.astype(jnp.int32)])

    n_shards = len(shards)
    code_rows = -(-blocks // 16) * 16
    sent_shape = jax.ShapeDtypeStruct((hidden + code_rows, tokens), jnp.int16)
    full, own, *coded = pl.pallas_call(
        functools.partial(terms_kernel, n_shards, n_parts, pair, min(512, width)),
        grid=(blocks // pair,),
        in_specs=[in_smem()]
        + [in_vmem()] * n_shards
        + [pl.BlockSpec((pair * BLOCK, width), lambda i: (i, 0)), in_vmem()],
        out_specs=[in_vmem(), pl.BlockSpec((pair * BLOCK, tokens), lambda i: (i, 0))]
        + [in_vmem()] * n_parts,
        out_shape=[
            jax.ShapeDtypeStruct((all_tokens, width), jnp.bfloat16),
            jax.ShapeDtypeStruct((hidden, tokens), jnp.float32),
        ]
        + [sent_shape] * n_parts,
        scratch_shapes=[
            pltpu.VMEM((width, all_tokens), jnp.bfloat16),
            pltpu.VMEM((blocks, width), jnp.float32),
            pltpu.VMEM((n_parts, code_rows, tokens), jnp.int32),
        ],
        compiler_params=params(),
        cost_estimate=pl.CostEstimate(
            flops=2 * all_tokens * hidden * width,
            bytes_accessed=2 * hidden * width,
            transcendentals=0,
        ),
        name="terms",
    )(idx, *shards, weight, block_mask)
    parts = [send_row(coded[k], k + 1) for k in range(n_parts)]

    columns = min(512, width)
    grad_weight = pl.pallas_call(
        functools.partial(weight_grad_kernel, n_rows),
        grid=(width // columns,),
        in_specs=[in_smem()]
        + [in_vmem()] * n_rows
        + [pl.BlockSpec((all_tokens, columns), lambda i: (0, i)), in_vmem()],
        out_specs=pl.BlockSpec((hidden, columns), lambda i: (0, i)),
        out_shape=jax.ShapeDtypeStruct((hidden, width), jnp.bfloat16),
        scratch_shapes=[pltpu.VMEM((hidden, all_tokens), jnp.bfloat16)],
        compiler_params=params(),
        cost_estimate=pl.CostEstimate(
            flops=2 * all_tokens * hidden * width,
            bytes_accessed=2 * hidden * width,
            transcendentals=0,
        ),
        name="weight_grad",
    )(idx, *acts, full, block_mask)

    grad_input = pl.pallas_call(
        functools.partial(finish_kernel, n_parts),
        in_specs=[in_vmem()] * (1 + n_parts),
        out_specs=in_vmem(),
        out_shape=jax.ShapeDtypeStruct((tokens, hidden), jnp.bfloat16),
        compiler_params=params(),
        name="add_terms",
    )(own, *parts)
    return (grad_input, grad_weight)


def solution(mesh):
    return jax.shard_map(
        functools.partial(per_device, mesh.shape["row"], mesh.shape["col"]),
        mesh=mesh,
        in_specs=(P("col", "row"), P("row", "col"), P("col", "row"), P("col", None)),
        out_specs=(P("row", "col"), P("col", "row")),
        check_vma=False,
    )
```

time: 144 us -> 55.2 us (0.38)
  matrix products: 38.1 us -> 0 us
  waiting for transfers between devices: 46.3 us -> 19.4 us
  blocking collectives: 20.9 us -> 0 us
  Pallas kernels: 0 us -> 17 us
  local copies, waits for them, and re-layouts: 22.1 us -> 6.77 us
  between operations: 14.1 us -> 0.69 us
  starting transfers between devices: 0.08 us -> 10.4 us
    all_gather x1 -> x0, waiting for transfers between devices: 45.6 us -> none  [per_device(): grads_all = lax.all_gather(grad_output, 'col', axis=0, tiled=True)]
    dot_general x2 -> x0, matrix products: 38.1 us -> none  [the longest x1 23.8 us: per_device(): lax.dot_general(inputs_all, grads_all, (((0,), (0,)), ((), ())), preferre...]
    mul x2 -> x0, local copies, waits for them, and re-layouts: 21.1 us -> none  [the longest x1 13.7 us: per_device(): product.reshape(rows // BLOCK, BLOCK, cols // BLOCK, BLOCK) * factor]
    all_gather x1 -> x0, blocking collectives: 20.9 us -> none  [per_device(): inputs_all = lax.all_gather(inputs, 'row', axis=0, tiled=True)]
    ppermute x0 -> x17, waiting for transfers between devices: none -> 19.4 us  [the longest x7 16.3 us: send_ring(): return lax.ppermute(x, 'col', perm)]
    pallas_call x0 -> x3, Pallas kernels: none -> 17 us  [the longest x1 9.16 us: per_device(): pl.pallas_call(functools.partial(weight_grad_kernel, n_rows), grid=(width...]
    ppermute x0 -> x17, starting transfers between devices: none -> 10.4 us  [the longest x7 6.82 us: send_ring(): return lax.ppermute(x, 'col', perm)]
    unnamed x5 -> x8, local copies, waits for them, and re-layouts: 0.99 us -> 6.77 us
  transfers between devices with their start and end apart: 2 -> 17, of which waited for: 1 -> 7; matrix products, arithmetic and copies ran while one was open for 27% -> 1% of each run, Pallas kernels for 0% -> 29%
where the time goes in v2:
time: 55.2 us; the launch traced here: 55 us
  waiting for transfers between devices  19.4 us (35%)
  Pallas kernels  17 us (31%)
  starting transfers between devices  10.4 us (19%)
  local copies, waits for them, and re-layouts  6.77 us (12%)
  other arithmetic  0.78 us (1%)
  between operations  0.69 us (1%)
    ppermute x7, waiting for transfers between devices, send_ring(): return lax.ppermute(x, 'col', perm)  16.3 us
    pallas_call x1, Pallas kernels, per_device(): pl.pallas_call(functools.partial(weight_grad_kernel, n_rows), grid=(width...  9.16 us
    ppermute x7, starting transfers between devices, send_ring(): return lax.ppermute(x, 'col', perm)  6.82 us
    pallas_call x1, Pallas kernels, per_device(): pl.pallas_call(functools.partial(terms_kernel, n_shards, n_parts, pair, m...  6.8 us
    unnamed x8, local copies, waits for them, and re-layouts  6.77 us
    ppermute x2, waiting for transfers between devices, send_row(): lax.ppermute(x, 'row', [(r, (r + by) % n_rows) for r in range(n_rows)])  3.04 us
    ppermute x2, starting transfers between devices, send_row(): lax.ppermute(x, 'row', [(r, (r + by) % n_rows) for r in range(n_rows)])  2.45 us
  transfers between devices with their start and end apart: 17, of which 7 were waited for; matrix products, arithmetic and copies ran while one was open for 1% of the time, Pallas kernels for 29%

profile of v2, /device:TPU:0, one launch (start us, length us, event | category | flops | bytes accessed | tf_op | source)
XLA Modules:
  0.0 55.0 jit_solution(6378567390273875239)
XLA Ops:
  0.6 3.0 %collective-permute-start.1 = (bf16[16,4096]{1,0:T(8,128)(2,1)}, bf16[16,4096]{1,0:T(8,128)(2,1)S(1)}, u32[]{:S(2)}, u32[]{:S(2)}) collective-permute-start(bf16[16,4096]{1,0:T(8,128)(2,1)} %refs_0_.2), channel_id=1, source_target_pairs={{2,6},{3,1},{6,10},{7,3},{10,14},{11,7},{14,12},{15,11},{12,8},{13... | collective-permute-start | bytes 393224 | tf_op jit(solution)/shard_map/ppermute | solution.py:168
  3.6 0.2 collective-permute-start.3
  3.8 4.0 %collective-permute-done.1.refs_2_ = bf16[16,4096]{1,0:T(8,128)(2,1)S(1)} collective-permute-done((bf16[16,4096]{1,0:T(8,128)(2,1)}, bf16[16,4096]{1,0:T(8,128)(2,1)S(1)}, u32[]{:S(2)}, u32[]{:S(2)}) %collective-permute-start.1) | collective-permute-done | bytes 131104 | tf_op jit(solution)/shard_map/ppermute | solution.py:168
  7.7 1.5 %collective-permute-start.5 = (bf16[16,4096]{1,0:T(8,128)(2,1)S(1)}, bf16[16,4096]{1,0:T(8,128)(2,1)S(1)}, u32[]{:S(2)}, u32[]{:S(2)}) collective-permute-start(bf16[16,4096]{1,0:T(8,128)(2,1)S(1)} %collective-permute-done.1.refs_2_), channel_id=1, source_target_pairs={{2,6},{3,1},{6,10},{7,3},{10,14},{11,7},{14,12},{15,11},{12,8},{13... | collective-permute-start | bytes 393224 | tf_op jit(solution)/shard_map/ppermute | solution.py:168
  9.2 0.0 collective-permute-done.3.refs_4_
  9.2 0.9 %collective-permute-start.7 = (bf16[16,4096]{1,0:T(8,128)(2,1)S(1)}, bf16[16,4096]{1,0:T(8,128)(2,1)S(1)}, u32[]{:S(2)}, u32[]{:S(2)}) collective-permute-start(bf16[16,4096]{1,0:T(8,128)(2,1)S(1)} %collective-permute-done.3.refs_4_), channel_id=1, source_target_pairs={{2,0},{3,7},{6,2},{7,11},{10,6},{11,15},{14,10},{15,13},{12,14},{1... | collective-permute-start | bytes 393224 | tf_op jit(solution)/shard_map/ppermute | solution.py:168
  10.1 3.8 %collective-permute-done.5.refs_6_ = bf16[16,4096]{1,0:T(8,128)(2,1)S(1)} collective-permute-done((bf16[16,4096]{1,0:T(8,128)(2,1)S(1)}, bf16[16,4096]{1,0:T(8,128)(2,1)S(1)}, u32[]{:S(2)}, u32[]{:S(2)}) %collective-permute-start.5) | collective-permute-done | bytes 131104 | tf_op jit(solution)/shard_map/ppermute | solution.py:168
  13.9 0.3 collective-permute-start.9
  14.2 0.0 collective-permute-start
  14.2 0.5 collective-permute-start.2
  14.7 0.0 collective-permute-start.4
  14.7 0.8 %collective-permute-done.7.refs_8_ = bf16[16,4096]{1,0:T(8,128)(2,1)S(1)} collective-permute-done((bf16[16,4096]{1,0:T(8,128)(2,1)S(1)}, bf16[16,4096]{1,0:T(8,128)(2,1)S(1)}, u32[]{:S(2)}, u32[]{:S(2)}) %collective-permute-start.7) | collective-permute-done | bytes 131104 | tf_op jit(solution)/shard_map/ppermute | solution.py:168
  15.4 1.0 %collective-permute-start.11 = (bf16[16,4096]{1,0:T(8,128)(2,1)S(1)}, bf16[16,4096]{1,0:T(8,128)(2,1)S(1)}, u32[]{:S(2)}, u32[]{:S(2)}) collective-permute-start(bf16[16,4096]{1,0:T(8,128)(2,1)S(1)} %collective-permute-done.7.refs_8_), channel_id=1, source_target_pairs={{2,0},{3,7},{6,2},{7,11},{10,6},{11,15},{14,10},{15,13},{12,14},{1... | collective-permute-start | bytes 393224 | tf_op jit(solution)/shard_map/ppermute | solution.py:168
  16.4 3.5 %collective-permute-done.9.refs_10_ = bf16[16,4096]{1,0:T(8,128)(2,1)S(1)} collective-permute-done((bf16[16,4096]{1,0:T(8,128)(2,1)S(1)}, bf16[16,4096]{1,0:T(8,128)(2,1)S(1)}, u32[]{:S(2)}, u32[]{:S(2)}) %collective-permute-start.9) | collective-permute-done | bytes 131104 | tf_op jit(solution)/shard_map/ppermute | solution.py:168
  19.9 0.0 collective-permute-start.13
  19.9 0.0 collective-permute-done.refs_1_
  19.9 0.0 collective-permute-start.6
  19.9 0.0 collective-permute-done.2.refs_3_
  20.0 0.5 collective-permute-start.8
  20.5 0.0 collective-permute-done.4.refs_5_
  20.5 0.1 collective-permute-start.10
  20.5 1.1 %collective-permute-done.11.refs_12_ = bf16[16,4096]{1,0:T(8,128)(2,1)S(1)} collective-permute-done((bf16[16,4096]{1,0:T(8,128)(2,1)S(1)}, bf16[16,4096]{1,0:T(8,128)(2,1)S(1)}, u32[]{:S(2)}, u32[]{:S(2)}) %collective-permute-start.11) | collective-permute-done | bytes 131104 | tf_op jit(solution)/shard_map/ppermute | solution.py:168
  21.7 0.0 collective-permute-start.12
  21.7 3.2 %collective-permute-done.13.refs_14_ = bf16[16,4096]{1,0:T(8,128)(2,1)S(1)} collective-permute-done((bf16[16,4096]{1,0:T(8,128)(2,1)S(1)}, bf16[16,4096]{1,0:T(8,128)(2,1)S(1)}, u32[]{:S(2)}, u32[]{:S(2)}) %collective-permute-start.13) | collective-permute-done | bytes 131104 | tf_op jit(solution)/shard_map/ppermute | solution.py:168
  24.9 0.0 collective-permute-start.14
  24.9 0.7 %and_select_fusion = s32[16]{0:T(128)S(1)} fusion(s32[16,16]{1,0:T(8,128)} %constant.32.clone, s32[]{:T(128)S(6)} %select_n.11, s32[]{:T(128)S(6)} %mul.3), kind=kLoop, calls=%fused_computation.2 | loop fusion | flops 192 | bytes 136 | tf_op jit(solution)/shard_map/jit(remainder)/select_n | solution.py:200
  25.6 0.1 pad_add_fusion.idx
  25.7 0.0 collective-permute-done.6.refs_7_
  25.7 1.9 %collective-permute-start.16 = (bf16[128,1792]{1,0:T(8,128)(2,1)}, bf16[128,1792]{1,0:T(8,128)(2,1)S(1)}, u32[]{:S(2)}, u32[]{:S(2)}) collective-permute-start(bf16[128,1792]{1,0:T(8,128)(2,1)} %refs_0_.3), channel_id=1, source_target_pairs={{0,16},{16,0},{1,17},{17,1},{2,18},{18,2},{3,19},{19,3},{4,20},{20... | collective-permute-start | bytes 1376264 | tf_op jit(solution)/shard_map/ppermute | solution.py:174
  27.5 0.0 collective-permute-done.8.refs_9_
  27.5 0.0 collective-permute-done.10.refs_11_
  27.5 0.0 collective-permute-done.12.refs_13_
  27.6 0.0 collective-permute-done.14.refs_15_
  27.6 0.0 copy-start
  27.6 5.2 %copy-done = bf16[1792,4096]{1,0:T(8,128)(2,1)S(1)} copy-done((bf16[1792,4096]{1,0:T(8,128)(2,1)S(1)}, bf16[1792,4096]{1,0:T(8,128)(2,1)}, u32[]{:S(2)}) %copy-start) | copy-done | bytes 14680088
  32.7 0.0 copy-start.2
  32.7 0.9 %copy-done.2 = bf16[16,4096]{1,0:T(8,128)(2,1)S(1)} copy-done((bf16[16,4096]{1,0:T(8,128)(2,1)S(1)}, bf16[16,4096]{1,0:T(8,128)(2,1)}, u32[]{:S(2)}) %copy-start.2) | copy-done | bytes 131096
  33.6 0.0 copy-start.3
  33.6 0.7 %copy-done.3 = s32[14,64]{1,0:T(8,128)S(1)} copy-done((s32[14,64]{1,0:T(8,128)S(1)}, s32[14,64]{1,0:T(8,128)}, u32[]{:S(2)}) %copy-start.3) | copy-done | bytes 3608
  34.3 0.0 copy-start.1
  34.3 6.8 %terms.1 = (bf16[256,4096]{1,0:T(8,128)(2,1)S(1)}, f32[1792,128]{1,0:T(8,128)S(1)}, s16[1808,128]{1,0:T(8,128)(2,1)S(1)}) custom-call(s32[17]{0:T(128)S(1)} %pad_add_fusion.idx, bf16[16,4096]{1,0:T(8,128)(2,1)S(1)} %copy-done.2, bf16[16,4096]{1,0:T(8,128)(2,1)S(1)} %collective-permute-done.refs_1_, bf16[16,4096]{1,0:T(8,128)(2,1)S(1)} %collective-permute-done.1.refs_2_, ...), custom_call_target="tpu_custom_call" | custom-call | flops 3758096384 | bytes 14680064 | tf_op jit(solution)/shard_map/terms/pallas_call | solution.py:206
  41.2 0.6 %collective-permute-start.15 = (s16[1808,128]{1,0:T(8,128)(2,1)S(1)}, s16[1808,128]{1,0:T(8,128)(2,1)S(1)}, u32[]{:S(2)}, u32[]{:S(2)}) collective-permute-start(s16[1808,128]{1,0:T(8,128)(2,1)S(1)} %get-tuple-element.6), channel_id=1, source_target_pairs={{0,16},{16,0},{1,17},{17,1},{2,18},{18,2},{3,19},{19,3},{4,20},{20... | collective-permute-start | bytes 1388552 | tf_op jit(solution)/shard_map/ppermute | solution.py:174
  41.7 0.0 collective-permute-done.16.refs_1_
  41.8 0.0 copy-done.1
  41.8 9.2 %weight_grad.1 = bf16[1792,4096]{1,0:T(8,128)(2,1)} custom-call(s32[17]{0:T(128)S(1)} %pad_add_fusion.idx, bf16[128,1792]{1,0:T(8,128)(2,1)S(1)} %copy-done.1, bf16[128,1792]{1,0:T(8,128)(2,1)S(1)} %collective-permute-done.16.refs_1_, bf16[256,4096]{1,0:T(8,128)(2,1)S(1)} %get-tuple-element.7.refs_2_, s32[14,64]{1,0:T(8,128)S(1)} %copy-done.3), custom_call_target="tpu_custom_call" | custom-call | flops 3758096384 | bytes 14680064 | tf_op jit(solution)/shard_map/weight_grad/pallas_call | solution.py:235
  50.9 3.0 %collective-permute-done.15.refs_0_ = s16[1808,128]{1,0:T(8,128)(2,1)S(1)} collective-permute-done((s16[1808,128]{1,0:T(8,128)(2,1)S(1)}, s16[1808,128]{1,0:T(8,128)(2,1)S(1)}, u32[]{:S(2)}, u32[]{:S(2)}) %collective-permute-start.15) | collective-permute-done | bytes 462880 | tf_op jit(solution)/shard_map/ppermute | solution.py:174
  54.0 1.0 %add_terms.1 = bf16[128,1792]{1,0:T(8,128)(2,1)} custom-call(f32[1792,128]{1,0:T(8,128)S(1)} %get-tuple-element.5.own, s16[1808,128]{1,0:T(8,128)(2,1)S(1)} %collective-permute-done.15.refs_0_), custom_call_target="tpu_custom_call" | custom-call | tf_op jit(solution)/shard_map/add_terms/pallas_call | solution.py:253
Async XLA Ops:
  0.6 7.1 %collective-permute-start.1 = (bf16[16,4096]{1,0:T(8,128)(2,1)}, bf16[16,4096]{1,0:T(8,128)(2,1)S(1)}, u32[]{:S(2)}, u32[]{:S(2)}) collective-permute-start(bf16[16,4096]{1,0:T(8,128)(2,1)} %refs_0_.2), channel_id=1, source_target_pairs={{2,6},{3,1},{6,10},{7,3},{10,14},{11,7},{14,12},{15,11},{12,8},{13... | collective-permute-start | bytes 393224 | tf_op jit(solution)/shard_map/ppermute | solution.py:168
  3.6 5.6 %collective-permute-start.3 = (bf16[16,4096]{1,0:T(8,128)(2,1)}, bf16[16,4096]{1,0:T(8,128)(2,1)S(1)}, u32[]{:S(2)}, u32[]{:S(2)}) collective-permute-start(bf16[16,4096]{1,0:T(8,128)(2,1)} %refs_0_.2), channel_id=1, source_target_pairs={{2,0},{3,7},{6,2},{7,11},{10,6},{11,15},{14,10},{15,13},{12,14},{1... | collective-permute-start | bytes 393224 | tf_op jit(solution)/shard_map/ppermute | solution.py:168
  7.7 6.2 %collective-permute-start.5 = (bf16[16,4096]{1,0:T(8,128)(2,1)S(1)}, bf16[16,4096]{1,0:T(8,128)(2,1)S(1)}, u32[]{:S(2)}, u32[]{:S(2)}) collective-permute-start(bf16[16,4096]{1,0:T(8,128)(2,1)S(1)} %collective-permute-done.1.refs_2_), channel_id=1, source_target_pairs={{2,6},{3,1},{6,10},{7,3},{10,14},{11,7},{14,12},{15,11},{12,8},{13... | collective-permute-start | bytes 393224 | tf_op jit(solution)/shard_map/ppermute | solution.py:168
  9.2 6.2 %collective-permute-start.7 = (bf16[16,4096]{1,0:T(8,128)(2,1)S(1)}, bf16[16,4096]{1,0:T(8,128)(2,1)S(1)}, u32[]{:S(2)}, u32[]{:S(2)}) collective-permute-start(bf16[16,4096]{1,0:T(8,128)(2,1)S(1)} %collective-permute-done.3.refs_4_), channel_id=1, source_target_pairs={{2,0},{3,7},{6,2},{7,11},{10,6},{11,15},{14,10},{15,13},{12,14},{1... | collective-permute-start | bytes 393224 | tf_op jit(solution)/shard_map/ppermute | solution.py:168
  13.9 6.0 %collective-permute-start.9 = (bf16[16,4096]{1,0:T(8,128)(2,1)S(1)}, bf16[16,4096]{1,0:T(8,128)(2,1)S(1)}, u32[]{:S(2)}, u32[]{:S(2)}) collective-permute-start(bf16[16,4096]{1,0:T(8,128)(2,1)S(1)} %collective-permute-done.5.refs_6_), channel_id=1, source_target_pairs={{2,6},{3,1},{6,10},{7,3},{10,14},{11,7},{14,12},{15,11},{12,8},{13... | collective-permute-start | bytes 393224 | tf_op jit(solution)/shard_map/ppermute | solution.py:168
  14.2 5.8 %collective-permute-start = (bf16[16,4096]{1,0:T(8,128)(2,1)}, bf16[16,4096]{1,0:T(8,128)(2,1)S(1)}, u32[]{:S(2)}, u32[]{:S(2)}) collective-permute-start(bf16[16,4096]{1,0:T(8,128)(2,1)} %refs_0_.2), channel_id=1, source_target_pairs={{0,1},{1,0},{2,3},{3,2},{4,5},{5,4},{6,7},{7,6},{8,9},{9,8},{10,11... | collective-permute-start | bytes 393224 | tf_op jit(solution)/shard_map/ppermute | solution.py:171
  14.2 5.8 %collective-permute-start.2 = (bf16[16,4096]{1,0:T(8,128)(2,1)S(1)}, bf16[16,4096]{1,0:T(8,128)(2,1)S(1)}, u32[]{:S(2)}, u32[]{:S(2)}) collective-permute-start(bf16[16,4096]{1,0:T(8,128)(2,1)S(1)} %collective-permute-done.1.refs_2_), channel_id=1, source_target_pairs={{0,1},{1,0},{2,3},{3,2},{4,5},{5,4},{6,7},{7,6},{8,9},{9,8},{10,11... | collective-permute-start | bytes 393224 | tf_op jit(solution)/shard_map/ppermute | solution.py:171
  14.7 5.8 %collective-permute-start.4 = (bf16[16,4096]{1,0:T(8,128)(2,1)S(1)}, bf16[16,4096]{1,0:T(8,128)(2,1)S(1)}, u32[]{:S(2)}, u32[]{:S(2)}) collective-permute-start(bf16[16,4096]{1,0:T(8,128)(2,1)S(1)} %collective-permute-done.3.refs_4_), channel_id=1, source_target_pairs={{0,1},{1,0},{2,3},{3,2},{4,5},{5,4},{6,7},{7,6},{8,9},{9,8},{10,11... | collective-permute-start | bytes 393224 | tf_op jit(solution)/shard_map/ppermute | solution.py:171
  15.4 6.2 %collective-permute-start.11 = (bf16[16,4096]{1,0:T(8,128)(2,1)S(1)}, bf16[16,4096]{1,0:T(8,128)(2,1)S(1)}, u32[]{:S(2)}, u32[]{:S(2)}) collective-permute-start(bf16[16,4096]{1,0:T(8,128)(2,1)S(1)} %collective-permute-done.7.refs_8_), channel_id=1, source_target_pairs={{2,0},{3,7},{6,2},{7,11},{10,6},{11,15},{14,10},{15,13},{12,14},{1... | collective-permute-start | bytes 393224 | tf_op jit(solution)/shard_map/ppermute | solution.py:168
  19.9 5.0 %collective-permute-start.13 = (bf16[16,4096]{1,0:T(8,128)(2,1)S(1)}, bf16[16,4096]{1,0:T(8,128)(2,1)S(1)}, u32[]{:S(2)}, u32[]{:S(2)}) collective-permute-start(bf16[16,4096]{1,0:T(8,128)(2,1)S(1)} %collective-permute-done.9.refs_10_), channel_id=1, source_target_pairs={{2,6},{3,1},{6,10},{7,3},{10,14},{11,7},{14,12},{15,11},{12,8},{13... | collective-permute-start | bytes 393224 | tf_op jit(solution)/shard_map/ppermute | solution.py:168
  19.9 5.7 %collective-permute-start.6 = (bf16[16,4096]{1,0:T(8,128)(2,1)S(1)}, bf16[16,4096]{1,0:T(8,128)(2,1)S(1)}, u32[]{:S(2)}, u32[]{:S(2)}) collective-permute-start(bf16[16,4096]{1,0:T(8,128)(2,1)S(1)} %collective-permute-done.5.refs_6_), channel_id=1, source_target_pairs={{0,1},{1,0},{2,3},{3,2},{4,5},{5,4},{6,7},{7,6},{8,9},{9,8},{10,11... | collective-permute-start | bytes 393224 | tf_op jit(solution)/shard_map/ppermute | solution.py:171
  20.0 7.6 %collective-permute-start.8 = (bf16[16,4096]{1,0:T(8,128)(2,1)S(1)}, bf16[16,4096]{1,0:T(8,128)(2,1)S(1)}, u32[]{:S(2)}, u32[]{:S(2)}) collective-permute-start(bf16[16,4096]{1,0:T(8,128)(2,1)S(1)} %collective-permute-done.7.refs_8_), channel_id=1, source_target_pairs={{0,1},{1,0},{2,3},{3,2},{4,5},{5,4},{6,7},{7,6},{8,9},{9,8},{10,11... | collective-permute-start | bytes 393224 | tf_op jit(solution)/shard_map/ppermute | solution.py:171
  20.5 7.1 %collective-permute-start.10 = (bf16[16,4096]{1,0:T(8,128)(2,1)S(1)}, bf16[16,4096]{1,0:T(8,128)(2,1)S(1)}, u32[]{:S(2)}, u32[]{:S(2)}) collective-permute-start(bf16[16,4096]{1,0:T(8,128)(2,1)S(1)} %collective-permute-done.9.refs_10_), channel_id=1, source_target_pairs={{0,1},{1,0},{2,3},{3,2},{4,5},{5,4},{6,7},{7,6},{8,9},{9,8},{10,11... | collective-permute-start | bytes 393224 | tf_op jit(solution)/shard_map/ppermute | solution.py:171
  21.7 5.9 %collective-permute-start.12 = (bf16[16,4096]{1,0:T(8,128)(2,1)S(1)}, bf16[16,4096]{1,0:T(8,128)(2,1)S(1)}, u32[]{:S(2)}, u32[]{:S(2)}) collective-permute-start(bf16[16,4096]{1,0:T(8,128)(2,1)S(1)} %collective-permute-done.11.refs_12_), channel_id=1, source_target_pairs={{0,1},{1,0},{2,3},{3,2},{4,5},{5,4},{6,7},{7,6},{8,9},{9,8},{10,11... | collective-permute-start | bytes 393224 | tf_op jit(solution)/shard_map/ppermute | solution.py:171
  24.9 2.7 %collective-permute-start.14 = (bf16[16,4096]{1,0:T(8,128)(2,1)S(1)}, bf16[16,4096]{1,0:T(8,128)(2,1)S(1)}, u32[]{:S(2)}, u32[]{:S(2)}) collective-permute-start(bf16[16,4096]{1,0:T(8,128)(2,1)S(1)} %collective-permute-done.13.refs_14_), channel_id=1, source_target_pairs={{0,1},{1,0},{2,3},{3,2},{4,5},{5,4},{6,7},{7,6},{8,9},{9,8},{10,11... | collective-permute-start | bytes 393224 | tf_op jit(solution)/shard_map/ppermute | solution.py:171
  25.7 16.1 %collective-permute-start.16 = (bf16[128,1792]{1,0:T(8,128)(2,1)}, bf16[128,1792]{1,0:T(8,128)(2,1)S(1)}, u32[]{:S(2)}, u32[]{:S(2)}) collective-permute-start(bf16[128,1792]{1,0:T(8,128)(2,1)} %refs_0_.3), channel_id=1, source_target_pairs={{0,16},{16,0},{1,17},{17,1},{2,18},{18,2},{3,19},{19,3},{4,20},{20... | collective-permute-start | bytes 1376264 | tf_op jit(solution)/shard_map/ppermute | solution.py:174
  27.6 5.2 %copy-start = (bf16[1792,4096]{1,0:T(8,128)(2,1)S(1)}, bf16[1792,4096]{1,0:T(8,128)(2,1)}, u32[]{:S(2)}) copy-start(bf16[1792,4096]{1,0:T(8,128)(2,1)} %refs_16_.1) | copy-start | bytes 44040196
  32.7 0.9 %copy-start.2 = (bf16[16,4096]{1,0:T(8,128)(2,1)S(1)}, bf16[16,4096]{1,0:T(8,128)(2,1)}, u32[]{:S(2)}) copy-start(bf16[16,4096]{1,0:T(8,128)(2,1)} %refs_0_.2) | copy-start | bytes 393220
  33.6 0.7 %copy-start.3 = (s32[14,64]{1,0:T(8,128)S(1)}, s32[14,64]{1,0:T(8,128)}, u32[]{:S(2)}) copy-start(s32[14,64]{1,0:T(8,128)} %refs_3_.1) | copy-start | bytes 10756
  34.3 7.4 %copy-start.1 = (bf16[128,1792]{1,0:T(8,128)(2,1)S(1)}, bf16[128,1792]{1,0:T(8,128)(2,1)}, u32[]{:S(2)}) copy-start(bf16[128,1792]{1,0:T(8,128)(2,1)} %refs_0_.3) | copy-start | bytes 1376260
  41.2 12.8 %collective-permute-start.15 = (s16[1808,128]{1,0:T(8,128)(2,1)S(1)}, s16[1808,128]{1,0:T(8,128)(2,1)S(1)}, u32[]{:S(2)}, u32[]{:S(2)}) collective-permute-start(s16[1808,128]{1,0:T(8,128)(2,1)S(1)} %get-tuple-element.6), channel_id=1, source_target_pairs={{0,16},{16,0},{1,17},{17,1},{2,18},{18,2},{3,19},{19,3},{4,20},{20... | collective-permute-start | bytes 1388552 | tf_op jit(solution)/shard_map/ppermute | solution.py:174

commit v3 on v2

v3 whole, which is shorter than its diff:
```python
import functools

import jax
import jax.numpy as jnp
from jax import lax
from jax.experimental import pallas as pl
from jax.experimental.pallas import tpu as pltpu
from jax.sharding import PartitionSpec as P

BLOCK = 128
CODE = 32700.0
STEPS = 64.0
VMEM_LIMIT = 32 * 1024 * 1024


def chip_ring(cols):
    half, fast = cols // 2, 1
    while half % (fast * 2) == 0 and fast * 2 * fast * 2 <= half:
        fast *= 2
    slow = half // fast
    ring = []
    for s in range(slow):
        along = range(1, fast) if s % 2 == 0 else range(fast - 1, 0, -1)
        ring += [s * fast + f for f in along]
    ring += [s * fast for s in range(slow - 1, -1, -1)]
    return ring


def encode(part):
    top = jnp.max(jnp.abs(part), axis=0, keepdims=True)
    code = jnp.ceil(STEPS * jnp.log2(jnp.maximum(top, 1e-30)))
    scaled = part * (jnp.exp2(code * (-1.0 / STEPS)) * CODE)
    whole = jnp.clip(jnp.round(scaled), -32767.0, 32767.0)
    return whole.astype(jnp.int32), code.astype(jnp.int32)


def wide_mask(mask, first, width):
    cols = mask.shape[1]
    of_column = first + lax.broadcasted_iota(jnp.int32, (cols, width), 1) // BLOCK
    spread = of_column == lax.broadcasted_iota(jnp.int32, (cols, width), 0)
    return jnp.dot(
        mask.astype(jnp.float32).astype(jnp.bfloat16),
        spread.astype(jnp.float32).astype(jnp.bfloat16),
        preferred_element_type=jnp.float32,
    )


def keep_kernel(idx, shard, weight, mask, kept, shard_copy, sems):
    rows, width = kept.shape
    blocks = rows // BLOCK
    copies = []
    for b in range(blocks):
        at = pl.ds(b * BLOCK, BLOCK)
        copies.append(pltpu.make_async_copy(weight.at[at, :], kept.at[at, :], sems.at[b]))
        copies[-1].start()
    shard_copy[...] = shard[...]
    spread = wide_mask(mask[...], idx[0] * (width // BLOCK), width).astype(jnp.bfloat16)
    for b in range(blocks):
        copies[b].wait()
        at = slice(b * BLOCK, (b + 1) * BLOCK)
        kept[at, :] = kept[at, :] * spread[b : b + 1, :]


def turn_kernel(n_rows, *refs):
    acts, out = refs[:n_rows], refs[n_rows]
    tokens, hidden = acts[0].shape
    for k in range(n_rows):
        place = (n_rows - k) % n_rows
        for c in range(0, hidden, BLOCK):
            out[c : c + BLOCK, place * tokens : (place + 1) * tokens] = acts[k][:, c : c + BLOCK].T


def store_terms(total, own, outs):
    rows, tokens = own.shape
    own[...] = total[:, :tokens]
    for k, out in enumerate(outs):
        of_code = lax.broadcasted_iota(jnp.int32, (out.shape[0] - rows, tokens), 0)
        codes = jnp.zeros(of_code.shape, jnp.int32)
        for b in range(rows // BLOCK):
            at = slice(b * BLOCK, (b + 1) * BLOCK)
            whole, code = encode(total[at, (k + 1) * tokens : (k + 2) * tokens])
            out[at, :] = whole.astype(jnp.int16)
            codes = jnp.where(of_code == b, code, codes)
        out[rows:, :] = codes.astype(jnp.int16)


def first_terms_kernel(n_shards, n_parts, chunk, idx, *refs):
    shards = refs[:n_shards]
    kept, _, full, turned, own = refs[n_shards : n_shards + 5]
    outs = refs[n_shards + 5 : n_shards + 5 + n_parts]
    total = refs[n_shards + 5 + n_parts]
    rows = shards[0].shape[0]
    for n, shard in enumerate(shards):
        full[pl.ds(pl.multiple_of(idx[n + 1] * rows, rows), rows), :] = shard[...]
    for c in range(0, full.shape[1], chunk):
        turned[c : c + chunk, :] = full[:, c : c + chunk].T
        terms = jnp.dot(
            kept[:, c : c + chunk], turned[c : c + chunk, :], preferred_element_type=jnp.float32
        )
        total[...] = terms if c == 0 else total[...] + terms
    store_terms(total, own, outs)


def more_terms_kernel(n_parts, first_block, idx, turned, weight, mask, own, *refs):
    outs, total = refs[:n_parts], refs[n_parts]
    step = pl.program_id(0)
    rows, chunk = weight.shape
    per_row = pl.num_programs(0) * (chunk // BLOCK)
    first = idx[0] * per_row + step * (chunk // BLOCK)
    spread = wide_mask(mask[...], first, chunk).astype(jnp.bfloat16)
    kept = []
    for b in range(rows // BLOCK):
        at = first_block + b
        kept.append(weight[b * BLOCK : (b + 1) * BLOCK, :] * spread[at : at + 1, :])
    terms = jnp.dot(
        jnp.concatenate(kept, axis=0), turned[...], preferred_element_type=jnp.float32
    )

    @pl.when(step == 0)
    def _():
        total[...] = terms

    @pl.when(step > 0)
    def _():
        total[...] += terms

    @pl.when(step == pl.num_programs(0) - 1)
    def _():
        store_terms(total, own, outs)


def weight_grad_kernel(idx, acts, full, mask, out):
    hidden, width = out.shape
    step = pl.program_id(0)
    first = idx[0] * (pl.num_programs(0) * (width // BLOCK)) + step * (width // BLOCK)
    spread = wide_mask(mask[...], first, width)
    product = jnp.dot(acts[...], full[...], preferred_element_type=jnp.float32)
    for b in range(hidden // BLOCK):
        rows = slice(b * BLOCK, (b + 1) * BLOCK)
        out[rows, :] = (product[rows, :] * spread[b : b + 1, :]).astype(out.dtype)


def finish_kernel(n_pieces, n_parts, *refs):
    owns, parts, out = refs[:n_pieces], refs[n_pieces:-1], refs[-1]
    rows = owns[0].shape[0]
    for p, own in enumerate(owns):
        mine = parts[p * n_parts : (p + 1) * n_parts]
        scales = []
        for part in mine:
            code = part[rows:, :].astype(jnp.int32).astype(jnp.float32)
            scales.append(jnp.exp2(code * (1.0 / STEPS)) * (1.0 / CODE))
        for b in range(rows // BLOCK):
            at = slice(b * BLOCK, (b + 1) * BLOCK)
            total = own[at, :]
            for part, scale in zip(mine, scales, strict=True):
                got = part[at, :].astype(jnp.int32).astype(jnp.float32)
                total = total + got * scale[b : b + 1, :]
            to = p * rows + b * BLOCK
            out[:, to : to + BLOCK] = total.T.astype(out.dtype)


def in_vmem():
    return pl.BlockSpec(memory_space=pltpu.VMEM)


def in_smem():
    return pl.BlockSpec(memory_space=pltpu.SMEM)


def in_hbm():
    return pl.BlockSpec(memory_space=pl.ANY)


def params():
    return pltpu.CompilerParams(vmem_limit_bytes=VMEM_LIMIT)


def cost(flops, nbytes):
    return pl.CostEstimate(flops=flops, bytes_accessed=nbytes, transcendentals=0)


def per_device(n_rows, n_cols, grad_output, inputs, weight, block_mask):
    row, col = lax.axis_index("row"), lax.axis_index("col")
    hidden, width = weight.shape
    blocks = hidden // BLOCK
    n_pieces = 2 if blocks % 2 == 0 else 1
    piece = hidden // n_pieces
    n_parts = n_rows - 1
    tokens = inputs.shape[0]
    shard_rows = grad_output.shape[0]
    all_tokens = tokens * n_rows
    chunk = min(512, width)
    bf16 = jnp.bfloat16

    ring = chip_ring(n_cols)
    n_chips = len(ring)

    def send_ring(x, by):
        perm = []
        for p in range(n_chips):
            for core in range(2):
                q = (p + (by if core == 0 else -by)) % n_chips
                perm.append((ring[p] * 2 + core, ring[q] * 2 + core))
        return lax.ppermute(x, "col", perm)

    def send_core(x):
        return lax.ppermute(x, "col", [(c, c ^ 1) for c in range(n_cols)])

    def send_row(x, by):
        return lax.ppermute(x, "row", [(r, (r + by) % n_rows) for r in range(n_rows)])

    reach = [0]
    for j in range(1, n_chips // 2 + 1):
        reach += [j] if 2 * j == n_chips else [j, -j]
    steps = [(j, other) for j in reach for other in range(2)]
    table = []
    for c in range(n_cols):
        p, core = ring.index(c // 2), c % 2
        line = []
        for j, other in steps:
            of_core = core ^ other
            q = (p - j if of_core == 0 else p + j) % n_chips
            line.append(ring[q] * 2 + of_core)
        table.append(line)
    sources = lax.dynamic_index_in_dim(jnp.array(table, jnp.int32), col, 0, keepdims=False)
    places = (sources - row * (tokens // shard_rows)) % n_cols
    idx = jnp.concatenate([row.astype(jnp.int32).reshape(1), places.astype(jnp.int32)])

    weight = pltpu.with_memory_space_constraint(weight, pltpu.HBM)
    kept, shard_copy = pl.pallas_call(
        keep_kernel,
        in_specs=[in_smem(), in_vmem(), in_hbm(), in_vmem()],
        out_specs=[in_vmem(), in_vmem()],
        out_shape=[
            pltpu.VMEM((piece, width), bf16),
            jax.ShapeDtypeStruct(grad_output.shape, bf16),
        ],
        scratch_shapes=[pltpu.SemaphoreType.DMA((piece // BLOCK,))],
        compiler_params=params(),
        cost_estimate=cost(piece * width, 2 * piece * width),
        name="keep",
    )(idx, grad_output, weight, block_mask)

    held = {0: grad_output}
    there, back = grad_output, shard_copy
    for j in range(1, n_chips // 2 + 1):
        there = send_ring(there, 1)
        held[j] = there
        if 2 * j < n_chips:
            back = send_ring(back, -1)
            held[-j] = back
    shards = []
    for j in reach:
        shards += [held[j], send_core(held[j])]

    acts = [inputs] + [send_row(inputs, k) for k in range(1, n_rows)]
    acts_turned = pl.pallas_call(
        functools.partial(turn_kernel, n_rows),
        in_specs=[in_vmem()] * n_rows,
        out_specs=in_vmem(),
        out_shape=jax.ShapeDtypeStruct((hidden, all_tokens), bf16),
        compiler_params=params(),
        cost_estimate=cost(all_tokens * hidden, 4 * all_tokens * hidden),
        name="turn",
    )(*acts)

    n_shards = len(shards)
    code_rows = -(-(piece // BLOCK) // 16) * 16
    sent_shape = jax.ShapeDtypeStruct((piece + code_rows, tokens), jnp.int16)
    own_shape = jax.ShapeDtypeStruct((piece, tokens), jnp.float32)
    piece_cost = cost(2 * all_tokens * piece * width, 2 * piece * width)
    full, turned, own, *coded = pl.pallas_call(
        functools.partial(first_terms_kernel, n_shards, n_parts, chunk),
        in_specs=[in_smem()] + [in_vmem()] * n_shards + [in_vmem(), in_hbm()],
        out_specs=[in_vmem()] * (3 + n_parts),
        out_shape=[
            jax.ShapeDtypeStruct((all_tokens, width), bf16),
            jax.ShapeDtypeStruct((width, all_tokens), bf16),
            own_shape,
        ]
        + [sent_shape] * n_parts,
        scratch_shapes=[pltpu.VMEM((piece, all_tokens), jnp.float32)],
        compiler_params=params(),
        cost_estimate=piece_cost,
        name="first_terms",
    )(idx, *shards, kept, acts_turned)
    owns = [own]
    parts = [send_row(coded[k], k + 1) for k in range(n_parts)]

    for p in range(1, n_pieces):
        own, *coded = pl.pallas_call(
            functools.partial(more_terms_kernel, n_parts, p * (piece // BLOCK)),
            grid=(width // chunk,),
            in_specs=[
                in_smem(),
                pl.BlockSpec((chunk, all_tokens), lambda i: (i, 0)),
                pl.BlockSpec((piece, chunk), lambda i, p=p: (p, i)),
                in_vmem(),
            ],
            out_specs=[in_vmem()] * (1 + n_parts),
            out_shape=[own_shape] + [sent_shape] * n_parts,
            scratch_shapes=[pltpu.VMEM((piece, all_tokens), jnp.float32)],
            compiler_params=params(),
            cost_estimate=piece_cost,
            name="more_terms",
        )(idx, turned, weight, block_mask)
        owns.append(own)
        parts += [send_row(coded[k], k + 1) for k in range(n_parts)]

    grad_weight = pl.pallas_call(
        weight_grad_kernel,
        grid=(width // chunk,),
        in_specs=[
            in_smem(),
            in_vmem(),
            pl.BlockSpec((all_tokens, chunk), lambda i: (0, i)),
            in_vmem(),
        ],
        out_specs=pl.BlockSpec((hidden, chunk), lambda i: (0, i)),
        out_shape=jax.ShapeDtypeStruct((hidden, width), bf16),
        compiler_params=params(),
        cost_estimate=cost(2 * all_tokens * hidden * width, 2 * hidden * width),
        name="weight_grad",
    )(idx, acts_turned, full, block_mask)

    grad_input = pl.pallas_call(
        functools.partial(finish_kernel, n_pieces, n_parts),
        in_specs=[in_vmem()] * (n_pieces * (1 + n_parts)),
        out_specs=in_vmem(),
        out_shape=jax.ShapeDtypeStruct((tokens, hidden), bf16),
        compiler_params=params(),
        name="add_terms",
    )(*owns, *parts)
    return (grad_input, grad_weight)


def solution(mesh):
    return jax.shard_map(
        functools.partial(per_device, mesh.shape["row"], mesh.shape["col"]),
        mesh=mesh,
        in_specs=(P("col", "row"), P("row", "col"), P("col", "row"), P("col", None)),
        out_specs=(P("row", "col"), P("col", "row")),
        check_vma=False,
    )
```

time: 55.2 us -> 53.9 us (0.976)
  waiting for transfers between devices: 19.4 us -> 11 us
  Pallas kernels: 17 us -> 25.1 us
  local copies, waits for them, and re-layouts: 6.77 us -> 1.61 us
  starting transfers between devices: 10.4 us -> 14.3 us
    pallas_call x3 -> x6, Pallas kernels: 17 us -> 25.1 us  [the longest x1 8.86 us: per_device(): pl.pallas_call(weight_grad_kernel, grid=(width // chunk,), in_specs=[in_s...]
    ppermute x7, waiting for transfers between devices: 16.3 us -> 9.94 us  [send_ring(): return lax.ppermute(x, 'col', perm)]
    unnamed x8 -> x10, local copies, waits for them, and re-layouts: 6.77 us -> 1.61 us
    ppermute x2 -> x3, waiting for transfers between devices: 3.04 us -> 0.01 us  [send_row(): lax.ppermute(x, 'row', [(r, (r + by) % n_rows) for r in range(n_rows)])]
    ppermute x7, starting transfers between devices: 6.82 us -> 9.15 us  [send_ring(): return lax.ppermute(x, 'col', perm)]
    ppermute x2 -> x3, starting transfers between devices: 2.45 us -> 3.67 us  [send_row(): lax.ppermute(x, 'row', [(r, (r + by) % n_rows) for r in range(n_rows)])]
    ppermute x8, waiting for transfers between devices: 0.02 us -> 1.03 us  [send_core(): return lax.ppermute(x, 'col', [(c, c ^ 1) for c in range(n_cols)])]
  transfers between devices with their start and end apart: 17 -> 18, of which waited for: 7 -> 6; matrix products, arithmetic and copies ran while one was open for 1% -> 1% of each run, Pallas kernels for 29% -> 39%
where the time goes in v3:
time: 53.9 us; the launch traced here: 53.6 us
  Pallas kernels  25.1 us (47%)
  starting transfers between devices  14.3 us (27%)
  waiting for transfers between devices  11 us (20%)
  local copies, waits for them, and re-layouts  1.61 us (3%)
  other arithmetic  0.78 us (1%)
  between operations  0.73 us (1%)
    ppermute x7, waiting for transfers between devices, send_ring(): return lax.ppermute(x, 'col', perm)  9.94 us
    ppermute x7, starting transfers between devices, send_ring(): return lax.ppermute(x, 'col', perm)  9.15 us
    pallas_call x1, Pallas kernels, per_device(): pl.pallas_call(weight_grad_kernel, grid=(width // chunk,), in_specs=[in_s...  8.86 us
    pallas_call x1, Pallas kernels, per_device(): pl.pallas_call(functools.partial(more_terms_kernel, n_parts, p * (piece /...  8.15 us
    pallas_call x1, Pallas kernels, per_device(): pl.pallas_call(keep_kernel, in_specs=[in_smem(), in_vmem(), in_hbm(), in_...  3.79 us
    ppermute x3, starting transfers between devices, send_row(): lax.ppermute(x, 'row', [(r, (r + by) % n_rows) for r in range(n_rows)])  3.67 us
    pallas_call x1, Pallas kernels, per_device(): pl.pallas_call(functools.partial(first_terms_kernel, n_shards, n_parts, c...  3 us
    unnamed x10, local copies, waits for them, and re-layouts  1.61 us
  transfers between devices with their start and end apart: 18, of which 6 were waited for; matrix products, arithmetic and copies ran while one was open for 1% of the time, Pallas kernels for 39%

profile of v3, /device:TPU:0, one launch (start us, length us, event | category | flops | bytes accessed | tf_op | source)
XLA Modules:
  0.0 53.6 jit_solution(18021587192990465884)
XLA Ops:
  0.6 3.0 %collective-permute-start.1 = (bf16[16,4096]{1,0:T(8,128)(2,1)}, bf16[16,4096]{1,0:T(8,128)(2,1)S(1)}, u32[]{:S(2)}, u32[]{:S(2)}) collective-permute-start(bf16[16,4096]{1,0:T(8,128)(2,1)} %refs_0_.3), channel_id=1, source_target_pairs={{2,6},{3,1},{6,10},{7,3},{10,14},{11,7},{14,12},{15,11},{12,8},{13... | collective-permute-start | bytes 393224 | tf_op jit(solution)/shard_map/ppermute | solution.py:204
  3.6 1.5 %collective-permute-start.15 = (bf16[128,1792]{1,0:T(8,128)(2,1)}, bf16[128,1792]{1,0:T(8,128)(2,1)S(1)}, u32[]{:S(2)}, u32[]{:S(2)}) collective-permute-start(bf16[128,1792]{1,0:T(8,128)(2,1)} %refs_0_.2), channel_id=1, source_target_pairs={{0,16},{16,0},{1,17},{17,1},{2,18},{18,2},{3,19},{19,3},{4,20},{20... | collective-permute-start | bytes 1376264 | tf_op jit(solution)/shard_map/ppermute | solution.py:210
  5.1 0.7 %and_select_fusion = s32[16]{0:T(128)S(1)} fusion(s32[16,16]{1,0:T(8,128)} %constant.32.clone, s32[]{:T(128)S(6)} %select_n.11, s32[]{:T(128)S(6)} %mul.3), kind=kLoop, calls=%fused_computation.2 | loop fusion | flops 192 | bytes 136 | tf_op jit(solution)/shard_map/jit(remainder)/select_n | solution.py:226
  5.8 0.1 pad_add_fusion.idx
  5.9 0.0 copy-start
  5.9 0.9 %copy-done = bf16[16,4096]{1,0:T(8,128)(2,1)S(1)} copy-done((bf16[16,4096]{1,0:T(8,128)(2,1)S(1)}, bf16[16,4096]{1,0:T(8,128)(2,1)}, u32[]{:S(2)}) %copy-start) | copy-done | bytes 131096
  6.8 0.0 copy-start.3
  6.8 0.7 %copy-done.3 = s32[14,64]{1,0:T(8,128)S(1)} copy-done((s32[14,64]{1,0:T(8,128)S(1)}, s32[14,64]{1,0:T(8,128)}, u32[]{:S(2)}) %copy-start.3) | copy-done | bytes 3608
  7.5 0.0 copy-start.2
  7.5 0.0 copy-start.1
  7.5 3.8 %keep.1 = (bf16[896,4096]{1,0:T(8,128)(2,1)S(1)}, bf16[16,4096]{1,0:T(8,128)(2,1)S(1)}) custom-call(s32[17]{0:T(128)S(1)} %pad_add_fusion.idx, bf16[16,4096]{1,0:T(8,128)(2,1)S(1)} %copy-done, bf16[1792,4096]{1,0:T(8,128)(2,1)} %weight.3, s32[14,64]{1,0:T(8,128)S(1)} %copy-done.3), custom_call_target="tpu_custom_call" | custom-call | flops 3670016 | bytes 7340032 | tf_op jit(solution)/shard_map/keep/pallas_call | solution.py:230
  11.3 0.0 copy-start.4
  11.3 0.6 %collective-permute-start.3 = (bf16[16,4096]{1,0:T(8,128)(2,1)S(1)}, bf16[16,4096]{1,0:T(8,128)(2,1)S(1)}, u32[]{:S(2)}, u32[]{:S(2)}) collective-permute-start(bf16[16,4096]{1,0:T(8,128)(2,1)S(1)} %get-tuple-element.10), channel_id=1, source_target_pairs={{2,0},{3,7},{6,2},{7,11},{10,6},{11,15},{14,10},{15,13},{12,14},{1... | collective-permute-start | bytes 393224 | tf_op jit(solution)/shard_map/ppermute | solution.py:204
  11.9 0.0 collective-permute-done.1.refs_2_
  11.9 1.5 %collective-permute-start.5 = (bf16[16,4096]{1,0:T(8,128)(2,1)S(1)}, bf16[16,4096]{1,0:T(8,128)(2,1)S(1)}, u32[]{:S(2)}, u32[]{:S(2)}) collective-permute-start(bf16[16,4096]{1,0:T(8,128)(2,1)S(1)} %collective-permute-done.1.refs_2_), channel_id=1, source_target_pairs={{2,6},{3,1},{6,10},{7,3},{10,14},{11,7},{14,12},{15,11},{12,8},{13... | collective-permute-start | bytes 393224 | tf_op jit(solution)/shard_map/ppermute | solution.py:204
  13.4 0.0 collective-permute-start
  13.4 2.9 %collective-permute-done.3.refs_4_ = bf16[16,4096]{1,0:T(8,128)(2,1)S(1)} collective-permute-done((bf16[16,4096]{1,0:T(8,128)(2,1)S(1)}, bf16[16,4096]{1,0:T(8,128)(2,1)S(1)}, u32[]{:S(2)}, u32[]{:S(2)}) %collective-permute-start.3) | collective-permute-done | bytes 131104 | tf_op jit(solution)/shard_map/ppermute | solution.py:204
  16.4 1.5 %collective-permute-start.7 = (bf16[16,4096]{1,0:T(8,128)(2,1)S(1)}, bf16[16,4096]{1,0:T(8,128)(2,1)S(1)}, u32[]{:S(2)}, u32[]{:S(2)}) collective-permute-start(bf16[16,4096]{1,0:T(8,128)(2,1)S(1)} %collective-permute-done.3.refs_4_), channel_id=1, source_target_pairs={{2,0},{3,7},{6,2},{7,11},{10,6},{11,15},{14,10},{15,13},{12,14},{1... | collective-permute-start | bytes 393224 | tf_op jit(solution)/shard_map/ppermute | solution.py:204
  17.9 0.0 collective-permute-done.5.refs_6_
  17.9 0.7 %collective-permute-start.9 = (bf16[16,4096]{1,0:T(8,128)(2,1)S(1)}, bf16[16,4096]{1,0:T(8,128)(2,1)S(1)}, u32[]{:S(2)}, u32[]{:S(2)}) collective-permute-start(bf16[16,4096]{1,0:T(8,128)(2,1)S(1)} %collective-permute-done.5.refs_6_), channel_id=1, source_target_pairs={{2,6},{3,1},{6,10},{7,3},{10,14},{11,7},{14,12},{15,11},{12,8},{13... | collective-permute-start | bytes 393224 | tf_op jit(solution)/shard_map/ppermute | solution.py:204
  18.6 0.0 collective-permute-start.2
  18.7 0.0 collective-permute-done.refs_1_
  18.7 0.5 collective-permute-start.4
  19.2 2.2 %collective-permute-done.7.refs_8_ = bf16[16,4096]{1,0:T(8,128)(2,1)S(1)} collective-permute-done((bf16[16,4096]{1,0:T(8,128)(2,1)S(1)}, bf16[16,4096]{1,0:T(8,128)(2,1)S(1)}, u32[]{:S(2)}, u32[]{:S(2)}) %collective-permute-start.7) | collective-permute-done | bytes 131104 | tf_op jit(solution)/shard_map/ppermute | solution.py:204
  21.3 1.8 %collective-permute-start.11 = (bf16[16,4096]{1,0:T(8,128)(2,1)S(1)}, bf16[16,4096]{1,0:T(8,128)(2,1)S(1)}, u32[]{:S(2)}, u32[]{:S(2)}) collective-permute-start(bf16[16,4096]{1,0:T(8,128)(2,1)S(1)} %collective-permute-done.7.refs_8_), channel_id=1, source_target_pairs={{2,0},{3,7},{6,2},{7,11},{10,6},{11,15},{14,10},{15,13},{12,14},{1... | collective-permute-start | bytes 393224 | tf_op jit(solution)/shard_map/ppermute | solution.py:204
  23.1 0.9 %collective-permute-done.9.refs_10_ = bf16[16,4096]{1,0:T(8,128)(2,1)S(1)} collective-permute-done((bf16[16,4096]{1,0:T(8,128)(2,1)S(1)}, bf16[16,4096]{1,0:T(8,128)(2,1)S(1)}, u32[]{:S(2)}, u32[]{:S(2)}) %collective-permute-start.9) | collective-permute-done | bytes 131104 | tf_op jit(solution)/shard_map/ppermute | solution.py:204
  24.0 0.0 collective-permute-start.13
  24.0 0.0 collective-permute-done.2.refs_3_
  24.0 0.0 collective-permute-start.6
  24.0 0.0 collective-permute-done.4.refs_5_
  24.0 0.5 collective-permute-start.8
  24.5 1.8 %collective-permute-done.11.refs_12_ = bf16[16,4096]{1,0:T(8,128)(2,1)S(1)} collective-permute-done((bf16[16,4096]{1,0:T(8,128)(2,1)S(1)}, bf16[16,4096]{1,0:T(8,128)(2,1)S(1)}, u32[]{:S(2)}, u32[]{:S(2)}) %collective-permute-start.11) | collective-permute-done | bytes 131104 | tf_op jit(solution)/shard_map/ppermute | solution.py:204
  26.3 0.0 collective-permute-start.10
  26.3 0.0 collective-permute-done.15.refs_1_
  26.3 0.5 collective-permute-start.12
  26.8 2.2 %collective-permute-done.13.refs_14_ = bf16[16,4096]{1,0:T(8,128)(2,1)S(1)} collective-permute-done((bf16[16,4096]{1,0:T(8,128)(2,1)S(1)}, bf16[16,4096]{1,0:T(8,128)(2,1)S(1)}, u32[]{:S(2)}, u32[]{:S(2)}) %collective-permute-start.13) | collective-permute-done | bytes 131104 | tf_op jit(solution)/shard_map/ppermute | solution.py:204
  29.0 0.0 collective-permute-start.14
  29.0 0.0 copy-done.2
  29.0 0.3 turn.1.refs_17_.acts
  29.3 0.0 collective-permute-done.6.refs_7_
  29.3 0.0 collective-permute-done.8.refs_9_
  29.3 0.0 collective-permute-done.10.refs_11_
  29.3 0.0 collective-permute-done.12.refs_13_
  29.3 1.0 %collective-permute-done.14.refs_15_ = bf16[16,4096]{1,0:T(8,128)(2,1)S(1)} collective-permute-done((bf16[16,4096]{1,0:T(8,128)(2,1)S(1)}, bf16[16,4096]{1,0:T(8,128)(2,1)S(1)}, u32[]{:S(2)}, u32[]{:S(2)}) %collective-permute-start.14) | collective-permute-done | bytes 131104 | tf_op jit(solution)/shard_map/ppermute | solution.py:207
  30.3 0.0 copy-done.1
  30.3 3.0 %first_terms.1 = (bf16[256,4096]{1,0:T(8,128)(2,1)S(1)}, bf16[4096,256]{1,0:T(8,128)(2,1)S(1)}, f32[896,128]{1,0:T(8,128)S(1)}, s16[912,128]{1,0:T(8,128)(2,1)S(1)}) custom-call(s32[17]{0:T(128)S(1)} %pad_add_fusion.idx, bf16[16,4096]{1,0:T(8,128)(2,1)S(1)} %copy-done.1, bf16[16,4096]{1,0:T(8,128)(2,1)S(1)} %collective-permute-done.refs_1_, ...), custom_call_target="tpu_custom_call" | custom-call | flops 1879048192 | bytes 7340032 | tf_op jit(solution)/shard_map/first_terms/pallas_call | solution.py:272
  33.4 0.6 %collective-permute-start.16 = (s16[912,128]{1,0:T(8,128)(2,1)S(1)}, s16[912,128]{1,0:T(8,128)(2,1)S(1)}, u32[]{:S(2)}, u32[]{:S(2)}) collective-permute-start(s16[912,128]{1,0:T(8,128)(2,1)S(1)} %get-tuple-element.15), channel_id=1, source_target_pairs={{0,16},{16,0},{1,17},{17,1},{2,18},{18,2},{3,19},{19,3},{4,20},{20... | collective-permute-start | bytes 700424 | tf_op jit(solution)/shard_map/ppermute | solution.py:210
  33.9 0.0 copy-done.4
  33.9 8.2 %more_terms.1 = (f32[896,128]{1,0:T(8,128)S(1)}, s16[912,128]{1,0:T(8,128)(2,1)S(1)}) custom-call(s32[17]{0:T(128)S(1)} %pad_add_fusion.idx, bf16[4096,256]{1,0:T(8,128)(2,1)S(1)} %get-tuple-element.13.turned, bf16[1792,4096]{1,0:T(8,128)(2,1)} %weight.3, s32[14,64]{1,0:T(8,128)S(1)} %copy-done.4), custom_call_target="tpu_custom_call" | custom-call | flops 1879048192 | bytes 7340032 | tf_op jit(solution)/shard_map/more_terms/pallas_call | solution.py:291
  42.1 1.6 %collective-permute-start.17 = (s16[912,128]{1,0:T(8,128)(2,1)S(1)}, s16[912,128]{1,0:T(8,128)(2,1)S(1)}, u32[]{:S(2)}, u32[]{:S(2)}) collective-permute-start(s16[912,128]{1,0:T(8,128)(2,1)S(1)} %get-tuple-element.16), channel_id=1, source_target_pairs={{0,16},{16,0},{1,17},{17,1},{2,18},{18,2},{3,19},{19,3},{4,20},{20... | collective-permute-start | bytes 700424 | tf_op jit(solution)/shard_map/ppermute | solution.py:210
  43.7 8.9 %weight_grad.1 = bf16[1792,4096]{1,0:T(8,128)(2,1)} custom-call(s32[17]{0:T(128)S(1)} %pad_add_fusion.idx, bf16[1792,256]{1,0:T(8,128)(2,1)S(1)} %turn.1.refs_17_.acts, bf16[256,4096]{1,0:T(8,128)(2,1)S(1)} %get-tuple-element.17.full, s32[14,64]{1,0:T(8,128)S(1)} %copy-done.4), custom_call_target="tpu_custom_call" | custom-call | flops 3758096384 | bytes 14680064 | tf_op jit(solution)/shard_map/weight_grad/pallas_call | solution.py:310
  52.5 0.0 collective-permute-done.16.refs_2_
  52.5 0.0 collective-permute-done.17.refs_3_
  52.5 1.0 %add_terms.1 = bf16[128,1792]{1,0:T(8,128)(2,1)} custom-call(f32[896,128]{1,0:T(8,128)S(1)} %get-tuple-element.12.refs_0_, f32[896,128]{1,0:T(8,128)S(1)} %get-tuple-element.14.refs_1_, s16[912,128]{1,0:T(8,128)(2,1)S(1)} %collective-permute-done.16.refs_2_, s16[912,128]{1,0:T(8,128)(2,1)S(1)} %collective-permute-done.17.refs_3_), custom_call_target="tpu_custom_call" | custom-call | tf_op jit(solution)/shard_map/add_terms/pallas_call | solution.py:326
Async XLA Ops:
  0.6 11.3 %collective-permute-start.1 = (bf16[16,4096]{1,0:T(8,128)(2,1)}, bf16[16,4096]{1,0:T(8,128)(2,1)S(1)}, u32[]{:S(2)}, u32[]{:S(2)}) collective-permute-start(bf16[16,4096]{1,0:T(8,128)(2,1)} %refs_0_.3), channel_id=1, source_target_pairs={{2,6},{3,1},{6,10},{7,3},{10,14},{11,7},{14,12},{15,11},{12,8},{13... | collective-permute-start | bytes 393224 | tf_op jit(solution)/shard_map/ppermute | solution.py:204
  3.6 22.7 %collective-permute-start.15 = (bf16[128,1792]{1,0:T(8,128)(2,1)}, bf16[128,1792]{1,0:T(8,128)(2,1)S(1)}, u32[]{:S(2)}, u32[]{:S(2)}) collective-permute-start(bf16[128,1792]{1,0:T(8,128)(2,1)} %refs_0_.2), channel_id=1, source_target_pairs={{0,16},{16,0},{1,17},{17,1},{2,18},{18,2},{3,19},{19,3},{4,20},{20... | collective-permute-start | bytes 1376264 | tf_op jit(solution)/shard_map/ppermute | solution.py:210
  5.9 0.9 %copy-start = (bf16[16,4096]{1,0:T(8,128)(2,1)S(1)}, bf16[16,4096]{1,0:T(8,128)(2,1)}, u32[]{:S(2)}) copy-start(bf16[16,4096]{1,0:T(8,128)(2,1)} %refs_0_.3) | copy-start | bytes 393220
  6.8 0.7 %copy-start.3 = (s32[14,64]{1,0:T(8,128)S(1)}, s32[14,64]{1,0:T(8,128)}, u32[]{:S(2)}) copy-start(s32[14,64]{1,0:T(8,128)} %mask.5) | copy-start | bytes 10756
  7.5 21.5 %copy-start.2 = (bf16[128,1792]{1,0:T(8,128)(2,1)S(1)}, bf16[128,1792]{1,0:T(8,128)(2,1)}, u32[]{:S(2)}) copy-start(bf16[128,1792]{1,0:T(8,128)(2,1)} %refs_0_.2) | copy-start | bytes 1376260
  7.5 22.8 %copy-start.1 = (bf16[16,4096]{1,0:T(8,128)(2,1)S(1)}, bf16[16,4096]{1,0:T(8,128)(2,1)}, u32[]{:S(2)}) copy-start(bf16[16,4096]{1,0:T(8,128)(2,1)} %refs_0_.3) | copy-start | bytes 393220
  11.3 22.6 %copy-start.4 = (s32[14,64]{1,0:T(8,128)S(1)}, s32[14,64]{1,0:T(8,128)}, u32[]{:S(2)}) copy-start(s32[14,64]{1,0:T(8,128)} %mask.5) | copy-start | bytes 10756
  11.3 5.0 %collective-permute-start.3 = (bf16[16,4096]{1,0:T(8,128)(2,1)S(1)}, bf16[16,4096]{1,0:T(8,128)(2,1)S(1)}, u32[]{:S(2)}, u32[]{:S(2)}) collective-permute-start(bf16[16,4096]{1,0:T(8,128)(2,1)S(1)} %get-tuple-element.10), channel_id=1, source_target_pairs={{2,0},{3,7},{6,2},{7,11},{10,6},{11,15},{14,10},{15,13},{12,14},{1... | collective-permute-start | bytes 393224 | tf_op jit(solution)/shard_map/ppermute | solution.py:204
  11.9 6.0 %collective-permute-start.5 = (bf16[16,4096]{1,0:T(8,128)(2,1)S(1)}, bf16[16,4096]{1,0:T(8,128)(2,1)S(1)}, u32[]{:S(2)}, u32[]{:S(2)}) collective-permute-start(bf16[16,4096]{1,0:T(8,128)(2,1)S(1)} %collective-permute-done.1.refs_2_), channel_id=1, source_target_pairs={{2,6},{3,1},{6,10},{7,3},{10,14},{11,7},{14,12},{15,11},{12,8},{13... | collective-permute-start | bytes 393224 | tf_op jit(solution)/shard_map/ppermute | solution.py:204
  13.4 5.2 %collective-permute-start = (bf16[16,4096]{1,0:T(8,128)(2,1)S(1)}, bf16[16,4096]{1,0:T(8,128)(2,1)S(1)}, u32[]{:S(2)}, u32[]{:S(2)}) collective-permute-start(bf16[16,4096]{1,0:T(8,128)(2,1)S(1)} %copy-done), channel_id=1, source_target_pairs={{0,1},{1,0},{2,3},{3,2},{4,5},{5,4},{6,7},{7,6},{8,9},{9,8},{10,11... | collective-permute-start | bytes 393224 | tf_op jit(solution)/shard_map/ppermute | solution.py:207
  16.4 5.0 %collective-permute-start.7 = (bf16[16,4096]{1,0:T(8,128)(2,1)S(1)}, bf16[16,4096]{1,0:T(8,128)(2,1)S(1)}, u32[]{:S(2)}, u32[]{:S(2)}) collective-permute-start(bf16[16,4096]{1,0:T(8,128)(2,1)S(1)} %collective-permute-done.3.refs_4_), channel_id=1, source_target_pairs={{2,0},{3,7},{6,2},{7,11},{10,6},{11,15},{14,10},{15,13},{12,14},{1... | collective-permute-start | bytes 393224 | tf_op jit(solution)/shard_map/ppermute | solution.py:204
  17.9 6.1 %collective-permute-start.9 = (bf16[16,4096]{1,0:T(8,128)(2,1)S(1)}, bf16[16,4096]{1,0:T(8,128)(2,1)S(1)}, u32[]{:S(2)}, u32[]{:S(2)}) collective-permute-start(bf16[16,4096]{1,0:T(8,128)(2,1)S(1)} %collective-permute-done.5.refs_6_), channel_id=1, source_target_pairs={{2,6},{3,1},{6,10},{7,3},{10,14},{11,7},{14,12},{15,11},{12,8},{13... | collective-permute-start | bytes 393224 | tf_op jit(solution)/shard_map/ppermute | solution.py:204
  18.6 5.4 %collective-permute-start.2 = (bf16[16,4096]{1,0:T(8,128)(2,1)S(1)}, bf16[16,4096]{1,0:T(8,128)(2,1)S(1)}, u32[]{:S(2)}, u32[]{:S(2)}) collective-permute-start(bf16[16,4096]{1,0:T(8,128)(2,1)S(1)} %collective-permute-done.1.refs_2_), channel_id=1, source_target_pairs={{0,1},{1,0},{2,3},{3,2},{4,5},{5,4},{6,7},{7,6},{8,9},{9,8},{10,11... | collective-permute-start | bytes 393224 | tf_op jit(solution)/shard_map/ppermute | solution.py:207
  18.7 5.4 %collective-permute-start.4 = (bf16[16,4096]{1,0:T(8,128)(2,1)S(1)}, bf16[16,4096]{1,0:T(8,128)(2,1)S(1)}, u32[]{:S(2)}, u32[]{:S(2)}) collective-permute-start(bf16[16,4096]{1,0:T(8,128)(2,1)S(1)} %collective-permute-done.3.refs_4_), channel_id=1, source_target_pairs={{0,1},{1,0},{2,3},{3,2},{4,5},{5,4},{6,7},{7,6},{8,9},{9,8},{10,11... | collective-permute-start | bytes 393224 | tf_op jit(solution)/shard_map/ppermute | solution.py:207
  21.3 5.0 %collective-permute-start.11 = (bf16[16,4096]{1,0:T(8,128)(2,1)S(1)}, bf16[16,4096]{1,0:T(8,128)(2,1)S(1)}, u32[]{:S(2)}, u32[]{:S(2)}) collective-permute-start(bf16[16,4096]{1,0:T(8,128)(2,1)S(1)} %collective-permute-done.7.refs_8_), channel_id=1, source_target_pairs={{2,0},{3,7},{6,2},{7,11},{10,6},{11,15},{14,10},{15,13},{12,14},{1... | collective-permute-start | bytes 393224 | tf_op jit(solution)/shard_map/ppermute | solution.py:204
  24.0 5.0 %collective-permute-start.13 = (bf16[16,4096]{1,0:T(8,128)(2,1)S(1)}, bf16[16,4096]{1,0:T(8,128)(2,1)S(1)}, u32[]{:S(2)}, u32[]{:S(2)}) collective-permute-start(bf16[16,4096]{1,0:T(8,128)(2,1)S(1)} %collective-permute-done.9.refs_10_), channel_id=1, source_target_pairs={{2,6},{3,1},{6,10},{7,3},{10,14},{11,7},{14,12},{15,11},{12,8},{13... | collective-permute-start | bytes 393224 | tf_op jit(solution)/shard_map/ppermute | solution.py:204
  24.0 5.3 %collective-permute-start.6 = (bf16[16,4096]{1,0:T(8,128)(2,1)S(1)}, bf16[16,4096]{1,0:T(8,128)(2,1)S(1)}, u32[]{:S(2)}, u32[]{:S(2)}) collective-permute-start(bf16[16,4096]{1,0:T(8,128)(2,1)S(1)} %collective-permute-done.5.refs_6_), channel_id=1, source_target_pairs={{0,1},{1,0},{2,3},{3,2},{4,5},{5,4},{6,7},{7,6},{8,9},{9,8},{10,11... | collective-permute-start | bytes 393224 | tf_op jit(solution)/shard_map/ppermute | solution.py:207
  24.0 5.3 %collective-permute-start.8 = (bf16[16,4096]{1,0:T(8,128)(2,1)S(1)}, bf16[16,4096]{1,0:T(8,128)(2,1)S(1)}, u32[]{:S(2)}, u32[]{:S(2)}) collective-permute-start(bf16[16,4096]{1,0:T(8,128)(2,1)S(1)} %collective-permute-done.7.refs_8_), channel_id=1, source_target_pairs={{0,1},{1,0},{2,3},{3,2},{4,5},{5,4},{6,7},{7,6},{8,9},{9,8},{10,11... | collective-permute-start | bytes 393224 | tf_op jit(solution)/shard_map/ppermute | solution.py:207
  26.3 3.0 %collective-permute-start.10 = (bf16[16,4096]{1,0:T(8,128)(2,1)S(1)}, bf16[16,4096]{1,0:T(8,128)(2,1)S(1)}, u32[]{:S(2)}, u32[]{:S(2)}) collective-permute-start(bf16[16,4096]{1,0:T(8,128)(2,1)S(1)} %collective-permute-done.9.refs_10_), channel_id=1, source_target_pairs={{0,1},{1,0},{2,3},{3,2},{4,5},{5,4},{6,7},{7,6},{8,9},{9,8},{10,11... | collective-permute-start | bytes 393224 | tf_op jit(solution)/shard_map/ppermute | solution.py:207
  26.3 3.0 %collective-permute-start.12 = (bf16[16,4096]{1,0:T(8,128)(2,1)S(1)}, bf16[16,4096]{1,0:T(8,128)(2,1)S(1)}, u32[]{:S(2)}, u32[]{:S(2)}) collective-permute-start(bf16[16,4096]{1,0:T(8,128)(2,1)S(1)} %collective-permute-done.11.refs_12_), channel_id=1, source_target_pairs={{0,1},{1,0},{2,3},{3,2},{4,5},{5,4},{6,7},{7,6},{8,9},{9,8},{10,11... | collective-permute-start | bytes 393224 | tf_op jit(solution)/shard_map/ppermute | solution.py:207
  29.0 1.3 %collective-permute-start.14 = (bf16[16,4096]{1,0:T(8,128)(2,1)S(1)}, bf16[16,4096]{1,0:T(8,128)(2,1)S(1)}, u32[]{:S(2)}, u32[]{:S(2)}) collective-permute-start(bf16[16,4096]{1,0:T(8,128)(2,1)S(1)} %collective-permute-done.13.refs_14_), channel_id=1, source_target_pairs={{0,1},{1,0},{2,3},{3,2},{4,5},{5,4},{6,7},{7,6},{8,9},{9,8},{10,11... | collective-permute-start | bytes 393224 | tf_op jit(solution)/shard_map/ppermute | solution.py:207
  33.4 19.2 %collective-permute-start.16 = (s16[912,128]{1,0:T(8,128)(2,1)S(1)}, s16[912,128]{1,0:T(8,128)(2,1)S(1)}, u32[]{:S(2)}, u32[]{:S(2)}) collective-permute-start(s16[912,128]{1,0:T(8,128)(2,1)S(1)} %get-tuple-element.15), channel_id=1, source_target_pairs={{0,16},{16,0},{1,17},{17,1},{2,18},{18,2},{3,19},{19,3},{4,20},{20... | collective-permute-start | bytes 700424 | tf_op jit(solution)/shard_map/ppermute | solution.py:210
  42.1 10.5 %collective-permute-start.17 = (s16[912,128]{1,0:T(8,128)(2,1)S(1)}, s16[912,128]{1,0:T(8,128)(2,1)S(1)}, u32[]{:S(2)}, u32[]{:S(2)}) collective-permute-start(s16[912,128]{1,0:T(8,128)(2,1)S(1)} %get-tuple-element.16), channel_id=1, source_target_pairs={{0,16},{16,0},{1,17},{17,1},{2,18},{18,2},{3,19},{19,3},{4,20},{20... | collective-permute-start | bytes 700424 | tf_op jit(solution)/shard_map/ppermute | solution.py:210

commit v4 on v3

--- a/solution.py
+++ b/solution.py
@@ -10,7 +10,7 @@
 BLOCK = 128
 CODE = 32700.0
 STEPS = 64.0
-VMEM_LIMIT = 32 * 1024 * 1024
+VMEM_LIMIT = 24 * 1024 * 1024
 
 
 def chip_ring(cols):
@@ -45,7 +45,7 @@
     )
 
 
-def keep_kernel(idx, shard, weight, mask, kept, shard_copy, sems):
+def keep_kernel(idx, weight, mask, kept, sems):
     rows, width = kept.shape
     blocks = rows // BLOCK
     copies = []
@@ -53,7 +53,6 @@
         at = pl.ds(b * BLOCK, BLOCK)
         copies.append(pltpu.make_async_copy(weight.at[at, :], kept.at[at, :], sems.at[b]))
         copies[-1].start()
-    shard_copy[...] = shard[...]
     spread = wide_mask(mask[...], idx[0] * (width // BLOCK), width).astype(jnp.bfloat16)
     for b in range(blocks):
         copies[b].wait()
@@ -95,38 +94,23 @@
     for c in range(0, full.shape[1], chunk):
         turned[c : c + chunk, :] = full[:, c : c + chunk].T
         terms = jnp.dot(
-            kept[:, c : c + chunk], turned[c : c + chunk, :], preferred_element_type=jnp.float32
+            kept[: own.shape[0], c : c + chunk],
+            turned[c : c + chunk, :],
+            preferred_element_type=jnp.float32,
         )
         total[...] = terms if c == 0 else total[...] + terms
     store_terms(total, own, outs)
 
 
-def more_terms_kernel(n_parts, first_block, idx, turned, weight, mask, own, *refs):
+def more_terms_kernel(n_parts, first_row, chunk, turned, kept, own, *refs):
     outs, total = refs[:n_parts], refs[n_parts]
-    step = pl.program_id(0)
-    rows, chunk = weight.shape
-    per_row = pl.num_programs(0) * (chunk // BLOCK)
-    first = idx[0] * per_row + step * (chunk // BLOCK)
-    spread = wide_mask(mask[...], first, chunk).astype(jnp.bfloat16)
-    kept = []
-    for b in range(rows // BLOCK):
-        at = first_block + b
-        kept.append(weight[b * BLOCK : (b + 1) * BLOCK, :] * spread[at : at + 1, :])
-    terms = jnp.dot(
-        jnp.concatenate(kept, axis=0), turned[...], preferred_element_type=jnp.float32
-    )
-
-    @pl.when(step == 0)
-    def _():
-        total[...] = terms
-
-    @pl.when(step > 0)
-    def _():
-        total[...] += terms
-
-    @pl.when(step == pl.num_programs(0) - 1)
-    def _():
-        store_terms(total, own, outs)
+    rows = slice(first_row, first_row + own.shape[0])
+    for c in range(0, kept.shape[1], chunk):
+        terms = jnp.dot(
+            kept[rows, c : c + chunk], turned[c : c + chunk, :], preferred_element_type=jnp.float32
+        )
+        total[...] = terms if c == 0 else total[...] + terms
+    store_terms(total, own, outs)
 
 
 def weight_grad_kernel(idx, acts, full, mask, out):
@@ -134,29 +118,28 @@
     step = pl.program_id(0)
     first = idx[0] * (pl.num_programs(0) * (width // BLOCK)) + step * (width // BLOCK)
     spread = wide_mask(mask[...], first, width)
-    product = jnp.dot(acts[...], full[...], preferred_element_type=jnp.float32)
-    for b in range(hidden // BLOCK):
-        rows = slice(b * BLOCK, (b + 1) * BLOCK)
-        out[rows, :] = (product[rows, :] * spread[b : b + 1, :]).astype(out.dtype)
-
-
-def finish_kernel(n_pieces, n_parts, *refs):
-    owns, parts, out = refs[:n_pieces], refs[n_pieces:-1], refs[-1]
-    rows = owns[0].shape[0]
-    for p, own in enumerate(owns):
-        mine = parts[p * n_parts : (p + 1) * n_parts]
-        scales = []
-        for part in mine:
-            code = part[rows:, :].astype(jnp.int32).astype(jnp.float32)
-            scales.append(jnp.exp2(code * (1.0 / STEPS)) * (1.0 / CODE))
-        for b in range(rows // BLOCK):
-            at = slice(b * BLOCK, (b + 1) * BLOCK)
-            total = own[at, :]
-            for part, scale in zip(mine, scales, strict=True):
-                got = part[at, :].astype(jnp.int32).astype(jnp.float32)
-                total = total + got * scale[b : b + 1, :]
-            to = p * rows + b * BLOCK
-            out[:, to : to + BLOCK] = total.T.astype(out.dtype)
+    height = 2 * BLOCK if hidden % (2 * BLOCK) == 0 else BLOCK
+    for r in range(0, hidden, height):
+        product = jnp.dot(acts[r : r + height, :], full[...], preferred_element_type=jnp.float32)
+        for b in range(0, height, BLOCK):
+            factor = spread[(r + b) // BLOCK : (r + b) // BLOCK + 1, :]
+            out[r + b : r + b + BLOCK, :] = (product[b : b + BLOCK, :] * factor).astype(out.dtype)
+
+
+def finish_kernel(n_parts, own, *refs):
+    parts, out = refs[:n_parts], refs[-1]
+    rows = own.shape[0]
+    scales = []
+    for part in parts:
+        code = part[rows:, :].astype(jnp.int32).astype(jnp.float32)
+        scales.append(jnp.exp2(code * (1.0 / STEPS)) * (1.0 / CODE))
+    for b in range(rows // BLOCK):
+        at = slice(b * BLOCK, (b + 1) * BLOCK)
+        total = own[at, :]
+        for part, scale in zip(parts, scales, strict=True):
+            got = part[at, :].astype(jnp.int32).astype(jnp.float32)
+            total = total + got * scale[b : b + 1, :]
+        out[:, at] = total.T.astype(out.dtype)
 
 
 def in_vmem():
@@ -227,28 +210,29 @@
     idx = jnp.concatenate([row.astype(jnp.int32).reshape(1), places.astype(jnp.int32)])
 
     weight = pltpu.with_memory_space_constraint(weight, pltpu.HBM)
-    kept, shard_copy = pl.pallas_call(
+    kept = pl.pallas_call(
         keep_kernel,
-        in_specs=[in_smem(), in_vmem(), in_hbm(), in_vmem()],
-        out_specs=[in_vmem(), in_vmem()],
-        out_shape=[
-            pltpu.VMEM((piece, width), bf16),
-            jax.ShapeDtypeStruct(grad_output.shape, bf16),
-        ],
-        scratch_shapes=[pltpu.SemaphoreType.DMA((piece // BLOCK,))],
+        in_specs=[in_smem(), in_hbm(), in_vmem()],
+        out_specs=in_vmem(),
+        out_shape=pltpu.VMEM((hidden, width), bf16),
+        scratch_shapes=[pltpu.SemaphoreType.DMA((blocks,))],
         compiler_params=params(),
-        cost_estimate=cost(piece * width, 2 * piece * width),
+        cost_estimate=cost(hidden * width, 2 * hidden * width),
         name="keep",
-    )(idx, grad_output, weight, block_mask)
+    )(idx, weight, block_mask)
 
     held = {0: grad_output}
-    there, back = grad_output, shard_copy
-    for j in range(1, n_chips // 2 + 1):
-        there = send_ring(there, 1)
-        held[j] = there
+    for j in (1, -1, 2, -2):
+        if abs(j) < n_chips // 2 or j == n_chips // 2:
+            held[j] = send_ring(grad_output, j)
+    waits = [j for j in held if j]
+    kept, *ready = lax.optimization_barrier((kept, *(held[j] for j in waits)))
+    held.update(zip(waits, ready, strict=True))
+    for j in range(3, n_chips // 2 + 1):
+        by = 1 if j % 2 else 2
+        held[j] = send_ring(held[j - by], by)
         if 2 * j < n_chips:
-            back = send_ring(back, -1)
-            held[-j] = back
+            held[-j] = send_ring(held[by - j], -by)
     shards = []
     for j in reach:
         shards += [held[j], send_core(held[j])]
@@ -268,7 +252,7 @@
     code_rows = -(-(piece // BLOCK) // 16) * 16
     sent_shape = jax.ShapeDtypeStruct((piece + code_rows, tokens), jnp.int16)
     own_shape = jax.ShapeDtypeStruct((piece, tokens), jnp.float32)
-    piece_cost = cost(2 * all_tokens * piece * width, 2 * piece * width)
+    piece_cost = cost(piece * width, piece * width // 8)
     full, turned, own, *coded = pl.pallas_call(
         functools.partial(first_terms_kernel, n_shards, n_parts, chunk),
         in_specs=[in_smem()] + [in_vmem()] * n_shards + [in_vmem(), in_hbm()],
@@ -289,21 +273,15 @@
 
     for p in range(1, n_pieces):
         own, *coded = pl.pallas_call(
-            functools.partial(more_terms_kernel, n_parts, p * (piece // BLOCK)),
-            grid=(width // chunk,),
-            in_specs=[
-                in_smem(),
-                pl.BlockSpec((chunk, all_tokens), lambda i: (i, 0)),
-                pl.BlockSpec((piece, chunk), lambda i, p=p: (p, i)),
-                in_vmem(),
-            ],
+            functools.partial(more_terms_kernel, n_parts, p * piece, chunk),
+            in_specs=[in_vmem()] * 2,
             out_specs=[in_vmem()] * (1 + n_parts),
             out_shape=[own_shape] + [sent_shape] * n_parts,
             scratch_shapes=[pltpu.VMEM((piece, all_tokens), jnp.float32)],
             compiler_params=params(),
             cost_estimate=piece_cost,
             name="more_terms",
-        )(idx, turned, weight, block_mask)
+        )(turned, kept)
         owns.append(own)
         parts += [send_row(coded[k], k + 1) for k in range(n_parts)]
 
@@ -319,18 +297,27 @@
         out_specs=pl.BlockSpec((hidden, chunk), lambda i: (0, i)),
         out_shape=jax.ShapeDtypeStruct((hidden, width), bf16),
         compiler_params=params(),
-        cost_estimate=cost(2 * all_tokens * hidden * width, 2 * hidden * width),
+        cost_estimate=cost(hidden * width, hidden * width // 8),
         name="weight_grad",
     )(idx, acts_turned, full, block_mask)
 
-    grad_input = pl.pallas_call(
-        functools.partial(finish_kernel, n_pieces, n_parts),
-        in_specs=[in_vmem()] * (n_pieces * (1 + n_parts)),
-        out_specs=in_vmem(),
-        out_shape=jax.ShapeDtypeStruct((tokens, hidden), bf16),
-        compiler_params=params(),
-        name="add_terms",
-    )(*owns, *parts)
+    grad_input = None
+    for p in range(n_pieces):
+        operands = [owns[p], *parts[p * n_parts : (p + 1) * n_parts]]
+        specs = [in_vmem()] * len(operands)
+        if p:
+            operands.append(grad_input)
+            specs.append(in_hbm())
+        grad_input = pl.pallas_call(
+            functools.partial(finish_kernel, n_parts),
+            grid=(1,),
+            in_specs=specs,
+            out_specs=pl.BlockSpec((tokens, piece), lambda i, p=p: (0, p)),
+            out_shape=jax.ShapeDtypeStruct((tokens, hidden), bf16),
+            input_output_aliases={len(operands) - 1: 0} if p else {},
+            compiler_params=params(),
+            name="add_terms",
+        )(*operands)
     return (grad_input, grad_weight)
 
 

time: 53.9 us -> 45.8 us (0.85)
  waiting for transfers between devices: 11 us -> 5.02 us
  Pallas kernels: 25.1 us -> 21.9 us
  starting transfers between devices: 14.3 us -> 16.4 us
  local copies, waits for them, and re-layouts: 1.61 us -> 0.7 us
    ppermute x7, waiting for transfers between devices: 9.94 us -> 4.3 us  [send_ring(): return lax.ppermute(x, 'col', perm)]
    pallas_call x3 -> x4, Pallas kernels: 13 us -> 9.74 us  [the longest x1 5.93 us: per_device(): pl.pallas_call(keep_kernel, in_specs=[in_smem(), in_hbm(), in_vmem()], ou...]
    ppermute x7, starting transfers between devices: 9.15 us -> 10.9 us  [send_ring(): return lax.ppermute(x, 'col', perm)]
    unnamed x10 -> x6, local copies, waits for them, and re-layouts: 1.61 us -> 0.7 us
  transfers between devices with their start and end apart: 18 -> 18, of which waited for: 6 -> 5; matrix products, arithmetic and copies ran while one was open for 1% -> 2% of each run, Pallas kernels for 39% -> 40%
where the time goes in v4:
time: 45.8 us; the launch traced here: 45.6 us
  Pallas kernels  21.9 us (48%)
  starting transfers between devices  16.4 us (36%)
  waiting for transfers between devices  5.02 us (11%)
  other arithmetic  0.78 us (2%)
  between operations  0.75 us (2%)
  local copies, waits for them, and re-layouts  0.7 us (2%)
    ppermute x7, starting transfers between devices, send_ring(): return lax.ppermute(x, 'col', perm)  10.9 us
    pallas_call x1, Pallas kernels, per_device(): pl.pallas_call(weight_grad_kernel, grid=(width // chunk,), in_specs=[in_s...  8.89 us
    pallas_call x1, Pallas kernels, per_device(): pl.pallas_call(keep_kernel, in_specs=[in_smem(), in_hbm(), in_vmem()], ou...  5.93 us
    ppermute x7, waiting for transfers between devices, send_ring(): return lax.ppermute(x, 'col', perm)  4.3 us
    ppermute x3, starting transfers between devices, send_row(): lax.ppermute(x, 'row', [(r, (r + by) % n_rows) for r in range(n_rows)])  3.94 us
    pallas_call x1, Pallas kernels, per_device(): pl.pallas_call(functools.partial(first_terms_kernel, n_shards, n_parts, c...  3 us
    pallas_call x1, Pallas kernels, per_device(): pl.pallas_call(functools.partial(more_terms_kernel, n_parts, p * piece, c...  2.13 us
    pallas_call x2, Pallas kernels, per_device(): pl.pallas_call(functools.partial(finish_kernel, n_parts), grid=(1,), in_s...  1.68 us
  transfers between devices with their start and end apart: 18, of which 5 were waited for; matrix products, arithmetic and copies ran while one was open for 2% of the time, Pallas kernels for 40%

profile of v4, /device:TPU:0, one launch (start us, length us, event | category | flops | bytes accessed | tf_op | source)
XLA Modules:
  0.0 45.6 jit_solution(16771958393706569776)
XLA Ops:
  0.6 4.0 %collective-permute-start.3 = (bf16[16,4096]{1,0:T(8,128)(2,1)}, bf16[16,4096]{1,0:T(8,128)(2,1)S(1)}, u32[]{:S(2)}, u32[]{:S(2)}) collective-permute-start(bf16[16,4096]{1,0:T(8,128)(2,1)} %refs_0_.3), channel_id=1, source_target_pairs={{2,10},{3,5},{6,14},{7,1},{10,12},{11,3},{14,8},{15,7},{12,4},{13,... | collective-permute-start | bytes 393224 | tf_op jit(solution)/shard_map/ppermute | solution.py:187
  4.6 0.4 collective-permute-start.2
  5.1 1.6 %collective-permute-start.1 = (bf16[16,4096]{1,0:T(8,128)(2,1)}, bf16[16,4096]{1,0:T(8,128)(2,1)S(1)}, u32[]{:S(2)}, u32[]{:S(2)}) collective-permute-start(bf16[16,4096]{1,0:T(8,128)(2,1)} %refs_0_.3), channel_id=1, source_target_pairs={{2,6},{3,1},{6,10},{7,3},{10,14},{11,7},{14,12},{15,11},{12,8},{13... | collective-permute-start | bytes 393224 | tf_op jit(solution)/shard_map/ppermute | solution.py:187
  6.7 0.2 collective-permute-start.4
  6.8 1.8 %collective-permute-start.15 = (bf16[128,1792]{1,0:T(8,128)(2,1)}, bf16[128,1792]{1,0:T(8,128)(2,1)S(1)}, u32[]{:S(2)}, u32[]{:S(2)}) collective-permute-start(bf16[128,1792]{1,0:T(8,128)(2,1)} %refs_0_.2), channel_id=1, source_target_pairs={{0,16},{16,0},{1,17},{17,1},{2,18},{18,2},{3,19},{19,3},{4,20},{20... | collective-permute-start | bytes 1376264 | tf_op jit(solution)/shard_map/ppermute | solution.py:193
  8.6 0.7 %and_select_fusion = s32[16]{0:T(128)S(1)} fusion(s32[16,16]{1,0:T(8,128)} %constant.32.clone, s32[]{:T(128)S(6)} %select_n.11, s32[]{:T(128)S(6)} %mul.3), kind=kLoop, calls=%fused_computation.2 | loop fusion | flops 192 | bytes 136 | tf_op jit(solution)/shard_map/jit(remainder)/select_n | solution.py:209
  9.3 0.1 pad_add_fusion.idx
  9.4 0.0 copy-start.2
  9.4 0.7 %copy-done.2 = s32[14,64]{1,0:T(8,128)S(1)} copy-done((s32[14,64]{1,0:T(8,128)S(1)}, s32[14,64]{1,0:T(8,128)}, u32[]{:S(2)}) %copy-start.2) | copy-done | bytes 3608
  10.1 0.0 copy-start.1
  10.1 0.0 copy-start
  10.1 5.9 %keep.1.refs_16_.kept = bf16[1792,4096]{1,0:T(8,128)(2,1)S(1)} custom-call(s32[17]{0:T(128)S(1)} %pad_add_fusion.idx, bf16[1792,4096]{1,0:T(8,128)(2,1)} %weight.1, s32[14,64]{1,0:T(8,128)S(1)} %copy-done.2), custom_call_target="tpu_custom_call" | custom-call | flops 7340032 | bytes 14680064 | tf_op jit(solution)/shard_map/keep/pallas_call | solution.py:213
  16.0 0.0 collective-permute-done.3.refs_6_
  16.0 0.0 copy-done.1
  16.0 0.1 collective-permute-start
  16.1 0.0 collective-permute-done.2.refs_4_
  16.1 0.0 collective-permute-done.1.refs_2_
  16.1 0.0 collective-permute-done.4.refs_8_
  16.2 0.5 %collective-permute-start.5 = (bf16[16,4096]{1,0:T(8,128)(2,1)S(1)}, bf16[16,4096]{1,0:T(8,128)(2,1)S(1)}, u32[]{:S(2)}, u32[]{:S(2)}) collective-permute-start(bf16[16,4096]{1,0:T(8,128)(2,1)S(1)} %collective-permute-done.1.refs_2_), channel_id=1, source_target_pairs={{0,1},{1,0},{2,3},{3,2},{4,5},{5,4},{6,7},{7,6},{8,9},{9,8},{10,11... | collective-permute-start | bytes 393224 | tf_op jit(solution)/shard_map/ppermute | solution.py:190
  16.7 0.1 collective-permute-start.6
  16.8 1.6 %collective-permute-start.11 = (bf16[16,4096]{1,0:T(8,128)(2,1)S(1)}, bf16[16,4096]{1,0:T(8,128)(2,1)S(1)}, u32[]{:S(2)}, u32[]{:S(2)}) collective-permute-start(bf16[16,4096]{1,0:T(8,128)(2,1)S(1)} %collective-permute-done.4.refs_8_), channel_id=1, source_target_pairs={{2,0},{3,7},{6,2},{7,11},{10,6},{11,15},{14,10},{15,13},{12,14},{1... | collective-permute-start | bytes 393224 | tf_op jit(solution)/shard_map/ppermute | solution.py:187
  18.4 0.0 collective-permute-done.refs_1_
  18.4 1.6 %collective-permute-start.13 = (bf16[16,4096]{1,0:T(8,128)(2,1)S(1)}, bf16[16,4096]{1,0:T(8,128)(2,1)S(1)}, u32[]{:S(2)}, u32[]{:S(2)}) collective-permute-start(bf16[16,4096]{1,0:T(8,128)(2,1)S(1)} %collective-permute-done.3.refs_6_), channel_id=1, source_target_pairs={{2,10},{3,5},{6,14},{7,1},{10,12},{11,3},{14,8},{15,7},{12,4},{13,... | collective-permute-start | bytes 393224 | tf_op jit(solution)/shard_map/ppermute | solution.py:187
  20.0 0.0 collective-permute-done.5.refs_3_
  20.0 1.6 %collective-permute-start.9 = (bf16[16,4096]{1,0:T(8,128)(2,1)S(1)}, bf16[16,4096]{1,0:T(8,128)(2,1)S(1)}, u32[]{:S(2)}, u32[]{:S(2)}) collective-permute-start(bf16[16,4096]{1,0:T(8,128)(2,1)S(1)} %collective-permute-done.3.refs_6_), channel_id=1, source_target_pairs={{2,6},{3,1},{6,10},{7,3},{10,14},{11,7},{14,12},{15,11},{12,8},{13... | collective-permute-start | bytes 393224 | tf_op jit(solution)/shard_map/ppermute | solution.py:187
  21.5 0.0 collective-permute-done.6.refs_5_
  21.5 0.0 collective-permute-start.8
  21.5 0.2 collective-permute-done.11.refs_12_
  21.7 0.3 collective-permute-start.7
  22.1 2.9 %collective-permute-done.13.refs_14_ = bf16[16,4096]{1,0:T(8,128)(2,1)S(1)} collective-permute-done((bf16[16,4096]{1,0:T(8,128)(2,1)S(1)}, bf16[16,4096]{1,0:T(8,128)(2,1)S(1)}, u32[]{:S(2)}, u32[]{:S(2)}) %collective-permute-start.13) | collective-permute-done | bytes 131104 | tf_op jit(solution)/shard_map/ppermute | solution.py:187
  24.9 0.0 collective-permute-start.12
  24.9 1.2 %collective-permute-done.9.refs_10_ = bf16[16,4096]{1,0:T(8,128)(2,1)S(1)} collective-permute-done((bf16[16,4096]{1,0:T(8,128)(2,1)S(1)}, bf16[16,4096]{1,0:T(8,128)(2,1)S(1)}, u32[]{:S(2)}, u32[]{:S(2)}) %collective-permute-start.9) | collective-permute-done | bytes 131104 | tf_op jit(solution)/shard_map/ppermute | solution.py:187
  26.2 0.0 collective-permute-start.14
  26.2 0.0 collective-permute-done.15.refs_1_
  26.2 0.5 %collective-permute-start.10 = (bf16[16,4096]{1,0:T(8,128)(2,1)S(1)}, bf16[16,4096]{1,0:T(8,128)(2,1)S(1)}, u32[]{:S(2)}, u32[]{:S(2)}) collective-permute-start(bf16[16,4096]{1,0:T(8,128)(2,1)S(1)} %collective-permute-done.9.refs_10_), channel_id=1, source_target_pairs={{0,1},{1,0},{2,3},{3,2},{4,5},{5,4},{6,7},{7,6},{8,9},{9,8},{10,11... | collective-permute-start | bytes 393224 | tf_op jit(solution)/shard_map/ppermute | solution.py:190
  26.7 0.0 copy-done
  26.7 0.3 turn.1.refs_17_.acts
  27.0 0.0 collective-permute-done.8.refs_9_
  27.0 0.0 collective-permute-done.7.refs_7_
  27.0 0.0 collective-permute-done.12.refs_13_
  27.0 0.5 %collective-permute-done.14.refs_15_ = bf16[16,4096]{1,0:T(8,128)(2,1)S(1)} collective-permute-done((bf16[16,4096]{1,0:T(8,128)(2,1)S(1)}, bf16[16,4096]{1,0:T(8,128)(2,1)S(1)}, u32[]{:S(2)}, u32[]{:S(2)}) %collective-permute-start.14) | collective-permute-done | bytes 131104 | tf_op jit(solution)/shard_map/ppermute | solution.py:190
  27.5 0.2 collective-permute-done.10.refs_11_
  27.7 3.0 %first_terms.1 = (bf16[256,4096]{1,0:T(8,128)(2,1)S(1)}, bf16[4096,256]{1,0:T(8,128)(2,1)S(1)}, f32[896,128]{1,0:T(8,128)S(1)}, s16[912,128]{1,0:T(8,128)(2,1)S(1)}) custom-call(s32[17]{0:T(128)S(1)} %pad_add_fusion.idx, bf16[16,4096]{1,0:T(8,128)(2,1)S(1)} %copy-done.1, bf16[16,4096]{1,0:T(8,128)(2,1)S(1)} %collective-permute-done.refs_1_, ...), custom_call_target="tpu_custom_call" | custom-call | flops 3670016 | bytes 458752 | tf_op jit(solution)/shard_map/first_terms/pallas_call | solution.py:256
  30.7 0.6 %collective-permute-start.17 = (s16[912,128]{1,0:T(8,128)(2,1)S(1)}, s16[912,128]{1,0:T(8,128)(2,1)S(1)}, u32[]{:S(2)}, u32[]{:S(2)}) collective-permute-start(s16[912,128]{1,0:T(8,128)(2,1)S(1)} %get-tuple-element.22), channel_id=1, source_target_pairs={{0,16},{16,0},{1,17},{17,1},{2,18},{18,2},{3,19},{19,3},{4,20},{20... | collective-permute-start | bytes 700424 | tf_op jit(solution)/shard_map/ppermute | solution.py:193
  31.3 2.1 %more_terms.1 = (f32[896,128]{1,0:T(8,128)S(1)}, s16[912,128]{1,0:T(8,128)(2,1)S(1)}) custom-call(bf16[4096,256]{1,0:T(8,128)(2,1)S(1)} %get-tuple-element.18.turned, bf16[1792,4096]{1,0:T(8,128)(2,1)S(1)} %keep.1.refs_16_.kept), custom_call_target="tpu_custom_call" | custom-call | flops 3670016 | bytes 458752 | tf_op jit(solution)/shard_map/more_terms/pallas_call | solution.py:275
  33.4 1.6 %collective-permute-start.16 = (s16[912,128]{1,0:T(8,128)(2,1)S(1)}, s16[912,128]{1,0:T(8,128)(2,1)S(1)}, u32[]{:S(2)}, u32[]{:S(2)}) collective-permute-start(s16[912,128]{1,0:T(8,128)(2,1)S(1)} %get-tuple-element.20), channel_id=1, source_target_pairs={{0,16},{16,0},{1,17},{17,1},{2,18},{18,2},{3,19},{19,3},{4,20},{20... | collective-permute-start | bytes 700424 | tf_op jit(solution)/shard_map/ppermute | solution.py:193
  35.0 8.9 %weight_grad.1 = bf16[1792,4096]{1,0:T(8,128)(2,1)} custom-call(s32[17]{0:T(128)S(1)} %pad_add_fusion.idx, bf16[1792,256]{1,0:T(8,128)(2,1)S(1)} %turn.1.refs_17_.acts, bf16[256,4096]{1,0:T(8,128)(2,1)S(1)} %get-tuple-element.23.full, s32[14,64]{1,0:T(8,128)S(1)} %copy-done.2), custom_call_target="tpu_custom_call" | custom-call | flops 7340032 | bytes 917504 | tf_op jit(solution)/shard_map/weight_grad/pallas_call | solution.py:288
  43.9 0.0 collective-permute-done.17.refs_0_
  43.9 0.8 %add_terms.2.refs_1_ = bf16[128,1792]{1,0:T(8,128)(2,1)} custom-call(f32[896,128]{1,0:T(8,128)S(1)} %get-tuple-element.21.own, s16[912,128]{1,0:T(8,128)(2,1)S(1)} %collective-permute-done.17.refs_0_), custom_call_target="tpu_custom_call" | custom-call | tf_op jit(solution)/shard_map/add_terms/pallas_call | solution.py:311
  44.7 0.0 collective-permute-done.16.refs_0_
  44.7 0.8 %add_terms.3 = bf16[128,1792]{1,0:T(8,128)(2,1)} custom-call(f32[896,128]{1,0:T(8,128)S(1)} %get-tuple-element.19.own, s16[912,128]{1,0:T(8,128)(2,1)S(1)} %collective-permute-done.16.refs_0_, bf16[128,1792]{1,0:T(8,128)(2,1)} %add_terms.2.refs_1_), custom_call_target="tpu_custom_call", output_to_operand_aliasing={{}: (2, {})} | custom-call | tf_op jit(solution)/shard_map/add_terms/pallas_call | solution.py:311
Async XLA Ops:
  0.6 15.4 %collective-permute-start.3 = (bf16[16,4096]{1,0:T(8,128)(2,1)}, bf16[16,4096]{1,0:T(8,128)(2,1)S(1)}, u32[]{:S(2)}, u32[]{:S(2)}) collective-permute-start(bf16[16,4096]{1,0:T(8,128)(2,1)} %refs_0_.3), channel_id=1, source_target_pairs={{2,10},{3,5},{6,14},{7,1},{10,12},{11,3},{14,8},{15,7},{12,4},{13,... | collective-permute-start | bytes 393224 | tf_op jit(solution)/shard_map/ppermute | solution.py:187
  4.6 11.5 %collective-permute-start.2 = (bf16[16,4096]{1,0:T(8,128)(2,1)}, bf16[16,4096]{1,0:T(8,128)(2,1)S(1)}, u32[]{:S(2)}, u32[]{:S(2)}) collective-permute-start(bf16[16,4096]{1,0:T(8,128)(2,1)} %refs_0_.3), channel_id=1, source_target_pairs={{2,0},{3,7},{6,2},{7,11},{10,6},{11,15},{14,10},{15,13},{12,14},{1... | collective-permute-start | bytes 393224 | tf_op jit(solution)/shard_map/ppermute | solution.py:187
  5.1 11.1 %collective-permute-start.1 = (bf16[16,4096]{1,0:T(8,128)(2,1)}, bf16[16,4096]{1,0:T(8,128)(2,1)S(1)}, u32[]{:S(2)}, u32[]{:S(2)}) collective-permute-start(bf16[16,4096]{1,0:T(8,128)(2,1)} %refs_0_.3), channel_id=1, source_target_pairs={{2,6},{3,1},{6,10},{7,3},{10,14},{11,7},{14,12},{15,11},{12,8},{13... | collective-permute-start | bytes 393224 | tf_op jit(solution)/shard_map/ppermute | solution.py:187
  6.7 9.5 %collective-permute-start.4 = (bf16[16,4096]{1,0:T(8,128)(2,1)}, bf16[16,4096]{1,0:T(8,128)(2,1)S(1)}, u32[]{:S(2)}, u32[]{:S(2)}) collective-permute-start(bf16[16,4096]{1,0:T(8,128)(2,1)} %refs_0_.3), channel_id=1, source_target_pairs={{2,4},{3,11},{6,0},{7,15},{10,2},{11,13},{14,6},{15,9},{12,10},{13... | collective-permute-start | bytes 393224 | tf_op jit(solution)/shard_map/ppermute | solution.py:187
  6.8 19.4 %collective-permute-start.15 = (bf16[128,1792]{1,0:T(8,128)(2,1)}, bf16[128,1792]{1,0:T(8,128)(2,1)S(1)}, u32[]{:S(2)}, u32[]{:S(2)}) collective-permute-start(bf16[128,1792]{1,0:T(8,128)(2,1)} %refs_0_.2), channel_id=1, source_target_pairs={{0,16},{16,0},{1,17},{17,1},{2,18},{18,2},{3,19},{19,3},{4,20},{20... | collective-permute-start | bytes 1376264 | tf_op jit(solution)/shard_map/ppermute | solution.py:193
  9.4 0.7 %copy-start.2 = (s32[14,64]{1,0:T(8,128)S(1)}, s32[14,64]{1,0:T(8,128)}, u32[]{:S(2)}) copy-start(s32[14,64]{1,0:T(8,128)} %mask.3) | copy-start | bytes 10756
  10.1 6.0 %copy-start.1 = (bf16[16,4096]{1,0:T(8,128)(2,1)S(1)}, bf16[16,4096]{1,0:T(8,128)(2,1)}, u32[]{:S(2)}) copy-start(bf16[16,4096]{1,0:T(8,128)(2,1)} %refs_0_.3) | copy-start | bytes 393220
  10.1 16.6 %copy-start = (bf16[128,1792]{1,0:T(8,128)(2,1)S(1)}, bf16[128,1792]{1,0:T(8,128)(2,1)}, u32[]{:S(2)}) copy-start(bf16[128,1792]{1,0:T(8,128)(2,1)} %refs_0_.2) | copy-start | bytes 1376260
  16.0 2.3 %collective-permute-start = (bf16[16,4096]{1,0:T(8,128)(2,1)S(1)}, bf16[16,4096]{1,0:T(8,128)(2,1)S(1)}, u32[]{:S(2)}, u32[]{:S(2)}) collective-permute-start(bf16[16,4096]{1,0:T(8,128)(2,1)S(1)} %copy-done.1), channel_id=1, source_target_pairs={{0,1},{1,0},{2,3},{3,2},{4,5},{5,4},{6,7},{7,6},{8,9},{9,8},{10,11... | collective-permute-start | bytes 393224 | tf_op jit(solution)/shard_map/ppermute | solution.py:190
  16.2 3.8 %collective-permute-start.5 = (bf16[16,4096]{1,0:T(8,128)(2,1)S(1)}, bf16[16,4096]{1,0:T(8,128)(2,1)S(1)}, u32[]{:S(2)}, u32[]{:S(2)}) collective-permute-start(bf16[16,4096]{1,0:T(8,128)(2,1)S(1)} %collective-permute-done.1.refs_2_), channel_id=1, source_target_pairs={{0,1},{1,0},{2,3},{3,2},{4,5},{5,4},{6,7},{7,6},{8,9},{9,8},{10,11... | collective-permute-start | bytes 393224 | tf_op jit(solution)/shard_map/ppermute | solution.py:190
  16.7 4.8 %collective-permute-start.6 = (bf16[16,4096]{1,0:T(8,128)(2,1)S(1)}, bf16[16,4096]{1,0:T(8,128)(2,1)S(1)}, u32[]{:S(2)}, u32[]{:S(2)}) collective-permute-start(bf16[16,4096]{1,0:T(8,128)(2,1)S(1)} %collective-permute-done.2.refs_4_), channel_id=1, source_target_pairs={{0,1},{1,0},{2,3},{3,2},{4,5},{5,4},{6,7},{7,6},{8,9},{9,8},{10,11... | collective-permute-start | bytes 393224 | tf_op jit(solution)/shard_map/ppermute | solution.py:190
  16.8 5.0 %collective-permute-start.11 = (bf16[16,4096]{1,0:T(8,128)(2,1)S(1)}, bf16[16,4096]{1,0:T(8,128)(2,1)S(1)}, u32[]{:S(2)}, u32[]{:S(2)}) collective-permute-start(bf16[16,4096]{1,0:T(8,128)(2,1)S(1)} %collective-permute-done.4.refs_8_), channel_id=1, source_target_pairs={{2,0},{3,7},{6,2},{7,11},{10,6},{11,15},{14,10},{15,13},{12,14},{1... | collective-permute-start | bytes 393224 | tf_op jit(solution)/shard_map/ppermute | solution.py:187
  18.4 6.6 %collective-permute-start.13 = (bf16[16,4096]{1,0:T(8,128)(2,1)S(1)}, bf16[16,4096]{1,0:T(8,128)(2,1)S(1)}, u32[]{:S(2)}, u32[]{:S(2)}) collective-permute-start(bf16[16,4096]{1,0:T(8,128)(2,1)S(1)} %collective-permute-done.3.refs_6_), channel_id=1, source_target_pairs={{2,10},{3,5},{6,14},{7,1},{10,12},{11,3},{14,8},{15,7},{12,4},{13,... | collective-permute-start | bytes 393224 | tf_op jit(solution)/shard_map/ppermute | solution.py:187
  20.0 6.2 %collective-permute-start.9 = (bf16[16,4096]{1,0:T(8,128)(2,1)S(1)}, bf16[16,4096]{1,0:T(8,128)(2,1)S(1)}, u32[]{:S(2)}, u32[]{:S(2)}) collective-permute-start(bf16[16,4096]{1,0:T(8,128)(2,1)S(1)} %collective-permute-done.3.refs_6_), channel_id=1, source_target_pairs={{2,6},{3,1},{6,10},{7,3},{10,14},{11,7},{14,12},{15,11},{12,8},{13... | collective-permute-start | bytes 393224 | tf_op jit(solution)/shard_map/ppermute | solution.py:187
  21.5 5.4 %collective-permute-start.8 = (bf16[16,4096]{1,0:T(8,128)(2,1)S(1)}, bf16[16,4096]{1,0:T(8,128)(2,1)S(1)}, u32[]{:S(2)}, u32[]{:S(2)}) collective-permute-start(bf16[16,4096]{1,0:T(8,128)(2,1)S(1)} %collective-permute-done.4.refs_8_), channel_id=1, source_target_pairs={{0,1},{1,0},{2,3},{3,2},{4,5},{5,4},{6,7},{7,6},{8,9},{9,8},{10,11... | collective-permute-start | bytes 393224 | tf_op jit(solution)/shard_map/ppermute | solution.py:190
  21.7 5.2 %collective-permute-start.7 = (bf16[16,4096]{1,0:T(8,128)(2,1)S(1)}, bf16[16,4096]{1,0:T(8,128)(2,1)S(1)}, u32[]{:S(2)}, u32[]{:S(2)}) collective-permute-start(bf16[16,4096]{1,0:T(8,128)(2,1)S(1)} %collective-permute-done.3.refs_6_), channel_id=1, source_target_pairs={{0,1},{1,0},{2,3},{3,2},{4,5},{5,4},{6,7},{7,6},{8,9},{9,8},{10,11... | collective-permute-start | bytes 393224 | tf_op jit(solution)/shard_map/ppermute | solution.py:190
  24.9 2.1 %collective-permute-start.12 = (bf16[16,4096]{1,0:T(8,128)(2,1)S(1)}, bf16[16,4096]{1,0:T(8,128)(2,1)S(1)}, u32[]{:S(2)}, u32[]{:S(2)}) collective-permute-start(bf16[16,4096]{1,0:T(8,128)(2,1)S(1)} %collective-permute-done.11.refs_12_), channel_id=1, source_target_pairs={{0,1},{1,0},{2,3},{3,2},{4,5},{5,4},{6,7},{7,6},{8,9},{9,8},{10,11... | collective-permute-start | bytes 393224 | tf_op jit(solution)/shard_map/ppermute | solution.py:190
  26.2 1.3 %collective-permute-start.14 = (bf16[16,4096]{1,0:T(8,128)(2,1)S(1)}, bf16[16,4096]{1,0:T(8,128)(2,1)S(1)}, u32[]{:S(2)}, u32[]{:S(2)}) collective-permute-start(bf16[16,4096]{1,0:T(8,128)(2,1)S(1)} %collective-permute-done.13.refs_14_), channel_id=1, source_target_pairs={{0,1},{1,0},{2,3},{3,2},{4,5},{5,4},{6,7},{7,6},{8,9},{9,8},{10,11... | collective-permute-start | bytes 393224 | tf_op jit(solution)/shard_map/ppermute | solution.py:190
  26.2 1.5 %collective-permute-start.10 = (bf16[16,4096]{1,0:T(8,128)(2,1)S(1)}, bf16[16,4096]{1,0:T(8,128)(2,1)S(1)}, u32[]{:S(2)}, u32[]{:S(2)}) collective-permute-start(bf16[16,4096]{1,0:T(8,128)(2,1)S(1)} %collective-permute-done.9.refs_10_), channel_id=1, source_target_pairs={{0,1},{1,0},{2,3},{3,2},{4,5},{5,4},{6,7},{7,6},{8,9},{9,8},{10,11... | collective-permute-start | bytes 393224 | tf_op jit(solution)/shard_map/ppermute | solution.py:190
  30.7 13.2 %collective-permute-start.17 = (s16[912,128]{1,0:T(8,128)(2,1)S(1)}, s16[912,128]{1,0:T(8,128)(2,1)S(1)}, u32[]{:S(2)}, u32[]{:S(2)}) collective-permute-start(s16[912,128]{1,0:T(8,128)(2,1)S(1)} %get-tuple-element.22), channel_id=1, source_target_pairs={{0,16},{16,0},{1,17},{17,1},{2,18},{18,2},{3,19},{19,3},{4,20},{20... | collective-permute-start | bytes 700424 | tf_op jit(solution)/shard_map/ppermute | solution.py:193
  33.4 11.3 %collective-permute-start.16 = (s16[912,128]{1,0:T(8,128)(2,1)S(1)}, s16[912,128]{1,0:T(8,128)(2,1)S(1)}, u32[]{:S(2)}, u32[]{:S(2)}) collective-permute-start(s16[912,128]{1,0:T(8,128)(2,1)S(1)} %get-tuple-element.20), channel_id=1, source_target_pairs={{0,16},{16,0},{1,17},{17,1},{2,18},{18,2},{3,19},{19,3},{4,20},{20... | collective-permute-start | bytes 700424 | tf_op jit(solution)/shard_map/ppermute | solution.py:193

commit v5 on v4

--- a/solution.py
+++ b/solution.py
@@ -45,19 +45,22 @@
     )
 
 
-def keep_kernel(idx, weight, mask, kept, sems):
+def keep_kernel(place, weight, mask, kept, spread, mask_here, mask_sem, sems):
     rows, width = kept.shape
-    blocks = rows // BLOCK
+    mask_copy = pltpu.make_async_copy(mask, mask_here, mask_sem)
+    mask_copy.start()
     copies = []
-    for b in range(blocks):
+    for b in range(rows // BLOCK):
         at = pl.ds(b * BLOCK, BLOCK)
         copies.append(pltpu.make_async_copy(weight.at[at, :], kept.at[at, :], sems.at[b]))
         copies[-1].start()
-    spread = wide_mask(mask[...], idx[0] * (width // BLOCK), width).astype(jnp.bfloat16)
-    for b in range(blocks):
-        copies[b].wait()
+    mask_copy.wait()
+    spread[...] = wide_mask(mask_here[...], place[0] * (width // BLOCK), width)
+    factors = spread[...].astype(jnp.bfloat16)
+    for b, copy in enumerate(copies):
+        copy.wait()
         at = slice(b * BLOCK, (b + 1) * BLOCK)
-        kept[at, :] = kept[at, :] * spread[b : b + 1, :]
+        kept[at, :] = kept[at, :] * factors[b : b + 1, :]
 
 
 def turn_kernel(n_rows, *refs):
@@ -83,47 +86,73 @@
         out[rows:, :] = codes.astype(jnp.int16)
 
 
-def first_terms_kernel(n_shards, n_parts, chunk, idx, *refs):
+def first_terms_kernel(n_shards, n_parts, shift, chunk, place, table, *refs):
     shards = refs[:n_shards]
-    kept, _, full, turned, own = refs[n_shards : n_shards + 5]
-    outs = refs[n_shards + 5 : n_shards + 5 + n_parts]
-    total = refs[n_shards + 5 + n_parts]
+    kept, weight, _, full, turned, own = refs[n_shards : n_shards + 6]
+    outs = refs[n_shards + 6 : n_shards + 6 + n_parts]
+    *rest, total, sems = refs[n_shards + 6 + n_parts :]
+    piece = own.shape[0]
+    copies = []
+    for p, later in enumerate(rest):
+        at = pl.ds((p + 1) * piece, piece)
+        copies.append(pltpu.make_async_copy(weight.at[at, :], later, sems.at[p]))
+        copies[-1].start()
     rows = shards[0].shape[0]
+    n_cols = table.shape[0]
     for n, shard in enumerate(shards):
-        full[pl.ds(pl.multiple_of(idx[n + 1] * rows, rows), rows), :] = shard[...]
+        to = lax.rem(table[place[1], n] + n_cols - place[0] * shift, n_cols)
+        full[pl.ds(pl.multiple_of(to * rows, rows), rows), :] = shard[...]
     for c in range(0, full.shape[1], chunk):
         turned[c : c + chunk, :] = full[:, c : c + chunk].T
         terms = jnp.dot(
-            kept[: own.shape[0], c : c + chunk],
-            turned[c : c + chunk, :],
-            preferred_element_type=jnp.float32,
+            kept[:, c : c + chunk], turned[c : c + chunk, :], preferred_element_type=jnp.float32
         )
         total[...] = terms if c == 0 else total[...] + terms
     store_terms(total, own, outs)
-
-
-def more_terms_kernel(n_parts, first_row, chunk, turned, kept, own, *refs):
+    for copy in copies:
+        copy.wait()
+
+
+def more_terms_kernel(n_parts, first_block, chunk, turned, weight, spread, own, *refs):
     outs, total = refs[:n_parts], refs[n_parts]
-    rows = slice(first_row, first_row + own.shape[0])
-    for c in range(0, kept.shape[1], chunk):
-        terms = jnp.dot(
-            kept[rows, c : c + chunk], turned[c : c + chunk, :], preferred_element_type=jnp.float32
+    blocks = own.shape[0] // BLOCK
+    for c in range(0, weight.shape[1], chunk):
+        cols = slice(c, c + chunk)
+        factors = spread[first_block : first_block + blocks, cols].astype(jnp.bfloat16)
+        kept = jnp.concatenate(
+            [weight[b * BLOCK : (b + 1) * BLOCK, cols] * factors[b : b + 1, :] for b in range(blocks)],
+            axis=0,
         )
+        terms = jnp.dot(kept, turned[cols, :], preferred_element_type=jnp.float32)
         total[...] = terms if c == 0 else total[...] + terms
     store_terms(total, own, outs)
 
 
-def weight_grad_kernel(idx, acts, full, mask, out):
+def weight_grad_kernel(chunk, acts, full, spread, out, held, sems):
     hidden, width = out.shape
-    step = pl.program_id(0)
-    first = idx[0] * (pl.num_programs(0) * (width // BLOCK)) + step * (width // BLOCK)
-    spread = wide_mask(mask[...], first, width)
-    height = 2 * BLOCK if hidden % (2 * BLOCK) == 0 else BLOCK
-    for r in range(0, hidden, height):
-        product = jnp.dot(acts[r : r + height, :], full[...], preferred_element_type=jnp.float32)
-        for b in range(0, height, BLOCK):
-            factor = spread[(r + b) // BLOCK : (r + b) // BLOCK + 1, :]
-            out[r + b : r + b + BLOCK, :] = (product[b : b + BLOCK, :] * factor).astype(out.dtype)
+    blocks = hidden // BLOCK
+    pair = 2 if blocks % 2 == 0 else 1
+
+    def leave(block):
+        at = pl.ds(pl.multiple_of(block * BLOCK, BLOCK), BLOCK)
+        return pltpu.make_async_copy(held.at[at, :], out.at[at, :], sems.at[block])
+
+    def rows(step, _):
+        first = step * pair
+        left = acts[pl.ds(pl.multiple_of(first * BLOCK, pair * BLOCK), pair * BLOCK), :]
+        for c in range(0, width, chunk):
+            cols = slice(c, c + chunk)
+            product = jnp.dot(left, full[:, cols], preferred_element_type=jnp.float32)
+            for b in range(pair):
+                at = pl.ds(pl.multiple_of((first + b) * BLOCK, BLOCK), BLOCK)
+                part = product[b * BLOCK : (b + 1) * BLOCK, :] * spread[pl.ds(first + b, 1), cols]
+                held[at, cols] = part.astype(out.dtype)
+        for b in range(pair):
+            leave(first + b).start()
+        return 0
+
+    lax.fori_loop(0, blocks // pair, rows, 0)
+    lax.fori_loop(0, blocks, lambda block, _: (leave(block).wait(), 0)[1], 0)
 
 
 def finish_kernel(n_parts, own, *refs):
@@ -205,29 +234,34 @@
             q = (p - j if of_core == 0 else p + j) % n_chips
             line.append(ring[q] * 2 + of_core)
         table.append(line)
-    sources = lax.dynamic_index_in_dim(jnp.array(table, jnp.int32), col, 0, keepdims=False)
-    places = (sources - row * (tokens // shard_rows)) % n_cols
-    idx = jnp.concatenate([row.astype(jnp.int32).reshape(1), places.astype(jnp.int32)])
+    place = jnp.stack([row, col]).astype(jnp.int32)
 
     weight = pltpu.with_memory_space_constraint(weight, pltpu.HBM)
-    kept = pl.pallas_call(
+    kept, spread = pl.pallas_call(
         keep_kernel,
-        in_specs=[in_smem(), in_hbm(), in_vmem()],
-        out_specs=in_vmem(),
-        out_shape=pltpu.VMEM((hidden, width), bf16),
-        scratch_shapes=[pltpu.SemaphoreType.DMA((blocks,))],
+        in_specs=[in_smem(), in_hbm(), in_hbm()],
+        out_specs=[in_vmem()] * 2,
+        out_shape=[
+            pltpu.VMEM((piece, width), bf16),
+            pltpu.VMEM((blocks, width), jnp.float32),
+        ],
+        scratch_shapes=[
+            pltpu.VMEM(block_mask.shape, jnp.int32),
+            pltpu.SemaphoreType.DMA,
+            pltpu.SemaphoreType.DMA((piece // BLOCK,)),
+        ],
         compiler_params=params(),
-        cost_estimate=cost(hidden * width, 2 * hidden * width),
+        cost_estimate=cost(piece * width, 2 * piece * width),
         name="keep",
-    )(idx, weight, block_mask)
+    )(place, weight, block_mask)
 
     held = {0: grad_output}
-    for j in (1, -1, 2, -2):
+    for j in (2, -2, 1, -1):
         if abs(j) < n_chips // 2 or j == n_chips // 2:
             held[j] = send_ring(grad_output, j)
-    waits = [j for j in held if j]
-    kept, *ready = lax.optimization_barrier((kept, *(held[j] for j in waits)))
-    held.update(zip(waits, ready, strict=True))
+    near = [j for j in held if j]
+    kept, *ready = lax.optimization_barrier((kept, *(held[j] for j in near)))
+    held.update(zip(near, ready, strict=True))
     for j in range(3, n_chips // 2 + 1):
         by = 1 if j % 2 else 2
         held[j] = send_ring(held[j - by], by)
@@ -252,54 +286,58 @@
     code_rows = -(-(piece // BLOCK) // 16) * 16
     sent_shape = jax.ShapeDtypeStruct((piece + code_rows, tokens), jnp.int16)
     own_shape = jax.ShapeDtypeStruct((piece, tokens), jnp.float32)
-    piece_cost = cost(piece * width, piece * width // 8)
+    small_cost = cost(piece * width, piece * width // 8)
+    later = n_pieces - 1
     full, turned, own, *coded = pl.pallas_call(
-        functools.partial(first_terms_kernel, n_shards, n_parts, chunk),
-        in_specs=[in_smem()] + [in_vmem()] * n_shards + [in_vmem(), in_hbm()],
-        out_specs=[in_vmem()] * (3 + n_parts),
+        functools.partial(first_terms_kernel, n_shards, n_parts, tokens // shard_rows, chunk),
+        in_specs=[in_smem()] * 2 + [in_vmem()] * n_shards + [in_vmem(), in_hbm(), in_hbm()],
+        out_specs=[in_vmem()] * (3 + n_parts + later),
         out_shape=[
             jax.ShapeDtypeStruct((all_tokens, width), bf16),
             jax.ShapeDtypeStruct((width, all_tokens), bf16),
             own_shape,
         ]
-        + [sent_shape] * n_parts,
-        scratch_shapes=[pltpu.VMEM((piece, all_tokens), jnp.float32)],
+        + [sent_shape] * n_parts
+        + [pltpu.VMEM((piece, width), bf16)] * later,
+        scratch_shapes=[
+            pltpu.VMEM((piece, all_tokens), jnp.float32),
+            pltpu.SemaphoreType.DMA((max(later, 1),)),
+        ],
         compiler_params=params(),
-        cost_estimate=piece_cost,
+        cost_estimate=small_cost,
         name="first_terms",
-    )(idx, *shards, kept, acts_turned)
+    )(place, jnp.array(table, jnp.int32), *shards, kept, weight, acts_turned)
     owns = [own]
+    coded, rest = coded[:n_parts], coded[n_parts:]
     parts = [send_row(coded[k], k + 1) for k in range(n_parts)]
 
     for p in range(1, n_pieces):
         own, *coded = pl.pallas_call(
-            functools.partial(more_terms_kernel, n_parts, p * piece, chunk),
-            in_specs=[in_vmem()] * 2,
+            functools.partial(more_terms_kernel, n_parts, p * (piece // BLOCK), chunk),
+            in_specs=[in_vmem()] * 3,
             out_specs=[in_vmem()] * (1 + n_parts),
             out_shape=[own_shape] + [sent_shape] * n_parts,
             scratch_shapes=[pltpu.VMEM((piece, all_tokens), jnp.float32)],
             compiler_params=params(),
-            cost_estimate=piece_cost,
+            cost_estimate=small_cost,
             name="more_terms",
-        )(turned, kept)
+        )(turned, rest[p - 1], spread)
         owns.append(own)
         parts += [send_row(coded[k], k + 1) for k in range(n_parts)]
 
     grad_weight = pl.pallas_call(
-        weight_grad_kernel,
-        grid=(width // chunk,),
-        in_specs=[
-            in_smem(),
-            in_vmem(),
-            pl.BlockSpec((all_tokens, chunk), lambda i: (0, i)),
-            in_vmem(),
+        functools.partial(weight_grad_kernel, chunk),
+        in_specs=[in_vmem()] * 3,
+        out_specs=in_hbm(),
+        out_shape=jax.ShapeDtypeStruct((hidden, width), bf16),
+        scratch_shapes=[
+            pltpu.VMEM((hidden, width), bf16),
+            pltpu.SemaphoreType.DMA((blocks,)),
         ],
-        out_specs=pl.BlockSpec((hidden, chunk), lambda i: (0, i)),
-        out_shape=jax.ShapeDtypeStruct((hidden, width), bf16),
         compiler_params=params(),
-        cost_estimate=cost(hidden * width, hidden * width // 8),
+        cost_estimate=small_cost,
         name="weight_grad",
-    )(idx, acts_turned, full, block_mask)
+    )(acts_turned, full, spread)
 
     grad_input = None
     for p in range(n_pieces):

time: 45.8 us -> 45.6 us (level)
  waiting for transfers between devices: 5.02 us -> 9.61 us
  Pallas kernels: 21.9 us -> 18.2 us
  other arithmetic: 0.78 us -> 0.07 us
    pallas_call x4, Pallas kernels: 20 us -> 16.2 us  [the longest x1 6.43 us: per_device(): pl.pallas_call(functools.partial(weight_grad_kernel, chunk), in_specs=[in...]
    ppermute x7, waiting for transfers between devices: 4.3 us -> 7.35 us  [send_ring(): return lax.ppermute(x, 'col', perm)]
    ppermute x7, starting transfers between devices: 10.9 us -> 9.57 us  [send_ring(): return lax.ppermute(x, 'col', perm)]
    ppermute x3, waiting for transfers between devices: 0.01 us -> 1.29 us  [send_row(): lax.ppermute(x, 'row', [(r, (r + by) % n_rows) for r in range(n_rows)])]
    ppermute x3, starting transfers between devices: 3.94 us -> 5.19 us  [send_row(): lax.ppermute(x, 'row', [(r, (r + by) % n_rows) for r in range(n_rows)])]
    select_n x1 -> x0, other arithmetic: 0.7 us -> none  [per_device(): places = (sources - row * (tokens // shard_rows)) % n_cols]
  transfers between devices with their start and end apart: 18 -> 18, of which waited for: 5 -> 8; matrix products, arithmetic and copies ran while one was open for 2% -> 0% of each run, Pallas kernels for 40% -> 30%
where the time goes in v5:
time: 45.6 us; the launch traced here: 45.4 us
  Pallas kernels  18.2 us (40%)
  starting transfers between devices  16.1 us (35%)
  waiting for transfers between devices  9.61 us (21%)
  between operations  0.73 us (2%)
  local copies, waits for them, and re-layouts  0.71 us (2%)
    ppermute x7, starting transfers between devices, send_ring(): return lax.ppermute(x, 'col', perm)  9.57 us
    ppermute x7, waiting for transfers between devices, send_ring(): return lax.ppermute(x, 'col', perm)  7.35 us
    pallas_call x1, Pallas kernels, per_device(): pl.pallas_call(functools.partial(weight_grad_kernel, chunk), in_specs=[in...  6.43 us
    ppermute x3, starting transfers between devices, send_row(): lax.ppermute(x, 'row', [(r, (r + by) % n_rows) for r in range(n_rows)])  5.19 us
    pallas_call x1, Pallas kernels, per_device(): pl.pallas_call(functools.partial(first_terms_kernel, n_shards, n_parts, t...  3.88 us
    pallas_call x1, Pallas kernels, per_device(): pl.pallas_call(keep_kernel, in_specs=[in_smem(), in_hbm(), in_hbm()], out...  3.8 us
    pallas_call x1, Pallas kernels, per_device(): pl.pallas_call(functools.partial(more_terms_kernel, n_parts, p * (piece /...  2.1 us
    pallas_call x2, Pallas kernels, per_device(): pl.pallas_call(functools.partial(finish_kernel, n_parts), grid=(1,), in_s...  1.69 us
  transfers between devices with their start and end apart: 18, of which 8 were waited for; matrix products, arithmetic and copies ran while one was open for 0% of the time, Pallas kernels for 30%

profile of v5, /device:TPU:0, one launch (start us, length us, event | category | flops | bytes accessed | tf_op | source)
XLA Modules:
  0.0 45.4 jit_solution(17583191207734403722)
XLA Ops:
  0.6 3.0 %collective-permute-start.15 = (bf16[128,1792]{1,0:T(8,128)(2,1)}, bf16[128,1792]{1,0:T(8,128)(2,1)S(1)}, u32[]{:S(2)}, u32[]{:S(2)}) collective-permute-start(bf16[128,1792]{1,0:T(8,128)(2,1)} %refs_0_.2), channel_id=1, source_target_pairs={{0,16},{16,0},{1,17},{17,1},{2,18},{18,2},{3,19},{19,3},{4,20},{20... | collective-permute-start | bytes 1376264 | tf_op jit(solution)/shard_map/ppermute | solution.py:222
  3.7 1.5 %collective-permute-start.3 = (bf16[16,4096]{1,0:T(8,128)(2,1)}, bf16[16,4096]{1,0:T(8,128)(2,1)S(1)}, u32[]{:S(2)}, u32[]{:S(2)}) collective-permute-start(bf16[16,4096]{1,0:T(8,128)(2,1)} %refs_0_.3), channel_id=1, source_target_pairs={{2,6},{3,1},{6,10},{7,3},{10,14},{11,7},{14,12},{15,11},{12,8},{13... | collective-permute-start | bytes 393224 | tf_op jit(solution)/shard_map/ppermute | solution.py:216
  5.2 1.5 %collective-permute-start.2 = (bf16[16,4096]{1,0:T(8,128)(2,1)}, bf16[16,4096]{1,0:T(8,128)(2,1)S(1)}, u32[]{:S(2)}, u32[]{:S(2)}) collective-permute-start(bf16[16,4096]{1,0:T(8,128)(2,1)} %refs_0_.3), channel_id=1, source_target_pairs={{2,4},{3,11},{6,0},{7,15},{10,2},{11,13},{14,6},{15,9},{12,10},{13... | collective-permute-start | bytes 393224 | tf_op jit(solution)/shard_map/ppermute | solution.py:216
  6.7 1.4 %collective-permute-start.1 = (bf16[16,4096]{1,0:T(8,128)(2,1)}, bf16[16,4096]{1,0:T(8,128)(2,1)S(1)}, u32[]{:S(2)}, u32[]{:S(2)}) collective-permute-start(bf16[16,4096]{1,0:T(8,128)(2,1)} %refs_0_.3), channel_id=1, source_target_pairs={{2,10},{3,5},{6,14},{7,1},{10,12},{11,3},{14,8},{15,7},{12,4},{13,... | collective-permute-start | bytes 393224 | tf_op jit(solution)/shard_map/ppermute | solution.py:216
  8.1 0.5 %collective-permute-start.4 = (bf16[16,4096]{1,0:T(8,128)(2,1)}, bf16[16,4096]{1,0:T(8,128)(2,1)S(1)}, u32[]{:S(2)}, u32[]{:S(2)}) collective-permute-start(bf16[16,4096]{1,0:T(8,128)(2,1)} %refs_0_.3), channel_id=1, source_target_pairs={{2,0},{3,7},{6,2},{7,11},{10,6},{11,15},{14,10},{15,13},{12,14},{1... | collective-permute-start | bytes 393224 | tf_op jit(solution)/shard_map/ppermute | solution.py:216
  8.6 0.1 pad_add_fusion.place
  8.7 0.0 copy-start.3
  8.7 0.7 %copy-done.3 = s32[14,64]{1,0:T(8,128)S(1)} copy-done((s32[14,64]{1,0:T(8,128)S(1)}, s32[14,64]{1,0:T(8,128)}, u32[]{:S(2)}) %copy-start.3) | copy-done | bytes 3608
  9.4 0.0 copy-start.1
  9.4 0.0 copy-start
  9.4 0.0 copy-start.2
  9.4 3.8 %keep.1 = (bf16[896,4096]{1,0:T(8,128)(2,1)S(1)}, f32[14,4096]{1,0:T(8,128)S(1)}) custom-call(s32[2]{0:T(128)S(1)} %pad_add_fusion.place, bf16[1792,4096]{1,0:T(8,128)(2,1)} %refs_17_.1, s32[14,64]{1,0:T(8,128)S(1)} %copy-done.3), custom_call_target="tpu_custom_call" | custom-call | flops 3670016 | bytes 7340032 | tf_op jit(solution)/shard_map/keep/pallas_call | solution.py:240
  13.2 0.0 collective-permute-done.3.refs_2_
  13.2 0.0 copy-done.1
  13.2 0.1 collective-permute-start
  13.3 0.4 collective-permute-done.2.refs_8_
  13.7 1.7 %collective-permute-done.1.refs_6_ = bf16[16,4096]{1,0:T(8,128)(2,1)S(1)} collective-permute-done((bf16[16,4096]{1,0:T(8,128)(2,1)}, bf16[16,4096]{1,0:T(8,128)(2,1)S(1)}, u32[]{:S(2)}, u32[]{:S(2)}) %collective-permute-start.1) | collective-permute-done | bytes 131104 | tf_op jit(solution)/shard_map/ppermute | solution.py:216
  15.4 0.0 collective-permute-done.4.refs_4_
  15.4 0.1 collective-permute-start.5
  15.5 0.4 collective-permute-start.6
  15.9 2.8 %collective-permute-start.11 = (bf16[16,4096]{1,0:T(8,128)(2,1)S(1)}, bf16[16,4096]{1,0:T(8,128)(2,1)S(1)}, u32[]{:S(2)}, u32[]{:S(2)}) collective-permute-start(bf16[16,4096]{1,0:T(8,128)(2,1)S(1)} %collective-permute-done.2.refs_8_), channel_id=1, source_target_pairs={{2,0},{3,7},{6,2},{7,11},{10,6},{11,15},{14,10},{15,13},{12,14},{1... | collective-permute-start | bytes 393224 | tf_op jit(solution)/shard_map/ppermute | solution.py:216
  18.7 0.0 collective-permute-done.refs_1_
  18.7 0.4 collective-permute-start.13
  19.1 0.0 collective-permute-done.5.refs_3_
  19.1 1.5 %collective-permute-start.9 = (bf16[16,4096]{1,0:T(8,128)(2,1)S(1)}, bf16[16,4096]{1,0:T(8,128)(2,1)S(1)}, u32[]{:S(2)}, u32[]{:S(2)}) collective-permute-start(bf16[16,4096]{1,0:T(8,128)(2,1)S(1)} %collective-permute-done.1.refs_6_), channel_id=1, source_target_pairs={{2,6},{3,1},{6,10},{7,3},{10,14},{11,7},{14,12},{15,11},{12,8},{13... | collective-permute-start | bytes 393224 | tf_op jit(solution)/shard_map/ppermute | solution.py:216
  20.6 0.0 collective-permute-done.6.refs_5_
  20.6 0.2 collective-permute-start.8
  20.7 1.7 %collective-permute-done.11.refs_12_ = bf16[16,4096]{1,0:T(8,128)(2,1)S(1)} collective-permute-done((bf16[16,4096]{1,0:T(8,128)(2,1)S(1)}, bf16[16,4096]{1,0:T(8,128)(2,1)S(1)}, u32[]{:S(2)}, u32[]{:S(2)}) %collective-permute-start.11) | collective-permute-done | bytes 131104 | tf_op jit(solution)/shard_map/ppermute | solution.py:216
  22.4 0.0 collective-permute-start.7
  22.4 3.5 %collective-permute-done.13.refs_14_ = bf16[16,4096]{1,0:T(8,128)(2,1)S(1)} collective-permute-done((bf16[16,4096]{1,0:T(8,128)(2,1)S(1)}, bf16[16,4096]{1,0:T(8,128)(2,1)S(1)}, u32[]{:S(2)}, u32[]{:S(2)}) %collective-permute-start.13) | collective-permute-done | bytes 131104 | tf_op jit(solution)/shard_map/ppermute | solution.py:216
  26.0 0.0 collective-permute-start.12
  26.0 0.0 collective-permute-done.9.refs_10_
  26.0 0.5 %collective-permute-start.14 = (bf16[16,4096]{1,0:T(8,128)(2,1)S(1)}, bf16[16,4096]{1,0:T(8,128)(2,1)S(1)}, u32[]{:S(2)}, u32[]{:S(2)}) collective-permute-start(bf16[16,4096]{1,0:T(8,128)(2,1)S(1)} %collective-permute-done.13.refs_14_), channel_id=1, source_target_pairs={{0,1},{1,0},{2,3},{3,2},{4,5},{5,4},{6,7},{7,6},{8,9},{9,8},{10,11... | collective-permute-start | bytes 393224 | tf_op jit(solution)/shard_map/ppermute | solution.py:219
  26.5 0.0 collective-permute-done.15.refs_1_
  26.5 0.1 collective-permute-start.10
  26.5 0.0 copy-done
  26.5 0.3 turn.1.refs_18_.acts
  26.8 0.0 collective-permute-done.8.refs_9_
  26.8 0.0 collective-permute-done.7.refs_7_
  26.9 0.4 collective-permute-done.12.refs_13_
  27.3 0.2 collective-permute-done.14.refs_15_
  27.5 0.3 collective-permute-done.10.refs_11_
  27.8 0.0 copy-done.2
  27.8 3.9 %first_terms.1 = (bf16[256,4096]{1,0:T(8,128)(2,1)S(1)}, bf16[4096,256]{1,0:T(8,128)(2,1)S(1)}, f32[896,128]{1,0:T(8,128)S(1)}, s16[912,128]{1,0:T(8,128)(2,1)S(1)}, bf16[896,4096]{1,0:T(8,128)(2,1)S(1)}) custom-call(s32[2]{0:T(128)S(1)} %pad_add_fusion.place, s32[16,16]{1,0:T(8,128)S(1)} %copy-done.2, bf16[16,4096]{1,0:T(8,128)(2,1)S(1)} %copy-done.1, ...), custom_call_target="tpu_custom_call" | custom-call | flops 3670016 | bytes 458752 | tf_op jit(solution)/shard_map/first_terms/pallas_call | solution.py:291
  31.7 0.5 %collective-permute-start.17 = (s16[912,128]{1,0:T(8,128)(2,1)S(1)}, s16[912,128]{1,0:T(8,128)(2,1)S(1)}, u32[]{:S(2)}, u32[]{:S(2)}) collective-permute-start(s16[912,128]{1,0:T(8,128)(2,1)S(1)} %get-tuple-element.28), channel_id=1, source_target_pairs={{0,16},{16,0},{1,17},{17,1},{2,18},{18,2},{3,19},{19,3},{4,20},{20... | collective-permute-start | bytes 700424 | tf_op jit(solution)/shard_map/ppermute | solution.py:222
  32.2 2.1 %more_terms.1 = (f32[896,128]{1,0:T(8,128)S(1)}, s16[912,128]{1,0:T(8,128)(2,1)S(1)}) custom-call(bf16[4096,256]{1,0:T(8,128)(2,1)S(1)} %get-tuple-element.22.turned, bf16[896,4096]{1,0:T(8,128)(2,1)S(1)} %get-tuple-element.23.weight, f32[14,4096]{1,0:T(8,128)S(1)} %get-tuple-element.24.spread), custom_call_target="tpu_custom_call" | custom-call | flops 3670016 | bytes 458752 | tf_op jit(solution)/shard_map/more_terms/pallas_call | solution.py:315
  34.4 1.6 %collective-permute-start.16 = (s16[912,128]{1,0:T(8,128)(2,1)S(1)}, s16[912,128]{1,0:T(8,128)(2,1)S(1)}, u32[]{:S(2)}, u32[]{:S(2)}) collective-permute-start(s16[912,128]{1,0:T(8,128)(2,1)S(1)} %get-tuple-element.26), channel_id=1, source_target_pairs={{0,16},{16,0},{1,17},{17,1},{2,18},{18,2},{3,19},{19,3},{4,20},{20... | collective-permute-start | bytes 700424 | tf_op jit(solution)/shard_map/ppermute | solution.py:222
  36.0 6.4 %weight_grad.1 = bf16[1792,4096]{1,0:T(8,128)(2,1)} custom-call(bf16[1792,256]{1,0:T(8,128)(2,1)S(1)} %turn.1.refs_18_.acts, bf16[256,4096]{1,0:T(8,128)(2,1)S(1)} %get-tuple-element.29.full, f32[14,4096]{1,0:T(8,128)S(1)} %get-tuple-element.24.spread), custom_call_target="tpu_custom_call" | custom-call | flops 3670016 | bytes 458752 | tf_op jit(solution)/shard_map/weight_grad/pallas_call | solution.py:328
  42.4 0.0 collective-permute-done.17.refs_0_
  42.4 0.8 %add_terms.2.refs_1_ = bf16[128,1792]{1,0:T(8,128)(2,1)} custom-call(f32[896,128]{1,0:T(8,128)S(1)} %get-tuple-element.27.own, s16[912,128]{1,0:T(8,128)(2,1)S(1)} %collective-permute-done.17.refs_0_), custom_call_target="tpu_custom_call" | custom-call | tf_op jit(solution)/shard_map/add_terms/pallas_call | solution.py:349
  43.3 1.3 %collective-permute-done.16.refs_0_ = s16[912,128]{1,0:T(8,128)(2,1)S(1)} collective-permute-done((s16[912,128]{1,0:T(8,128)(2,1)S(1)}, s16[912,128]{1,0:T(8,128)(2,1)S(1)}, u32[]{:S(2)}, u32[]{:S(2)}) %collective-permute-start.16) | collective-permute-done | bytes 233504 | tf_op jit(solution)/shard_map/ppermute | solution.py:222
  44.6 0.8 %add_terms.3 = bf16[128,1792]{1,0:T(8,128)(2,1)} custom-call(f32[896,128]{1,0:T(8,128)S(1)} %get-tuple-element.25.own, s16[912,128]{1,0:T(8,128)(2,1)S(1)} %collective-permute-done.16.refs_0_, bf16[128,1792]{1,0:T(8,128)(2,1)} %add_terms.2.refs_1_), custom_call_target="tpu_custom_call", output_to_operand_aliasing={{}: (2, {})} | custom-call | tf_op jit(solution)/shard_map/add_terms/pallas_call | solution.py:349
Async XLA Ops:
  0.6 25.8 %collective-permute-start.15 = (bf16[128,1792]{1,0:T(8,128)(2,1)}, bf16[128,1792]{1,0:T(8,128)(2,1)S(1)}, u32[]{:S(2)}, u32[]{:S(2)}) collective-permute-start(bf16[128,1792]{1,0:T(8,128)(2,1)} %refs_0_.2), channel_id=1, source_target_pairs={{0,16},{16,0},{1,17},{17,1},{2,18},{18,2},{3,19},{19,3},{4,20},{20... | collective-permute-start | bytes 1376264 | tf_op jit(solution)/shard_map/ppermute | solution.py:222
  3.7 9.5 %collective-permute-start.3 = (bf16[16,4096]{1,0:T(8,128)(2,1)}, bf16[16,4096]{1,0:T(8,128)(2,1)S(1)}, u32[]{:S(2)}, u32[]{:S(2)}) collective-permute-start(bf16[16,4096]{1,0:T(8,128)(2,1)} %refs_0_.3), channel_id=1, source_target_pairs={{2,6},{3,1},{6,10},{7,3},{10,14},{11,7},{14,12},{15,11},{12,8},{13... | collective-permute-start | bytes 393224 | tf_op jit(solution)/shard_map/ppermute | solution.py:216
  5.2 8.6 %collective-permute-start.2 = (bf16[16,4096]{1,0:T(8,128)(2,1)}, bf16[16,4096]{1,0:T(8,128)(2,1)S(1)}, u32[]{:S(2)}, u32[]{:S(2)}) collective-permute-start(bf16[16,4096]{1,0:T(8,128)(2,1)} %refs_0_.3), channel_id=1, source_target_pairs={{2,4},{3,11},{6,0},{7,15},{10,2},{11,13},{14,6},{15,9},{12,10},{13... | collective-permute-start | bytes 393224 | tf_op jit(solution)/shard_map/ppermute | solution.py:216
  6.7 8.7 %collective-permute-start.1 = (bf16[16,4096]{1,0:T(8,128)(2,1)}, bf16[16,4096]{1,0:T(8,128)(2,1)S(1)}, u32[]{:S(2)}, u32[]{:S(2)}) collective-permute-start(bf16[16,4096]{1,0:T(8,128)(2,1)} %refs_0_.3), channel_id=1, source_target_pairs={{2,10},{3,5},{6,14},{7,1},{10,12},{11,3},{14,8},{15,7},{12,4},{13,... | collective-permute-start | bytes 393224 | tf_op jit(solution)/shard_map/ppermute | solution.py:216
  8.1 7.4 %collective-permute-start.4 = (bf16[16,4096]{1,0:T(8,128)(2,1)}, bf16[16,4096]{1,0:T(8,128)(2,1)S(1)}, u32[]{:S(2)}, u32[]{:S(2)}) collective-permute-start(bf16[16,4096]{1,0:T(8,128)(2,1)} %refs_0_.3), channel_id=1, source_target_pairs={{2,0},{3,7},{6,2},{7,11},{10,6},{11,15},{14,10},{15,13},{12,14},{1... | collective-permute-start | bytes 393224 | tf_op jit(solution)/shard_map/ppermute | solution.py:216
  8.7 0.7 %copy-start.3 = (s32[14,64]{1,0:T(8,128)S(1)}, s32[14,64]{1,0:T(8,128)}, u32[]{:S(2)}) copy-start(s32[14,64]{1,0:T(8,128)} %mask.1) | copy-start | bytes 10756
  9.4 3.8 %copy-start.1 = (bf16[16,4096]{1,0:T(8,128)(2,1)S(1)}, bf16[16,4096]{1,0:T(8,128)(2,1)}, u32[]{:S(2)}) copy-start(bf16[16,4096]{1,0:T(8,128)(2,1)} %refs_0_.3) | copy-start | bytes 393220
  9.4 17.2 %copy-start = (bf16[128,1792]{1,0:T(8,128)(2,1)S(1)}, bf16[128,1792]{1,0:T(8,128)(2,1)}, u32[]{:S(2)}) copy-start(bf16[128,1792]{1,0:T(8,128)(2,1)} %refs_0_.2) | copy-start | bytes 1376260
  9.4 18.4 %copy-start.2 = (s32[16,16]{1,0:T(8,128)S(1)}, s32[16,16]{1,0:T(8,128)}, u32[]{:S(2)}) copy-start(s32[16,16]{1,0:T(8,128)} %constant.11.clone.table) | copy-start | bytes 3076
  13.2 5.5 %collective-permute-start = (bf16[16,4096]{1,0:T(8,128)(2,1)S(1)}, bf16[16,4096]{1,0:T(8,128)(2,1)S(1)}, u32[]{:S(2)}, u32[]{:S(2)}) collective-permute-start(bf16[16,4096]{1,0:T(8,128)(2,1)S(1)} %copy-done.1), channel_id=1, source_target_pairs={{0,1},{1,0},{2,3},{3,2},{4,5},{5,4},{6,7},{7,6},{8,9},{9,8},{10,11... | collective-permute-start | bytes 393224 | tf_op jit(solution)/shard_map/ppermute | solution.py:219
  15.4 3.7 %collective-permute-start.5 = (bf16[16,4096]{1,0:T(8,128)(2,1)S(1)}, bf16[16,4096]{1,0:T(8,128)(2,1)S(1)}, u32[]{:S(2)}, u32[]{:S(2)}) collective-permute-start(bf16[16,4096]{1,0:T(8,128)(2,1)S(1)} %collective-permute-done.3.refs_2_), channel_id=1, source_target_pairs={{0,1},{1,0},{2,3},{3,2},{4,5},{5,4},{6,7},{7,6},{8,9},{9,8},{10,11... | collective-permute-start | bytes 393224 | tf_op jit(solution)/shard_map/ppermute | solution.py:219
  15.5 5.0 %collective-permute-start.6 = (bf16[16,4096]{1,0:T(8,128)(2,1)S(1)}, bf16[16,4096]{1,0:T(8,128)(2,1)S(1)}, u32[]{:S(2)}, u32[]{:S(2)}) collective-permute-start(bf16[16,4096]{1,0:T(8,128)(2,1)S(1)} %collective-permute-done.4.refs_4_), channel_id=1, source_target_pairs={{0,1},{1,0},{2,3},{3,2},{4,5},{5,4},{6,7},{7,6},{8,9},{9,8},{10,11... | collective-permute-start | bytes 393224 | tf_op jit(solution)/shard_map/ppermute | solution.py:219
  15.9 6.5 %collective-permute-start.11 = (bf16[16,4096]{1,0:T(8,128)(2,1)S(1)}, bf16[16,4096]{1,0:T(8,128)(2,1)S(1)}, u32[]{:S(2)}, u32[]{:S(2)}) collective-permute-start(bf16[16,4096]{1,0:T(8,128)(2,1)S(1)} %collective-permute-done.2.refs_8_), channel_id=1, source_target_pairs={{2,0},{3,7},{6,2},{7,11},{10,6},{11,15},{14,10},{15,13},{12,14},{1... | collective-permute-start | bytes 393224 | tf_op jit(solution)/shard_map/ppermute | solution.py:216
  18.7 7.2 %collective-permute-start.13 = (bf16[16,4096]{1,0:T(8,128)(2,1)S(1)}, bf16[16,4096]{1,0:T(8,128)(2,1)S(1)}, u32[]{:S(2)}, u32[]{:S(2)}) collective-permute-start(bf16[16,4096]{1,0:T(8,128)(2,1)S(1)} %collective-permute-done.1.refs_6_), channel_id=1, source_target_pairs={{2,10},{3,5},{6,14},{7,1},{10,12},{11,3},{14,8},{15,7},{12,4},{13,... | collective-permute-start | bytes 393224 | tf_op jit(solution)/shard_map/ppermute | solution.py:216
  19.1 6.9 %collective-permute-start.9 = (bf16[16,4096]{1,0:T(8,128)(2,1)S(1)}, bf16[16,4096]{1,0:T(8,128)(2,1)S(1)}, u32[]{:S(2)}, u32[]{:S(2)}) collective-permute-start(bf16[16,4096]{1,0:T(8,128)(2,1)S(1)} %collective-permute-done.1.refs_6_), channel_id=1, source_target_pairs={{2,6},{3,1},{6,10},{7,3},{10,14},{11,7},{14,12},{15,11},{12,8},{13... | collective-permute-start | bytes 393224 | tf_op jit(solution)/shard_map/ppermute | solution.py:216
  20.6 6.3 %collective-permute-start.8 = (bf16[16,4096]{1,0:T(8,128)(2,1)S(1)}, bf16[16,4096]{1,0:T(8,128)(2,1)S(1)}, u32[]{:S(2)}, u32[]{:S(2)}) collective-permute-start(bf16[16,4096]{1,0:T(8,128)(2,1)S(1)} %collective-permute-done.2.refs_8_), channel_id=1, source_target_pairs={{0,1},{1,0},{2,3},{3,2},{4,5},{5,4},{6,7},{7,6},{8,9},{9,8},{10,11... | collective-permute-start | bytes 393224 | tf_op jit(solution)/shard_map/ppermute | solution.py:219
  22.4 4.4 %collective-permute-start.7 = (bf16[16,4096]{1,0:T(8,128)(2,1)S(1)}, bf16[16,4096]{1,0:T(8,128)(2,1)S(1)}, u32[]{:S(2)}, u32[]{:S(2)}) collective-permute-start(bf16[16,4096]{1,0:T(8,128)(2,1)S(1)} %collective-permute-done.1.refs_6_), channel_id=1, source_target_pairs={{0,1},{1,0},{2,3},{3,2},{4,5},{5,4},{6,7},{7,6},{8,9},{9,8},{10,11... | collective-permute-start | bytes 393224 | tf_op jit(solution)/shard_map/ppermute | solution.py:219
  26.0 1.3 %collective-permute-start.12 = (bf16[16,4096]{1,0:T(8,128)(2,1)S(1)}, bf16[16,4096]{1,0:T(8,128)(2,1)S(1)}, u32[]{:S(2)}, u32[]{:S(2)}) collective-permute-start(bf16[16,4096]{1,0:T(8,128)(2,1)S(1)} %collective-permute-done.11.refs_12_), channel_id=1, source_target_pairs={{0,1},{1,0},{2,3},{3,2},{4,5},{5,4},{6,7},{7,6},{8,9},{9,8},{10,11... | collective-permute-start | bytes 393224 | tf_op jit(solution)/shard_map/ppermute | solution.py:219
  26.0 1.5 %collective-permute-start.14 = (bf16[16,4096]{1,0:T(8,128)(2,1)S(1)}, bf16[16,4096]{1,0:T(8,128)(2,1)S(1)}, u32[]{:S(2)}, u32[]{:S(2)}) collective-permute-start(bf16[16,4096]{1,0:T(8,128)(2,1)S(1)} %collective-permute-done.13.refs_14_), channel_id=1, source_target_pairs={{0,1},{1,0},{2,3},{3,2},{4,5},{5,4},{6,7},{7,6},{8,9},{9,8},{10,11... | collective-permute-start | bytes 393224 | tf_op jit(solution)/shard_map/ppermute | solution.py:219
  26.5 1.3 %collective-permute-start.10 = (bf16[16,4096]{1,0:T(8,128)(2,1)S(1)}, bf16[16,4096]{1,0:T(8,128)(2,1)S(1)}, u32[]{:S(2)}, u32[]{:S(2)}) collective-permute-start(bf16[16,4096]{1,0:T(8,128)(2,1)S(1)} %collective-permute-done.9.refs_10_), channel_id=1, source_target_pairs={{0,1},{1,0},{2,3},{3,2},{4,5},{5,4},{6,7},{7,6},{8,9},{9,8},{10,11... | collective-permute-start | bytes 393224 | tf_op jit(solution)/shard_map/ppermute | solution.py:219
  31.7 10.7 %collective-permute-start.17 = (s16[912,128]{1,0:T(8,128)(2,1)S(1)}, s16[912,128]{1,0:T(8,128)(2,1)S(1)}, u32[]{:S(2)}, u32[]{:S(2)}) collective-permute-start(s16[912,128]{1,0:T(8,128)(2,1)S(1)} %get-tuple-element.28), channel_id=1, source_target_pairs={{0,16},{16,0},{1,17},{17,1},{2,18},{18,2},{3,19},{19,3},{4,20},{20... | collective-permute-start | bytes 700424 | tf_op jit(solution)/shard_map/ppermute | solution.py:222
  34.4 10.2 %collective-permute-start.16 = (s16[912,128]{1,0:T(8,128)(2,1)S(1)}, s16[912,128]{1,0:T(8,128)(2,1)S(1)}, u32[]{:S(2)}, u32[]{:S(2)}) collective-permute-start(s16[912,128]{1,0:T(8,128)(2,1)S(1)} %get-tuple-element.26), channel_id=1, source_target_pairs={{0,16},{16,0},{1,17},{17,1},{2,18},{18,2},{3,19},{19,3},{4,20},{20... | collective-permute-start | bytes 700424 | tf_op jit(solution)/shard_map/ppermute | solution.py:222

commit v6 on v5

--- a/solution.py
+++ b/solution.py
@@ -45,18 +45,37 @@
     )
 
 
-def keep_kernel(place, weight, mask, kept, spread, mask_here, mask_sem, sems):
+def spread_and_keep_kernel(place, weight, mask, kept, spread, mask_here, mask_sem, sems):
     rows, width = kept.shape
     mask_copy = pltpu.make_async_copy(mask, mask_here, mask_sem)
     mask_copy.start()
-    copies = []
-    for b in range(rows // BLOCK):
-        at = pl.ds(b * BLOCK, BLOCK)
-        copies.append(pltpu.make_async_copy(weight.at[at, :], kept.at[at, :], sems.at[b]))
-        copies[-1].start()
+    copies = fetch(weight, 0, kept, sems)
     mask_copy.wait()
     spread[...] = wide_mask(mask_here[...], place[0] * (width // BLOCK), width)
-    factors = spread[...].astype(jnp.bfloat16)
+    drop_blocks(copies, kept, spread[: rows // BLOCK, :])
+
+
+def keep_kernel(first, spread, weight, kept, sems):
+    copies = fetch(weight, first, kept, sems)
+    drop_blocks(copies, kept, spread[first : first + kept.shape[0] // BLOCK, :])
+
+
+def fetch(weight, first, kept, sems):
+    copies = []
+    for b in range(kept.shape[0] // BLOCK):
+        copies.append(
+            pltpu.make_async_copy(
+                weight.at[pl.ds((first + b) * BLOCK, BLOCK), :],
+                kept.at[pl.ds(b * BLOCK, BLOCK), :],
+                sems.at[b],
+            )
+        )
+        copies[-1].start()
+    return copies
+
+
+def drop_blocks(copies, kept, spread):
+    factors = spread.astype(jnp.bfloat16)
     for b, copy in enumerate(copies):
         copy.wait()
         at = slice(b * BLOCK, (b + 1) * BLOCK)
@@ -86,41 +105,45 @@
         out[rows:, :] = codes.astype(jnp.int16)
 
 
-def first_terms_kernel(n_shards, n_parts, shift, chunk, place, table, *refs):
-    shards = refs[:n_shards]
-    kept, weight, _, full, turned, own = refs[n_shards : n_shards + 6]
-    outs = refs[n_shards + 6 : n_shards + 6 + n_parts]
-    *rest, total, sems = refs[n_shards + 6 + n_parts :]
-    piece = own.shape[0]
-    copies = []
-    for p, later in enumerate(rest):
-        at = pl.ds((p + 1) * piece, piece)
-        copies.append(pltpu.make_async_copy(weight.at[at, :], later, sems.at[p]))
-        copies[-1].start()
+def first_terms_kernel(n_shards, n_kept, n_parts, shift, chunk, place, table, *refs):
+    shards, kepts = refs[:n_shards], refs[n_shards : n_shards + n_kept]
+    _, full, turned, own, *outs, total = refs[n_shards + n_kept :]
     rows = shards[0].shape[0]
     n_cols = table.shape[0]
     for n, shard in enumerate(shards):
         to = lax.rem(table[place[1], n] + n_cols - place[0] * shift, n_cols)
         full[pl.ds(pl.multiple_of(to * rows, rows), rows), :] = shard[...]
     for c in range(0, full.shape[1], chunk):
-        turned[c : c + chunk, :] = full[:, c : c + chunk].T
-        terms = jnp.dot(
-            kept[:, c : c + chunk], turned[c : c + chunk, :], preferred_element_type=jnp.float32
+        cols = slice(c, c + chunk)
+        turned[cols, :] = full[:, cols].T
+        at = 0
+        for kept in kepts:
+            to = slice(at, at + kept.shape[0])
+            terms = jnp.dot(kept[:, cols], turned[cols, :], preferred_element_type=jnp.float32)
+            total[to, :] = terms if c == 0 else total[to, :] + terms
+            at += kept.shape[0]
+    store_terms(total, own, outs)
+
+
+def more_terms_kernel(n_parts, first, chunk, turned, weight, spread, own, *refs):
+    outs, (here, total, sems) = refs[:n_parts], refs[n_parts:]
+    rows = own.shape[0]
+    blocks = rows // BLOCK
+    copies = []
+    for c in range(0, weight.shape[1], chunk):
+        cols = pl.ds(c, chunk)
+        copies.append(
+            pltpu.make_async_copy(
+                weight.at[pl.ds(first * BLOCK, rows), cols], here.at[:, cols], sems.at[c // chunk]
+            )
         )
-        total[...] = terms if c == 0 else total[...] + terms
-    store_terms(total, own, outs)
-    for copy in copies:
+        copies[-1].start()
+    for c, copy in zip(range(0, weight.shape[1], chunk), copies, strict=True):
+        cols = slice(c, c + chunk)
+        factors = spread[first : first + blocks, cols].astype(jnp.bfloat16)
         copy.wait()
-
-
-def more_terms_kernel(n_parts, first_block, chunk, turned, weight, spread, own, *refs):
-    outs, total = refs[:n_parts], refs[n_parts]
-    blocks = own.shape[0] // BLOCK
-    for c in range(0, weight.shape[1], chunk):
-        cols = slice(c, c + chunk)
-        factors = spread[first_block : first_block + blocks, cols].astype(jnp.bfloat16)
         kept = jnp.concatenate(
-            [weight[b * BLOCK : (b + 1) * BLOCK, cols] * factors[b : b + 1, :] for b in range(blocks)],
+            [here[b * BLOCK : (b + 1) * BLOCK, cols] * factors[b : b + 1, :] for b in range(blocks)],
             axis=0,
         )
         terms = jnp.dot(kept, turned[cols, :], preferred_element_type=jnp.float32)
@@ -237,41 +260,67 @@
     place = jnp.stack([row, col]).astype(jnp.int32)
 
     weight = pltpu.with_memory_space_constraint(weight, pltpu.HBM)
-    kept, spread = pl.pallas_call(
-        keep_kernel,
+    block_mask = pltpu.with_memory_space_constraint(block_mask, pltpu.HBM)
+    piece_blocks = piece // BLOCK
+    early = max(1, piece_blocks * 3 // 7)
+    kept_early, spread = pl.pallas_call(
+        spread_and_keep_kernel,
         in_specs=[in_smem(), in_hbm(), in_hbm()],
         out_specs=[in_vmem()] * 2,
         out_shape=[
-            pltpu.VMEM((piece, width), bf16),
+            pltpu.VMEM((early * BLOCK, width), bf16),
             pltpu.VMEM((blocks, width), jnp.float32),
         ],
         scratch_shapes=[
             pltpu.VMEM(block_mask.shape, jnp.int32),
             pltpu.SemaphoreType.DMA,
-            pltpu.SemaphoreType.DMA((piece // BLOCK,)),
+            pltpu.SemaphoreType.DMA((early,)),
         ],
         compiler_params=params(),
-        cost_estimate=cost(piece * width, 2 * piece * width),
-        name="keep",
+        cost_estimate=cost(early * BLOCK * width, 2 * early * BLOCK * width),
+        name="spread_and_keep",
     )(place, weight, block_mask)
 
     held = {0: grad_output}
-    for j in (2, -2, 1, -1):
+    for j in (2, -2):
         if abs(j) < n_chips // 2 or j == n_chips // 2:
             held[j] = send_ring(grad_output, j)
-    near = [j for j in held if j]
-    kept, *ready = lax.optimization_barrier((kept, *(held[j] for j in near)))
-    held.update(zip(near, ready, strict=True))
-    for j in range(3, n_chips // 2 + 1):
+    far = [j for j in held if j]
+    spread, again = lax.optimization_barrier((spread, grad_output))
+    held[1], held[-1] = send_ring(again, 1), send_ring(again, -1)
+    acts = [inputs] + [send_row(inputs, k) for k in range(1, n_rows)]
+    spread, *ready = lax.optimization_barrier((spread, *(held[j] for j in far)))
+    held.update(zip(far, ready, strict=True))
+    last = range(3, n_chips // 2 + 1)
+    for j in last:
         by = 1 if j % 2 else 2
         held[j] = send_ring(held[j - by], by)
         if 2 * j < n_chips:
             held[-j] = send_ring(held[by - j], -by)
+
+    kepts = [kept_early]
+    if early < piece_blocks:
+        late = piece_blocks - early
+        spread, held[1], held[-1] = lax.optimization_barrier((spread, held[1], held[-1]))
+        kept_late = pl.pallas_call(
+            functools.partial(keep_kernel, early),
+            in_specs=[in_vmem(), in_hbm()],
+            out_specs=in_vmem(),
+            out_shape=pltpu.VMEM((late * BLOCK, width), bf16),
+            scratch_shapes=[pltpu.SemaphoreType.DMA((late,))],
+            compiler_params=params(),
+            cost_estimate=cost(late * BLOCK * width, 2 * late * BLOCK * width),
+            name="keep",
+        )(spread, weight)
+        kept_late, *ready = lax.optimization_barrier(
+            (kept_late, *(held[j] for j in reach if abs(j) > 2))
+        )
+        held.update(zip([j for j in reach if abs(j) > 2], ready, strict=True))
+        kepts.append(kept_late)
     shards = []
     for j in reach:
         shards += [held[j], send_core(held[j])]
 
-    acts = [inputs] + [send_row(inputs, k) for k in range(1, n_rows)]
     acts_turned = pl.pallas_call(
         functools.partial(turn_kernel, n_rows),
         in_specs=[in_vmem()] * n_rows,
@@ -287,41 +336,41 @@
     sent_shape = jax.ShapeDtypeStruct((piece + code_rows, tokens), jnp.int16)
     own_shape = jax.ShapeDtypeStruct((piece, tokens), jnp.float32)
     small_cost = cost(piece * width, piece * width // 8)
-    later = n_pieces - 1
     full, turned, own, *coded = pl.pallas_call(
-        functools.partial(first_terms_kernel, n_shards, n_parts, tokens // shard_rows, chunk),
-        in_specs=[in_smem()] * 2 + [in_vmem()] * n_shards + [in_vmem(), in_hbm(), in_hbm()],
-        out_specs=[in_vmem()] * (3 + n_parts + later),
+        functools.partial(
+            first_terms_kernel, n_shards, len(kepts), n_parts, tokens // shard_rows, chunk
+        ),
+        in_specs=[in_smem()] * 2 + [in_vmem()] * (n_shards + len(kepts)) + [in_hbm()],
+        out_specs=[in_vmem()] * (3 + n_parts),
         out_shape=[
             jax.ShapeDtypeStruct((all_tokens, width), bf16),
             jax.ShapeDtypeStruct((width, all_tokens), bf16),
             own_shape,
         ]
-        + [sent_shape] * n_parts
-        + [pltpu.VMEM((piece, width), bf16)] * later,
-        scratch_shapes=[
-            pltpu.VMEM((piece, all_tokens), jnp.float32),
-            pltpu.SemaphoreType.DMA((max(later, 1),)),
-        ],
+        + [sent_shape] * n_parts,
+        scratch_shapes=[pltpu.VMEM((piece, all_tokens), jnp.float32)],
         compiler_params=params(),
         cost_estimate=small_cost,
         name="first_terms",
-    )(place, jnp.array(table, jnp.int32), *shards, kept, weight, acts_turned)
+    )(place, jnp.array(table, jnp.int32), *shards, *kepts, acts_turned)
     owns = [own]
-    coded, rest = coded[:n_parts], coded[n_parts:]
     parts = [send_row(coded[k], k + 1) for k in range(n_parts)]
 
     for p in range(1, n_pieces):
         own, *coded = pl.pallas_call(
-            functools.partial(more_terms_kernel, n_parts, p * (piece // BLOCK), chunk),
-            in_specs=[in_vmem()] * 3,
+            functools.partial(more_terms_kernel, n_parts, p * piece_blocks, chunk),
+            in_specs=[in_vmem(), in_hbm(), in_vmem()],
             out_specs=[in_vmem()] * (1 + n_parts),
             out_shape=[own_shape] + [sent_shape] * n_parts,
-            scratch_shapes=[pltpu.VMEM((piece, all_tokens), jnp.float32)],
+            scratch_shapes=[
+                pltpu.VMEM((piece, width), bf16),
+                pltpu.VMEM((piece, all_tokens), jnp.float32),
+                pltpu.SemaphoreType.DMA((width // chunk,)),
+            ],
             compiler_params=params(),
             cost_estimate=small_cost,
             name="more_terms",
-        )(turned, rest[p - 1], spread)
+        )(turned, weight, spread)
         owns.append(own)
         parts += [send_row(coded[k], k + 1) for k in range(n_parts)]
 

time: 45.6 us -> 46.5 us (1.020)
  Pallas kernels: 18.2 us -> 22 us
  waiting for transfers between devices: 9.61 us -> 7.48 us
  local copies, waits for them, and re-layouts: 0.71 us -> 0.02 us
    pallas_call x3 -> x4, Pallas kernels: 9.77 us -> 13.5 us  [the longest x1 5.58 us: per_device(): pl.pallas_call(functools.partial(more_terms_kernel, n_parts, p * piece_bl...]
    ppermute x3, waiting for transfers between devices: 1.29 us -> 0.01 us  [send_row(): lax.ppermute(x, 'row', [(r, (r + by) % n_rows) for r in range(n_rows)])]
    ppermute x7, starting transfers between devices: 9.57 us -> 8.45 us  [send_ring(): return lax.ppermute(x, 'col', perm)]
    ppermute x8, starting transfers between devices: 1.34 us -> 2.36 us  [send_core(): return lax.ppermute(x, 'col', [(c, c ^ 1) for c in range(n_cols)])]
    ppermute x7, waiting for transfers between devices: 7.35 us -> 6.5 us  [send_ring(): return lax.ppermute(x, 'col', perm)]
    unnamed x8 -> x6, local copies, waits for them, and re-layouts: 0.71 us -> 0.02 us
  transfers between devices with their start and end apart: 18 -> 18, of which waited for: 8 -> 8; matrix products, arithmetic and copies ran while one was open for 0% -> 0% of each run, Pallas kernels for 30% -> 39%
where the time goes in v6:
time: 46.5 us; the launch traced here: 46.3 us
  Pallas kernels  22 us (47%)
  starting transfers between devices  16 us (34%)
  waiting for transfers between devices  7.48 us (16%)
  between operations  0.76 us (2%)
    ppermute x7, starting transfers between devices, send_ring(): return lax.ppermute(x, 'col', perm)  8.45 us
    pallas_call x1, Pallas kernels, per_device(): pl.pallas_call(functools.partial(weight_grad_kernel, chunk), in_specs=[in...  6.56 us
    ppermute x7, waiting for transfers between devices, send_ring(): return lax.ppermute(x, 'col', perm)  6.5 us
    pallas_call x1, Pallas kernels, per_device(): pl.pallas_call(functools.partial(more_terms_kernel, n_parts, p * piece_bl...  5.58 us
    ppermute x3, starting transfers between devices, send_row(): lax.ppermute(x, 'row', [(r, (r + by) % n_rows) for r in range(n_rows)])  5.18 us
    pallas_call x1, Pallas kernels, per_device(): pl.pallas_call(functools.partial(first_terms_kernel, n_shards, len(kepts)...  3.1 us
    pallas_call x1, Pallas kernels, per_device(): pl.pallas_call(spread_and_keep_kernel, in_specs=[in_smem(), in_hbm(), in_...  2.52 us
    ppermute x8, starting transfers between devices, send_core(): return lax.ppermute(x, 'col', [(c, c ^ 1) for c in range(n_cols)])  2.36 us
  transfers between devices with their start and end apart: 18, of which 8 were waited for; matrix products, arithmetic and copies ran while one was open for 0% of the time, Pallas kernels for 39%

profile of v6, /device:TPU:0, one launch (start us, length us, event | category | flops | bytes accessed | tf_op | source)
XLA Modules:
  0.0 46.3 jit_solution(10617461251560309569)
XLA Ops:
  0.6 3.0 %collective-permute-start.15 = (bf16[128,1792]{1,0:T(8,128)(2,1)}, bf16[128,1792]{1,0:T(8,128)(2,1)S(1)}, u32[]{:S(2)}, u32[]{:S(2)}) collective-permute-start(bf16[128,1792]{1,0:T(8,128)(2,1)} %refs_0_.2), channel_id=1, source_target_pairs={{0,16},{16,0},{1,17},{17,1},{2,18},{18,2},{3,19},{19,3},{4,20},{20... | collective-permute-start | bytes 1376264 | tf_op jit(solution)/shard_map/ppermute | solution.py:245
  3.7 2.5 %collective-permute-start.1 = (bf16[16,4096]{1,0:T(8,128)(2,1)}, bf16[16,4096]{1,0:T(8,128)(2,1)S(1)}, u32[]{:S(2)}, u32[]{:S(2)}) collective-permute-start(bf16[16,4096]{1,0:T(8,128)(2,1)} %refs_0_.3), channel_id=1, source_target_pairs={{2,10},{3,5},{6,14},{7,1},{10,12},{11,3},{14,8},{15,7},{12,4},{13,... | collective-permute-start | bytes 393224 | tf_op jit(solution)/shard_map/ppermute | solution.py:239
  6.2 0.4 collective-permute-start.2
  6.6 0.1 pad_add_fusion.place
  6.7 0.0 copy-start.1
  6.7 2.5 %spread_and_keep.1 = (bf16[384,4096]{1,0:T(8,128)(2,1)S(1)}, f32[14,4096]{1,0:T(8,128)S(1)}) custom-call(s32[2]{0:T(128)S(1)} %pad_add_fusion.place, bf16[1792,4096]{1,0:T(8,128)(2,1)} %weight.5, s32[14,64]{1,0:T(8,128)} %mask.1), custom_call_target="tpu_custom_call" | custom-call | flops 1572864 | bytes 3145728 | tf_op jit(solution)/shard_map/spread_and_keep/pallas_call | solution.py:266
  9.2 0.0 copy-done.1
  9.2 0.0 copy-start
  9.2 0.0 copy-start.2
  9.2 1.6 %collective-permute-start.4 = (bf16[16,4096]{1,0:T(8,128)(2,1)S(1)}, bf16[16,4096]{1,0:T(8,128)(2,1)S(1)}, u32[]{:S(2)}, u32[]{:S(2)}) collective-permute-start(bf16[16,4096]{1,0:T(8,128)(2,1)S(1)} %copy-done.1), channel_id=1, source_target_pairs={{2,0},{3,7},{6,2},{7,11},{10,6},{11,15},{14,10},{15,13},{12,14},{1... | collective-permute-start | bytes 393224 | tf_op jit(solution)/shard_map/ppermute | solution.py:239
  10.9 0.4 collective-permute-start.3
  11.3 0.1 collective-permute-done.1.refs_6_
  11.4 2.5 %collective-permute-done.2.refs_8_ = bf16[16,4096]{1,0:T(8,128)(2,1)S(1)} collective-permute-done((bf16[16,4096]{1,0:T(8,128)(2,1)}, bf16[16,4096]{1,0:T(8,128)(2,1)S(1)}, u32[]{:S(2)}, u32[]{:S(2)}) %collective-permute-start.2) | collective-permute-done | bytes 131104 | tf_op jit(solution)/shard_map/ppermute | solution.py:239
  13.8 1.1 %collective-permute-start.10 = (bf16[16,4096]{1,0:T(8,128)(2,1)S(1)}, bf16[16,4096]{1,0:T(8,128)(2,1)S(1)}, u32[]{:S(2)}, u32[]{:S(2)}) collective-permute-start(bf16[16,4096]{1,0:T(8,128)(2,1)S(1)} %collective-permute-done.2.refs_8_), channel_id=1, source_target_pairs={{2,0},{3,7},{6,2},{7,11},{10,6},{11,15},{14,10},{15,13},{12,14},{1... | collective-permute-start | bytes 393224 | tf_op jit(solution)/shard_map/ppermute | solution.py:239
  14.9 2.0 %collective-permute-start.11 = (bf16[16,4096]{1,0:T(8,128)(2,1)S(1)}, bf16[16,4096]{1,0:T(8,128)(2,1)S(1)}, u32[]{:S(2)}, u32[]{:S(2)}) collective-permute-start(bf16[16,4096]{1,0:T(8,128)(2,1)S(1)} %collective-permute-done.1.refs_6_), channel_id=1, source_target_pairs={{2,10},{3,5},{6,14},{7,1},{10,12},{11,3},{14,8},{15,7},{12,4},{13,... | collective-permute-start | bytes 393224 | tf_op jit(solution)/shard_map/ppermute | solution.py:239
  16.9 0.0 collective-permute-done.4.refs_4_
  16.9 0.4 collective-permute-start.9
  17.3 0.0 collective-permute-done.3.refs_2_
  17.3 0.0 collective-permute-start
  17.3 1.9 %collective-permute-done.10.refs_12_ = bf16[16,4096]{1,0:T(8,128)(2,1)S(1)} collective-permute-done((bf16[16,4096]{1,0:T(8,128)(2,1)S(1)}, bf16[16,4096]{1,0:T(8,128)(2,1)S(1)}, u32[]{:S(2)}, u32[]{:S(2)}) %collective-permute-start.10) | collective-permute-done | bytes 131104 | tf_op jit(solution)/shard_map/ppermute | solution.py:239
  19.2 0.0 collective-permute-start.8
  19.2 2.1 %collective-permute-done.11.refs_14_ = bf16[16,4096]{1,0:T(8,128)(2,1)S(1)} collective-permute-done((bf16[16,4096]{1,0:T(8,128)(2,1)S(1)}, bf16[16,4096]{1,0:T(8,128)(2,1)S(1)}, u32[]{:S(2)}, u32[]{:S(2)}) %collective-permute-start.11) | collective-permute-done | bytes 131104 | tf_op jit(solution)/shard_map/ppermute | solution.py:239
  21.3 1.2 %collective-permute-start.7 = (bf16[16,4096]{1,0:T(8,128)(2,1)S(1)}, bf16[16,4096]{1,0:T(8,128)(2,1)S(1)}, u32[]{:S(2)}, u32[]{:S(2)}) collective-permute-start(bf16[16,4096]{1,0:T(8,128)(2,1)S(1)} %collective-permute-done.1.refs_6_), channel_id=1, source_target_pairs={{0,1},{1,0},{2,3},{3,2},{4,5},{5,4},{6,7},{7,6},{8,9},{9,8},{10,11... | collective-permute-start | bytes 393224 | tf_op jit(solution)/shard_map/ppermute | solution.py:242
  22.5 2.3 %keep.1.refs_17_ = bf16[512,4096]{1,0:T(8,128)(2,1)S(1)} custom-call(f32[14,4096]{1,0:T(8,128)S(1)} %get-tuple-element.30.spread, bf16[1792,4096]{1,0:T(8,128)(2,1)} %weight.5), custom_call_target="tpu_custom_call" | custom-call | flops 2097152 | bytes 4194304 | tf_op jit(solution)/shard_map/keep/pallas_call | solution.py:305
  24.8 0.0 collective-permute-done.9.refs_10_
  24.8 0.1 collective-permute-start.5
  24.8 0.0 collective-permute-done.refs_1_
  24.9 0.5 %collective-permute-start.6 = (bf16[16,4096]{1,0:T(8,128)(2,1)S(1)}, bf16[16,4096]{1,0:T(8,128)(2,1)S(1)}, u32[]{:S(2)}, u32[]{:S(2)}) collective-permute-start(bf16[16,4096]{1,0:T(8,128)(2,1)S(1)} %collective-permute-done.4.refs_4_), channel_id=1, source_target_pairs={{0,1},{1,0},{2,3},{3,2},{4,5},{5,4},{6,7},{7,6},{8,9},{9,8},{10,11... | collective-permute-start | bytes 393224 | tf_op jit(solution)/shard_map/ppermute | solution.py:242
  25.4 0.0 collective-permute-done.8.refs_9_
  25.4 0.1 collective-permute-start.12
  25.4 0.0 collective-permute-done.7.refs_7_
  25.4 0.4 collective-permute-start.13
  25.9 0.0 collective-permute-done.15.refs_1_
  25.9 0.1 collective-permute-start.14
  26.0 0.0 copy-done
  26.0 0.3 turn.1.refs_18_.acts
  26.3 0.0 collective-permute-done.5.refs_3_
  26.3 0.1 collective-permute-done.6.refs_5_
  26.4 0.3 collective-permute-done.12.refs_11_
  26.7 0.2 collective-permute-done.13.refs_13_
  26.9 0.3 collective-permute-done.14.refs_15_
  27.2 0.0 copy-done.2
  27.2 3.1 %first_terms.1 = (bf16[256,4096]{1,0:T(8,128)(2,1)S(1)}, bf16[4096,256]{1,0:T(8,128)(2,1)S(1)}, f32[896,128]{1,0:T(8,128)S(1)}, s16[912,128]{1,0:T(8,128)(2,1)S(1)}) custom-call(s32[2]{0:T(128)S(1)} %pad_add_fusion.place, s32[16,16]{1,0:T(8,128)S(1)} %copy-done.2, bf16[16,4096]{1,0:T(8,128)(2,1)S(1)} %copy-done.1, ...), custom_call_target="tpu_custom_call" | custom-call | flops 3670016 | bytes 458752 | tf_op jit(solution)/shard_map/first_terms/pallas_call | solution.py:339
  30.3 0.5 %collective-permute-start.17 = (s16[912,128]{1,0:T(8,128)(2,1)S(1)}, s16[912,128]{1,0:T(8,128)(2,1)S(1)}, u32[]{:S(2)}, u32[]{:S(2)}) collective-permute-start(s16[912,128]{1,0:T(8,128)(2,1)S(1)} %get-tuple-element.40), channel_id=1, source_target_pairs={{0,16},{16,0},{1,17},{17,1},{2,18},{18,2},{3,19},{19,3},{4,20},{20... | collective-permute-start | bytes 700424 | tf_op jit(solution)/shard_map/ppermute | solution.py:245
  30.8 5.6 %more_terms.1 = (f32[896,128]{1,0:T(8,128)S(1)}, s16[912,128]{1,0:T(8,128)(2,1)S(1)}) custom-call(bf16[4096,256]{1,0:T(8,128)(2,1)S(1)} %get-tuple-element.36.turned, bf16[1792,4096]{1,0:T(8,128)(2,1)} %weight.5, f32[14,4096]{1,0:T(8,128)S(1)} %get-tuple-element.30.spread), custom_call_target="tpu_custom_call" | custom-call | flops 3670016 | bytes 458752 | tf_op jit(solution)/shard_map/more_terms/pallas_call | solution.py:360
  36.4 1.7 %collective-permute-start.16 = (s16[912,128]{1,0:T(8,128)(2,1)S(1)}, s16[912,128]{1,0:T(8,128)(2,1)S(1)}, u32[]{:S(2)}, u32[]{:S(2)}) collective-permute-start(s16[912,128]{1,0:T(8,128)(2,1)S(1)} %get-tuple-element.38), channel_id=1, source_target_pairs={{0,16},{16,0},{1,17},{17,1},{2,18},{18,2},{3,19},{19,3},{4,20},{20... | collective-permute-start | bytes 700424 | tf_op jit(solution)/shard_map/ppermute | solution.py:245
  38.1 6.6 %weight_grad.1 = bf16[1792,4096]{1,0:T(8,128)(2,1)} custom-call(bf16[1792,256]{1,0:T(8,128)(2,1)S(1)} %turn.1.refs_18_.acts, bf16[256,4096]{1,0:T(8,128)(2,1)S(1)} %get-tuple-element.41.full, f32[14,4096]{1,0:T(8,128)S(1)} %get-tuple-element.30.spread), custom_call_target="tpu_custom_call" | custom-call | flops 3670016 | bytes 458752 | tf_op jit(solution)/shard_map/weight_grad/pallas_call | solution.py:377
  44.6 0.0 collective-permute-done.17.refs_0_
  44.6 0.8 %add_terms.2.refs_1_ = bf16[128,1792]{1,0:T(8,128)(2,1)} custom-call(f32[896,128]{1,0:T(8,128)S(1)} %get-tuple-element.39.own, s16[912,128]{1,0:T(8,128)(2,1)S(1)} %collective-permute-done.17.refs_0_), custom_call_target="tpu_custom_call" | custom-call | tf_op jit(solution)/shard_map/add_terms/pallas_call | solution.py:398
  45.5 0.0 collective-permute-done.16.refs_0_
  45.5 0.8 %add_terms.3 = bf16[128,1792]{1,0:T(8,128)(2,1)} custom-call(f32[896,128]{1,0:T(8,128)S(1)} %get-tuple-element.37.own, s16[912,128]{1,0:T(8,128)(2,1)S(1)} %collective-permute-done.16.refs_0_, bf16[128,1792]{1,0:T(8,128)(2,1)} %add_terms.2.refs_1_), custom_call_target="tpu_custom_call", output_to_operand_aliasing={{}: (2, {})} | custom-call | tf_op jit(solution)/shard_map/add_terms/pallas_call | solution.py:398
Async XLA Ops:
  0.6 25.2 %collective-permute-start.15 = (bf16[128,1792]{1,0:T(8,128)(2,1)}, bf16[128,1792]{1,0:T(8,128)(2,1)S(1)}, u32[]{:S(2)}, u32[]{:S(2)}) collective-permute-start(bf16[128,1792]{1,0:T(8,128)(2,1)} %refs_0_.2), channel_id=1, source_target_pairs={{0,16},{16,0},{1,17},{17,1},{2,18},{18,2},{3,19},{19,3},{4,20},{20... | collective-permute-start | bytes 1376264 | tf_op jit(solution)/shard_map/ppermute | solution.py:245
  3.7 7.7 %collective-permute-start.1 = (bf16[16,4096]{1,0:T(8,128)(2,1)}, bf16[16,4096]{1,0:T(8,128)(2,1)S(1)}, u32[]{:S(2)}, u32[]{:S(2)}) collective-permute-start(bf16[16,4096]{1,0:T(8,128)(2,1)} %refs_0_.3), channel_id=1, source_target_pairs={{2,10},{3,5},{6,14},{7,1},{10,12},{11,3},{14,8},{15,7},{12,4},{13,... | collective-permute-start | bytes 393224 | tf_op jit(solution)/shard_map/ppermute | solution.py:239
  6.2 7.7 %collective-permute-start.2 = (bf16[16,4096]{1,0:T(8,128)(2,1)}, bf16[16,4096]{1,0:T(8,128)(2,1)S(1)}, u32[]{:S(2)}, u32[]{:S(2)}) collective-permute-start(bf16[16,4096]{1,0:T(8,128)(2,1)} %refs_0_.3), channel_id=1, source_target_pairs={{2,4},{3,11},{6,0},{7,15},{10,2},{11,13},{14,6},{15,9},{12,10},{13... | collective-permute-start | bytes 393224 | tf_op jit(solution)/shard_map/ppermute | solution.py:239
  6.7 2.5 %copy-start.1 = (bf16[16,4096]{1,0:T(8,128)(2,1)S(1)}, bf16[16,4096]{1,0:T(8,128)(2,1)}, u32[]{:S(2)}) copy-start(bf16[16,4096]{1,0:T(8,128)(2,1)} %refs_0_.3) | copy-start | bytes 393220
  9.2 16.8 %copy-start = (bf16[128,1792]{1,0:T(8,128)(2,1)S(1)}, bf16[128,1792]{1,0:T(8,128)(2,1)}, u32[]{:S(2)}) copy-start(bf16[128,1792]{1,0:T(8,128)(2,1)} %refs_0_.2) | copy-start | bytes 1376260
  9.2 18.0 %copy-start.2 = (s32[16,16]{1,0:T(8,128)S(1)}, s32[16,16]{1,0:T(8,128)}, u32[]{:S(2)}) copy-start(s32[16,16]{1,0:T(8,128)} %constant.11.clone.table) | copy-start | bytes 3076
  9.2 7.7 %collective-permute-start.4 = (bf16[16,4096]{1,0:T(8,128)(2,1)S(1)}, bf16[16,4096]{1,0:T(8,128)(2,1)S(1)}, u32[]{:S(2)}, u32[]{:S(2)}) collective-permute-start(bf16[16,4096]{1,0:T(8,128)(2,1)S(1)} %copy-done.1), channel_id=1, source_target_pairs={{2,0},{3,7},{6,2},{7,11},{10,6},{11,15},{14,10},{15,13},{12,14},{1... | collective-permute-start | bytes 393224 | tf_op jit(solution)/shard_map/ppermute | solution.py:239
  10.9 6.4 %collective-permute-start.3 = (bf16[16,4096]{1,0:T(8,128)(2,1)S(1)}, bf16[16,4096]{1,0:T(8,128)(2,1)S(1)}, u32[]{:S(2)}, u32[]{:S(2)}) collective-permute-start(bf16[16,4096]{1,0:T(8,128)(2,1)S(1)} %copy-done.1), channel_id=1, source_target_pairs={{2,6},{3,1},{6,10},{7,3},{10,14},{11,7},{14,12},{15,11},{12,8},{13... | collective-permute-start | bytes 393224 | tf_op jit(solution)/shard_map/ppermute | solution.py:239
  13.8 5.4 %collective-permute-start.10 = (bf16[16,4096]{1,0:T(8,128)(2,1)S(1)}, bf16[16,4096]{1,0:T(8,128)(2,1)S(1)}, u32[]{:S(2)}, u32[]{:S(2)}) collective-permute-start(bf16[16,4096]{1,0:T(8,128)(2,1)S(1)} %collective-permute-done.2.refs_8_), channel_id=1, source_target_pairs={{2,0},{3,7},{6,2},{7,11},{10,6},{11,15},{14,10},{15,13},{12,14},{1... | collective-permute-start | bytes 393224 | tf_op jit(solution)/shard_map/ppermute | solution.py:239
  14.9 6.4 %collective-permute-start.11 = (bf16[16,4096]{1,0:T(8,128)(2,1)S(1)}, bf16[16,4096]{1,0:T(8,128)(2,1)S(1)}, u32[]{:S(2)}, u32[]{:S(2)}) collective-permute-start(bf16[16,4096]{1,0:T(8,128)(2,1)S(1)} %collective-permute-done.1.refs_6_), channel_id=1, source_target_pairs={{2,10},{3,5},{6,14},{7,1},{10,12},{11,3},{14,8},{15,7},{12,4},{13,... | collective-permute-start | bytes 393224 | tf_op jit(solution)/shard_map/ppermute | solution.py:239
  16.9 7.9 %collective-permute-start.9 = (bf16[16,4096]{1,0:T(8,128)(2,1)S(1)}, bf16[16,4096]{1,0:T(8,128)(2,1)S(1)}, u32[]{:S(2)}, u32[]{:S(2)}) collective-permute-start(bf16[16,4096]{1,0:T(8,128)(2,1)S(1)} %collective-permute-done.1.refs_6_), channel_id=1, source_target_pairs={{2,6},{3,1},{6,10},{7,3},{10,14},{11,7},{14,12},{15,11},{12,8},{13... | collective-permute-start | bytes 393224 | tf_op jit(solution)/shard_map/ppermute | solution.py:239
  17.3 7.6 %collective-permute-start = (bf16[16,4096]{1,0:T(8,128)(2,1)S(1)}, bf16[16,4096]{1,0:T(8,128)(2,1)S(1)}, u32[]{:S(2)}, u32[]{:S(2)}) collective-permute-start(bf16[16,4096]{1,0:T(8,128)(2,1)S(1)} %copy-done.1), channel_id=1, source_target_pairs={{0,1},{1,0},{2,3},{3,2},{4,5},{5,4},{6,7},{7,6},{8,9},{9,8},{10,11... | collective-permute-start | bytes 393224 | tf_op jit(solution)/shard_map/ppermute | solution.py:242
  19.2 6.1 %collective-permute-start.8 = (bf16[16,4096]{1,0:T(8,128)(2,1)S(1)}, bf16[16,4096]{1,0:T(8,128)(2,1)S(1)}, u32[]{:S(2)}, u32[]{:S(2)}) collective-permute-start(bf16[16,4096]{1,0:T(8,128)(2,1)S(1)} %collective-permute-done.2.refs_8_), channel_id=1, source_target_pairs={{0,1},{1,0},{2,3},{3,2},{4,5},{5,4},{6,7},{7,6},{8,9},{9,8},{10,11... | collective-permute-start | bytes 393224 | tf_op jit(solution)/shard_map/ppermute | solution.py:242
  21.3 4.2 %collective-permute-start.7 = (bf16[16,4096]{1,0:T(8,128)(2,1)S(1)}, bf16[16,4096]{1,0:T(8,128)(2,1)S(1)}, u32[]{:S(2)}, u32[]{:S(2)}) collective-permute-start(bf16[16,4096]{1,0:T(8,128)(2,1)S(1)} %collective-permute-done.1.refs_6_), channel_id=1, source_target_pairs={{0,1},{1,0},{2,3},{3,2},{4,5},{5,4},{6,7},{7,6},{8,9},{9,8},{10,11... | collective-permute-start | bytes 393224 | tf_op jit(solution)/shard_map/ppermute | solution.py:242
  24.8 1.5 %collective-permute-start.5 = (bf16[16,4096]{1,0:T(8,128)(2,1)S(1)}, bf16[16,4096]{1,0:T(8,128)(2,1)S(1)}, u32[]{:S(2)}, u32[]{:S(2)}) collective-permute-start(bf16[16,4096]{1,0:T(8,128)(2,1)S(1)} %collective-permute-done.3.refs_2_), channel_id=1, source_target_pairs={{0,1},{1,0},{2,3},{3,2},{4,5},{5,4},{6,7},{7,6},{8,9},{9,8},{10,11... | collective-permute-start | bytes 393224 | tf_op jit(solution)/shard_map/ppermute | solution.py:242
  24.9 1.5 %collective-permute-start.6 = (bf16[16,4096]{1,0:T(8,128)(2,1)S(1)}, bf16[16,4096]{1,0:T(8,128)(2,1)S(1)}, u32[]{:S(2)}, u32[]{:S(2)}) collective-permute-start(bf16[16,4096]{1,0:T(8,128)(2,1)S(1)} %collective-permute-done.4.refs_4_), channel_id=1, source_target_pairs={{0,1},{1,0},{2,3},{3,2},{4,5},{5,4},{6,7},{7,6},{8,9},{9,8},{10,11... | collective-permute-start | bytes 393224 | tf_op jit(solution)/shard_map/ppermute | solution.py:242
  25.4 1.3 %collective-permute-start.12 = (bf16[16,4096]{1,0:T(8,128)(2,1)S(1)}, bf16[16,4096]{1,0:T(8,128)(2,1)S(1)}, u32[]{:S(2)}, u32[]{:S(2)}) collective-permute-start(bf16[16,4096]{1,0:T(8,128)(2,1)S(1)} %collective-permute-done.9.refs_10_), channel_id=1, source_target_pairs={{0,1},{1,0},{2,3},{3,2},{4,5},{5,4},{6,7},{7,6},{8,9},{9,8},{10,11... | collective-permute-start | bytes 393224 | tf_op jit(solution)/shard_map/ppermute | solution.py:242
  25.4 1.4 %collective-permute-start.13 = (bf16[16,4096]{1,0:T(8,128)(2,1)S(1)}, bf16[16,4096]{1,0:T(8,128)(2,1)S(1)}, u32[]{:S(2)}, u32[]{:S(2)}) collective-permute-start(bf16[16,4096]{1,0:T(8,128)(2,1)S(1)} %collective-permute-done.10.refs_12_), channel_id=1, source_target_pairs={{0,1},{1,0},{2,3},{3,2},{4,5},{5,4},{6,7},{7,6},{8,9},{9,8},{10,11... | collective-permute-start | bytes 393224 | tf_op jit(solution)/shard_map/ppermute | solution.py:242
  25.9 1.3 %collective-permute-start.14 = (bf16[16,4096]{1,0:T(8,128)(2,1)S(1)}, bf16[16,4096]{1,0:T(8,128)(2,1)S(1)}, u32[]{:S(2)}, u32[]{:S(2)}) collective-permute-start(bf16[16,4096]{1,0:T(8,128)(2,1)S(1)} %collective-permute-done.11.refs_14_), channel_id=1, source_target_pairs={{0,1},{1,0},{2,3},{3,2},{4,5},{5,4},{6,7},{7,6},{8,9},{9,8},{10,11... | collective-permute-start | bytes 393224 | tf_op jit(solution)/shard_map/ppermute | solution.py:242
  30.3 14.3 %collective-permute-start.17 = (s16[912,128]{1,0:T(8,128)(2,1)S(1)}, s16[912,128]{1,0:T(8,128)(2,1)S(1)}, u32[]{:S(2)}, u32[]{:S(2)}) collective-permute-start(s16[912,128]{1,0:T(8,128)(2,1)S(1)} %get-tuple-element.40), channel_id=1, source_target_pairs={{0,16},{16,0},{1,17},{17,1},{2,18},{18,2},{3,19},{19,3},{4,20},{20... | collective-permute-start | bytes 700424 | tf_op jit(solution)/shard_map/ppermute | solution.py:245
  36.4 9.1 %collective-permute-start.16 = (s16[912,128]{1,0:T(8,128)(2,1)S(1)}, s16[912,128]{1,0:T(8,128)(2,1)S(1)}, u32[]{:S(2)}, u32[]{:S(2)}) collective-permute-start(s16[912,128]{1,0:T(8,128)(2,1)S(1)} %get-tuple-element.38), channel_id=1, source_target_pairs={{0,16},{16,0},{1,17},{17,1},{2,18},{18,2},{3,19},{19,3},{4,20},{20... | collective-permute-start | bytes 700424 | tf_op jit(solution)/shard_map/ppermute | solution.py:245

commit v7 on v6

--- a/solution.py
+++ b/solution.py
@@ -105,9 +105,29 @@
         out[rows:, :] = codes.astype(jnp.int16)
 
 
-def first_terms_kernel(n_shards, n_kept, n_parts, shift, chunk, place, table, *refs):
+def add_products(total, at, weight, turned, chunk, factors=None):
+    rows = weight.shape[0]
+    for c in range(0, weight.shape[1], chunk):
+        cols = slice(c, c + chunk)
+        kept = weight[:, cols]
+        if factors is not None:
+            of_blocks = factors[:, cols].astype(jnp.bfloat16)
+            kept = jnp.concatenate(
+                [
+                    kept[b * BLOCK : (b + 1) * BLOCK, :] * of_blocks[b : b + 1, :]
+                    for b in range(rows // BLOCK)
+                ],
+                axis=0,
+            )
+        terms = jnp.dot(kept, turned[cols, :], preferred_element_type=jnp.float32)
+        to = slice(at, at + rows)
+        total[to, :] = terms if c == 0 else total[to, :] + terms
+
+
+def first_terms_kernel(n_shards, n_kept, n_parts, shift, chunk, first, place, table, *refs):
     shards, kepts = refs[:n_shards], refs[n_shards : n_shards + n_kept]
-    _, full, turned, own, *outs, total = refs[n_shards + n_kept :]
+    weight, _, full, turned, own, ahead, *outs, total, sems = refs[n_shards + n_kept :]
+    copies = fetch(weight, first, ahead, sems)
     rows = shards[0].shape[0]
     n_cols = table.shape[0]
     for n, shard in enumerate(shards):
@@ -123,31 +143,19 @@
             total[to, :] = terms if c == 0 else total[to, :] + terms
             at += kept.shape[0]
     store_terms(total, own, outs)
-
-
-def more_terms_kernel(n_parts, first, chunk, turned, weight, spread, own, *refs):
+    for copy in copies:
+        copy.wait()
+
+
+def more_terms_kernel(n_parts, first, chunk, turned, ahead, weight, spread, own, *refs):
     outs, (here, total, sems) = refs[:n_parts], refs[n_parts:]
-    rows = own.shape[0]
-    blocks = rows // BLOCK
-    copies = []
-    for c in range(0, weight.shape[1], chunk):
-        cols = pl.ds(c, chunk)
-        copies.append(
-            pltpu.make_async_copy(
-                weight.at[pl.ds(first * BLOCK, rows), cols], here.at[:, cols], sems.at[c // chunk]
-            )
-        )
-        copies[-1].start()
-    for c, copy in zip(range(0, weight.shape[1], chunk), copies, strict=True):
-        cols = slice(c, c + chunk)
-        factors = spread[first : first + blocks, cols].astype(jnp.bfloat16)
+    there = ahead.shape[0] // BLOCK
+    copies = fetch(weight, first + there, here, sems)
+    add_products(total, 0, ahead, turned, chunk, spread[first : first + there, :])
+    for copy in copies:
         copy.wait()
-        kept = jnp.concatenate(
-            [here[b * BLOCK : (b + 1) * BLOCK, cols] * factors[b : b + 1, :] for b in range(blocks)],
-            axis=0,
-        )
-        terms = jnp.dot(kept, turned[cols, :], preferred_element_type=jnp.float32)
-        total[...] = terms if c == 0 else total[...] + terms
+    last = first + there + here.shape[0] // BLOCK
+    add_products(total, ahead.shape[0], here, turned, chunk, spread[first + there : last, :])
     store_terms(total, own, outs)
 
 
@@ -289,19 +297,10 @@
     spread, again = lax.optimization_barrier((spread, grad_output))
     held[1], held[-1] = send_ring(again, 1), send_ring(again, -1)
     acts = [inputs] + [send_row(inputs, k) for k in range(1, n_rows)]
-    spread, *ready = lax.optimization_barrier((spread, *(held[j] for j in far)))
-    held.update(zip(far, ready, strict=True))
-    last = range(3, n_chips // 2 + 1)
-    for j in last:
-        by = 1 if j % 2 else 2
-        held[j] = send_ring(held[j - by], by)
-        if 2 * j < n_chips:
-            held[-j] = send_ring(held[by - j], -by)
 
     kepts = [kept_early]
     if early < piece_blocks:
         late = piece_blocks - early
-        spread, held[1], held[-1] = lax.optimization_barrier((spread, held[1], held[-1]))
         kept_late = pl.pallas_call(
             functools.partial(keep_kernel, early),
             in_specs=[in_vmem(), in_hbm()],
@@ -312,15 +311,16 @@
             cost_estimate=cost(late * BLOCK * width, 2 * late * BLOCK * width),
             name="keep",
         )(spread, weight)
-        kept_late, *ready = lax.optimization_barrier(
-            (kept_late, *(held[j] for j in reach if abs(j) > 2))
-        )
-        held.update(zip([j for j in reach if abs(j) > 2], ready, strict=True))
         kepts.append(kept_late)
-    shards = []
-    for j in reach:
-        shards += [held[j], send_core(held[j])]
-
+    kepts[-1], *ready = lax.optimization_barrier((kepts[-1], *(held[j] for j in far)))
+    held.update(zip(far, ready, strict=True))
+    for j in range(3, n_chips // 2 + 1):
+        by = 1 if j % 2 else 2
+        held[j] = send_ring(held[j - by], by)
+        if 2 * j < n_chips:
+            held[-j] = send_ring(held[by - j], -by)
+
+    *acts, held[1], held[-1] = lax.optimization_barrier((*acts, held[1], held[-1]))
     acts_turned = pl.pallas_call(
         functools.partial(turn_kernel, n_rows),
         in_specs=[in_vmem()] * n_rows,
@@ -330,47 +330,64 @@
         cost_estimate=cost(all_tokens * hidden, 4 * all_tokens * hidden),
         name="turn",
     )(*acts)
+    last = [j for j in reach if abs(j) > 2]
+    acts_turned, *ready = lax.optimization_barrier((acts_turned, *(held[j] for j in last)))
+    held.update(zip(last, ready, strict=True))
+    shards = []
+    for j in reach:
+        shards += [held[j], send_core(held[j])]
 
     n_shards = len(shards)
     code_rows = -(-(piece // BLOCK) // 16) * 16
     sent_shape = jax.ShapeDtypeStruct((piece + code_rows, tokens), jnp.int16)
     own_shape = jax.ShapeDtypeStruct((piece, tokens), jnp.float32)
     small_cost = cost(piece * width, piece * width // 8)
-    full, turned, own, *coded = pl.pallas_call(
+    n_ahead = piece_blocks - early if n_pieces > 1 else 1
+    full, turned, own, ahead, *coded = pl.pallas_call(
         functools.partial(
-            first_terms_kernel, n_shards, len(kepts), n_parts, tokens // shard_rows, chunk
+            first_terms_kernel,
+            n_shards,
+            len(kepts),
+            n_parts,
+            tokens // shard_rows,
+            chunk,
+            (n_pieces - 1) * piece_blocks,
         ),
-        in_specs=[in_smem()] * 2 + [in_vmem()] * (n_shards + len(kepts)) + [in_hbm()],
-        out_specs=[in_vmem()] * (3 + n_parts),
+        in_specs=[in_smem()] * 2 + [in_vmem()] * (n_shards + len(kepts)) + [in_hbm()] * 2,
+        out_specs=[in_vmem()] * (4 + n_parts),
         out_shape=[
             jax.ShapeDtypeStruct((all_tokens, width), bf16),
             jax.ShapeDtypeStruct((width, all_tokens), bf16),
             own_shape,
+            pltpu.VMEM((n_ahead * BLOCK, width), bf16),
         ]
         + [sent_shape] * n_parts,
-        scratch_shapes=[pltpu.VMEM((piece, all_tokens), jnp.float32)],
+        scratch_shapes=[
+            pltpu.VMEM((piece, all_tokens), jnp.float32),
+            pltpu.SemaphoreType.DMA((n_ahead,)),
+        ],
         compiler_params=params(),
         cost_estimate=small_cost,
         name="first_terms",
-    )(place, jnp.array(table, jnp.int32), *shards, *kepts, acts_turned)
+    )(place, jnp.array(table, jnp.int32), *shards, *kepts, weight, acts_turned)
     owns = [own]
     parts = [send_row(coded[k], k + 1) for k in range(n_parts)]
 
-    for p in range(1, n_pieces):
+    if n_pieces > 1:
         own, *coded = pl.pallas_call(
-            functools.partial(more_terms_kernel, n_parts, p * piece_blocks, chunk),
-            in_specs=[in_vmem(), in_hbm(), in_vmem()],
+            functools.partial(more_terms_kernel, n_parts, piece_blocks, chunk),
+            in_specs=[in_vmem(), in_vmem(), in_hbm(), in_vmem()],
             out_specs=[in_vmem()] * (1 + n_parts),
             out_shape=[own_shape] + [sent_shape] * n_parts,
             scratch_shapes=[
-                pltpu.VMEM((piece, width), bf16),
+                pltpu.VMEM((early * BLOCK, width), bf16),
                 pltpu.VMEM((piece, all_tokens), jnp.float32),
-                pltpu.SemaphoreType.DMA((width // chunk,)),
+                pltpu.SemaphoreType.DMA((early,)),
             ],
             compiler_params=params(),
             cost_estimate=small_cost,
             name="more_terms",
-        )(turned, weight, spread)
+        )(turned, ahead, weight, spread)
         owns.append(own)
         parts += [send_row(coded[k], k + 1) for k in range(n_parts)]
 

time: 46.5 us -> 46 us (0.989)
  waiting for transfers between devices: 7.48 us -> 5.27 us
  Pallas kernels: 22 us -> 23.6 us
    ppermute x7, waiting for transfers between devices: 6.5 us -> 4.24 us  [send_ring(): return lax.ppermute(x, 'col', perm)]
    pallas_call x1, Pallas kernels: 3.1 us -> 4.65 us  [per_device(): pl.pallas_call(functools.partial(first_terms_kernel, n_shards, len(kepts)...]
    ppermute x7, starting transfers between devices: 8.45 us -> 9.39 us  [send_ring(): return lax.ppermute(x, 'col', perm)]
    ppermute x8, starting transfers between devices: 2.36 us -> 1.54 us  [send_core(): return lax.ppermute(x, 'col', [(c, c ^ 1) for c in range(n_cols)])]
  transfers between devices with their start and end apart: 18 -> 18, of which waited for: 8 -> 8; matrix products, arithmetic and copies ran while one was open for 0% -> 0% of each run, Pallas kernels for 39% -> 40%
where the time goes in v7:
time: 46 us; the launch traced here: 45.8 us
  Pallas kernels  23.6 us (51%)
  starting transfers between devices  16.1 us (35%)
  waiting for transfers between devices  5.27 us (11%)
  between operations  0.73 us (2%)
    ppermute x7, starting transfers between devices, send_ring(): return lax.ppermute(x, 'col', perm)  9.39 us
    pallas_call x1, Pallas kernels, per_device(): pl.pallas_call(functools.partial(weight_grad_kernel, chunk), in_specs=[in...  6.57 us
    pallas_call x1, Pallas kernels, per_device(): pl.pallas_call(functools.partial(more_terms_kernel, n_parts, piece_blocks...  5.62 us
    ppermute x3, starting transfers between devices, send_row(): lax.ppermute(x, 'row', [(r, (r + by) % n_rows) for r in range(n_rows)])  5.19 us
    pallas_call x1, Pallas kernels, per_device(): pl.pallas_call(functools.partial(first_terms_kernel, n_shards, len(kepts)...  4.65 us
    ppermute x7, waiting for transfers between devices, send_ring(): return lax.ppermute(x, 'col', perm)  4.24 us
    pallas_call x1, Pallas kernels, per_device(): pl.pallas_call(spread_and_keep_kernel, in_specs=[in_smem(), in_hbm(), in_...  2.52 us
    pallas_call x1, Pallas kernels, per_device(): pl.pallas_call(functools.partial(keep_kernel, early), in_specs=[in_vmem()...  2.28 us
  transfers between devices with their start and end apart: 18, of which 8 were waited for; matrix products, arithmetic and copies ran while one was open for 0% of the time, Pallas kernels for 40%

profile of v7, /device:TPU:0, one launch (start us, length us, event | category | flops | bytes accessed | tf_op | source)
XLA Modules:
  0.0 45.8 jit_solution(14215396786227455427)
XLA Ops:
  0.6 3.0 %collective-permute-start.1 = (bf16[128,1792]{1,0:T(8,128)(2,1)}, bf16[128,1792]{1,0:T(8,128)(2,1)S(1)}, u32[]{:S(2)}, u32[]{:S(2)}) collective-permute-start(bf16[128,1792]{1,0:T(8,128)(2,1)} %refs_0_.1), channel_id=1, source_target_pairs={{0,16},{16,0},{1,17},{17,1},{2,18},{18,2},{3,19},{19,3},{4,20},{20... | collective-permute-start | bytes 1376264 | tf_op jit(solution)/shard_map/ppermute | solution.py:253
  3.7 2.5 %collective-permute-start.6 = (bf16[16,4096]{1,0:T(8,128)(2,1)}, bf16[16,4096]{1,0:T(8,128)(2,1)S(1)}, u32[]{:S(2)}, u32[]{:S(2)}) collective-permute-start(bf16[16,4096]{1,0:T(8,128)(2,1)} %refs_0_.2), channel_id=1, source_target_pairs={{2,10},{3,5},{6,14},{7,1},{10,12},{11,3},{14,8},{15,7},{12,4},{13,... | collective-permute-start | bytes 393224 | tf_op jit(solution)/shard_map/ppermute | solution.py:247
  6.2 0.4 collective-permute-start.7
  6.6 0.1 pad_add_fusion.place
  6.7 0.0 copy-start.1
  6.7 2.5 %spread_and_keep.1 = (bf16[384,4096]{1,0:T(8,128)(2,1)S(1)}, f32[14,4096]{1,0:T(8,128)S(1)}) custom-call(s32[2]{0:T(128)S(1)} %pad_add_fusion.place, bf16[1792,4096]{1,0:T(8,128)(2,1)} %weight.5, s32[14,64]{1,0:T(8,128)} %mask.1), custom_call_target="tpu_custom_call" | custom-call | flops 1572864 | bytes 3145728 | tf_op jit(solution)/shard_map/spread_and_keep/pallas_call | solution.py:274
  9.2 0.0 copy-done.1
  9.2 0.0 copy-start
  9.2 0.0 copy-start.2
  9.2 1.6 %collective-permute-start.3 = (bf16[16,4096]{1,0:T(8,128)(2,1)S(1)}, bf16[16,4096]{1,0:T(8,128)(2,1)S(1)}, u32[]{:S(2)}, u32[]{:S(2)}) collective-permute-start(bf16[16,4096]{1,0:T(8,128)(2,1)S(1)} %copy-done.1), channel_id=1, source_target_pairs={{2,0},{3,7},{6,2},{7,11},{10,6},{11,15},{14,10},{15,13},{12,14},{1... | collective-permute-start | bytes 393224 | tf_op jit(solution)/shard_map/ppermute | solution.py:247
  10.9 0.4 collective-permute-start.2
  11.3 2.3 %keep.1.refs_17_ = bf16[512,4096]{1,0:T(8,128)(2,1)S(1)} custom-call(f32[14,4096]{1,0:T(8,128)S(1)} %get-tuple-element.28.spread, bf16[1792,4096]{1,0:T(8,128)(2,1)} %weight.5), custom_call_target="tpu_custom_call" | custom-call | flops 2097152 | bytes 4194304 | tf_op jit(solution)/shard_map/keep/pallas_call | solution.py:304
  13.6 0.0 collective-permute-done.6.refs_6_
  13.6 0.2 collective-permute-done.7.refs_8_
  13.8 1.4 %collective-permute-start.11 = (bf16[16,4096]{1,0:T(8,128)(2,1)S(1)}, bf16[16,4096]{1,0:T(8,128)(2,1)S(1)}, u32[]{:S(2)}, u32[]{:S(2)}) collective-permute-start(bf16[16,4096]{1,0:T(8,128)(2,1)S(1)} %collective-permute-done.7.refs_8_), channel_id=1, source_target_pairs={{2,0},{3,7},{6,2},{7,11},{10,6},{11,15},{14,10},{15,13},{12,14},{1... | collective-permute-start | bytes 393224 | tf_op jit(solution)/shard_map/ppermute | solution.py:247
  15.3 1.7 %collective-permute-start.12 = (bf16[16,4096]{1,0:T(8,128)(2,1)S(1)}, bf16[16,4096]{1,0:T(8,128)(2,1)S(1)}, u32[]{:S(2)}, u32[]{:S(2)}) collective-permute-start(bf16[16,4096]{1,0:T(8,128)(2,1)S(1)} %collective-permute-done.6.refs_6_), channel_id=1, source_target_pairs={{2,10},{3,5},{6,14},{7,1},{10,12},{11,3},{14,8},{15,7},{12,4},{13,... | collective-permute-start | bytes 393224 | tf_op jit(solution)/shard_map/ppermute | solution.py:247
  16.9 0.0 collective-permute-done.3.refs_4_
  16.9 1.3 %collective-permute-start.10 = (bf16[16,4096]{1,0:T(8,128)(2,1)S(1)}, bf16[16,4096]{1,0:T(8,128)(2,1)S(1)}, u32[]{:S(2)}, u32[]{:S(2)}) collective-permute-start(bf16[16,4096]{1,0:T(8,128)(2,1)S(1)} %collective-permute-done.6.refs_6_), channel_id=1, source_target_pairs={{2,6},{3,1},{6,10},{7,3},{10,14},{11,7},{14,12},{15,11},{12,8},{13... | collective-permute-start | bytes 393224 | tf_op jit(solution)/shard_map/ppermute | solution.py:247
  18.2 0.0 collective-permute-done.2.refs_2_
  18.2 0.0 collective-permute-start
  18.2 0.9 %collective-permute-done.11.refs_12_ = bf16[16,4096]{1,0:T(8,128)(2,1)S(1)} collective-permute-done((bf16[16,4096]{1,0:T(8,128)(2,1)S(1)}, bf16[16,4096]{1,0:T(8,128)(2,1)S(1)}, u32[]{:S(2)}, u32[]{:S(2)}) %collective-permute-start.11) | collective-permute-done | bytes 131104 | tf_op jit(solution)/shard_map/ppermute | solution.py:247
  19.1 0.0 collective-permute-start.9
  19.1 0.0 collective-permute-done.1.refs_1_
  19.1 0.5 %collective-permute-start.8 = (bf16[16,4096]{1,0:T(8,128)(2,1)S(1)}, bf16[16,4096]{1,0:T(8,128)(2,1)S(1)}, u32[]{:S(2)}, u32[]{:S(2)}) collective-permute-start(bf16[16,4096]{1,0:T(8,128)(2,1)S(1)} %collective-permute-done.6.refs_6_), channel_id=1, source_target_pairs={{0,1},{1,0},{2,3},{3,2},{4,5},{5,4},{6,7},{7,6},{8,9},{9,8},{10,11... | collective-permute-start | bytes 393224 | tf_op jit(solution)/shard_map/ppermute | solution.py:250
  19.7 0.0 copy-done
  19.7 0.3 turn.1.refs_19_.acts
  19.9 2.7 %collective-permute-done.12.refs_14_ = bf16[16,4096]{1,0:T(8,128)(2,1)S(1)} collective-permute-done((bf16[16,4096]{1,0:T(8,128)(2,1)S(1)}, bf16[16,4096]{1,0:T(8,128)(2,1)S(1)}, u32[]{:S(2)}, u32[]{:S(2)}) %collective-permute-start.12) | collective-permute-done | bytes 131104 | tf_op jit(solution)/shard_map/ppermute | solution.py:247
  22.7 0.0 collective-permute-start.4
  22.7 0.4 collective-permute-done.10.refs_10_
  23.1 0.1 collective-permute-start.5
  23.2 0.0 collective-permute-done.refs_1_
  23.2 0.4 collective-permute-start.13
  23.6 0.0 collective-permute-done.9.refs_9_
  23.6 0.1 collective-permute-start.14
  23.7 0.0 collective-permute-done.8.refs_7_
  23.7 0.4 collective-permute-start.15
  24.1 0.0 collective-permute-done.4.refs_3_
  24.1 0.3 collective-permute-done.5.refs_5_
  24.4 0.2 collective-permute-done.13.refs_11_
  24.6 0.3 collective-permute-done.14.refs_13_
  24.9 0.2 collective-permute-done.15.refs_15_
  25.1 0.0 copy-done.2
  25.1 4.7 %first_terms.1 = (bf16[256,4096]{1,0:T(8,128)(2,1)S(1)}, bf16[4096,256]{1,0:T(8,128)(2,1)S(1)}, f32[896,128]{1,0:T(8,128)S(1)}, bf16[512,4096]{1,0:T(8,128)(2,1)S(1)}, s16[912,128]{1,0:T(8,128)(2,1)S(1)}) custom-call(s32[2]{0:T(128)S(1)} %pad_add_fusion.place, s32[16,16]{1,0:T(8,128)S(1)} %copy-done.2, bf16[16,4096]{1,0:T(8,128)(2,1)S(1)} %copy-done.1, ...), custom_call_target="tpu_custom_call" | custom-call | flops 3670016 | bytes 458752 | tf_op jit(solution)/shard_map/first_terms/pallas_call | solution.py:346
  29.8 0.6 %collective-permute-start.17 = (s16[912,128]{1,0:T(8,128)(2,1)S(1)}, s16[912,128]{1,0:T(8,128)(2,1)S(1)}, u32[]{:S(2)}, u32[]{:S(2)}) collective-permute-start(s16[912,128]{1,0:T(8,128)(2,1)S(1)} %get-tuple-element.44), channel_id=1, source_target_pairs={{0,16},{16,0},{1,17},{17,1},{2,18},{18,2},{3,19},{19,3},{4,20},{20... | collective-permute-start | bytes 700424 | tf_op jit(solution)/shard_map/ppermute | solution.py:253
  30.3 5.6 %more_terms.1 = (f32[896,128]{1,0:T(8,128)S(1)}, s16[912,128]{1,0:T(8,128)(2,1)S(1)}) custom-call(bf16[4096,256]{1,0:T(8,128)(2,1)S(1)} %get-tuple-element.39.turned, bf16[512,4096]{1,0:T(8,128)(2,1)S(1)} %get-tuple-element.40.ahead, bf16[1792,4096]{1,0:T(8,128)(2,1)} %weight.5, f32[14,4096]{1,0:T(8,128)S(1)} %get-tuple-element.28.spread), custom_call_target="tpu_custom_call" | custom-call | flops 3670016 | bytes 458752 | tf_op jit(solution)/shard_map/more_terms/pallas_call | solution.py:377
  36.0 1.6 %collective-permute-start.16 = (s16[912,128]{1,0:T(8,128)(2,1)S(1)}, s16[912,128]{1,0:T(8,128)(2,1)S(1)}, u32[]{:S(2)}, u32[]{:S(2)}) collective-permute-start(s16[912,128]{1,0:T(8,128)(2,1)S(1)} %get-tuple-element.42), channel_id=1, source_target_pairs={{0,16},{16,0},{1,17},{17,1},{2,18},{18,2},{3,19},{19,3},{4,20},{20... | collective-permute-start | bytes 700424 | tf_op jit(solution)/shard_map/ppermute | solution.py:253
  37.6 6.6 %weight_grad.1 = bf16[1792,4096]{1,0:T(8,128)(2,1)} custom-call(bf16[1792,256]{1,0:T(8,128)(2,1)S(1)} %turn.1.refs_19_.acts, bf16[256,4096]{1,0:T(8,128)(2,1)S(1)} %get-tuple-element.45.full, f32[14,4096]{1,0:T(8,128)S(1)} %get-tuple-element.28.spread), custom_call_target="tpu_custom_call" | custom-call | flops 3670016 | bytes 458752 | tf_op jit(solution)/shard_map/weight_grad/pallas_call | solution.py:394
  44.1 0.0 collective-permute-done.17.refs_0_
  44.1 0.8 %add_terms.2.refs_1_ = bf16[128,1792]{1,0:T(8,128)(2,1)} custom-call(f32[896,128]{1,0:T(8,128)S(1)} %get-tuple-element.43.own, s16[912,128]{1,0:T(8,128)(2,1)S(1)} %collective-permute-done.17.refs_0_), custom_call_target="tpu_custom_call" | custom-call | tf_op jit(solution)/shard_map/add_terms/pallas_call | solution.py:415
  45.0 0.0 collective-permute-done.16.refs_0_
  45.0 0.8 %add_terms.3 = bf16[128,1792]{1,0:T(8,128)(2,1)} custom-call(f32[896,128]{1,0:T(8,128)S(1)} %get-tuple-element.41.own, s16[912,128]{1,0:T(8,128)(2,1)S(1)} %collective-permute-done.16.refs_0_, bf16[128,1792]{1,0:T(8,128)(2,1)} %add_terms.2.refs_1_), custom_call_target="tpu_custom_call", output_to_operand_aliasing={{}: (2, {})} | custom-call | tf_op jit(solution)/shard_map/add_terms/pallas_call | solution.py:415
Async XLA Ops:
  0.6 18.5 %collective-permute-start.1 = (bf16[128,1792]{1,0:T(8,128)(2,1)}, bf16[128,1792]{1,0:T(8,128)(2,1)S(1)}, u32[]{:S(2)}, u32[]{:S(2)}) collective-permute-start(bf16[128,1792]{1,0:T(8,128)(2,1)} %refs_0_.1), channel_id=1, source_target_pairs={{0,16},{16,0},{1,17},{17,1},{2,18},{18,2},{3,19},{19,3},{4,20},{20... | collective-permute-start | bytes 1376264 | tf_op jit(solution)/shard_map/ppermute | solution.py:253
  3.7 9.9 %collective-permute-start.6 = (bf16[16,4096]{1,0:T(8,128)(2,1)}, bf16[16,4096]{1,0:T(8,128)(2,1)S(1)}, u32[]{:S(2)}, u32[]{:S(2)}) collective-permute-start(bf16[16,4096]{1,0:T(8,128)(2,1)} %refs_0_.2), channel_id=1, source_target_pairs={{2,10},{3,5},{6,14},{7,1},{10,12},{11,3},{14,8},{15,7},{12,4},{13,... | collective-permute-start | bytes 393224 | tf_op jit(solution)/shard_map/ppermute | solution.py:247
  6.2 7.7 %collective-permute-start.7 = (bf16[16,4096]{1,0:T(8,128)(2,1)}, bf16[16,4096]{1,0:T(8,128)(2,1)S(1)}, u32[]{:S(2)}, u32[]{:S(2)}) collective-permute-start(bf16[16,4096]{1,0:T(8,128)(2,1)} %refs_0_.2), channel_id=1, source_target_pairs={{2,4},{3,11},{6,0},{7,15},{10,2},{11,13},{14,6},{15,9},{12,10},{13... | collective-permute-start | bytes 393224 | tf_op jit(solution)/shard_map/ppermute | solution.py:247
  6.7 2.5 %copy-start.1 = (bf16[16,4096]{1,0:T(8,128)(2,1)S(1)}, bf16[16,4096]{1,0:T(8,128)(2,1)}, u32[]{:S(2)}) copy-start(bf16[16,4096]{1,0:T(8,128)(2,1)} %refs_0_.2) | copy-start | bytes 393220
  9.2 10.4 %copy-start = (bf16[128,1792]{1,0:T(8,128)(2,1)S(1)}, bf16[128,1792]{1,0:T(8,128)(2,1)}, u32[]{:S(2)}) copy-start(bf16[128,1792]{1,0:T(8,128)(2,1)} %refs_0_.1) | copy-start | bytes 1376260
  9.2 15.9 %copy-start.2 = (s32[16,16]{1,0:T(8,128)S(1)}, s32[16,16]{1,0:T(8,128)}, u32[]{:S(2)}) copy-start(s32[16,16]{1,0:T(8,128)} %constant.11.clone.table) | copy-start | bytes 3076
  9.2 7.7 %collective-permute-start.3 = (bf16[16,4096]{1,0:T(8,128)(2,1)S(1)}, bf16[16,4096]{1,0:T(8,128)(2,1)S(1)}, u32[]{:S(2)}, u32[]{:S(2)}) collective-permute-start(bf16[16,4096]{1,0:T(8,128)(2,1)S(1)} %copy-done.1), channel_id=1, source_target_pairs={{2,0},{3,7},{6,2},{7,11},{10,6},{11,15},{14,10},{15,13},{12,14},{1... | collective-permute-start | bytes 393224 | tf_op jit(solution)/shard_map/ppermute | solution.py:247
  10.9 7.4 %collective-permute-start.2 = (bf16[16,4096]{1,0:T(8,128)(2,1)S(1)}, bf16[16,4096]{1,0:T(8,128)(2,1)S(1)}, u32[]{:S(2)}, u32[]{:S(2)}) collective-permute-start(bf16[16,4096]{1,0:T(8,128)(2,1)S(1)} %copy-done.1), channel_id=1, source_target_pairs={{2,6},{3,1},{6,10},{7,3},{10,14},{11,7},{14,12},{15,11},{12,8},{13... | collective-permute-start | bytes 393224 | tf_op jit(solution)/shard_map/ppermute | solution.py:247
  13.8 5.3 %collective-permute-start.11 = (bf16[16,4096]{1,0:T(8,128)(2,1)S(1)}, bf16[16,4096]{1,0:T(8,128)(2,1)S(1)}, u32[]{:S(2)}, u32[]{:S(2)}) collective-permute-start(bf16[16,4096]{1,0:T(8,128)(2,1)S(1)} %collective-permute-done.7.refs_8_), channel_id=1, source_target_pairs={{2,0},{3,7},{6,2},{7,11},{10,6},{11,15},{14,10},{15,13},{12,14},{1... | collective-permute-start | bytes 393224 | tf_op jit(solution)/shard_map/ppermute | solution.py:247
  15.3 7.4 %collective-permute-start.12 = (bf16[16,4096]{1,0:T(8,128)(2,1)S(1)}, bf16[16,4096]{1,0:T(8,128)(2,1)S(1)}, u32[]{:S(2)}, u32[]{:S(2)}) collective-permute-start(bf16[16,4096]{1,0:T(8,128)(2,1)S(1)} %collective-permute-done.6.refs_6_), channel_id=1, source_target_pairs={{2,10},{3,5},{6,14},{7,1},{10,12},{11,3},{14,8},{15,7},{12,4},{13,... | collective-permute-start | bytes 393224 | tf_op jit(solution)/shard_map/ppermute | solution.py:247
  16.9 6.2 %collective-permute-start.10 = (bf16[16,4096]{1,0:T(8,128)(2,1)S(1)}, bf16[16,4096]{1,0:T(8,128)(2,1)S(1)}, u32[]{:S(2)}, u32[]{:S(2)}) collective-permute-start(bf16[16,4096]{1,0:T(8,128)(2,1)S(1)} %collective-permute-done.6.refs_6_), channel_id=1, source_target_pairs={{2,6},{3,1},{6,10},{7,3},{10,14},{11,7},{14,12},{15,11},{12,8},{13... | collective-permute-start | bytes 393224 | tf_op jit(solution)/shard_map/ppermute | solution.py:247
  18.2 5.0 %collective-permute-start = (bf16[16,4096]{1,0:T(8,128)(2,1)S(1)}, bf16[16,4096]{1,0:T(8,128)(2,1)S(1)}, u32[]{:S(2)}, u32[]{:S(2)}) collective-permute-start(bf16[16,4096]{1,0:T(8,128)(2,1)S(1)} %copy-done.1), channel_id=1, source_target_pairs={{0,1},{1,0},{2,3},{3,2},{4,5},{5,4},{6,7},{7,6},{8,9},{9,8},{10,11... | collective-permute-start | bytes 393224 | tf_op jit(solution)/shard_map/ppermute | solution.py:250
  19.1 4.4 %collective-permute-start.9 = (bf16[16,4096]{1,0:T(8,128)(2,1)S(1)}, bf16[16,4096]{1,0:T(8,128)(2,1)S(1)}, u32[]{:S(2)}, u32[]{:S(2)}) collective-permute-start(bf16[16,4096]{1,0:T(8,128)(2,1)S(1)} %collective-permute-done.7.refs_8_), channel_id=1, source_target_pairs={{0,1},{1,0},{2,3},{3,2},{4,5},{5,4},{6,7},{7,6},{8,9},{9,8},{10,11... | collective-permute-start | bytes 393224 | tf_op jit(solution)/shard_map/ppermute | solution.py:250
  19.1 4.6 %collective-permute-start.8 = (bf16[16,4096]{1,0:T(8,128)(2,1)S(1)}, bf16[16,4096]{1,0:T(8,128)(2,1)S(1)}, u32[]{:S(2)}, u32[]{:S(2)}) collective-permute-start(bf16[16,4096]{1,0:T(8,128)(2,1)S(1)} %collective-permute-done.6.refs_6_), channel_id=1, source_target_pairs={{0,1},{1,0},{2,3},{3,2},{4,5},{5,4},{6,7},{7,6},{8,9},{9,8},{10,11... | collective-permute-start | bytes 393224 | tf_op jit(solution)/shard_map/ppermute | solution.py:250
  22.7 1.4 %collective-permute-start.4 = (bf16[16,4096]{1,0:T(8,128)(2,1)S(1)}, bf16[16,4096]{1,0:T(8,128)(2,1)S(1)}, u32[]{:S(2)}, u32[]{:S(2)}) collective-permute-start(bf16[16,4096]{1,0:T(8,128)(2,1)S(1)} %collective-permute-done.2.refs_2_), channel_id=1, source_target_pairs={{0,1},{1,0},{2,3},{3,2},{4,5},{5,4},{6,7},{7,6},{8,9},{9,8},{10,11... | collective-permute-start | bytes 393224 | tf_op jit(solution)/shard_map/ppermute | solution.py:250
  23.1 1.3 %collective-permute-start.5 = (bf16[16,4096]{1,0:T(8,128)(2,1)S(1)}, bf16[16,4096]{1,0:T(8,128)(2,1)S(1)}, u32[]{:S(2)}, u32[]{:S(2)}) collective-permute-start(bf16[16,4096]{1,0:T(8,128)(2,1)S(1)} %collective-permute-done.3.refs_4_), channel_id=1, source_target_pairs={{0,1},{1,0},{2,3},{3,2},{4,5},{5,4},{6,7},{7,6},{8,9},{9,8},{10,11... | collective-permute-start | bytes 393224 | tf_op jit(solution)/shard_map/ppermute | solution.py:250
  23.2 1.4 %collective-permute-start.13 = (bf16[16,4096]{1,0:T(8,128)(2,1)S(1)}, bf16[16,4096]{1,0:T(8,128)(2,1)S(1)}, u32[]{:S(2)}, u32[]{:S(2)}) collective-permute-start(bf16[16,4096]{1,0:T(8,128)(2,1)S(1)} %collective-permute-done.10.refs_10_), channel_id=1, source_target_pairs={{0,1},{1,0},{2,3},{3,2},{4,5},{5,4},{6,7},{7,6},{8,9},{9,8},{10,11... | collective-permute-start | bytes 393224 | tf_op jit(solution)/shard_map/ppermute | solution.py:250
  23.6 1.3 %collective-permute-start.14 = (bf16[16,4096]{1,0:T(8,128)(2,1)S(1)}, bf16[16,4096]{1,0:T(8,128)(2,1)S(1)}, u32[]{:S(2)}, u32[]{:S(2)}) collective-permute-start(bf16[16,4096]{1,0:T(8,128)(2,1)S(1)} %collective-permute-done.11.refs_12_), channel_id=1, source_target_pairs={{0,1},{1,0},{2,3},{3,2},{4,5},{5,4},{6,7},{7,6},{8,9},{9,8},{10,11... | collective-permute-start | bytes 393224 | tf_op jit(solution)/shard_map/ppermute | solution.py:250
  23.7 1.4 %collective-permute-start.15 = (bf16[16,4096]{1,0:T(8,128)(2,1)S(1)}, bf16[16,4096]{1,0:T(8,128)(2,1)S(1)}, u32[]{:S(2)}, u32[]{:S(2)}) collective-permute-start(bf16[16,4096]{1,0:T(8,128)(2,1)S(1)} %collective-permute-done.12.refs_14_), channel_id=1, source_target_pairs={{0,1},{1,0},{2,3},{3,2},{4,5},{5,4},{6,7},{7,6},{8,9},{9,8},{10,11... | collective-permute-start | bytes 393224 | tf_op jit(solution)/shard_map/ppermute | solution.py:250
  29.8 14.4 %collective-permute-start.17 = (s16[912,128]{1,0:T(8,128)(2,1)S(1)}, s16[912,128]{1,0:T(8,128)(2,1)S(1)}, u32[]{:S(2)}, u32[]{:S(2)}) collective-permute-start(s16[912,128]{1,0:T(8,128)(2,1)S(1)} %get-tuple-element.44), channel_id=1, source_target_pairs={{0,16},{16,0},{1,17},{17,1},{2,18},{18,2},{3,19},{19,3},{4,20},{20... | collective-permute-start | bytes 700424 | tf_op jit(solution)/shard_map/ppermute | solution.py:253
  36.0 9.0 %collective-permute-start.16 = (s16[912,128]{1,0:T(8,128)(2,1)S(1)}, s16[912,128]{1,0:T(8,128)(2,1)S(1)}, u32[]{:S(2)}, u32[]{:S(2)}) collective-permute-start(s16[912,128]{1,0:T(8,128)(2,1)S(1)} %get-tuple-element.42), channel_id=1, source_target_pairs={{0,16},{16,0},{1,17},{17,1},{2,18},{18,2},{3,19},{19,3},{4,20},{20... | collective-permute-start | bytes 700424 | tf_op jit(solution)/shard_map/ppermute | solution.py:253

commit v8 on v7

--- a/solution.py
+++ b/solution.py
@@ -49,37 +49,43 @@
     rows, width = kept.shape
     mask_copy = pltpu.make_async_copy(mask, mask_here, mask_sem)
     mask_copy.start()
-    copies = fetch(weight, 0, kept, sems)
+    fetch(weight, 0, kept, sems)
     mask_copy.wait()
     spread[...] = wide_mask(mask_here[...], place[0] * (width // BLOCK), width)
-    drop_blocks(copies, kept, spread[: rows // BLOCK, :])
+    drop_blocks(weight, 0, kept, spread, sems)
 
 
 def keep_kernel(first, spread, weight, kept, sems):
-    copies = fetch(weight, first, kept, sems)
-    drop_blocks(copies, kept, spread[first : first + kept.shape[0] // BLOCK, :])
-
-
-def fetch(weight, first, kept, sems):
-    copies = []
-    for b in range(kept.shape[0] // BLOCK):
-        copies.append(
-            pltpu.make_async_copy(
-                weight.at[pl.ds((first + b) * BLOCK, BLOCK), :],
-                kept.at[pl.ds(b * BLOCK, BLOCK), :],
-                sems.at[b],
-            )
-        )
-        copies[-1].start()
-    return copies
-
-
-def drop_blocks(copies, kept, spread):
-    factors = spread.astype(jnp.bfloat16)
-    for b, copy in enumerate(copies):
-        copy.wait()
-        at = slice(b * BLOCK, (b + 1) * BLOCK)
-        kept[at, :] = kept[at, :] * factors[b : b + 1, :]
+    fetch(weight, first, kept, sems)
+    drop_blocks(weight, first, kept, spread, sems)
+
+
+def row_copy(weight, first, here, sems, block):
+    to = pl.multiple_of(block * BLOCK, BLOCK)
+    at = pl.multiple_of((first + block) * BLOCK, BLOCK)
+    return pltpu.make_async_copy(
+        weight.at[pl.ds(at, BLOCK), :], here.at[pl.ds(to, BLOCK), :], sems.at[block]
+    )
+
+
+def fetch(weight, first, here, sems):
+    blocks = here.shape[0] // BLOCK
+    lax.fori_loop(0, blocks, lambda b, _: (row_copy(weight, first, here, sems, b).start(), 0)[1], 0)
+
+
+def fetched(weight, first, here, sems):
+    blocks = here.shape[0] // BLOCK
+    lax.fori_loop(0, blocks, lambda b, _: (row_copy(weight, first, here, sems, b).wait(), 0)[1], 0)
+
+
+def drop_blocks(weight, first, kept, spread, sems):
+    def one(b, _):
+        row_copy(weight, first, kept, sems, b).wait()
+        at = pl.ds(pl.multiple_of(b * BLOCK, BLOCK), BLOCK)
+        kept[at, :] = kept[at, :] * spread[pl.ds(first + b, 1), :].astype(kept.dtype)
+        return 0
+
+    lax.fori_loop(0, kept.shape[0] // BLOCK, one, 0)
 
 
 def turn_kernel(n_rows, *refs):
@@ -96,66 +102,70 @@
     own[...] = total[:, :tokens]
     for k, out in enumerate(outs):
         of_code = lax.broadcasted_iota(jnp.int32, (out.shape[0] - rows, tokens), 0)
-        codes = jnp.zeros(of_code.shape, jnp.int32)
-        for b in range(rows // BLOCK):
-            at = slice(b * BLOCK, (b + 1) * BLOCK)
+
+        def one(b, codes, k=k, out=out, of_code=of_code):
+            at = pl.ds(pl.multiple_of(b * BLOCK, BLOCK), BLOCK)
             whole, code = encode(total[at, (k + 1) * tokens : (k + 2) * tokens])
             out[at, :] = whole.astype(jnp.int16)
-            codes = jnp.where(of_code == b, code, codes)
+            return jnp.where(of_code == b, code, codes)
+
+        codes = lax.fori_loop(0, rows // BLOCK, one, jnp.zeros(of_code.shape, jnp.int32))
         out[rows:, :] = codes.astype(jnp.int16)
-
-
-def add_products(total, at, weight, turned, chunk, factors=None):
-    rows = weight.shape[0]
-    for c in range(0, weight.shape[1], chunk):
-        cols = slice(c, c + chunk)
-        kept = weight[:, cols]
-        if factors is not None:
-            of_blocks = factors[:, cols].astype(jnp.bfloat16)
-            kept = jnp.concatenate(
-                [
-                    kept[b * BLOCK : (b + 1) * BLOCK, :] * of_blocks[b : b + 1, :]
-                    for b in range(rows // BLOCK)
-                ],
-                axis=0,
-            )
-        terms = jnp.dot(kept, turned[cols, :], preferred_element_type=jnp.float32)
-        to = slice(at, at + rows)
-        total[to, :] = terms if c == 0 else total[to, :] + terms
 
 
 def first_terms_kernel(n_shards, n_kept, n_parts, shift, chunk, first, place, table, *refs):
     shards, kepts = refs[:n_shards], refs[n_shards : n_shards + n_kept]
     weight, _, full, turned, own, ahead, *outs, total, sems = refs[n_shards + n_kept :]
-    copies = fetch(weight, first, ahead, sems)
+    fetch(weight, first, ahead, sems)
     rows = shards[0].shape[0]
     n_cols = table.shape[0]
     for n, shard in enumerate(shards):
         to = lax.rem(table[place[1], n] + n_cols - place[0] * shift, n_cols)
         full[pl.ds(pl.multiple_of(to * rows, rows), rows), :] = shard[...]
-    for c in range(0, full.shape[1], chunk):
-        cols = slice(c, c + chunk)
-        turned[cols, :] = full[:, cols].T
+    n_chunks = full.shape[1] // chunk
+
+    def columns(c):
+        return pl.ds(pl.multiple_of(c * chunk, chunk), chunk)
+
+    turned[:chunk, :] = full[:, :chunk].T
+    total[...] = jnp.zeros_like(total)
+
+    def one(c, _):
+        cols, after = columns(c), columns(lax.rem(c + 1, n_chunks))
         at = 0
         for kept in kepts:
             to = slice(at, at + kept.shape[0])
-            terms = jnp.dot(kept[:, cols], turned[cols, :], preferred_element_type=jnp.float32)
-            total[to, :] = terms if c == 0 else total[to, :] + terms
+            total[to, :] += jnp.dot(
+                kept[:, cols], turned[cols, :], preferred_element_type=jnp.float32
+            )
             at += kept.shape[0]
+        turned[after, :] = full[:, after].T
+        return 0
+
+    lax.fori_loop(0, n_chunks, one, 0)
     store_terms(total, own, outs)
-    for copy in copies:
-        copy.wait()
-
-
-def more_terms_kernel(n_parts, first, chunk, turned, ahead, weight, spread, own, *refs):
-    outs, (here, total, sems) = refs[:n_parts], refs[n_parts:]
-    there = ahead.shape[0] // BLOCK
-    copies = fetch(weight, first + there, here, sems)
-    add_products(total, 0, ahead, turned, chunk, spread[first : first + there, :])
-    for copy in copies:
-        copy.wait()
-    last = first + there + here.shape[0] // BLOCK
-    add_products(total, ahead.shape[0], here, turned, chunk, spread[first + there : last, :])
+    fetched(weight, first, ahead, sems)
+
+
+def more_terms_kernel(n_parts, first, chunk, turned, ahead, spread, own, *refs):
+    outs, (total,) = refs[:n_parts], refs[n_parts:]
+    blocks = own.shape[0] // BLOCK
+    total[...] = jnp.zeros_like(total)
+
+    def one(c, _):
+        cols = pl.ds(pl.multiple_of(c * chunk, chunk), chunk)
+        factors = spread[first : first + blocks, cols].astype(jnp.bfloat16)
+        kept = jnp.concatenate(
+            [
+                ahead[b * BLOCK : (b + 1) * BLOCK, cols] * factors[b : b + 1, :]
+                for b in range(blocks)
+            ],
+            axis=0,
+        )
+        total[...] += jnp.dot(kept, turned[cols, :], preferred_element_type=jnp.float32)
+        return 0
+
+    lax.fori_loop(0, turned.shape[0] // chunk, one, 0)
     store_terms(total, own, outs)
 
 
@@ -193,13 +203,21 @@
     for part in parts:
         code = part[rows:, :].astype(jnp.int32).astype(jnp.float32)
         scales.append(jnp.exp2(code * (1.0 / STEPS)) * (1.0 / CODE))
-    for b in range(rows // BLOCK):
-        at = slice(b * BLOCK, (b + 1) * BLOCK)
+
+    of_code = lax.broadcasted_iota(jnp.int32, scales[0].shape, 0)
+
+    def one(b, _):
+        at = pl.ds(pl.multiple_of(b * BLOCK, BLOCK), BLOCK)
         total = own[at, :]
         for part, scale in zip(parts, scales, strict=True):
             got = part[at, :].astype(jnp.int32).astype(jnp.float32)
-            total = total + got * scale[b : b + 1, :]
+            total = total + got * jnp.sum(
+                jnp.where(of_code == b, scale, 0.0), axis=0, keepdims=True
+            )
         out[:, at] = total.T.astype(out.dtype)
+        return 0
+
+    lax.fori_loop(0, rows // BLOCK, one, 0)
 
 
 def in_vmem():
@@ -330,19 +348,24 @@
         cost_estimate=cost(all_tokens * hidden, 4 * all_tokens * hidden),
         name="turn",
     )(*acts)
+    first = [j for j in reach if abs(j) == 1]
     last = [j for j in reach if abs(j) > 2]
-    acts_turned, *ready = lax.optimization_barrier((acts_turned, *(held[j] for j in last)))
+    acts_turned, *ready = lax.optimization_barrier(
+        (acts_turned, *(send_core(held[j]) for j in first), *(held[j] for j in last))
+    )
+    across = dict(zip(first, ready[: len(first)], strict=True))
+    ready = ready[len(first) :]
     held.update(zip(last, ready, strict=True))
     shards = []
     for j in reach:
-        shards += [held[j], send_core(held[j])]
+        shards += [held[j], across[j] if j in across else send_core(held[j])]
 
     n_shards = len(shards)
     code_rows = -(-(piece // BLOCK) // 16) * 16
     sent_shape = jax.ShapeDtypeStruct((piece + code_rows, tokens), jnp.int16)
     own_shape = jax.ShapeDtypeStruct((piece, tokens), jnp.float32)
     small_cost = cost(piece * width, piece * width // 8)
-    n_ahead = piece_blocks - early if n_pieces > 1 else 1
+    n_ahead = piece_blocks if n_pieces > 1 else 1
     full, turned, own, ahead, *coded = pl.pallas_call(
         functools.partial(
             first_terms_kernel,
@@ -376,18 +399,14 @@
     if n_pieces > 1:
         own, *coded = pl.pallas_call(
             functools.partial(more_terms_kernel, n_parts, piece_blocks, chunk),
-            in_specs=[in_vmem(), in_vmem(), in_hbm(), in_vmem()],
+            in_specs=[in_vmem()] * 3,
             out_specs=[in_vmem()] * (1 + n_parts),
             out_shape=[own_shape] + [sent_shape] * n_parts,
-            scratch_shapes=[
-                pltpu.VMEM((early * BLOCK, width), bf16),
-                pltpu.VMEM((piece, all_tokens), jnp.float32),
-                pltpu.SemaphoreType.DMA((early,)),
-            ],
+            scratch_shapes=[pltpu.VMEM((piece, all_tokens), jnp.float32)],
             compiler_params=params(),
             cost_estimate=small_cost,
             name="more_terms",
-        )(turned, ahead, weight, spread)
+        )(turned, ahead, spread)
         owns.append(own)
         parts += [send_row(coded[k], k + 1) for k in range(n_parts)]
 

time: 46 us -> 45.2 us (0.983)
  Pallas kernels: 23.6 us -> 22.9 us
    pallas_call x1, Pallas kernels: 5.62 us -> 3.64 us  [per_device(): pl.pallas_call(functools.partial(more_terms_kernel, n_parts, piece_blocks...]
    pallas_call x2, Pallas kernels: 1.69 us -> 2.97 us  [per_device(): pl.pallas_call(functools.partial(finish_kernel, n_parts), grid=(1,), in_s...]
  transfers between devices with their start and end apart: 18 -> 18, of which waited for: 8 -> 8; matrix products, arithmetic and copies ran while one was open for 0% -> 0% of each run, Pallas kernels for 40% -> 37%
where the time goes in v8:
time: 45.2 us; the launch traced here: 45.1 us
  Pallas kernels  22.9 us (51%)
  starting transfers between devices  16.1 us (36%)
  waiting for transfers between devices  5.22 us (12%)
  between operations  0.74 us (2%)
    ppermute x7, starting transfers between devices, send_ring(): return lax.ppermute(x, 'col', perm)  9.42 us
    pallas_call x1, Pallas kernels, per_device(): pl.pallas_call(functools.partial(weight_grad_kernel, chunk), in_specs=[in...  6.43 us
    ppermute x3, starting transfers between devices, send_row(): lax.ppermute(x, 'row', [(r, (r + by) % n_rows) for r in range(n_rows)])  5.19 us
    pallas_call x1, Pallas kernels, per_device(): pl.pallas_call(functools.partial(first_terms_kernel, n_shards, len(kepts)...  4.73 us
    ppermute x7, waiting for transfers between devices, send_ring(): return lax.ppermute(x, 'col', perm)  4.19 us
    pallas_call x1, Pallas kernels, per_device(): pl.pallas_call(functools.partial(more_terms_kernel, n_parts, piece_blocks...  3.64 us
    pallas_call x2, Pallas kernels, per_device(): pl.pallas_call(functools.partial(finish_kernel, n_parts), grid=(1,), in_s...  2.97 us
    pallas_call x1, Pallas kernels, per_device(): pl.pallas_call(spread_and_keep_kernel, in_specs=[in_smem(), in_hbm(), in_...  2.53 us
  transfers between devices with their start and end apart: 18, of which 8 were waited for; matrix products, arithmetic and copies ran while one was open for 0% of the time, Pallas kernels for 37%

profile of v8, /device:TPU:0, one launch (start us, length us, event | category | flops | bytes accessed | tf_op | source)
XLA Modules:
  0.0 45.1 jit_solution(10818920406168407693)
XLA Ops:
  0.6 3.0 %collective-permute-start.1 = (bf16[128,1792]{1,0:T(8,128)(2,1)}, bf16[128,1792]{1,0:T(8,128)(2,1)S(1)}, u32[]{:S(2)}, u32[]{:S(2)}) collective-permute-start(bf16[128,1792]{1,0:T(8,128)(2,1)} %refs_0_.1), channel_id=1, source_target_pairs={{0,16},{16,0},{1,17},{17,1},{2,18},{18,2},{3,19},{19,3},{4,20},{20... | collective-permute-start | bytes 1376264 | tf_op jit(solution)/shard_map/ppermute | solution.py:271
  3.7 2.5 %collective-permute-start.6 = (bf16[16,4096]{1,0:T(8,128)(2,1)}, bf16[16,4096]{1,0:T(8,128)(2,1)S(1)}, u32[]{:S(2)}, u32[]{:S(2)}) collective-permute-start(bf16[16,4096]{1,0:T(8,128)(2,1)} %refs_0_.2), channel_id=1, source_target_pairs={{2,10},{3,5},{6,14},{7,1},{10,12},{11,3},{14,8},{15,7},{12,4},{13,... | collective-permute-start | bytes 393224 | tf_op jit(solution)/shard_map/ppermute | solution.py:265
  6.2 0.4 collective-permute-start.7
  6.6 0.1 pad_add_fusion.place
  6.7 0.0 copy-start.1
  6.7 2.5 %spread_and_keep.1 = (bf16[384,4096]{1,0:T(8,128)(2,1)S(1)}, f32[14,4096]{1,0:T(8,128)S(1)}) custom-call(s32[2]{0:T(128)S(1)} %pad_add_fusion.place, bf16[1792,4096]{1,0:T(8,128)(2,1)} %refs_18_.1, s32[14,64]{1,0:T(8,128)} %mask.1), custom_call_target="tpu_custom_call" | custom-call | flops 1572864 | bytes 3145728 | tf_op jit(solution)/shard_map/spread_and_keep/pallas_call | solution.py:292
  9.2 0.0 copy-done.1
  9.2 0.0 copy-start
  9.2 0.0 copy-start.2
  9.2 1.6 %collective-permute-start.3 = (bf16[16,4096]{1,0:T(8,128)(2,1)S(1)}, bf16[16,4096]{1,0:T(8,128)(2,1)S(1)}, u32[]{:S(2)}, u32[]{:S(2)}) collective-permute-start(bf16[16,4096]{1,0:T(8,128)(2,1)S(1)} %copy-done.1), channel_id=1, source_target_pairs={{2,0},{3,7},{6,2},{7,11},{10,6},{11,15},{14,10},{15,13},{12,14},{1... | collective-permute-start | bytes 393224 | tf_op jit(solution)/shard_map/ppermute | solution.py:265
  10.9 0.4 collective-permute-start.2
  11.3 2.3 %keep.1.refs_17_ = bf16[512,4096]{1,0:T(8,128)(2,1)S(1)} custom-call(f32[14,4096]{1,0:T(8,128)S(1)} %get-tuple-element.32.spread, bf16[1792,4096]{1,0:T(8,128)(2,1)} %refs_18_.1), custom_call_target="tpu_custom_call" | custom-call | flops 2097152 | bytes 4194304 | tf_op jit(solution)/shard_map/keep/pallas_call | solution.py:322
  13.6 0.0 collective-permute-done.6.refs_6_
  13.6 0.2 collective-permute-done.7.refs_8_
  13.8 1.5 %collective-permute-start.9 = (bf16[16,4096]{1,0:T(8,128)(2,1)S(1)}, bf16[16,4096]{1,0:T(8,128)(2,1)S(1)}, u32[]{:S(2)}, u32[]{:S(2)}) collective-permute-start(bf16[16,4096]{1,0:T(8,128)(2,1)S(1)} %collective-permute-done.7.refs_8_), channel_id=1, source_target_pairs={{2,0},{3,7},{6,2},{7,11},{10,6},{11,15},{14,10},{15,13},{12,14},{1... | collective-permute-start | bytes 393224 | tf_op jit(solution)/shard_map/ppermute | solution.py:265
  15.3 1.6 %collective-permute-start.10 = (bf16[16,4096]{1,0:T(8,128)(2,1)S(1)}, bf16[16,4096]{1,0:T(8,128)(2,1)S(1)}, u32[]{:S(2)}, u32[]{:S(2)}) collective-permute-start(bf16[16,4096]{1,0:T(8,128)(2,1)S(1)} %collective-permute-done.6.refs_6_), channel_id=1, source_target_pairs={{2,10},{3,5},{6,14},{7,1},{10,12},{11,3},{14,8},{15,7},{12,4},{13,... | collective-permute-start | bytes 393224 | tf_op jit(solution)/shard_map/ppermute | solution.py:265
  16.9 0.0 collective-permute-done.3.refs_4_
  16.9 1.3 %collective-permute-start.8 = (bf16[16,4096]{1,0:T(8,128)(2,1)S(1)}, bf16[16,4096]{1,0:T(8,128)(2,1)S(1)}, u32[]{:S(2)}, u32[]{:S(2)}) collective-permute-start(bf16[16,4096]{1,0:T(8,128)(2,1)S(1)} %collective-permute-done.6.refs_6_), channel_id=1, source_target_pairs={{2,6},{3,1},{6,10},{7,3},{10,14},{11,7},{14,12},{15,11},{12,8},{13... | collective-permute-start | bytes 393224 | tf_op jit(solution)/shard_map/ppermute | solution.py:265
  18.2 0.0 collective-permute-done.2.refs_2_
  18.2 0.0 collective-permute-done.1.refs_1_
  18.2 0.0 collective-permute-start.4
  18.2 0.5 %collective-permute-start.5 = (bf16[16,4096]{1,0:T(8,128)(2,1)S(1)}, bf16[16,4096]{1,0:T(8,128)(2,1)S(1)}, u32[]{:S(2)}, u32[]{:S(2)}) collective-permute-start(bf16[16,4096]{1,0:T(8,128)(2,1)S(1)} %collective-permute-done.3.refs_4_), channel_id=1, source_target_pairs={{0,1},{1,0},{2,3},{3,2},{4,5},{5,4},{6,7},{7,6},{8,9},{9,8},{10,11... | collective-permute-start | bytes 393224 | tf_op jit(solution)/shard_map/ppermute | solution.py:268
  18.7 0.4 collective-permute-done.9.refs_12_
  19.2 0.0 collective-permute-start
  19.2 0.0 copy-done
  19.2 0.3 turn.1.refs_19_.acts
  19.5 3.2 %collective-permute-done.10.refs_14_ = bf16[16,4096]{1,0:T(8,128)(2,1)S(1)} collective-permute-done((bf16[16,4096]{1,0:T(8,128)(2,1)S(1)}, bf16[16,4096]{1,0:T(8,128)(2,1)S(1)}, u32[]{:S(2)}, u32[]{:S(2)}) %collective-permute-start.10) | collective-permute-done | bytes 131104 | tf_op jit(solution)/shard_map/ppermute | solution.py:265
  22.7 0.0 collective-permute-start.12
  22.7 0.4 collective-permute-done.8.refs_10_
  23.1 0.2 collective-permute-start.11
  23.2 0.0 collective-permute-done.4.refs_3_
  23.2 0.0 collective-permute-done.5.refs_5_
  23.2 0.4 collective-permute-start.13
  23.6 0.2 collective-permute-start.14
  23.7 0.0 collective-permute-done.refs_1_
  23.7 0.4 collective-permute-start.15
  24.1 0.0 collective-permute-done.12.refs_9_
  24.1 0.3 collective-permute-done.11.refs_7_
  24.4 0.2 collective-permute-done.13.refs_11_
  24.6 0.3 collective-permute-done.14.refs_13_
  24.9 0.2 collective-permute-done.15.refs_15_
  25.1 0.0 copy-done.2
  25.1 4.7 %first_terms.1 = (bf16[256,4096]{1,0:T(8,128)(2,1)S(1)}, bf16[4096,256]{1,0:T(8,128)(2,1)S(1)}, f32[896,128]{1,0:T(8,128)S(1)}, bf16[896,4096]{1,0:T(8,128)(2,1)S(1)}, s16[912,128]{1,0:T(8,128)(2,1)S(1)}) custom-call(s32[2]{0:T(128)S(1)} %pad_add_fusion.place, s32[16,16]{1,0:T(8,128)S(1)} %copy-done.2, bf16[16,4096]{1,0:T(8,128)(2,1)S(1)} %copy-done.1, ...), custom_call_target="tpu_custom_call" | custom-call | flops 3670016 | bytes 458752 | tf_op jit(solution)/shard_map/first_terms/pallas_call | solution.py:369
  29.8 0.6 %collective-permute-start.17 = (s16[912,128]{1,0:T(8,128)(2,1)S(1)}, s16[912,128]{1,0:T(8,128)(2,1)S(1)}, u32[]{:S(2)}, u32[]{:S(2)}) collective-permute-start(s16[912,128]{1,0:T(8,128)(2,1)S(1)} %get-tuple-element.48), channel_id=1, source_target_pairs={{0,16},{16,0},{1,17},{17,1},{2,18},{18,2},{3,19},{19,3},{4,20},{20... | collective-permute-start | bytes 700424 | tf_op jit(solution)/shard_map/ppermute | solution.py:271
  30.4 3.6 %more_terms.1 = (f32[896,128]{1,0:T(8,128)S(1)}, s16[912,128]{1,0:T(8,128)(2,1)S(1)}) custom-call(bf16[4096,256]{1,0:T(8,128)(2,1)S(1)} %get-tuple-element.43.turned, bf16[896,4096]{1,0:T(8,128)(2,1)S(1)} %get-tuple-element.44.ahead, f32[14,4096]{1,0:T(8,128)S(1)} %get-tuple-element.32.spread), custom_call_target="tpu_custom_call" | custom-call | flops 3670016 | bytes 458752 | tf_op jit(solution)/shard_map/more_terms/pallas_call | solution.py:400
  34.1 1.6 %collective-permute-start.16 = (s16[912,128]{1,0:T(8,128)(2,1)S(1)}, s16[912,128]{1,0:T(8,128)(2,1)S(1)}, u32[]{:S(2)}, u32[]{:S(2)}) collective-permute-start(s16[912,128]{1,0:T(8,128)(2,1)S(1)} %get-tuple-element.46), channel_id=1, source_target_pairs={{0,16},{16,0},{1,17},{17,1},{2,18},{18,2},{3,19},{19,3},{4,20},{20... | collective-permute-start | bytes 700424 | tf_op jit(solution)/shard_map/ppermute | solution.py:271
  35.7 6.4 %weight_grad.1 = bf16[1792,4096]{1,0:T(8,128)(2,1)} custom-call(bf16[1792,256]{1,0:T(8,128)(2,1)S(1)} %turn.1.refs_19_.acts, bf16[256,4096]{1,0:T(8,128)(2,1)S(1)} %get-tuple-element.49.full, f32[14,4096]{1,0:T(8,128)S(1)} %get-tuple-element.32.spread), custom_call_target="tpu_custom_call" | custom-call | flops 3670016 | bytes 458752 | tf_op jit(solution)/shard_map/weight_grad/pallas_call | solution.py:413
  42.1 0.0 collective-permute-done.17.refs_0_
  42.1 1.5 %add_terms.2.refs_1_ = bf16[128,1792]{1,0:T(8,128)(2,1)} custom-call(f32[896,128]{1,0:T(8,128)S(1)} %get-tuple-element.47.own, s16[912,128]{1,0:T(8,128)(2,1)S(1)} %collective-permute-done.17.refs_0_), custom_call_target="tpu_custom_call" | custom-call | tf_op jit(solution)/shard_map/add_terms/pallas_call | solution.py:434
  43.6 0.0 collective-permute-done.16.refs_0_
  43.6 1.5 %add_terms.3 = bf16[128,1792]{1,0:T(8,128)(2,1)} custom-call(f32[896,128]{1,0:T(8,128)S(1)} %get-tuple-element.45.own, s16[912,128]{1,0:T(8,128)(2,1)S(1)} %collective-permute-done.16.refs_0_, bf16[128,1792]{1,0:T(8,128)(2,1)} %add_terms.2.refs_1_), custom_call_target="tpu_custom_call", output_to_operand_aliasing={{}: (2, {})} | custom-call | tf_op jit(solution)/shard_map/add_terms/pallas_call | solution.py:434
Async XLA Ops:
  0.6 17.6 %collective-permute-start.1 = (bf16[128,1792]{1,0:T(8,128)(2,1)}, bf16[128,1792]{1,0:T(8,128)(2,1)S(1)}, u32[]{:S(2)}, u32[]{:S(2)}) collective-permute-start(bf16[128,1792]{1,0:T(8,128)(2,1)} %refs_0_.1), channel_id=1, source_target_pairs={{0,16},{16,0},{1,17},{17,1},{2,18},{18,2},{3,19},{19,3},{4,20},{20... | collective-permute-start | bytes 1376264 | tf_op jit(solution)/shard_map/ppermute | solution.py:271
  3.7 10.0 %collective-permute-start.6 = (bf16[16,4096]{1,0:T(8,128)(2,1)}, bf16[16,4096]{1,0:T(8,128)(2,1)S(1)}, u32[]{:S(2)}, u32[]{:S(2)}) collective-permute-start(bf16[16,4096]{1,0:T(8,128)(2,1)} %refs_0_.2), channel_id=1, source_target_pairs={{2,10},{3,5},{6,14},{7,1},{10,12},{11,3},{14,8},{15,7},{12,4},{13,... | collective-permute-start | bytes 393224 | tf_op jit(solution)/shard_map/ppermute | solution.py:265
  6.2 7.6 %collective-permute-start.7 = (bf16[16,4096]{1,0:T(8,128)(2,1)}, bf16[16,4096]{1,0:T(8,128)(2,1)S(1)}, u32[]{:S(2)}, u32[]{:S(2)}) collective-permute-start(bf16[16,4096]{1,0:T(8,128)(2,1)} %refs_0_.2), channel_id=1, source_target_pairs={{2,4},{3,11},{6,0},{7,15},{10,2},{11,13},{14,6},{15,9},{12,10},{13... | collective-permute-start | bytes 393224 | tf_op jit(solution)/shard_map/ppermute | solution.py:265
  6.7 2.5 %copy-start.1 = (bf16[16,4096]{1,0:T(8,128)(2,1)S(1)}, bf16[16,4096]{1,0:T(8,128)(2,1)}, u32[]{:S(2)}) copy-start(bf16[16,4096]{1,0:T(8,128)(2,1)} %refs_0_.2) | copy-start | bytes 393220
  9.2 9.9 %copy-start = (bf16[128,1792]{1,0:T(8,128)(2,1)S(1)}, bf16[128,1792]{1,0:T(8,128)(2,1)}, u32[]{:S(2)}) copy-start(bf16[128,1792]{1,0:T(8,128)(2,1)} %refs_0_.1) | copy-start | bytes 1376260
  9.2 15.9 %copy-start.2 = (s32[16,16]{1,0:T(8,128)S(1)}, s32[16,16]{1,0:T(8,128)}, u32[]{:S(2)}) copy-start(s32[16,16]{1,0:T(8,128)} %constant.11.clone.table) | copy-start | bytes 3076
  9.2 7.7 %collective-permute-start.3 = (bf16[16,4096]{1,0:T(8,128)(2,1)S(1)}, bf16[16,4096]{1,0:T(8,128)(2,1)S(1)}, u32[]{:S(2)}, u32[]{:S(2)}) collective-permute-start(bf16[16,4096]{1,0:T(8,128)(2,1)S(1)} %copy-done.1), channel_id=1, source_target_pairs={{2,0},{3,7},{6,2},{7,11},{10,6},{11,15},{14,10},{15,13},{12,14},{1... | collective-permute-start | bytes 393224 | tf_op jit(solution)/shard_map/ppermute | solution.py:265
  10.9 7.4 %collective-permute-start.2 = (bf16[16,4096]{1,0:T(8,128)(2,1)S(1)}, bf16[16,4096]{1,0:T(8,128)(2,1)S(1)}, u32[]{:S(2)}, u32[]{:S(2)}) collective-permute-start(bf16[16,4096]{1,0:T(8,128)(2,1)S(1)} %copy-done.1), channel_id=1, source_target_pairs={{2,6},{3,1},{6,10},{7,3},{10,14},{11,7},{14,12},{15,11},{12,8},{13... | collective-permute-start | bytes 393224 | tf_op jit(solution)/shard_map/ppermute | solution.py:265
  13.8 5.3 %collective-permute-start.9 = (bf16[16,4096]{1,0:T(8,128)(2,1)S(1)}, bf16[16,4096]{1,0:T(8,128)(2,1)S(1)}, u32[]{:S(2)}, u32[]{:S(2)}) collective-permute-start(bf16[16,4096]{1,0:T(8,128)(2,1)S(1)} %collective-permute-done.7.refs_8_), channel_id=1, source_target_pairs={{2,0},{3,7},{6,2},{7,11},{10,6},{11,15},{14,10},{15,13},{12,14},{1... | collective-permute-start | bytes 393224 | tf_op jit(solution)/shard_map/ppermute | solution.py:265
  15.3 7.4 %collective-permute-start.10 = (bf16[16,4096]{1,0:T(8,128)(2,1)S(1)}, bf16[16,4096]{1,0:T(8,128)(2,1)S(1)}, u32[]{:S(2)}, u32[]{:S(2)}) collective-permute-start(bf16[16,4096]{1,0:T(8,128)(2,1)S(1)} %collective-permute-done.6.refs_6_), channel_id=1, source_target_pairs={{2,10},{3,5},{6,14},{7,1},{10,12},{11,3},{14,8},{15,7},{12,4},{13,... | collective-permute-start | bytes 393224 | tf_op jit(solution)/shard_map/ppermute | solution.py:265
  16.9 6.1 %collective-permute-start.8 = (bf16[16,4096]{1,0:T(8,128)(2,1)S(1)}, bf16[16,4096]{1,0:T(8,128)(2,1)S(1)}, u32[]{:S(2)}, u32[]{:S(2)}) collective-permute-start(bf16[16,4096]{1,0:T(8,128)(2,1)S(1)} %collective-permute-done.6.refs_6_), channel_id=1, source_target_pairs={{2,6},{3,1},{6,10},{7,3},{10,14},{11,7},{14,12},{15,11},{12,8},{13... | collective-permute-start | bytes 393224 | tf_op jit(solution)/shard_map/ppermute | solution.py:265
  18.2 5.0 %collective-permute-start.4 = (bf16[16,4096]{1,0:T(8,128)(2,1)S(1)}, bf16[16,4096]{1,0:T(8,128)(2,1)S(1)}, u32[]{:S(2)}, u32[]{:S(2)}) collective-permute-start(bf16[16,4096]{1,0:T(8,128)(2,1)S(1)} %collective-permute-done.2.refs_2_), channel_id=1, source_target_pairs={{0,1},{1,0},{2,3},{3,2},{4,5},{5,4},{6,7},{7,6},{8,9},{9,8},{10,11... | collective-permute-start | bytes 393224 | tf_op jit(solution)/shard_map/ppermute | solution.py:268
  18.2 5.0 %collective-permute-start.5 = (bf16[16,4096]{1,0:T(8,128)(2,1)S(1)}, bf16[16,4096]{1,0:T(8,128)(2,1)S(1)}, u32[]{:S(2)}, u32[]{:S(2)}) collective-permute-start(bf16[16,4096]{1,0:T(8,128)(2,1)S(1)} %collective-permute-done.3.refs_4_), channel_id=1, source_target_pairs={{0,1},{1,0},{2,3},{3,2},{4,5},{5,4},{6,7},{7,6},{8,9},{9,8},{10,11... | collective-permute-start | bytes 393224 | tf_op jit(solution)/shard_map/ppermute | solution.py:268
  19.2 4.6 %collective-permute-start = (bf16[16,4096]{1,0:T(8,128)(2,1)S(1)}, bf16[16,4096]{1,0:T(8,128)(2,1)S(1)}, u32[]{:S(2)}, u32[]{:S(2)}) collective-permute-start(bf16[16,4096]{1,0:T(8,128)(2,1)S(1)} %copy-done.1), channel_id=1, source_target_pairs={{0,1},{1,0},{2,3},{3,2},{4,5},{5,4},{6,7},{7,6},{8,9},{9,8},{10,11... | collective-permute-start | bytes 393224 | tf_op jit(solution)/shard_map/ppermute | solution.py:268
  22.7 1.4 %collective-permute-start.12 = (bf16[16,4096]{1,0:T(8,128)(2,1)S(1)}, bf16[16,4096]{1,0:T(8,128)(2,1)S(1)}, u32[]{:S(2)}, u32[]{:S(2)}) collective-permute-start(bf16[16,4096]{1,0:T(8,128)(2,1)S(1)} %collective-permute-done.7.refs_8_), channel_id=1, source_target_pairs={{0,1},{1,0},{2,3},{3,2},{4,5},{5,4},{6,7},{7,6},{8,9},{9,8},{10,11... | collective-permute-start | bytes 393224 | tf_op jit(solution)/shard_map/ppermute | solution.py:268
  23.1 1.3 %collective-permute-start.11 = (bf16[16,4096]{1,0:T(8,128)(2,1)S(1)}, bf16[16,4096]{1,0:T(8,128)(2,1)S(1)}, u32[]{:S(2)}, u32[]{:S(2)}) collective-permute-start(bf16[16,4096]{1,0:T(8,128)(2,1)S(1)} %collective-permute-done.6.refs_6_), channel_id=1, source_target_pairs={{0,1},{1,0},{2,3},{3,2},{4,5},{5,4},{6,7},{7,6},{8,9},{9,8},{10,11... | collective-permute-start | bytes 393224 | tf_op jit(solution)/shard_map/ppermute | solution.py:268
  23.2 1.4 %collective-permute-start.13 = (bf16[16,4096]{1,0:T(8,128)(2,1)S(1)}, bf16[16,4096]{1,0:T(8,128)(2,1)S(1)}, u32[]{:S(2)}, u32[]{:S(2)}) collective-permute-start(bf16[16,4096]{1,0:T(8,128)(2,1)S(1)} %collective-permute-done.8.refs_10_), channel_id=1, source_target_pairs={{0,1},{1,0},{2,3},{3,2},{4,5},{5,4},{6,7},{7,6},{8,9},{9,8},{10,11... | collective-permute-start | bytes 393224 | tf_op jit(solution)/shard_map/ppermute | solution.py:268
  23.6 1.3 %collective-permute-start.14 = (bf16[16,4096]{1,0:T(8,128)(2,1)S(1)}, bf16[16,4096]{1,0:T(8,128)(2,1)S(1)}, u32[]{:S(2)}, u32[]{:S(2)}) collective-permute-start(bf16[16,4096]{1,0:T(8,128)(2,1)S(1)} %collective-permute-done.9.refs_12_), channel_id=1, source_target_pairs={{0,1},{1,0},{2,3},{3,2},{4,5},{5,4},{6,7},{7,6},{8,9},{9,8},{10,11... | collective-permute-start | bytes 393224 | tf_op jit(solution)/shard_map/ppermute | solution.py:268
  23.7 1.4 %collective-permute-start.15 = (bf16[16,4096]{1,0:T(8,128)(2,1)S(1)}, bf16[16,4096]{1,0:T(8,128)(2,1)S(1)}, u32[]{:S(2)}, u32[]{:S(2)}) collective-permute-start(bf16[16,4096]{1,0:T(8,128)(2,1)S(1)} %collective-permute-done.10.refs_14_), channel_id=1, source_target_pairs={{0,1},{1,0},{2,3},{3,2},{4,5},{5,4},{6,7},{7,6},{8,9},{9,8},{10,11... | collective-permute-start | bytes 393224 | tf_op jit(solution)/shard_map/ppermute | solution.py:268
  29.8 12.3 %collective-permute-start.17 = (s16[912,128]{1,0:T(8,128)(2,1)S(1)}, s16[912,128]{1,0:T(8,128)(2,1)S(1)}, u32[]{:S(2)}, u32[]{:S(2)}) collective-permute-start(s16[912,128]{1,0:T(8,128)(2,1)S(1)} %get-tuple-element.48), channel_id=1, source_target_pairs={{0,16},{16,0},{1,17},{17,1},{2,18},{18,2},{3,19},{19,3},{4,20},{20... | collective-permute-start | bytes 700424 | tf_op jit(solution)/shard_map/ppermute | solution.py:271
  34.1 9.5 %collective-permute-start.16 = (s16[912,128]{1,0:T(8,128)(2,1)S(1)}, s16[912,128]{1,0:T(8,128)(2,1)S(1)}, u32[]{:S(2)}, u32[]{:S(2)}) collective-permute-start(s16[912,128]{1,0:T(8,128)(2,1)S(1)} %get-tuple-element.46), channel_id=1, source_target_pairs={{0,16},{16,0},{1,17},{17,1},{2,18},{18,2},{3,19},{19,3},{4,20},{20... | collective-permute-start | bytes 700424 | tf_op jit(solution)/shard_map/ppermute | solution.py:271

commit v9 on v8

--- a/solution.py
+++ b/solution.py
@@ -88,13 +88,17 @@
     lax.fori_loop(0, kept.shape[0] // BLOCK, one, 0)
 
 
-def turn_kernel(n_rows, *refs):
-    acts, out = refs[:n_rows], refs[n_rows]
+def turn_kernel(n_rows, first, *refs):
+    acts, (weight, out, *rest) = refs[:n_rows], refs[n_rows:]
+    if rest:
+        fetch(weight, first, *rest)
     tokens, hidden = acts[0].shape
     for k in range(n_rows):
         place = (n_rows - k) % n_rows
         for c in range(0, hidden, BLOCK):
             out[c : c + BLOCK, place * tokens : (place + 1) * tokens] = acts[k][:, c : c + BLOCK].T
+    if rest:
+        fetched(weight, first, *rest)
 
 
 def store_terms(total, own, outs):
@@ -102,70 +106,47 @@
     own[...] = total[:, :tokens]
     for k, out in enumerate(outs):
         of_code = lax.broadcasted_iota(jnp.int32, (out.shape[0] - rows, tokens), 0)
-
-        def one(b, codes, k=k, out=out, of_code=of_code):
-            at = pl.ds(pl.multiple_of(b * BLOCK, BLOCK), BLOCK)
+        codes = jnp.zeros(of_code.shape, jnp.int32)
+        for b in range(rows // BLOCK):
+            at = slice(b * BLOCK, (b + 1) * BLOCK)
             whole, code = encode(total[at, (k + 1) * tokens : (k + 2) * tokens])
             out[at, :] = whole.astype(jnp.int16)
-            return jnp.where(of_code == b, code, codes)
-
-        codes = lax.fori_loop(0, rows // BLOCK, one, jnp.zeros(of_code.shape, jnp.int32))
+            codes = jnp.where(of_code == b, code, codes)
         out[rows:, :] = codes.astype(jnp.int16)
 
 
-def first_terms_kernel(n_shards, n_kept, n_parts, shift, chunk, first, place, table, *refs):
+def first_terms_kernel(n_shards, n_kept, n_parts, shift, chunk, place, table, *refs):
     shards, kepts = refs[:n_shards], refs[n_shards : n_shards + n_kept]
-    weight, _, full, turned, own, ahead, *outs, total, sems = refs[n_shards + n_kept :]
-    fetch(weight, first, ahead, sems)
+    full, turned, own, *outs, total = refs[n_shards + n_kept :]
     rows = shards[0].shape[0]
     n_cols = table.shape[0]
     for n, shard in enumerate(shards):
         to = lax.rem(table[place[1], n] + n_cols - place[0] * shift, n_cols)
         full[pl.ds(pl.multiple_of(to * rows, rows), rows), :] = shard[...]
-    n_chunks = full.shape[1] // chunk
-
-    def columns(c):
-        return pl.ds(pl.multiple_of(c * chunk, chunk), chunk)
-
-    turned[:chunk, :] = full[:, :chunk].T
-    total[...] = jnp.zeros_like(total)
-
-    def one(c, _):
-        cols, after = columns(c), columns(lax.rem(c + 1, n_chunks))
+    for c in range(0, full.shape[1], chunk):
+        cols = slice(c, c + chunk)
+        turned[cols, :] = full[:, cols].T
         at = 0
         for kept in kepts:
             to = slice(at, at + kept.shape[0])
-            total[to, :] += jnp.dot(
-                kept[:, cols], turned[cols, :], preferred_element_type=jnp.float32
-            )
+            terms = jnp.dot(kept[:, cols], turned[cols, :], preferred_element_type=jnp.float32)
+            total[to, :] = terms if c == 0 else total[to, :] + terms
             at += kept.shape[0]
-        turned[after, :] = full[:, after].T
-        return 0
-
-    lax.fori_loop(0, n_chunks, one, 0)
     store_terms(total, own, outs)
-    fetched(weight, first, ahead, sems)
-
-
-def more_terms_kernel(n_parts, first, chunk, turned, ahead, spread, own, *refs):
+
+
+def more_terms_kernel(n_parts, first, chunk, turned, weight, spread, own, *refs):
     outs, (total,) = refs[:n_parts], refs[n_parts:]
     blocks = own.shape[0] // BLOCK
-    total[...] = jnp.zeros_like(total)
-
-    def one(c, _):
-        cols = pl.ds(pl.multiple_of(c * chunk, chunk), chunk)
+    for c in range(0, weight.shape[1], chunk):
+        cols = slice(c, c + chunk)
         factors = spread[first : first + blocks, cols].astype(jnp.bfloat16)
         kept = jnp.concatenate(
-            [
-                ahead[b * BLOCK : (b + 1) * BLOCK, cols] * factors[b : b + 1, :]
-                for b in range(blocks)
-            ],
+            [weight[b * BLOCK : (b + 1) * BLOCK, cols] * factors[b : b + 1, :] for b in range(blocks)],
             axis=0,
         )
-        total[...] += jnp.dot(kept, turned[cols, :], preferred_element_type=jnp.float32)
-        return 0
-
-    lax.fori_loop(0, turned.shape[0] // chunk, one, 0)
+        terms = jnp.dot(kept, turned[cols, :], preferred_element_type=jnp.float32)
+        total[...] = terms if c == 0 else total[...] + terms
     store_terms(total, own, outs)
 
 
@@ -173,27 +154,22 @@
     hidden, width = out.shape
     blocks = hidden // BLOCK
     pair = 2 if blocks % 2 == 0 else 1
-
-    def leave(block):
-        at = pl.ds(pl.multiple_of(block * BLOCK, BLOCK), BLOCK)
-        return pltpu.make_async_copy(held.at[at, :], out.at[at, :], sems.at[block])
-
-    def rows(step, _):
-        first = step * pair
-        left = acts[pl.ds(pl.multiple_of(first * BLOCK, pair * BLOCK), pair * BLOCK), :]
+    copies = []
+    for first in range(0, blocks, pair):
+        left = acts[first * BLOCK : (first + pair) * BLOCK, :]
         for c in range(0, width, chunk):
             cols = slice(c, c + chunk)
             product = jnp.dot(left, full[:, cols], preferred_element_type=jnp.float32)
             for b in range(pair):
-                at = pl.ds(pl.multiple_of((first + b) * BLOCK, BLOCK), BLOCK)
-                part = product[b * BLOCK : (b + 1) * BLOCK, :] * spread[pl.ds(first + b, 1), cols]
-                held[at, cols] = part.astype(out.dtype)
-        for b in range(pair):
-            leave(first + b).start()
-        return 0
-
-    lax.fori_loop(0, blocks // pair, rows, 0)
-    lax.fori_loop(0, blocks, lambda block, _: (leave(block).wait(), 0)[1], 0)
+                part = product[b * BLOCK : (b + 1) * BLOCK, :].astype(out.dtype)
+                factor = spread[first + b : first + b + 1, cols].astype(out.dtype)
+                held[(first + b) * BLOCK : (first + b + 1) * BLOCK, cols] = part * factor
+        for b in range(first, first + pair):
+            at = pl.ds(b * BLOCK, BLOCK)
+            copies.append(pltpu.make_async_copy(held.at[at, :], out.at[at, :], sems.at[b]))
+            copies[-1].start()
+    for copy in copies:
+        copy.wait()
 
 
 def finish_kernel(n_parts, own, *refs):
@@ -203,21 +179,13 @@
     for part in parts:
         code = part[rows:, :].astype(jnp.int32).astype(jnp.float32)
         scales.append(jnp.exp2(code * (1.0 / STEPS)) * (1.0 / CODE))
-
-    of_code = lax.broadcasted_iota(jnp.int32, scales[0].shape, 0)
-
-    def one(b, _):
-        at = pl.ds(pl.multiple_of(b * BLOCK, BLOCK), BLOCK)
+    for b in range(rows // BLOCK):
+        at = slice(b * BLOCK, (b + 1) * BLOCK)
         total = own[at, :]
         for part, scale in zip(parts, scales, strict=True):
             got = part[at, :].astype(jnp.int32).astype(jnp.float32)
-            total = total + got * jnp.sum(
-                jnp.where(of_code == b, scale, 0.0), axis=0, keepdims=True
-            )
+            total = total + got * scale[b : b + 1, :]
         out[:, at] = total.T.astype(out.dtype)
-        return 0
-
-    lax.fori_loop(0, rows // BLOCK, one, 0)
 
 
 def in_vmem():
@@ -339,15 +307,18 @@
             held[-j] = send_ring(held[by - j], -by)
 
     *acts, held[1], held[-1] = lax.optimization_barrier((*acts, held[1], held[-1]))
-    acts_turned = pl.pallas_call(
-        functools.partial(turn_kernel, n_rows),
-        in_specs=[in_vmem()] * n_rows,
-        out_specs=in_vmem(),
-        out_shape=jax.ShapeDtypeStruct((hidden, all_tokens), bf16),
+    later = n_pieces - 1
+    acts_turned, *rest = pl.pallas_call(
+        functools.partial(turn_kernel, n_rows, piece_blocks),
+        in_specs=[in_vmem()] * n_rows + [in_hbm()],
+        out_specs=[in_vmem()] * (1 + later),
+        out_shape=[jax.ShapeDtypeStruct((hidden, all_tokens), bf16)]
+        + [pltpu.VMEM((piece, width), bf16)] * later,
+        scratch_shapes=[pltpu.SemaphoreType.DMA((piece_blocks,))] * later,
         compiler_params=params(),
         cost_estimate=cost(all_tokens * hidden, 4 * all_tokens * hidden),
         name="turn",
-    )(*acts)
+    )(*acts, weight)
     first = [j for j in reach if abs(j) == 1]
     last = [j for j in reach if abs(j) > 2]
     acts_turned, *ready = lax.optimization_barrier(
@@ -365,34 +336,23 @@
     sent_shape = jax.ShapeDtypeStruct((piece + code_rows, tokens), jnp.int16)
     own_shape = jax.ShapeDtypeStruct((piece, tokens), jnp.float32)
     small_cost = cost(piece * width, piece * width // 8)
-    n_ahead = piece_blocks if n_pieces > 1 else 1
-    full, turned, own, ahead, *coded = pl.pallas_call(
+    full, turned, own, *coded = pl.pallas_call(
         functools.partial(
-            first_terms_kernel,
-            n_shards,
-            len(kepts),
-            n_parts,
-            tokens // shard_rows,
-            chunk,
-            (n_pieces - 1) * piece_blocks,
+            first_terms_kernel, n_shards, len(kepts), n_parts, tokens // shard_rows, chunk
         ),
-        in_specs=[in_smem()] * 2 + [in_vmem()] * (n_shards + len(kepts)) + [in_hbm()] * 2,
-        out_specs=[in_vmem()] * (4 + n_parts),
+        in_specs=[in_smem()] * 2 + [in_vmem()] * (n_shards + len(kepts)),
+        out_specs=[in_vmem()] * (3 + n_parts),
         out_shape=[
             jax.ShapeDtypeStruct((all_tokens, width), bf16),
             jax.ShapeDtypeStruct((width, all_tokens), bf16),
             own_shape,
-            pltpu.VMEM((n_ahead * BLOCK, width), bf16),
         ]
         + [sent_shape] * n_parts,
-        scratch_shapes=[
-            pltpu.VMEM((piece, all_tokens), jnp.float32),
-            pltpu.SemaphoreType.DMA((n_ahead,)),
-        ],
+        scratch_shapes=[pltpu.VMEM((piece, all_tokens), jnp.float32)],
         compiler_params=params(),
         cost_estimate=small_cost,
         name="first_terms",
-    )(place, jnp.array(table, jnp.int32), *shards, *kepts, weight, acts_turned)
+    )(place, jnp.array(table, jnp.int32), *shards, *kepts)
     owns = [own]
     parts = [send_row(coded[k], k + 1) for k in range(n_parts)]
 
@@ -406,7 +366,7 @@
             compiler_params=params(),
             cost_estimate=small_cost,
             name="more_terms",
-        )(turned, ahead, spread)
+        )(turned, rest[0], spread)
         owns.append(own)
         parts += [send_row(coded[k], k + 1) for k in range(n_parts)]
 

time: 45.2 us -> 43 us (0.951)
  the two profiles are of different devices: /device:TPU:0 before, /device:TPU:2 now
where the time goes in v9:
time: 43 us; the launch traced here: 42.8 us
  Pallas kernels  20.9 us (49%)
  starting transfers between devices  15.2 us (35%)
  waiting for transfers between devices  5.86 us (14%)
  between operations  0.74 us (2%)
    ppermute x7, starting transfers between devices, send_ring(): return lax.ppermute(x, 'col', perm)  9.37 us
    pallas_call x1, Pallas kernels, per_device(): pl.pallas_call(functools.partial(weight_grad_kernel, chunk), in_specs=[in...  6.04 us
    ppermute x3, starting transfers between devices, send_row(): lax.ppermute(x, 'row', [(r, (r + by) % n_rows) for r in range(n_rows)])  3.74 us
    pallas_call x1, Pallas kernels, per_device(): pl.pallas_call(functools.partial(turn_kernel, n_rows, piece_blocks), in_s...  3.17 us
    pallas_call x1, Pallas kernels, per_device(): pl.pallas_call(functools.partial(first_terms_kernel, n_shards, len(kepts)...  3.07 us
    ppermute x7, waiting for transfers between devices, send_ring(): return lax.ppermute(x, 'col', perm)  3.02 us
    pallas_call x1, Pallas kernels, per_device(): pl.pallas_call(spread_and_keep_kernel, in_specs=[in_smem(), in_hbm(), in_...  2.53 us
    pallas_call x1, Pallas kernels, per_device(): pl.pallas_call(functools.partial(keep_kernel, early), in_specs=[in_vmem()...  2.29 us
  transfers between devices with their start and end apart: 18, of which 7 were waited for; matrix products, arithmetic and copies ran while one was open for 0% of the time, Pallas kernels for 40%

profile of v9, /device:TPU:2, one launch (start us, length us, event | category | flops | bytes accessed | tf_op | source)
XLA Modules:
  0.0 42.8 jit_solution(15326898654398867733)
XLA Ops:
  0.6 1.6 %collective-permute-start.1 = (bf16[128,1792]{1,0:T(8,128)(2,1)}, bf16[128,1792]{1,0:T(8,128)(2,1)S(1)}, u32[]{:S(2)}, u32[]{:S(2)}) collective-permute-start(bf16[128,1792]{1,0:T(8,128)(2,1)} %refs_0_.1), channel_id=1, source_target_pairs={{0,16},{16,0},{1,17},{17,1},{2,18},{18,2},{3,19},{19,3},{4,20},{20... | collective-permute-start | bytes 1376264 | tf_op jit(solution)/shard_map/ppermute | solution.py:239
  2.2 2.6 %collective-permute-start.6 = (bf16[16,4096]{1,0:T(8,128)(2,1)}, bf16[16,4096]{1,0:T(8,128)(2,1)S(1)}, u32[]{:S(2)}, u32[]{:S(2)}) collective-permute-start(bf16[16,4096]{1,0:T(8,128)(2,1)} %refs_0_.2), channel_id=1, source_target_pairs={{2,10},{3,5},{6,14},{7,1},{10,12},{11,3},{14,8},{15,7},{12,4},{13,... | collective-permute-start | bytes 393224 | tf_op jit(solution)/shard_map/ppermute | solution.py:233
  4.8 0.3 collective-permute-start.7
  5.1 0.1 pad_add_fusion.place
  5.2 0.0 copy-start.1
  5.2 2.5 %spread_and_keep.1 = (bf16[384,4096]{1,0:T(8,128)(2,1)S(1)}, f32[14,4096]{1,0:T(8,128)S(1)}) custom-call(s32[2]{0:T(128)S(1)} %pad_add_fusion.place, bf16[1792,4096]{1,0:T(8,128)(2,1)} %weight.3, s32[14,64]{1,0:T(8,128)} %mask.1), custom_call_target="tpu_custom_call" | custom-call | flops 1572864 | bytes 3145728 | tf_op jit(solution)/shard_map/spread_and_keep/pallas_call | solution.py:260
  7.8 0.0 copy-done.1
  7.8 0.0 copy-start
  7.8 0.6 %collective-permute-start.3 = (bf16[16,4096]{1,0:T(8,128)(2,1)S(1)}, bf16[16,4096]{1,0:T(8,128)(2,1)S(1)}, u32[]{:S(2)}, u32[]{:S(2)}) collective-permute-start(bf16[16,4096]{1,0:T(8,128)(2,1)S(1)} %copy-done.1), channel_id=1, source_target_pairs={{2,0},{3,7},{6,2},{7,11},{10,6},{11,15},{14,10},{15,13},{12,14},{1... | collective-permute-start | bytes 393224 | tf_op jit(solution)/shard_map/ppermute | solution.py:233
  8.4 1.5 %collective-permute-start.2 = (bf16[16,4096]{1,0:T(8,128)(2,1)S(1)}, bf16[16,4096]{1,0:T(8,128)(2,1)S(1)}, u32[]{:S(2)}, u32[]{:S(2)}) collective-permute-start(bf16[16,4096]{1,0:T(8,128)(2,1)S(1)} %copy-done.1), channel_id=1, source_target_pairs={{2,6},{3,1},{6,10},{7,3},{10,14},{11,7},{14,12},{15,11},{12,8},{13... | collective-permute-start | bytes 393224 | tf_op jit(solution)/shard_map/ppermute | solution.py:233
  9.9 2.3 %keep.1.refs_17_ = bf16[512,4096]{1,0:T(8,128)(2,1)S(1)} custom-call(f32[14,4096]{1,0:T(8,128)S(1)} %get-tuple-element.34.spread, bf16[1792,4096]{1,0:T(8,128)(2,1)} %weight.3), custom_call_target="tpu_custom_call" | custom-call | flops 2097152 | bytes 4194304 | tf_op jit(solution)/shard_map/keep/pallas_call | solution.py:290
  12.2 0.0 copy-start.2
  12.2 0.3 collective-permute-done.6.refs_6_
  12.5 0.0 collective-permute-done.7.refs_8_
  12.5 0.4 collective-permute-start.9
  12.9 2.4 %collective-permute-start.10 = (bf16[16,4096]{1,0:T(8,128)(2,1)S(1)}, bf16[16,4096]{1,0:T(8,128)(2,1)S(1)}, u32[]{:S(2)}, u32[]{:S(2)}) collective-permute-start(bf16[16,4096]{1,0:T(8,128)(2,1)S(1)} %collective-permute-done.6.refs_6_), channel_id=1, source_target_pairs={{2,10},{3,5},{6,14},{7,1},{10,12},{11,3},{14,8},{15,7},{12,4},{13,... | collective-permute-start | bytes 393224 | tf_op jit(solution)/shard_map/ppermute | solution.py:233
  15.3 0.0 collective-permute-done.3.refs_4_
  15.3 1.6 %collective-permute-start.8 = (bf16[16,4096]{1,0:T(8,128)(2,1)S(1)}, bf16[16,4096]{1,0:T(8,128)(2,1)S(1)}, u32[]{:S(2)}, u32[]{:S(2)}) collective-permute-start(bf16[16,4096]{1,0:T(8,128)(2,1)S(1)} %collective-permute-done.6.refs_6_), channel_id=1, source_target_pairs={{2,6},{3,1},{6,10},{7,3},{10,14},{11,7},{14,12},{15,11},{12,8},{13... | collective-permute-start | bytes 393224 | tf_op jit(solution)/shard_map/ppermute | solution.py:233
  16.9 0.0 collective-permute-done.2.refs_2_
  16.9 0.0 collective-permute-done.1.refs_1_
  16.9 0.0 collective-permute-start.4
  16.9 0.5 %collective-permute-start.5 = (bf16[16,4096]{1,0:T(8,128)(2,1)S(1)}, bf16[16,4096]{1,0:T(8,128)(2,1)S(1)}, u32[]{:S(2)}, u32[]{:S(2)}) collective-permute-start(bf16[16,4096]{1,0:T(8,128)(2,1)S(1)} %collective-permute-done.3.refs_4_), channel_id=1, source_target_pairs={{0,1},{1,0},{2,3},{3,2},{4,5},{5,4},{6,7},{7,6},{8,9},{9,8},{10,11... | collective-permute-start | bytes 393224 | tf_op jit(solution)/shard_map/ppermute | solution.py:236
  17.4 2.7 %collective-permute-done.9.refs_12_ = bf16[16,4096]{1,0:T(8,128)(2,1)S(1)} collective-permute-done((bf16[16,4096]{1,0:T(8,128)(2,1)S(1)}, bf16[16,4096]{1,0:T(8,128)(2,1)S(1)}, u32[]{:S(2)}, u32[]{:S(2)}) %collective-permute-start.9) | collective-permute-done | bytes 131104 | tf_op jit(solution)/shard_map/ppermute | solution.py:233
  20.1 0.0 collective-permute-start
  20.1 0.0 copy-done
  20.1 3.2 %turn.1 = (bf16[1792,256]{1,0:T(8,128)(2,1)S(1)}, bf16[896,4096]{1,0:T(8,128)(2,1)S(1)}) custom-call(bf16[128,1792]{1,0:T(8,128)(2,1)S(1)} %copy-done, bf16[128,1792]{1,0:T(8,128)(2,1)S(1)} %collective-permute-done.1.refs_1_, bf16[1792,4096]{1,0:T(8,128)(2,1)} %weight.3), custom_call_target="tpu_custom_call" | custom-call | flops 458752 | bytes 1835008 | tf_op jit(solution)/shard_map/turn/pallas_call | solution.py:311
  23.3 0.0 collective-permute-done.10.refs_14_
  23.3 0.6 %collective-permute-start.12 = (bf16[16,4096]{1,0:T(8,128)(2,1)S(1)}, bf16[16,4096]{1,0:T(8,128)(2,1)S(1)}, u32[]{:S(2)}, u32[]{:S(2)}) collective-permute-start(bf16[16,4096]{1,0:T(8,128)(2,1)S(1)} %collective-permute-done.7.refs_8_), channel_id=1, source_target_pairs={{0,1},{1,0},{2,3},{3,2},{4,5},{5,4},{6,7},{7,6},{8,9},{9,8},{10,11... | collective-permute-start | bytes 393224 | tf_op jit(solution)/shard_map/ppermute | solution.py:236
  23.8 0.0 collective-permute-done.8.refs_10_
  23.8 0.1 collective-permute-start.11
  23.9 0.0 collective-permute-done.4.refs_3_
  23.9 0.0 collective-permute-done.5.refs_5_
  23.9 0.4 collective-permute-start.13
  24.4 0.1 collective-permute-start.14
  24.5 0.0 collective-permute-done.refs_1_
  24.5 0.4 collective-permute-start.15
  24.9 0.0 collective-permute-done.12.refs_9_
  24.9 0.3 collective-permute-done.11.refs_7_
  25.2 0.2 collective-permute-done.13.refs_11_
  25.4 0.3 collective-permute-done.14.refs_13_
  25.7 0.2 collective-permute-done.15.refs_15_
  25.9 0.0 copy-done.2
  25.9 3.1 %first_terms.1 = (bf16[256,4096]{1,0:T(8,128)(2,1)S(1)}, bf16[4096,256]{1,0:T(8,128)(2,1)S(1)}, f32[896,128]{1,0:T(8,128)S(1)}, s16[912,128]{1,0:T(8,128)(2,1)S(1)}) custom-call(s32[2]{0:T(128)S(1)} %pad_add_fusion.place, s32[16,16]{1,0:T(8,128)S(1)} %copy-done.2, bf16[16,4096]{1,0:T(8,128)(2,1)S(1)} %copy-done.1, ...), custom_call_target="tpu_custom_call" | custom-call | flops 3670016 | bytes 458752 | tf_op jit(solution)/shard_map/first_terms/pallas_call | solution.py:339
  29.0 0.4 %collective-permute-start.17 = (s16[912,128]{1,0:T(8,128)(2,1)S(1)}, s16[912,128]{1,0:T(8,128)(2,1)S(1)}, u32[]{:S(2)}, u32[]{:S(2)}) collective-permute-start(s16[912,128]{1,0:T(8,128)(2,1)S(1)} %get-tuple-element.49), channel_id=1, source_target_pairs={{0,16},{16,0},{1,17},{17,1},{2,18},{18,2},{3,19},{19,3},{4,20},{20... | collective-permute-start | bytes 700424 | tf_op jit(solution)/shard_map/ppermute | solution.py:239
  29.4 2.1 %more_terms.1 = (f32[896,128]{1,0:T(8,128)S(1)}, s16[912,128]{1,0:T(8,128)(2,1)S(1)}) custom-call(bf16[4096,256]{1,0:T(8,128)(2,1)S(1)} %get-tuple-element.44.turned, bf16[896,4096]{1,0:T(8,128)(2,1)S(1)} %get-tuple-element.45.weight, f32[14,4096]{1,0:T(8,128)S(1)} %get-tuple-element.34.spread), custom_call_target="tpu_custom_call" | custom-call | flops 3670016 | bytes 458752 | tf_op jit(solution)/shard_map/more_terms/pallas_call | solution.py:360
  31.6 1.7 %collective-permute-start.16 = (s16[912,128]{1,0:T(8,128)(2,1)S(1)}, s16[912,128]{1,0:T(8,128)(2,1)S(1)}, u32[]{:S(2)}, u32[]{:S(2)}) collective-permute-start(s16[912,128]{1,0:T(8,128)(2,1)S(1)} %get-tuple-element.47), channel_id=1, source_target_pairs={{0,16},{16,0},{1,17},{17,1},{2,18},{18,2},{3,19},{19,3},{4,20},{20... | collective-permute-start | bytes 700424 | tf_op jit(solution)/shard_map/ppermute | solution.py:239
  33.3 6.0 %weight_grad.1 = bf16[1792,4096]{1,0:T(8,128)(2,1)} custom-call(bf16[1792,256]{1,0:T(8,128)(2,1)S(1)} %get-tuple-element.50.acts, bf16[256,4096]{1,0:T(8,128)(2,1)S(1)} %get-tuple-element.51.full, f32[14,4096]{1,0:T(8,128)S(1)} %get-tuple-element.34.spread), custom_call_target="tpu_custom_call" | custom-call | flops 3670016 | bytes 458752 | tf_op jit(solution)/shard_map/weight_grad/pallas_call | solution.py:373
  39.3 0.0 collective-permute-done.17.refs_0_
  39.3 0.8 %add_terms.2.refs_1_ = bf16[128,1792]{1,0:T(8,128)(2,1)} custom-call(f32[896,128]{1,0:T(8,128)S(1)} %get-tuple-element.48.own, s16[912,128]{1,0:T(8,128)(2,1)S(1)} %collective-permute-done.17.refs_0_), custom_call_target="tpu_custom_call" | custom-call | tf_op jit(solution)/shard_map/add_terms/pallas_call | solution.py:394
  40.2 1.8 %collective-permute-done.16.refs_0_ = s16[912,128]{1,0:T(8,128)(2,1)S(1)} collective-permute-done((s16[912,128]{1,0:T(8,128)(2,1)S(1)}, s16[912,128]{1,0:T(8,128)(2,1)S(1)}, u32[]{:S(2)}, u32[]{:S(2)}) %collective-permute-start.16) | collective-permute-done | bytes 233504 | tf_op jit(solution)/shard_map/ppermute | solution.py:239
  42.0 0.8 %add_terms.3 = bf16[128,1792]{1,0:T(8,128)(2,1)} custom-call(f32[896,128]{1,0:T(8,128)S(1)} %get-tuple-element.46.own, s16[912,128]{1,0:T(8,128)(2,1)S(1)} %collective-permute-done.16.refs_0_, bf16[128,1792]{1,0:T(8,128)(2,1)} %add_terms.2.refs_1_), custom_call_target="tpu_custom_call", output_to_operand_aliasing={{}: (2, {})} | custom-call | tf_op jit(solution)/shard_map/add_terms/pallas_call | solution.py:394
Async XLA Ops:
  0.6 16.2 %collective-permute-start.1 = (bf16[128,1792]{1,0:T(8,128)(2,1)}, bf16[128,1792]{1,0:T(8,128)(2,1)S(1)}, u32[]{:S(2)}, u32[]{:S(2)}) collective-permute-start(bf16[128,1792]{1,0:T(8,128)(2,1)} %refs_0_.1), channel_id=1, source_target_pairs={{0,16},{16,0},{1,17},{17,1},{2,18},{18,2},{3,19},{19,3},{4,20},{20... | collective-permute-start | bytes 1376264 | tf_op jit(solution)/shard_map/ppermute | solution.py:239
  2.2 10.3 %collective-permute-start.6 = (bf16[16,4096]{1,0:T(8,128)(2,1)}, bf16[16,4096]{1,0:T(8,128)(2,1)S(1)}, u32[]{:S(2)}, u32[]{:S(2)}) collective-permute-start(bf16[16,4096]{1,0:T(8,128)(2,1)} %refs_0_.2), channel_id=1, source_target_pairs={{2,10},{3,5},{6,14},{7,1},{10,12},{11,3},{14,8},{15,7},{12,4},{13,... | collective-permute-start | bytes 393224 | tf_op jit(solution)/shard_map/ppermute | solution.py:233
  4.8 7.7 %collective-permute-start.7 = (bf16[16,4096]{1,0:T(8,128)(2,1)}, bf16[16,4096]{1,0:T(8,128)(2,1)S(1)}, u32[]{:S(2)}, u32[]{:S(2)}) collective-permute-start(bf16[16,4096]{1,0:T(8,128)(2,1)} %refs_0_.2), channel_id=1, source_target_pairs={{2,4},{3,11},{6,0},{7,15},{10,2},{11,13},{14,6},{15,9},{12,10},{13... | collective-permute-start | bytes 393224 | tf_op jit(solution)/shard_map/ppermute | solution.py:233
  5.2 2.5 %copy-start.1 = (bf16[16,4096]{1,0:T(8,128)(2,1)S(1)}, bf16[16,4096]{1,0:T(8,128)(2,1)}, u32[]{:S(2)}) copy-start(bf16[16,4096]{1,0:T(8,128)(2,1)} %refs_0_.2) | copy-start | bytes 393220
  7.8 12.3 %copy-start = (bf16[128,1792]{1,0:T(8,128)(2,1)S(1)}, bf16[128,1792]{1,0:T(8,128)(2,1)}, u32[]{:S(2)}) copy-start(bf16[128,1792]{1,0:T(8,128)(2,1)} %refs_0_.1) | copy-start | bytes 1376260
  7.8 7.5 %collective-permute-start.3 = (bf16[16,4096]{1,0:T(8,128)(2,1)S(1)}, bf16[16,4096]{1,0:T(8,128)(2,1)S(1)}, u32[]{:S(2)}, u32[]{:S(2)}) collective-permute-start(bf16[16,4096]{1,0:T(8,128)(2,1)S(1)} %copy-done.1), channel_id=1, source_target_pairs={{2,0},{3,7},{6,2},{7,11},{10,6},{11,15},{14,10},{15,13},{12,14},{1... | collective-permute-start | bytes 393224 | tf_op jit(solution)/shard_map/ppermute | solution.py:233
  8.4 8.5 %collective-permute-start.2 = (bf16[16,4096]{1,0:T(8,128)(2,1)S(1)}, bf16[16,4096]{1,0:T(8,128)(2,1)S(1)}, u32[]{:S(2)}, u32[]{:S(2)}) collective-permute-start(bf16[16,4096]{1,0:T(8,128)(2,1)S(1)} %copy-done.1), channel_id=1, source_target_pairs={{2,6},{3,1},{6,10},{7,3},{10,14},{11,7},{14,12},{15,11},{12,8},{13... | collective-permute-start | bytes 393224 | tf_op jit(solution)/shard_map/ppermute | solution.py:233
  12.2 13.7 %copy-start.2 = (s32[16,16]{1,0:T(8,128)S(1)}, s32[16,16]{1,0:T(8,128)}, u32[]{:S(2)}) copy-start(s32[16,16]{1,0:T(8,128)} %constant.11.clone.table) | copy-start | bytes 3076
  12.5 7.6 %collective-permute-start.9 = (bf16[16,4096]{1,0:T(8,128)(2,1)S(1)}, bf16[16,4096]{1,0:T(8,128)(2,1)S(1)}, u32[]{:S(2)}, u32[]{:S(2)}) collective-permute-start(bf16[16,4096]{1,0:T(8,128)(2,1)S(1)} %collective-permute-done.7.refs_8_), channel_id=1, source_target_pairs={{2,0},{3,7},{6,2},{7,11},{10,6},{11,15},{14,10},{15,13},{12,14},{1... | collective-permute-start | bytes 393224 | tf_op jit(solution)/shard_map/ppermute | solution.py:233
  12.9 10.4 %collective-permute-start.10 = (bf16[16,4096]{1,0:T(8,128)(2,1)S(1)}, bf16[16,4096]{1,0:T(8,128)(2,1)S(1)}, u32[]{:S(2)}, u32[]{:S(2)}) collective-permute-start(bf16[16,4096]{1,0:T(8,128)(2,1)S(1)} %collective-permute-done.6.refs_6_), channel_id=1, source_target_pairs={{2,10},{3,5},{6,14},{7,1},{10,12},{11,3},{14,8},{15,7},{12,4},{13,... | collective-permute-start | bytes 393224 | tf_op jit(solution)/shard_map/ppermute | solution.py:233
  15.3 8.6 %collective-permute-start.8 = (bf16[16,4096]{1,0:T(8,128)(2,1)S(1)}, bf16[16,4096]{1,0:T(8,128)(2,1)S(1)}, u32[]{:S(2)}, u32[]{:S(2)}) collective-permute-start(bf16[16,4096]{1,0:T(8,128)(2,1)S(1)} %collective-permute-done.6.refs_6_), channel_id=1, source_target_pairs={{2,6},{3,1},{6,10},{7,3},{10,14},{11,7},{14,12},{15,11},{12,8},{13... | collective-permute-start | bytes 393224 | tf_op jit(solution)/shard_map/ppermute | solution.py:233
  16.9 7.1 %collective-permute-start.4 = (bf16[16,4096]{1,0:T(8,128)(2,1)S(1)}, bf16[16,4096]{1,0:T(8,128)(2,1)S(1)}, u32[]{:S(2)}, u32[]{:S(2)}) collective-permute-start(bf16[16,4096]{1,0:T(8,128)(2,1)S(1)} %collective-permute-done.2.refs_2_), channel_id=1, source_target_pairs={{0,1},{1,0},{2,3},{3,2},{4,5},{5,4},{6,7},{7,6},{8,9},{9,8},{10,11... | collective-permute-start | bytes 393224 | tf_op jit(solution)/shard_map/ppermute | solution.py:236
  16.9 7.0 %collective-permute-start.5 = (bf16[16,4096]{1,0:T(8,128)(2,1)S(1)}, bf16[16,4096]{1,0:T(8,128)(2,1)S(1)}, u32[]{:S(2)}, u32[]{:S(2)}) collective-permute-start(bf16[16,4096]{1,0:T(8,128)(2,1)S(1)} %collective-permute-done.3.refs_4_), channel_id=1, source_target_pairs={{0,1},{1,0},{2,3},{3,2},{4,5},{5,4},{6,7},{7,6},{8,9},{9,8},{10,11... | collective-permute-start | bytes 393224 | tf_op jit(solution)/shard_map/ppermute | solution.py:236
  20.1 4.4 %collective-permute-start = (bf16[16,4096]{1,0:T(8,128)(2,1)S(1)}, bf16[16,4096]{1,0:T(8,128)(2,1)S(1)}, u32[]{:S(2)}, u32[]{:S(2)}) collective-permute-start(bf16[16,4096]{1,0:T(8,128)(2,1)S(1)} %copy-done.1), channel_id=1, source_target_pairs={{0,1},{1,0},{2,3},{3,2},{4,5},{5,4},{6,7},{7,6},{8,9},{9,8},{10,11... | collective-permute-start | bytes 393224 | tf_op jit(solution)/shard_map/ppermute | solution.py:236
  23.3 1.6 %collective-permute-start.12 = (bf16[16,4096]{1,0:T(8,128)(2,1)S(1)}, bf16[16,4096]{1,0:T(8,128)(2,1)S(1)}, u32[]{:S(2)}, u32[]{:S(2)}) collective-permute-start(bf16[16,4096]{1,0:T(8,128)(2,1)S(1)} %collective-permute-done.7.refs_8_), channel_id=1, source_target_pairs={{0,1},{1,0},{2,3},{3,2},{4,5},{5,4},{6,7},{7,6},{8,9},{9,8},{10,11... | collective-permute-start | bytes 393224 | tf_op jit(solution)/shard_map/ppermute | solution.py:236
  23.8 1.3 %collective-permute-start.11 = (bf16[16,4096]{1,0:T(8,128)(2,1)S(1)}, bf16[16,4096]{1,0:T(8,128)(2,1)S(1)}, u32[]{:S(2)}, u32[]{:S(2)}) collective-permute-start(bf16[16,4096]{1,0:T(8,128)(2,1)S(1)} %collective-permute-done.6.refs_6_), channel_id=1, source_target_pairs={{0,1},{1,0},{2,3},{3,2},{4,5},{5,4},{6,7},{7,6},{8,9},{9,8},{10,11... | collective-permute-start | bytes 393224 | tf_op jit(solution)/shard_map/ppermute | solution.py:236
  23.9 1.4 %collective-permute-start.13 = (bf16[16,4096]{1,0:T(8,128)(2,1)S(1)}, bf16[16,4096]{1,0:T(8,128)(2,1)S(1)}, u32[]{:S(2)}, u32[]{:S(2)}) collective-permute-start(bf16[16,4096]{1,0:T(8,128)(2,1)S(1)} %collective-permute-done.8.refs_10_), channel_id=1, source_target_pairs={{0,1},{1,0},{2,3},{3,2},{4,5},{5,4},{6,7},{7,6},{8,9},{9,8},{10,11... | collective-permute-start | bytes 393224 | tf_op jit(solution)/shard_map/ppermute | solution.py:236
  24.4 1.3 %collective-permute-start.14 = (bf16[16,4096]{1,0:T(8,128)(2,1)S(1)}, bf16[16,4096]{1,0:T(8,128)(2,1)S(1)}, u32[]{:S(2)}, u32[]{:S(2)}) collective-permute-start(bf16[16,4096]{1,0:T(8,128)(2,1)S(1)} %collective-permute-done.9.refs_12_), channel_id=1, source_target_pairs={{0,1},{1,0},{2,3},{3,2},{4,5},{5,4},{6,7},{7,6},{8,9},{9,8},{10,11... | collective-permute-start | bytes 393224 | tf_op jit(solution)/shard_map/ppermute | solution.py:236
  24.5 1.4 %collective-permute-start.15 = (bf16[16,4096]{1,0:T(8,128)(2,1)S(1)}, bf16[16,4096]{1,0:T(8,128)(2,1)S(1)}, u32[]{:S(2)}, u32[]{:S(2)}) collective-permute-start(bf16[16,4096]{1,0:T(8,128)(2,1)S(1)} %collective-permute-done.10.refs_14_), channel_id=1, source_target_pairs={{0,1},{1,0},{2,3},{3,2},{4,5},{5,4},{6,7},{7,6},{8,9},{9,8},{10,11... | collective-permute-start | bytes 393224 | tf_op jit(solution)/shard_map/ppermute | solution.py:236
  29.0 10.3 %collective-permute-start.17 = (s16[912,128]{1,0:T(8,128)(2,1)S(1)}, s16[912,128]{1,0:T(8,128)(2,1)S(1)}, u32[]{:S(2)}, u32[]{:S(2)}) collective-permute-start(s16[912,128]{1,0:T(8,128)(2,1)S(1)} %get-tuple-element.49), channel_id=1, source_target_pairs={{0,16},{16,0},{1,17},{17,1},{2,18},{18,2},{3,19},{19,3},{4,20},{20... | collective-permute-start | bytes 700424 | tf_op jit(solution)/shard_map/ppermute | solution.py:239
  31.6 10.4 %collective-permute-start.16 = (s16[912,128]{1,0:T(8,128)(2,1)S(1)}, s16[912,128]{1,0:T(8,128)(2,1)S(1)}, u32[]{:S(2)}, u32[]{:S(2)}) collective-permute-start(s16[912,128]{1,0:T(8,128)(2,1)S(1)} %get-tuple-element.47), channel_id=1, source_target_pairs={{0,16},{16,0},{1,17},{17,1},{2,18},{18,2},{3,19},{19,3},{4,20},{20... | collective-permute-start | bytes 700424 | tf_op jit(solution)/shard_map/ppermute | solution.py:239

commit v10 on v9

--- a/solution.py
+++ b/solution.py
@@ -150,30 +150,31 @@
     store_terms(total, own, outs)
 
 
-def weight_grad_kernel(chunk, acts, full, spread, out, held, sems):
-    hidden, width = out.shape
-    blocks = hidden // BLOCK
+def weight_grad_kernel(begin, chunk, acts, full, spread, *refs):
+    out, held, sems = refs[-3:]
+    blocks = held.shape[0] // BLOCK
     pair = 2 if blocks % 2 == 0 else 1
     copies = []
     for first in range(0, blocks, pair):
-        left = acts[first * BLOCK : (first + pair) * BLOCK, :]
-        for c in range(0, width, chunk):
+        left = acts[(begin + first) * BLOCK : (begin + first + pair) * BLOCK, :]
+        for c in range(0, held.shape[1], chunk):
             cols = slice(c, c + chunk)
             product = jnp.dot(left, full[:, cols], preferred_element_type=jnp.float32)
             for b in range(pair):
                 part = product[b * BLOCK : (b + 1) * BLOCK, :].astype(out.dtype)
-                factor = spread[first + b : first + b + 1, cols].astype(out.dtype)
+                block = begin + first + b
+                factor = spread[block : block + 1, cols].astype(out.dtype)
                 held[(first + b) * BLOCK : (first + b + 1) * BLOCK, cols] = part * factor
         for b in range(first, first + pair):
-            at = pl.ds(b * BLOCK, BLOCK)
-            copies.append(pltpu.make_async_copy(held.at[at, :], out.at[at, :], sems.at[b]))
+            here, there = pl.ds(b * BLOCK, BLOCK), pl.ds((begin + b) * BLOCK, BLOCK)
+            copies.append(pltpu.make_async_copy(held.at[here, :], out.at[there, :], sems.at[b]))
             copies[-1].start()
     for copy in copies:
         copy.wait()
 
 
-def finish_kernel(n_parts, own, *refs):
-    parts, out = refs[:n_parts], refs[-1]
+def finish_kernel(first, n_parts, own, *refs):
+    parts, (*_, out, held, sem) = refs[:n_parts], refs[n_parts:]
     rows = own.shape[0]
     scales = []
     for part in parts:
@@ -185,7 +186,10 @@
         for part, scale in zip(parts, scales, strict=True):
             got = part[at, :].astype(jnp.int32).astype(jnp.float32)
             total = total + got * scale[b : b + 1, :]
-        out[:, at] = total.T.astype(out.dtype)
+        held[:, at] = total.T.astype(out.dtype)
+    copy = pltpu.make_async_copy(held, out.at[:, pl.ds(first, rows)], sem)
+    copy.start()
+    copy.wait()
 
 
 def in_vmem():
@@ -212,8 +216,9 @@
     row, col = lax.axis_index("row"), lax.axis_index("col")
     hidden, width = weight.shape
     blocks = hidden // BLOCK
-    n_pieces = 2 if blocks % 2 == 0 else 1
-    piece = hidden // n_pieces
+    n_pieces = 2 if blocks > 7 else 1
+    sizes = [hidden] if n_pieces == 1 else [(blocks + 1) // 2 * BLOCK, blocks // 2 * BLOCK]
+    piece, rest_rows = sizes[0], sizes[-1]
     n_parts = n_rows - 1
     tokens = inputs.shape[0]
     shard_rows = grad_output.shape[0]
@@ -313,14 +318,14 @@
         in_specs=[in_vmem()] * n_rows + [in_hbm()],
         out_specs=[in_vmem()] * (1 + later),
         out_shape=[jax.ShapeDtypeStruct((hidden, all_tokens), bf16)]
-        + [pltpu.VMEM((piece, width), bf16)] * later,
-        scratch_shapes=[pltpu.SemaphoreType.DMA((piece_blocks,))] * later,
+        + [pltpu.VMEM((rest_rows, width), bf16)] * later,
+        scratch_shapes=[pltpu.SemaphoreType.DMA((rest_rows // BLOCK,))] * later,
         compiler_params=params(),
         cost_estimate=cost(all_tokens * hidden, 4 * all_tokens * hidden),
         name="turn",
     )(*acts, weight)
     first = [j for j in reach if abs(j) == 1]
-    last = [j for j in reach if abs(j) > 2]
+    last = [j for j in reach if abs(j) != 1]
     acts_turned, *ready = lax.optimization_barrier(
         (acts_turned, *(send_core(held[j]) for j in first), *(held[j] for j in last))
     )
@@ -332,9 +337,11 @@
         shards += [held[j], across[j] if j in across else send_core(held[j])]
 
     n_shards = len(shards)
-    code_rows = -(-(piece // BLOCK) // 16) * 16
-    sent_shape = jax.ShapeDtypeStruct((piece + code_rows, tokens), jnp.int16)
-    own_shape = jax.ShapeDtypeStruct((piece, tokens), jnp.float32)
+    def out_shapes(rows):
+        code_rows = -(-(rows // BLOCK) // 16) * 16
+        sent_shape = jax.ShapeDtypeStruct((rows + code_rows, tokens), jnp.int16)
+        return [jax.ShapeDtypeStruct((rows, tokens), jnp.float32)] + [sent_shape] * n_parts
+
     small_cost = cost(piece * width, piece * width // 8)
     full, turned, own, *coded = pl.pallas_call(
         functools.partial(
@@ -345,9 +352,8 @@
         out_shape=[
             jax.ShapeDtypeStruct((all_tokens, width), bf16),
             jax.ShapeDtypeStruct((width, all_tokens), bf16),
-            own_shape,
         ]
-        + [sent_shape] * n_parts,
+        + out_shapes(piece),
         scratch_shapes=[pltpu.VMEM((piece, all_tokens), jnp.float32)],
         compiler_params=params(),
         cost_estimate=small_cost,
@@ -361,8 +367,8 @@
             functools.partial(more_terms_kernel, n_parts, piece_blocks, chunk),
             in_specs=[in_vmem()] * 3,
             out_specs=[in_vmem()] * (1 + n_parts),
-            out_shape=[own_shape] + [sent_shape] * n_parts,
-            scratch_shapes=[pltpu.VMEM((piece, all_tokens), jnp.float32)],
+            out_shape=out_shapes(rest_rows),
+            scratch_shapes=[pltpu.VMEM((rest_rows, all_tokens), jnp.float32)],
             compiler_params=params(),
             cost_estimate=small_cost,
             name="more_terms",
@@ -370,37 +376,39 @@
         owns.append(own)
         parts += [send_row(coded[k], k + 1) for k in range(n_parts)]
 
-    grad_weight = pl.pallas_call(
-        functools.partial(weight_grad_kernel, chunk),
-        in_specs=[in_vmem()] * 3,
-        out_specs=in_hbm(),
-        out_shape=jax.ShapeDtypeStruct((hidden, width), bf16),
-        scratch_shapes=[
-            pltpu.VMEM((hidden, width), bf16),
-            pltpu.SemaphoreType.DMA((blocks,)),
-        ],
-        compiler_params=params(),
-        cost_estimate=small_cost,
-        name="weight_grad",
-    )(acts_turned, full, spread)
-
-    grad_input = None
-    for p in range(n_pieces):
-        operands = [owns[p], *parts[p * n_parts : (p + 1) * n_parts]]
-        specs = [in_vmem()] * len(operands)
-        if p:
-            operands.append(grad_input)
-            specs.append(in_hbm())
-        grad_input = pl.pallas_call(
-            functools.partial(finish_kernel, n_parts),
-            grid=(1,),
-            in_specs=specs,
-            out_specs=pl.BlockSpec((tokens, piece), lambda i, p=p: (0, p)),
+    def weight_grad(begin, count, so_far):
+        return pl.pallas_call(
+            functools.partial(weight_grad_kernel, begin, chunk),
+            in_specs=[in_vmem()] * 3 + [in_hbm()] * len(so_far),
+            out_specs=in_hbm(),
+            out_shape=jax.ShapeDtypeStruct((hidden, width), bf16),
+            scratch_shapes=[
+                pltpu.VMEM((count * BLOCK, width), bf16),
+                pltpu.SemaphoreType.DMA((count,)),
+            ],
+            input_output_aliases={3: 0} if so_far else {},
+            compiler_params=params(),
+            cost_estimate=small_cost,
+            name="weight_grad",
+        )(acts_turned, full, spread, *so_far)
+
+    def finish(p, so_far):
+        operands = [owns[p], *parts[p * n_parts : (p + 1) * n_parts], *so_far]
+        return pl.pallas_call(
+            functools.partial(finish_kernel, sum(sizes[:p]), n_parts),
+            in_specs=[in_vmem()] * (1 + n_parts) + [in_hbm()] * len(so_far),
+            out_specs=in_hbm(),
             out_shape=jax.ShapeDtypeStruct((tokens, hidden), bf16),
-            input_output_aliases={len(operands) - 1: 0} if p else {},
+            scratch_shapes=[pltpu.VMEM((tokens, sizes[p]), bf16), pltpu.SemaphoreType.DMA],
+            input_output_aliases={1 + n_parts: 0} if so_far else {},
             compiler_params=params(),
             name="add_terms",
         )(*operands)
+
+    grad_weight = weight_grad(0, blocks, ())
+    grad_input = finish(0, ())
+    for p in range(1, n_pieces):
+        grad_input = finish(p, (grad_input,))
     return (grad_input, grad_weight)
 
 

time: 43 us -> 43.5 us (1.012)
  the two profiles are of different devices: /device:TPU:2 before, /device:TPU:0 now
where the time goes in v10:
time: 43.5 us; the launch traced here: 43.4 us
  Pallas kernels  20.9 us (48%)
  starting transfers between devices  16.4 us (38%)
  waiting for transfers between devices  5.24 us (12%)
  between operations  0.76 us (2%)
    ppermute x7, starting transfers between devices, send_ring(): return lax.ppermute(x, 'col', perm)  9.41 us
    pallas_call x1, Pallas kernels, weight_grad(): pl.pallas_call(functools.partial(weight_grad_kernel, begin, chunk), in_sp...  6.04 us
    ppermute x3, starting transfers between devices, send_row(): lax.ppermute(x, 'row', [(r, (r + by) % n_rows) for r in range(n_rows)])  5.19 us
    pallas_call x1, Pallas kernels, per_device(): pl.pallas_call(functools.partial(turn_kernel, n_rows, piece_blocks), in_s...  3.16 us
    pallas_call x1, Pallas kernels, per_device(): pl.pallas_call(functools.partial(first_terms_kernel, n_shards, len(kepts)...  3.07 us
    pallas_call x1, Pallas kernels, per_device(): pl.pallas_call(spread_and_keep_kernel, in_specs=[in_smem(), in_hbm(), in_...  2.53 us
    pallas_call x1, Pallas kernels, per_device(): pl.pallas_call(functools.partial(keep_kernel, early), in_specs=[in_vmem()...  2.29 us
    ppermute x7, waiting for transfers between devices, send_ring(): return lax.ppermute(x, 'col', perm)  2.16 us
  transfers between devices with their start and end apart: 18, of which 9 were waited for; matrix products, arithmetic and copies ran while one was open for 0% of the time, Pallas kernels for 39%

profile of v10, /device:TPU:0, one launch (start us, length us, event | category | flops | bytes accessed | tf_op | source)
XLA Modules:
  0.0 43.4 jit_solution(1325586683214241152)
XLA Ops:
  0.6 3.0 %collective-permute-start = (bf16[128,1792]{1,0:T(8,128)(2,1)}, bf16[128,1792]{1,0:T(8,128)(2,1)S(1)}, u32[]{:S(2)}, u32[]{:S(2)}) collective-permute-start(bf16[128,1792]{1,0:T(8,128)(2,1)} %refs_0_), channel_id=1, source_target_pairs={{0,16},{16,0},{1,17},{17,1},{2,18},{18,2},{3,19},{19,3},{4,20},{20... | collective-permute-start | bytes 1376264 | tf_op jit(solution)/shard_map/ppermute | solution.py:244
  3.7 2.5 %collective-permute-start.5 = (bf16[16,4096]{1,0:T(8,128)(2,1)}, bf16[16,4096]{1,0:T(8,128)(2,1)S(1)}, u32[]{:S(2)}, u32[]{:S(2)}) collective-permute-start(bf16[16,4096]{1,0:T(8,128)(2,1)} %refs_0_.1), channel_id=1, source_target_pairs={{2,10},{3,5},{6,14},{7,1},{10,12},{11,3},{14,8},{15,7},{12,4},{13,... | collective-permute-start | bytes 393224 | tf_op jit(solution)/shard_map/ppermute | solution.py:238
  6.2 0.4 collective-permute-start.6
  6.6 0.1 pad_add_fusion.place
  6.7 0.0 copy-start.1
  6.7 2.5 %spread_and_keep.1 = (bf16[384,4096]{1,0:T(8,128)(2,1)S(1)}, f32[14,4096]{1,0:T(8,128)S(1)}) custom-call(s32[2]{0:T(128)S(1)} %pad_add_fusion.place, bf16[1792,4096]{1,0:T(8,128)(2,1)} %weight.3, s32[14,64]{1,0:T(8,128)} %mask.1), custom_call_target="tpu_custom_call" | custom-call | flops 1572864 | bytes 3145728 | tf_op jit(solution)/shard_map/spread_and_keep/pallas_call | solution.py:265
  9.2 0.0 copy-done.1
  9.2 0.0 copy-start
  9.2 1.6 %collective-permute-start.2 = (bf16[16,4096]{1,0:T(8,128)(2,1)S(1)}, bf16[16,4096]{1,0:T(8,128)(2,1)S(1)}, u32[]{:S(2)}, u32[]{:S(2)}) collective-permute-start(bf16[16,4096]{1,0:T(8,128)(2,1)S(1)} %copy-done.1), channel_id=1, source_target_pairs={{2,0},{3,7},{6,2},{7,11},{10,6},{11,15},{14,10},{15,13},{12,14},{1... | collective-permute-start | bytes 393224 | tf_op jit(solution)/shard_map/ppermute | solution.py:238
  10.9 0.4 %collective-permute-start.1 = (bf16[16,4096]{1,0:T(8,128)(2,1)S(1)}, bf16[16,4096]{1,0:T(8,128)(2,1)S(1)}, u32[]{:S(2)}, u32[]{:S(2)}) collective-permute-start(bf16[16,4096]{1,0:T(8,128)(2,1)S(1)} %copy-done.1), channel_id=1, source_target_pairs={{2,6},{3,1},{6,10},{7,3},{10,14},{11,7},{14,12},{15,11},{12,8},{13... | collective-permute-start | bytes 393224 | tf_op jit(solution)/shard_map/ppermute | solution.py:238
  11.3 2.3 %keep.1.refs_17_ = bf16[512,4096]{1,0:T(8,128)(2,1)S(1)} custom-call(f32[14,4096]{1,0:T(8,128)S(1)} %get-tuple-element.37.spread, bf16[1792,4096]{1,0:T(8,128)(2,1)} %weight.3), custom_call_target="tpu_custom_call" | custom-call | flops 2097152 | bytes 4194304 | tf_op jit(solution)/shard_map/keep/pallas_call | solution.py:295
  13.6 0.0 copy-start.2
  13.6 0.0 collective-permute-done.5.refs_6_
  13.6 0.2 collective-permute-done.6.refs_8_
  13.8 2.4 %collective-permute-start.9 = (bf16[16,4096]{1,0:T(8,128)(2,1)S(1)}, bf16[16,4096]{1,0:T(8,128)(2,1)S(1)}, u32[]{:S(2)}, u32[]{:S(2)}) collective-permute-start(bf16[16,4096]{1,0:T(8,128)(2,1)S(1)} %collective-permute-done.5.refs_6_), channel_id=1, source_target_pairs={{2,10},{3,5},{6,14},{7,1},{10,12},{11,3},{14,8},{15,7},{12,4},{13,... | collective-permute-start | bytes 393224 | tf_op jit(solution)/shard_map/ppermute | solution.py:238
  16.2 1.6 %collective-permute-start.7 = (bf16[16,4096]{1,0:T(8,128)(2,1)S(1)}, bf16[16,4096]{1,0:T(8,128)(2,1)S(1)}, u32[]{:S(2)}, u32[]{:S(2)}) collective-permute-start(bf16[16,4096]{1,0:T(8,128)(2,1)S(1)} %collective-permute-done.5.refs_6_), channel_id=1, source_target_pairs={{2,6},{3,1},{6,10},{7,3},{10,14},{11,7},{14,12},{15,11},{12,8},{13... | collective-permute-start | bytes 393224 | tf_op jit(solution)/shard_map/ppermute | solution.py:238
  17.8 0.0 collective-permute-done.2.refs_4_
  17.8 0.4 %collective-permute-start.8 = (bf16[16,4096]{1,0:T(8,128)(2,1)S(1)}, bf16[16,4096]{1,0:T(8,128)(2,1)S(1)}, u32[]{:S(2)}, u32[]{:S(2)}) collective-permute-start(bf16[16,4096]{1,0:T(8,128)(2,1)S(1)} %collective-permute-done.6.refs_8_), channel_id=1, source_target_pairs={{2,0},{3,7},{6,2},{7,11},{10,6},{11,15},{14,10},{15,13},{12,14},{1... | collective-permute-start | bytes 393224 | tf_op jit(solution)/shard_map/ppermute | solution.py:238
  18.2 0.0 collective-permute-done.1.refs_2_
  18.2 0.0 collective-permute-done.refs_1_
  18.2 0.0 collective-permute-start.3
  18.2 0.5 %collective-permute-start.4 = (bf16[16,4096]{1,0:T(8,128)(2,1)S(1)}, bf16[16,4096]{1,0:T(8,128)(2,1)S(1)}, u32[]{:S(2)}, u32[]{:S(2)}) collective-permute-start(bf16[16,4096]{1,0:T(8,128)(2,1)S(1)} %collective-permute-done.2.refs_4_), channel_id=1, source_target_pairs={{0,1},{1,0},{2,3},{3,2},{4,5},{5,4},{6,7},{7,6},{8,9},{9,8},{10,11... | collective-permute-start | bytes 393224 | tf_op jit(solution)/shard_map/ppermute | solution.py:241
  18.7 0.0 copy-done
  18.8 3.2 %turn.1 = (bf16[1792,256]{1,0:T(8,128)(2,1)S(1)}, bf16[896,4096]{1,0:T(8,128)(2,1)S(1)}) custom-call(bf16[128,1792]{1,0:T(8,128)(2,1)S(1)} %copy-done, bf16[128,1792]{1,0:T(8,128)(2,1)S(1)} %collective-permute-done.refs_1_, bf16[1792,4096]{1,0:T(8,128)(2,1)} %weight.3), custom_call_target="tpu_custom_call" | custom-call | flops 458752 | bytes 1835008 | tf_op jit(solution)/shard_map/turn/pallas_call | solution.py:316
  21.9 0.8 %collective-permute-done.8.refs_12_ = bf16[16,4096]{1,0:T(8,128)(2,1)S(1)} collective-permute-done((bf16[16,4096]{1,0:T(8,128)(2,1)S(1)}, bf16[16,4096]{1,0:T(8,128)(2,1)S(1)}, u32[]{:S(2)}, u32[]{:S(2)}) %collective-permute-start.8) | collective-permute-done | bytes 131104 | tf_op jit(solution)/shard_map/ppermute | solution.py:238
  22.7 0.0 collective-permute-done.9.refs_14_
  22.8 1.1 %collective-permute-done.7.refs_10_ = bf16[16,4096]{1,0:T(8,128)(2,1)S(1)} collective-permute-done((bf16[16,4096]{1,0:T(8,128)(2,1)S(1)}, bf16[16,4096]{1,0:T(8,128)(2,1)S(1)}, u32[]{:S(2)}, u32[]{:S(2)}) %collective-permute-start.7) | collective-permute-done | bytes 131104 | tf_op jit(solution)/shard_map/ppermute | solution.py:238
  23.9 0.0 collective-permute-done.3.refs_3_
  23.9 0.0 collective-permute-done.4.refs_5_
  23.9 0.0 collective-permute-start.10
  23.9 0.5 %collective-permute-start.11 = (bf16[16,4096]{1,0:T(8,128)(2,1)S(1)}, bf16[16,4096]{1,0:T(8,128)(2,1)S(1)}, u32[]{:S(2)}, u32[]{:S(2)}) collective-permute-start(bf16[16,4096]{1,0:T(8,128)(2,1)S(1)} %collective-permute-done.5.refs_6_), channel_id=1, source_target_pairs={{0,1},{1,0},{2,3},{3,2},{4,5},{5,4},{6,7},{7,6},{8,9},{9,8},{10,11... | collective-permute-start | bytes 393224 | tf_op jit(solution)/shard_map/ppermute | solution.py:241
  24.4 0.1 collective-permute-start.12
  24.5 0.4 %collective-permute-start.13 = (bf16[16,4096]{1,0:T(8,128)(2,1)S(1)}, bf16[16,4096]{1,0:T(8,128)(2,1)S(1)}, u32[]{:S(2)}, u32[]{:S(2)}) collective-permute-start(bf16[16,4096]{1,0:T(8,128)(2,1)S(1)} %collective-permute-done.7.refs_10_), channel_id=1, source_target_pairs={{0,1},{1,0},{2,3},{3,2},{4,5},{5,4},{6,7},{7,6},{8,9},{9,8},{10,11... | collective-permute-start | bytes 393224 | tf_op jit(solution)/shard_map/ppermute | solution.py:241
  24.9 0.1 collective-permute-start.14
  25.0 0.3 collective-permute-done.10.refs_1_
  25.3 0.2 collective-permute-start.15
  25.4 0.0 collective-permute-done.11.refs_7_
  25.4 0.3 collective-permute-done.12.refs_9_
  25.8 0.2 collective-permute-done.13.refs_11_
  26.0 0.3 collective-permute-done.14.refs_13_
  26.3 0.3 collective-permute-done.15.refs_15_
  26.6 0.0 copy-done.2
  26.6 3.1 %first_terms.1 = (bf16[256,4096]{1,0:T(8,128)(2,1)S(1)}, bf16[4096,256]{1,0:T(8,128)(2,1)S(1)}, f32[896,128]{1,0:T(8,128)S(1)}, s16[912,128]{1,0:T(8,128)(2,1)S(1)}) custom-call(s32[2]{0:T(128)S(1)} %pad_add_fusion.place, s32[16,16]{1,0:T(8,128)S(1)} %copy-done.2, bf16[16,4096]{1,0:T(8,128)(2,1)S(1)} %copy-done.1, ...), custom_call_target="tpu_custom_call" | custom-call | flops 3670016 | bytes 458752 | tf_op jit(solution)/shard_map/first_terms/pallas_call | solution.py:346
  29.7 0.6 %collective-permute-start.17 = (s16[912,128]{1,0:T(8,128)(2,1)S(1)}, s16[912,128]{1,0:T(8,128)(2,1)S(1)}, u32[]{:S(2)}, u32[]{:S(2)}) collective-permute-start(s16[912,128]{1,0:T(8,128)(2,1)S(1)} %get-tuple-element.55), channel_id=1, source_target_pairs={{0,16},{16,0},{1,17},{17,1},{2,18},{18,2},{3,19},{19,3},{4,20},{20... | collective-permute-start | bytes 700424 | tf_op jit(solution)/shard_map/ppermute | solution.py:244
  30.3 2.1 %more_terms.1 = (f32[896,128]{1,0:T(8,128)S(1)}, s16[912,128]{1,0:T(8,128)(2,1)S(1)}) custom-call(bf16[4096,256]{1,0:T(8,128)(2,1)S(1)} %get-tuple-element.50.turned, bf16[896,4096]{1,0:T(8,128)(2,1)S(1)} %get-tuple-element.51.weight, f32[14,4096]{1,0:T(8,128)S(1)} %get-tuple-element.37.spread), custom_call_target="tpu_custom_call" | custom-call | flops 3670016 | bytes 458752 | tf_op jit(solution)/shard_map/more_terms/pallas_call | solution.py:366
  32.4 1.6 %collective-permute-start.16 = (s16[912,128]{1,0:T(8,128)(2,1)S(1)}, s16[912,128]{1,0:T(8,128)(2,1)S(1)}, u32[]{:S(2)}, u32[]{:S(2)}) collective-permute-start(s16[912,128]{1,0:T(8,128)(2,1)S(1)} %get-tuple-element.53), channel_id=1, source_target_pairs={{0,16},{16,0},{1,17},{17,1},{2,18},{18,2},{3,19},{19,3},{4,20},{20... | collective-permute-start | bytes 700424 | tf_op jit(solution)/shard_map/ppermute | solution.py:244
  34.0 6.0 %weight_grad.1 = bf16[1792,4096]{1,0:T(8,128)(2,1)} custom-call(bf16[1792,256]{1,0:T(8,128)(2,1)S(1)} %get-tuple-element.56.acts, bf16[256,4096]{1,0:T(8,128)(2,1)S(1)} %get-tuple-element.57.full, f32[14,4096]{1,0:T(8,128)S(1)} %get-tuple-element.37.spread), custom_call_target="tpu_custom_call" | custom-call | flops 3670016 | bytes 458752 | tf_op jit(solution)/shard_map/weight_grad/pallas_call | solution.py:380
  40.0 0.0 collective-permute-done.17.refs_0_
  40.0 0.9 %add_terms.2.refs_1_ = bf16[128,1792]{1,0:T(8,128)(2,1)} custom-call(f32[896,128]{1,0:T(8,128)S(1)} %get-tuple-element.54.own, s16[912,128]{1,0:T(8,128)(2,1)S(1)} %collective-permute-done.17.refs_0_), custom_call_target="tpu_custom_call" | custom-call | tf_op jit(solution)/shard_map/add_terms/pallas_call | solution.py:397
  40.9 1.7 %collective-permute-done.16.refs_0_ = s16[912,128]{1,0:T(8,128)(2,1)S(1)} collective-permute-done((s16[912,128]{1,0:T(8,128)(2,1)S(1)}, s16[912,128]{1,0:T(8,128)(2,1)S(1)}, u32[]{:S(2)}, u32[]{:S(2)}) %collective-permute-start.16) | collective-permute-done | bytes 233504 | tf_op jit(solution)/shard_map/ppermute | solution.py:244
  42.5 0.8 %add_terms.3 = bf16[128,1792]{1,0:T(8,128)(2,1)} custom-call(f32[896,128]{1,0:T(8,128)S(1)} %get-tuple-element.52.own, s16[912,128]{1,0:T(8,128)(2,1)S(1)} %collective-permute-done.16.refs_0_, bf16[128,1792]{1,0:T(8,128)(2,1)} %add_terms.2.refs_1_), custom_call_target="tpu_custom_call", output_to_operand_aliasing={{}: (2, {})} | custom-call | tf_op jit(solution)/shard_map/add_terms/pallas_call | solution.py:397
Async XLA Ops:
  0.6 17.6 %collective-permute-start = (bf16[128,1792]{1,0:T(8,128)(2,1)}, bf16[128,1792]{1,0:T(8,128)(2,1)S(1)}, u32[]{:S(2)}, u32[]{:S(2)}) collective-permute-start(bf16[128,1792]{1,0:T(8,128)(2,1)} %refs_0_), channel_id=1, source_target_pairs={{0,16},{16,0},{1,17},{17,1},{2,18},{18,2},{3,19},{19,3},{4,20},{20... | collective-permute-start | bytes 1376264 | tf_op jit(solution)/shard_map/ppermute | solution.py:244
  3.7 10.0 %collective-permute-start.5 = (bf16[16,4096]{1,0:T(8,128)(2,1)}, bf16[16,4096]{1,0:T(8,128)(2,1)S(1)}, u32[]{:S(2)}, u32[]{:S(2)}) collective-permute-start(bf16[16,4096]{1,0:T(8,128)(2,1)} %refs_0_.1), channel_id=1, source_target_pairs={{2,10},{3,5},{6,14},{7,1},{10,12},{11,3},{14,8},{15,7},{12,4},{13,... | collective-permute-start | bytes 393224 | tf_op jit(solution)/shard_map/ppermute | solution.py:238
  6.2 7.6 %collective-permute-start.6 = (bf16[16,4096]{1,0:T(8,128)(2,1)}, bf16[16,4096]{1,0:T(8,128)(2,1)S(1)}, u32[]{:S(2)}, u32[]{:S(2)}) collective-permute-start(bf16[16,4096]{1,0:T(8,128)(2,1)} %refs_0_.1), channel_id=1, source_target_pairs={{2,4},{3,11},{6,0},{7,15},{10,2},{11,13},{14,6},{15,9},{12,10},{13... | collective-permute-start | bytes 393224 | tf_op jit(solution)/shard_map/ppermute | solution.py:238
  6.7 2.5 %copy-start.1 = (bf16[16,4096]{1,0:T(8,128)(2,1)S(1)}, bf16[16,4096]{1,0:T(8,128)(2,1)}, u32[]{:S(2)}) copy-start(bf16[16,4096]{1,0:T(8,128)(2,1)} %refs_0_.1) | copy-start | bytes 393220
  9.2 9.5 %copy-start = (bf16[128,1792]{1,0:T(8,128)(2,1)S(1)}, bf16[128,1792]{1,0:T(8,128)(2,1)}, u32[]{:S(2)}) copy-start(bf16[128,1792]{1,0:T(8,128)(2,1)} %refs_0_) | copy-start | bytes 1376260
  9.2 8.6 %collective-permute-start.2 = (bf16[16,4096]{1,0:T(8,128)(2,1)S(1)}, bf16[16,4096]{1,0:T(8,128)(2,1)S(1)}, u32[]{:S(2)}, u32[]{:S(2)}) collective-permute-start(bf16[16,4096]{1,0:T(8,128)(2,1)S(1)} %copy-done.1), channel_id=1, source_target_pairs={{2,0},{3,7},{6,2},{7,11},{10,6},{11,15},{14,10},{15,13},{12,14},{1... | collective-permute-start | bytes 393224 | tf_op jit(solution)/shard_map/ppermute | solution.py:238
  10.9 7.4 %collective-permute-start.1 = (bf16[16,4096]{1,0:T(8,128)(2,1)S(1)}, bf16[16,4096]{1,0:T(8,128)(2,1)S(1)}, u32[]{:S(2)}, u32[]{:S(2)}) collective-permute-start(bf16[16,4096]{1,0:T(8,128)(2,1)S(1)} %copy-done.1), channel_id=1, source_target_pairs={{2,6},{3,1},{6,10},{7,3},{10,14},{11,7},{14,12},{15,11},{12,8},{13... | collective-permute-start | bytes 393224 | tf_op jit(solution)/shard_map/ppermute | solution.py:238
  13.6 13.0 %copy-start.2 = (s32[16,16]{1,0:T(8,128)S(1)}, s32[16,16]{1,0:T(8,128)}, u32[]{:S(2)}) copy-start(s32[16,16]{1,0:T(8,128)} %constant.11.clone.table) | copy-start | bytes 3076
  13.8 8.9 %collective-permute-start.9 = (bf16[16,4096]{1,0:T(8,128)(2,1)S(1)}, bf16[16,4096]{1,0:T(8,128)(2,1)S(1)}, u32[]{:S(2)}, u32[]{:S(2)}) collective-permute-start(bf16[16,4096]{1,0:T(8,128)(2,1)S(1)} %collective-permute-done.5.refs_6_), channel_id=1, source_target_pairs={{2,10},{3,5},{6,14},{7,1},{10,12},{11,3},{14,8},{15,7},{12,4},{13,... | collective-permute-start | bytes 393224 | tf_op jit(solution)/shard_map/ppermute | solution.py:238
  16.2 7.7 %collective-permute-start.7 = (bf16[16,4096]{1,0:T(8,128)(2,1)S(1)}, bf16[16,4096]{1,0:T(8,128)(2,1)S(1)}, u32[]{:S(2)}, u32[]{:S(2)}) collective-permute-start(bf16[16,4096]{1,0:T(8,128)(2,1)S(1)} %collective-permute-done.5.refs_6_), channel_id=1, source_target_pairs={{2,6},{3,1},{6,10},{7,3},{10,14},{11,7},{14,12},{15,11},{12,8},{13... | collective-permute-start | bytes 393224 | tf_op jit(solution)/shard_map/ppermute | solution.py:238
  17.8 5.0 %collective-permute-start.8 = (bf16[16,4096]{1,0:T(8,128)(2,1)S(1)}, bf16[16,4096]{1,0:T(8,128)(2,1)S(1)}, u32[]{:S(2)}, u32[]{:S(2)}) collective-permute-start(bf16[16,4096]{1,0:T(8,128)(2,1)S(1)} %collective-permute-done.6.refs_8_), channel_id=1, source_target_pairs={{2,0},{3,7},{6,2},{7,11},{10,6},{11,15},{14,10},{15,13},{12,14},{1... | collective-permute-start | bytes 393224 | tf_op jit(solution)/shard_map/ppermute | solution.py:238
  18.2 5.7 %collective-permute-start.3 = (bf16[16,4096]{1,0:T(8,128)(2,1)S(1)}, bf16[16,4096]{1,0:T(8,128)(2,1)S(1)}, u32[]{:S(2)}, u32[]{:S(2)}) collective-permute-start(bf16[16,4096]{1,0:T(8,128)(2,1)S(1)} %collective-permute-done.1.refs_2_), channel_id=1, source_target_pairs={{0,1},{1,0},{2,3},{3,2},{4,5},{5,4},{6,7},{7,6},{8,9},{9,8},{10,11... | collective-permute-start | bytes 393224 | tf_op jit(solution)/shard_map/ppermute | solution.py:241
  18.2 5.7 %collective-permute-start.4 = (bf16[16,4096]{1,0:T(8,128)(2,1)S(1)}, bf16[16,4096]{1,0:T(8,128)(2,1)S(1)}, u32[]{:S(2)}, u32[]{:S(2)}) collective-permute-start(bf16[16,4096]{1,0:T(8,128)(2,1)S(1)} %collective-permute-done.2.refs_4_), channel_id=1, source_target_pairs={{0,1},{1,0},{2,3},{3,2},{4,5},{5,4},{6,7},{7,6},{8,9},{9,8},{10,11... | collective-permute-start | bytes 393224 | tf_op jit(solution)/shard_map/ppermute | solution.py:241
  23.9 1.4 %collective-permute-start.10 = (bf16[16,4096]{1,0:T(8,128)(2,1)S(1)}, bf16[16,4096]{1,0:T(8,128)(2,1)S(1)}, u32[]{:S(2)}, u32[]{:S(2)}) collective-permute-start(bf16[16,4096]{1,0:T(8,128)(2,1)S(1)} %copy-done.1), channel_id=1, source_target_pairs={{0,1},{1,0},{2,3},{3,2},{4,5},{5,4},{6,7},{7,6},{8,9},{9,8},{10,11... | collective-permute-start | bytes 393224 | tf_op jit(solution)/shard_map/ppermute | solution.py:241
  23.9 1.5 %collective-permute-start.11 = (bf16[16,4096]{1,0:T(8,128)(2,1)S(1)}, bf16[16,4096]{1,0:T(8,128)(2,1)S(1)}, u32[]{:S(2)}, u32[]{:S(2)}) collective-permute-start(bf16[16,4096]{1,0:T(8,128)(2,1)S(1)} %collective-permute-done.5.refs_6_), channel_id=1, source_target_pairs={{0,1},{1,0},{2,3},{3,2},{4,5},{5,4},{6,7},{7,6},{8,9},{9,8},{10,11... | collective-permute-start | bytes 393224 | tf_op jit(solution)/shard_map/ppermute | solution.py:241
  24.4 1.3 %collective-permute-start.12 = (bf16[16,4096]{1,0:T(8,128)(2,1)S(1)}, bf16[16,4096]{1,0:T(8,128)(2,1)S(1)}, u32[]{:S(2)}, u32[]{:S(2)}) collective-permute-start(bf16[16,4096]{1,0:T(8,128)(2,1)S(1)} %collective-permute-done.6.refs_8_), channel_id=1, source_target_pairs={{0,1},{1,0},{2,3},{3,2},{4,5},{5,4},{6,7},{7,6},{8,9},{9,8},{10,11... | collective-permute-start | bytes 393224 | tf_op jit(solution)/shard_map/ppermute | solution.py:241
  24.5 1.5 %collective-permute-start.13 = (bf16[16,4096]{1,0:T(8,128)(2,1)S(1)}, bf16[16,4096]{1,0:T(8,128)(2,1)S(1)}, u32[]{:S(2)}, u32[]{:S(2)}) collective-permute-start(bf16[16,4096]{1,0:T(8,128)(2,1)S(1)} %collective-permute-done.7.refs_10_), channel_id=1, source_target_pairs={{0,1},{1,0},{2,3},{3,2},{4,5},{5,4},{6,7},{7,6},{8,9},{9,8},{10,11... | collective-permute-start | bytes 393224 | tf_op jit(solution)/shard_map/ppermute | solution.py:241
  24.9 1.3 %collective-permute-start.14 = (bf16[16,4096]{1,0:T(8,128)(2,1)S(1)}, bf16[16,4096]{1,0:T(8,128)(2,1)S(1)}, u32[]{:S(2)}, u32[]{:S(2)}) collective-permute-start(bf16[16,4096]{1,0:T(8,128)(2,1)S(1)} %collective-permute-done.8.refs_12_), channel_id=1, source_target_pairs={{0,1},{1,0},{2,3},{3,2},{4,5},{5,4},{6,7},{7,6},{8,9},{9,8},{10,11... | collective-permute-start | bytes 393224 | tf_op jit(solution)/shard_map/ppermute | solution.py:241
  25.3 1.3 %collective-permute-start.15 = (bf16[16,4096]{1,0:T(8,128)(2,1)S(1)}, bf16[16,4096]{1,0:T(8,128)(2,1)S(1)}, u32[]{:S(2)}, u32[]{:S(2)}) collective-permute-start(bf16[16,4096]{1,0:T(8,128)(2,1)S(1)} %collective-permute-done.9.refs_14_), channel_id=1, source_target_pairs={{0,1},{1,0},{2,3},{3,2},{4,5},{5,4},{6,7},{7,6},{8,9},{9,8},{10,11... | collective-permute-start | bytes 393224 | tf_op jit(solution)/shard_map/ppermute | solution.py:241
  29.7 10.3 %collective-permute-start.17 = (s16[912,128]{1,0:T(8,128)(2,1)S(1)}, s16[912,128]{1,0:T(8,128)(2,1)S(1)}, u32[]{:S(2)}, u32[]{:S(2)}) collective-permute-start(s16[912,128]{1,0:T(8,128)(2,1)S(1)} %get-tuple-element.55), channel_id=1, source_target_pairs={{0,16},{16,0},{1,17},{17,1},{2,18},{18,2},{3,19},{19,3},{4,20},{20... | collective-permute-start | bytes 700424 | tf_op jit(solution)/shard_map/ppermute | solution.py:244
  32.4 10.2 %collective-permute-start.16 = (s16[912,128]{1,0:T(8,128)(2,1)S(1)}, s16[912,128]{1,0:T(8,128)(2,1)S(1)}, u32[]{:S(2)}, u32[]{:S(2)}) collective-permute-start(s16[912,128]{1,0:T(8,128)(2,1)S(1)} %get-tuple-element.53), channel_id=1, source_target_pairs={{0,16},{16,0},{1,17},{17,1},{2,18},{18,2},{3,19},{19,3},{4,20},{20... | collective-permute-start | bytes 700424 | tf_op jit(solution)/shard_map/ppermute | solution.py:244

commit v11 on v9

--- a/solution.py
+++ b/solution.py
@@ -88,17 +88,13 @@
     lax.fori_loop(0, kept.shape[0] // BLOCK, one, 0)
 
 
-def turn_kernel(n_rows, first, *refs):
-    acts, (weight, out, *rest) = refs[:n_rows], refs[n_rows:]
-    if rest:
-        fetch(weight, first, *rest)
+def turn_kernel(n_rows, *refs):
+    acts, out = refs[:n_rows], refs[n_rows]
     tokens, hidden = acts[0].shape
     for k in range(n_rows):
         place = (n_rows - k) % n_rows
         for c in range(0, hidden, BLOCK):
             out[c : c + BLOCK, place * tokens : (place + 1) * tokens] = acts[k][:, c : c + BLOCK].T
-    if rest:
-        fetched(weight, first, *rest)
 
 
 def store_terms(total, own, outs):
@@ -113,6 +109,11 @@
             out[at, :] = whole.astype(jnp.int16)
             codes = jnp.where(of_code == b, code, codes)
         out[rows:, :] = codes.astype(jnp.int16)
+
+
+def fetch_kernel(first, weight, out, sems):
+    fetch(weight, first, out, sems)
+    fetched(weight, first, out, sems)
 
 
 def first_terms_kernel(n_shards, n_kept, n_parts, shift, chunk, place, table, *refs):
@@ -135,7 +136,7 @@
     store_terms(total, own, outs)
 
 
-def more_terms_kernel(n_parts, first, chunk, turned, weight, spread, own, *refs):
+def more_terms_kernel(n_parts, first, chunk, turned, weight, spread, _, own, *refs):
     outs, (total,) = refs[:n_parts], refs[n_parts:]
     blocks = own.shape[0] // BLOCK
     for c in range(0, weight.shape[1], chunk):
@@ -282,8 +283,6 @@
     far = [j for j in held if j]
     spread, again = lax.optimization_barrier((spread, grad_output))
     held[1], held[-1] = send_ring(again, 1), send_ring(again, -1)
-    acts = [inputs] + [send_row(inputs, k) for k in range(1, n_rows)]
-
     kepts = [kept_early]
     if early < piece_blocks:
         late = piece_blocks - early
@@ -298,38 +297,44 @@
             name="keep",
         )(spread, weight)
         kepts.append(kept_late)
-    kepts[-1], *ready = lax.optimization_barrier((kepts[-1], *(held[j] for j in far)))
+    kepts[-1], inputs, *ready = lax.optimization_barrier(
+        (kepts[-1], inputs, *(held[j] for j in far))
+    )
     held.update(zip(far, ready, strict=True))
+    acts = [inputs] + [send_row(inputs, k) for k in range(1, n_rows)]
     for j in range(3, n_chips // 2 + 1):
         by = 1 if j % 2 else 2
         held[j] = send_ring(held[j - by], by)
         if 2 * j < n_chips:
             held[-j] = send_ring(held[by - j], -by)
 
-    *acts, held[1], held[-1] = lax.optimization_barrier((*acts, held[1], held[-1]))
-    later = n_pieces - 1
-    acts_turned, *rest = pl.pallas_call(
-        functools.partial(turn_kernel, n_rows, piece_blocks),
-        in_specs=[in_vmem()] * n_rows + [in_hbm()],
-        out_specs=[in_vmem()] * (1 + later),
-        out_shape=[jax.ShapeDtypeStruct((hidden, all_tokens), bf16)]
-        + [pltpu.VMEM((piece, width), bf16)] * later,
-        scratch_shapes=[pltpu.SemaphoreType.DMA((piece_blocks,))] * later,
+    if n_pieces > 1:
+        weight, held[1], held[-1] = lax.optimization_barrier((weight, held[1], held[-1]))
+        rest = pl.pallas_call(
+            functools.partial(fetch_kernel, piece_blocks),
+            in_specs=[in_hbm()],
+            out_specs=in_vmem(),
+            out_shape=pltpu.VMEM((piece, width), bf16),
+            scratch_shapes=[pltpu.SemaphoreType.DMA((piece_blocks,))],
+            compiler_params=params(),
+            cost_estimate=cost(1 << 34, 2 * piece * width),
+            name="fetch",
+        )(weight)
+        first = [j for j in reach if abs(j) < 3 or j == 3]
+        rest, *ready = lax.optimization_barrier((rest, *(held[j] for j in first)))
+        held.update(zip(first, ready, strict=True))
+    shards = []
+    for j in reach:
+        shards += [held[j], send_core(held[j])]
+    acts_turned = pl.pallas_call(
+        functools.partial(turn_kernel, n_rows),
+        in_specs=[in_vmem()] * n_rows,
+        out_specs=in_vmem(),
+        out_shape=jax.ShapeDtypeStruct((hidden, all_tokens), bf16),
         compiler_params=params(),
         cost_estimate=cost(all_tokens * hidden, 4 * all_tokens * hidden),
         name="turn",
-    )(*acts, weight)
-    first = [j for j in reach if abs(j) == 1]
-    last = [j for j in reach if abs(j) > 2]
-    acts_turned, *ready = lax.optimization_barrier(
-        (acts_turned, *(send_core(held[j]) for j in first), *(held[j] for j in last))
-    )
-    across = dict(zip(first, ready[: len(first)], strict=True))
-    ready = ready[len(first) :]
-    held.update(zip(last, ready, strict=True))
-    shards = []
-    for j in reach:
-        shards += [held[j], across[j] if j in across else send_core(held[j])]
+    )(*acts)
 
     n_shards = len(shards)
     code_rows = -(-(piece // BLOCK) // 16) * 16
@@ -359,14 +364,14 @@
     if n_pieces > 1:
         own, *coded = pl.pallas_call(
             functools.partial(more_terms_kernel, n_parts, piece_blocks, chunk),
-            in_specs=[in_vmem()] * 3,
+            in_specs=[in_vmem()] * 3 + [in_hbm()],
             out_specs=[in_vmem()] * (1 + n_parts),
             out_shape=[own_shape] + [sent_shape] * n_parts,
             scratch_shapes=[pltpu.VMEM((piece, all_tokens), jnp.float32)],
             compiler_params=params(),
             cost_estimate=small_cost,
             name="more_terms",
-        )(turned, rest[0], spread)
+        )(turned, rest, spread, acts_turned)
         owns.append(own)
         parts += [send_row(coded[k], k + 1) for k in range(n_parts)]
 

time: 43 us -> 41.9 us (0.974)
  the two profiles are of different devices: /device:TPU:2 before, /device:TPU:0 now
where the time goes in v11:
time: 41.9 us; the launch traced here: 41.8 us
  Pallas kernels  21.2 us (51%)
  starting transfers between devices  16 us (38%)
  waiting for transfers between devices  3.72 us (9%)
  between operations  0.76 us (2%)
    ppermute x7, starting transfers between devices, send_ring(): return lax.ppermute(x, 'col', perm)  10.3 us
    pallas_call x1, Pallas kernels, per_device(): pl.pallas_call(functools.partial(weight_grad_kernel, chunk), in_specs=[in...  6.03 us
    ppermute x3, starting transfers between devices, send_row(): lax.ppermute(x, 'row', [(r, (r + by) % n_rows) for r in range(n_rows)])  3.68 us
    pallas_call x1, Pallas kernels, per_device(): pl.pallas_call(functools.partial(fetch_kernel, piece_blocks), in_specs=[i...  3.16 us
    pallas_call x1, Pallas kernels, per_device(): pl.pallas_call(functools.partial(first_terms_kernel, n_shards, len(kepts)...  3.07 us
    pallas_call x1, Pallas kernels, per_device(): pl.pallas_call(spread_and_keep_kernel, in_specs=[in_smem(), in_hbm(), in_...  2.53 us
    pallas_call x1, Pallas kernels, per_device(): pl.pallas_call(functools.partial(keep_kernel, early), in_specs=[in_vmem()...  2.29 us
    pallas_call x1, Pallas kernels, per_device(): pl.pallas_call(functools.partial(more_terms_kernel, n_parts, piece_blocks...  2.12 us
  transfers between devices with their start and end apart: 18, of which 7 were waited for; matrix products, arithmetic and copies ran while one was open for 0% of the time, Pallas kernels for 49%

profile of v11, /device:TPU:0, one launch (start us, length us, event | category | flops | bytes accessed | tf_op | source)
XLA Modules:
  0.0 41.8 jit_solution(17621998821481431917)
XLA Ops:
  0.6 4.0 %collective-permute-start.2 = (bf16[16,4096]{1,0:T(8,128)(2,1)}, bf16[16,4096]{1,0:T(8,128)(2,1)S(1)}, u32[]{:S(2)}, u32[]{:S(2)}) collective-permute-start(bf16[16,4096]{1,0:T(8,128)(2,1)} %refs_0_), channel_id=1, source_target_pairs={{2,10},{3,5},{6,14},{7,1},{10,12},{11,3},{14,8},{15,7},{12,4},{13,... | collective-permute-start | bytes 393224 | tf_op jit(solution)/shard_map/ppermute | solution.py:234
  4.6 0.2 collective-permute-start.3
  4.8 0.1 pad_add_fusion.place
  4.9 0.0 copy-start.1
  4.9 2.5 %spread_and_keep.1 = (bf16[384,4096]{1,0:T(8,128)(2,1)S(1)}, f32[14,4096]{1,0:T(8,128)S(1)}) custom-call(s32[2]{0:T(128)S(1)} %pad_add_fusion.place, bf16[1792,4096]{1,0:T(8,128)(2,1)} %weight.4, s32[14,64]{1,0:T(8,128)} %mask.1), custom_call_target="tpu_custom_call" | custom-call | flops 1572864 | bytes 3145728 | tf_op jit(solution)/shard_map/spread_and_keep/pallas_call | solution.py:261
  7.4 0.0 copy-done.1
  7.4 0.0 copy-start
  7.4 1.8 %collective-permute-start = (bf16[16,4096]{1,0:T(8,128)(2,1)S(1)}, bf16[16,4096]{1,0:T(8,128)(2,1)S(1)}, u32[]{:S(2)}, u32[]{:S(2)}) collective-permute-start(bf16[16,4096]{1,0:T(8,128)(2,1)S(1)} %copy-done.1), channel_id=1, source_target_pairs={{2,6},{3,1},{6,10},{7,3},{10,14},{11,7},{14,12},{15,11},{12,8},{13... | collective-permute-start | bytes 393224 | tf_op jit(solution)/shard_map/ppermute | solution.py:234
  9.2 0.3 collective-permute-start.1
  9.5 2.3 %keep.1.refs_17_ = bf16[512,4096]{1,0:T(8,128)(2,1)S(1)} custom-call(f32[14,4096]{1,0:T(8,128)S(1)} %get-tuple-element.31.spread, bf16[1792,4096]{1,0:T(8,128)(2,1)} %weight.4), custom_call_target="tpu_custom_call" | custom-call | flops 2097152 | bytes 4194304 | tf_op jit(solution)/shard_map/keep/pallas_call | solution.py:289
  11.8 0.0 copy-start.2
  11.8 0.0 collective-permute-done.2.refs_6_
  11.8 0.8 %collective-permute-done.3.refs_8_ = bf16[16,4096]{1,0:T(8,128)(2,1)S(1)} collective-permute-done((bf16[16,4096]{1,0:T(8,128)(2,1)}, bf16[16,4096]{1,0:T(8,128)(2,1)S(1)}, u32[]{:S(2)}, u32[]{:S(2)}) %collective-permute-start.3) | collective-permute-done | bytes 131104 | tf_op jit(solution)/shard_map/ppermute | solution.py:234
  12.6 1.0 %collective-permute-start.4 = (bf16[16,4096]{1,0:T(8,128)(2,1)S(1)}, bf16[16,4096]{1,0:T(8,128)(2,1)S(1)}, u32[]{:S(2)}, u32[]{:S(2)}) collective-permute-start(bf16[16,4096]{1,0:T(8,128)(2,1)S(1)} %collective-permute-done.2.refs_6_), channel_id=1, source_target_pairs={{2,6},{3,1},{6,10},{7,3},{10,14},{11,7},{14,12},{15,11},{12,8},{13... | collective-permute-start | bytes 393224 | tf_op jit(solution)/shard_map/ppermute | solution.py:234
  13.7 2.6 %collective-permute-start.13 = (bf16[16,4096]{1,0:T(8,128)(2,1)S(1)}, bf16[16,4096]{1,0:T(8,128)(2,1)S(1)}, u32[]{:S(2)}, u32[]{:S(2)}) collective-permute-start(bf16[16,4096]{1,0:T(8,128)(2,1)S(1)} %collective-permute-done.2.refs_6_), channel_id=1, source_target_pairs={{2,10},{3,5},{6,14},{7,1},{10,12},{11,3},{14,8},{15,7},{12,4},{13,... | collective-permute-start | bytes 393224 | tf_op jit(solution)/shard_map/ppermute | solution.py:234
  16.2 0.0 collective-permute-done.refs_2_
  16.2 0.0 collective-permute-done.1.refs_4_
  16.2 0.5 %collective-permute-start.11 = (bf16[16,4096]{1,0:T(8,128)(2,1)S(1)}, bf16[16,4096]{1,0:T(8,128)(2,1)S(1)}, u32[]{:S(2)}, u32[]{:S(2)}) collective-permute-start(bf16[16,4096]{1,0:T(8,128)(2,1)S(1)} %collective-permute-done.3.refs_8_), channel_id=1, source_target_pairs={{2,0},{3,7},{6,2},{7,11},{10,6},{11,15},{14,10},{15,13},{12,14},{1... | collective-permute-start | bytes 393224 | tf_op jit(solution)/shard_map/ppermute | solution.py:234
  16.7 0.0 copy-done
  16.7 1.5 %collective-permute-start.15 = (bf16[128,1792]{1,0:T(8,128)(2,1)S(1)}, bf16[128,1792]{1,0:T(8,128)(2,1)S(1)}, u32[]{:S(2)}, u32[]{:S(2)}) collective-permute-start(bf16[128,1792]{1,0:T(8,128)(2,1)S(1)} %copy-done), channel_id=1, source_target_pairs={{0,16},{16,0},{1,17},{17,1},{2,18},{18,2},{3,19},{19,3},{4,20},{20... | collective-permute-start | bytes 1376264 | tf_op jit(solution)/shard_map/ppermute | solution.py:240
  18.2 3.2 %fetch.1.weight = bf16[896,4096]{1,0:T(8,128)(2,1)S(1)} custom-call(bf16[1792,4096]{1,0:T(8,128)(2,1)} %weight.4), custom_call_target="tpu_custom_call" | custom-call | flops 17179869184 | bytes 7340032 | tf_op jit(solution)/shard_map/fetch/pallas_call | solution.py:313
  21.4 0.0 collective-permute-done.4.refs_10_
  21.4 0.1 collective-permute-start.5
  21.5 0.5 %collective-permute-start.6 = (bf16[16,4096]{1,0:T(8,128)(2,1)S(1)}, bf16[16,4096]{1,0:T(8,128)(2,1)S(1)}, u32[]{:S(2)}, u32[]{:S(2)}) collective-permute-start(bf16[16,4096]{1,0:T(8,128)(2,1)S(1)} %collective-permute-done.refs_2_), channel_id=1, source_target_pairs={{0,1},{1,0},{2,3},{3,2},{4,5},{5,4},{6,7},{7,6},{8,9},{9,8},{10,11... | collective-permute-start | bytes 393224 | tf_op jit(solution)/shard_map/ppermute | solution.py:237
  22.0 0.0 collective-permute-done.11.refs_12_
  22.0 0.1 collective-permute-start.7
  22.1 0.0 collective-permute-done.13.refs_14_
  22.1 0.4 %collective-permute-start.8 = (bf16[16,4096]{1,0:T(8,128)(2,1)S(1)}, bf16[16,4096]{1,0:T(8,128)(2,1)S(1)}, u32[]{:S(2)}, u32[]{:S(2)}) collective-permute-start(bf16[16,4096]{1,0:T(8,128)(2,1)S(1)} %collective-permute-done.2.refs_6_), channel_id=1, source_target_pairs={{0,1},{1,0},{2,3},{3,2},{4,5},{5,4},{6,7},{7,6},{8,9},{9,8},{10,11... | collective-permute-start | bytes 393224 | tf_op jit(solution)/shard_map/ppermute | solution.py:237
  22.5 0.3 collective-permute-done.5.refs_1_
  22.8 0.1 collective-permute-start.9
  23.0 0.0 collective-permute-done.6.refs_3_
  23.0 0.3 collective-permute-start.10
  23.3 0.0 collective-permute-done.7.refs_5_
  23.3 0.2 collective-permute-start.12
  23.5 0.0 collective-permute-done.8.refs_7_
  23.5 0.3 collective-permute-start.14
  23.9 0.3 collective-permute-done.9.refs_9_
  24.2 0.2 collective-permute-done.10.refs_11_
  24.4 0.3 collective-permute-done.12.refs_13_
  24.7 0.2 collective-permute-done.14.refs_15_
  24.9 0.0 copy-done.2
  24.9 3.1 %first_terms.1 = (bf16[256,4096]{1,0:T(8,128)(2,1)S(1)}, bf16[4096,256]{1,0:T(8,128)(2,1)S(1)}, f32[896,128]{1,0:T(8,128)S(1)}, s16[912,128]{1,0:T(8,128)(2,1)S(1)}) custom-call(s32[2]{0:T(128)S(1)} %pad_add_fusion.place, s32[16,16]{1,0:T(8,128)S(1)} %copy-done.2, bf16[16,4096]{1,0:T(8,128)(2,1)S(1)} %copy-done.1, ...), custom_call_target="tpu_custom_call" | custom-call | flops 3670016 | bytes 458752 | tf_op jit(solution)/shard_map/first_terms/pallas_call | solution.py:344
  28.0 1.4 %collective-permute-start.17 = (s16[912,128]{1,0:T(8,128)(2,1)S(1)}, s16[912,128]{1,0:T(8,128)(2,1)S(1)}, u32[]{:S(2)}, u32[]{:S(2)}) collective-permute-start(s16[912,128]{1,0:T(8,128)(2,1)S(1)} %get-tuple-element.48), channel_id=1, source_target_pairs={{0,16},{16,0},{1,17},{17,1},{2,18},{18,2},{3,19},{19,3},{4,20},{20... | collective-permute-start | bytes 700424 | tf_op jit(solution)/shard_map/ppermute | solution.py:240
  29.3 0.0 collective-permute-done.15.refs_1_
  29.3 0.3 turn.1._.acts
  29.6 2.1 %more_terms.1 = (f32[896,128]{1,0:T(8,128)S(1)}, s16[912,128]{1,0:T(8,128)(2,1)S(1)}) custom-call(bf16[4096,256]{1,0:T(8,128)(2,1)S(1)} %get-tuple-element.42.turned, bf16[896,4096]{1,0:T(8,128)(2,1)S(1)} %fetch.1.weight, f32[14,4096]{1,0:T(8,128)S(1)} %get-tuple-element.31.spread, bf16[1792,256]{1,0:T(8,128)(2,1)S(1)} %turn.1._.acts), custom_call_target="tpu_custom_call" | custom-call | flops 3670016 | bytes 458752 | tf_op jit(solution)/shard_map/more_terms/pallas_call | solution.py:365
  31.7 0.8 %collective-permute-start.16 = (s16[912,128]{1,0:T(8,128)(2,1)S(1)}, s16[912,128]{1,0:T(8,128)(2,1)S(1)}, u32[]{:S(2)}, u32[]{:S(2)}) collective-permute-start(s16[912,128]{1,0:T(8,128)(2,1)S(1)} %get-tuple-element.46), channel_id=1, source_target_pairs={{0,16},{16,0},{1,17},{17,1},{2,18},{18,2},{3,19},{19,3},{4,20},{20... | collective-permute-start | bytes 700424 | tf_op jit(solution)/shard_map/ppermute | solution.py:240
  32.5 6.0 %weight_grad.1 = bf16[1792,4096]{1,0:T(8,128)(2,1)} custom-call(bf16[1792,256]{1,0:T(8,128)(2,1)S(1)} %turn.1._.acts, bf16[256,4096]{1,0:T(8,128)(2,1)S(1)} %get-tuple-element.49.full, f32[14,4096]{1,0:T(8,128)S(1)} %get-tuple-element.31.spread), custom_call_target="tpu_custom_call" | custom-call | flops 3670016 | bytes 458752 | tf_op jit(solution)/shard_map/weight_grad/pallas_call | solution.py:378
  38.6 0.0 collective-permute-done.17.refs_0_
  38.6 0.8 %add_terms.2.refs_1_ = bf16[128,1792]{1,0:T(8,128)(2,1)} custom-call(f32[896,128]{1,0:T(8,128)S(1)} %get-tuple-element.47.own, s16[912,128]{1,0:T(8,128)(2,1)S(1)} %collective-permute-done.17.refs_0_), custom_call_target="tpu_custom_call" | custom-call | tf_op jit(solution)/shard_map/add_terms/pallas_call | solution.py:399
  39.4 1.5 %collective-permute-done.16.refs_0_ = s16[912,128]{1,0:T(8,128)(2,1)S(1)} collective-permute-done((s16[912,128]{1,0:T(8,128)(2,1)S(1)}, s16[912,128]{1,0:T(8,128)(2,1)S(1)}, u32[]{:S(2)}, u32[]{:S(2)}) %collective-permute-start.16) | collective-permute-done | bytes 233504 | tf_op jit(solution)/shard_map/ppermute | solution.py:240
  40.9 0.8 %add_terms.3 = bf16[128,1792]{1,0:T(8,128)(2,1)} custom-call(f32[896,128]{1,0:T(8,128)S(1)} %get-tuple-element.45.own, s16[912,128]{1,0:T(8,128)(2,1)S(1)} %collective-permute-done.16.refs_0_, bf16[128,1792]{1,0:T(8,128)(2,1)} %add_terms.2.refs_1_), custom_call_target="tpu_custom_call", output_to_operand_aliasing={{}: (2, {})} | custom-call | tf_op jit(solution)/shard_map/add_terms/pallas_call | solution.py:399
Async XLA Ops:
  0.6 11.2 %collective-permute-start.2 = (bf16[16,4096]{1,0:T(8,128)(2,1)}, bf16[16,4096]{1,0:T(8,128)(2,1)S(1)}, u32[]{:S(2)}, u32[]{:S(2)}) collective-permute-start(bf16[16,4096]{1,0:T(8,128)(2,1)} %refs_0_), channel_id=1, source_target_pairs={{2,10},{3,5},{6,14},{7,1},{10,12},{11,3},{14,8},{15,7},{12,4},{13,... | collective-permute-start | bytes 393224 | tf_op jit(solution)/shard_map/ppermute | solution.py:234
  4.6 8.0 %collective-permute-start.3 = (bf16[16,4096]{1,0:T(8,128)(2,1)}, bf16[16,4096]{1,0:T(8,128)(2,1)S(1)}, u32[]{:S(2)}, u32[]{:S(2)}) collective-permute-start(bf16[16,4096]{1,0:T(8,128)(2,1)} %refs_0_), channel_id=1, source_target_pairs={{2,4},{3,11},{6,0},{7,15},{10,2},{11,13},{14,6},{15,9},{12,10},{13... | collective-permute-start | bytes 393224 | tf_op jit(solution)/shard_map/ppermute | solution.py:234
  4.9 2.5 %copy-start.1 = (bf16[16,4096]{1,0:T(8,128)(2,1)S(1)}, bf16[16,4096]{1,0:T(8,128)(2,1)}, u32[]{:S(2)}) copy-start(bf16[16,4096]{1,0:T(8,128)(2,1)} %refs_0_) | copy-start | bytes 393220
  7.4 9.3 %copy-start = (bf16[128,1792]{1,0:T(8,128)(2,1)S(1)}, bf16[128,1792]{1,0:T(8,128)(2,1)}, u32[]{:S(2)}) copy-start(bf16[128,1792]{1,0:T(8,128)(2,1)} %refs_0_.1) | copy-start | bytes 1376260
  7.4 8.8 %collective-permute-start = (bf16[16,4096]{1,0:T(8,128)(2,1)S(1)}, bf16[16,4096]{1,0:T(8,128)(2,1)S(1)}, u32[]{:S(2)}, u32[]{:S(2)}) collective-permute-start(bf16[16,4096]{1,0:T(8,128)(2,1)S(1)} %copy-done.1), channel_id=1, source_target_pairs={{2,6},{3,1},{6,10},{7,3},{10,14},{11,7},{14,12},{15,11},{12,8},{13... | collective-permute-start | bytes 393224 | tf_op jit(solution)/shard_map/ppermute | solution.py:234
  9.2 7.0 %collective-permute-start.1 = (bf16[16,4096]{1,0:T(8,128)(2,1)S(1)}, bf16[16,4096]{1,0:T(8,128)(2,1)S(1)}, u32[]{:S(2)}, u32[]{:S(2)}) collective-permute-start(bf16[16,4096]{1,0:T(8,128)(2,1)S(1)} %copy-done.1), channel_id=1, source_target_pairs={{2,0},{3,7},{6,2},{7,11},{10,6},{11,15},{14,10},{15,13},{12,14},{1... | collective-permute-start | bytes 393224 | tf_op jit(solution)/shard_map/ppermute | solution.py:234
  11.8 13.1 %copy-start.2 = (s32[16,16]{1,0:T(8,128)S(1)}, s32[16,16]{1,0:T(8,128)}, u32[]{:S(2)}) copy-start(s32[16,16]{1,0:T(8,128)} %constant.11.clone.table) | copy-start | bytes 3076
  12.6 8.8 %collective-permute-start.4 = (bf16[16,4096]{1,0:T(8,128)(2,1)S(1)}, bf16[16,4096]{1,0:T(8,128)(2,1)S(1)}, u32[]{:S(2)}, u32[]{:S(2)}) collective-permute-start(bf16[16,4096]{1,0:T(8,128)(2,1)S(1)} %collective-permute-done.2.refs_6_), channel_id=1, source_target_pairs={{2,6},{3,1},{6,10},{7,3},{10,14},{11,7},{14,12},{15,11},{12,8},{13... | collective-permute-start | bytes 393224 | tf_op jit(solution)/shard_map/ppermute | solution.py:234
  13.7 8.4 %collective-permute-start.13 = (bf16[16,4096]{1,0:T(8,128)(2,1)S(1)}, bf16[16,4096]{1,0:T(8,128)(2,1)S(1)}, u32[]{:S(2)}, u32[]{:S(2)}) collective-permute-start(bf16[16,4096]{1,0:T(8,128)(2,1)S(1)} %collective-permute-done.2.refs_6_), channel_id=1, source_target_pairs={{2,10},{3,5},{6,14},{7,1},{10,12},{11,3},{14,8},{15,7},{12,4},{13,... | collective-permute-start | bytes 393224 | tf_op jit(solution)/shard_map/ppermute | solution.py:234
  16.2 5.7 %collective-permute-start.11 = (bf16[16,4096]{1,0:T(8,128)(2,1)S(1)}, bf16[16,4096]{1,0:T(8,128)(2,1)S(1)}, u32[]{:S(2)}, u32[]{:S(2)}) collective-permute-start(bf16[16,4096]{1,0:T(8,128)(2,1)S(1)} %collective-permute-done.3.refs_8_), channel_id=1, source_target_pairs={{2,0},{3,7},{6,2},{7,11},{10,6},{11,15},{14,10},{15,13},{12,14},{1... | collective-permute-start | bytes 393224 | tf_op jit(solution)/shard_map/ppermute | solution.py:234
  16.7 12.6 %collective-permute-start.15 = (bf16[128,1792]{1,0:T(8,128)(2,1)S(1)}, bf16[128,1792]{1,0:T(8,128)(2,1)S(1)}, u32[]{:S(2)}, u32[]{:S(2)}) collective-permute-start(bf16[128,1792]{1,0:T(8,128)(2,1)S(1)} %copy-done), channel_id=1, source_target_pairs={{0,16},{16,0},{1,17},{17,1},{2,18},{18,2},{3,19},{19,3},{4,20},{20... | collective-permute-start | bytes 1376264 | tf_op jit(solution)/shard_map/ppermute | solution.py:240
  21.4 1.4 %collective-permute-start.5 = (bf16[16,4096]{1,0:T(8,128)(2,1)S(1)}, bf16[16,4096]{1,0:T(8,128)(2,1)S(1)}, u32[]{:S(2)}, u32[]{:S(2)}) collective-permute-start(bf16[16,4096]{1,0:T(8,128)(2,1)S(1)} %copy-done.1), channel_id=1, source_target_pairs={{0,1},{1,0},{2,3},{3,2},{4,5},{5,4},{6,7},{7,6},{8,9},{9,8},{10,11... | collective-permute-start | bytes 393224 | tf_op jit(solution)/shard_map/ppermute | solution.py:237
  21.5 1.5 %collective-permute-start.6 = (bf16[16,4096]{1,0:T(8,128)(2,1)S(1)}, bf16[16,4096]{1,0:T(8,128)(2,1)S(1)}, u32[]{:S(2)}, u32[]{:S(2)}) collective-permute-start(bf16[16,4096]{1,0:T(8,128)(2,1)S(1)} %collective-permute-done.refs_2_), channel_id=1, source_target_pairs={{0,1},{1,0},{2,3},{3,2},{4,5},{5,4},{6,7},{7,6},{8,9},{9,8},{10,11... | collective-permute-start | bytes 393224 | tf_op jit(solution)/shard_map/ppermute | solution.py:237
  22.0 1.4 %collective-permute-start.7 = (bf16[16,4096]{1,0:T(8,128)(2,1)S(1)}, bf16[16,4096]{1,0:T(8,128)(2,1)S(1)}, u32[]{:S(2)}, u32[]{:S(2)}) collective-permute-start(bf16[16,4096]{1,0:T(8,128)(2,1)S(1)} %collective-permute-done.1.refs_4_), channel_id=1, source_target_pairs={{0,1},{1,0},{2,3},{3,2},{4,5},{5,4},{6,7},{7,6},{8,9},{9,8},{10,11... | collective-permute-start | bytes 393224 | tf_op jit(solution)/shard_map/ppermute | solution.py:237
  22.1 1.5 %collective-permute-start.8 = (bf16[16,4096]{1,0:T(8,128)(2,1)S(1)}, bf16[16,4096]{1,0:T(8,128)(2,1)S(1)}, u32[]{:S(2)}, u32[]{:S(2)}) collective-permute-start(bf16[16,4096]{1,0:T(8,128)(2,1)S(1)} %collective-permute-done.2.refs_6_), channel_id=1, source_target_pairs={{0,1},{1,0},{2,3},{3,2},{4,5},{5,4},{6,7},{7,6},{8,9},{9,8},{10,11... | collective-permute-start | bytes 393224 | tf_op jit(solution)/shard_map/ppermute | solution.py:237
  22.8 1.3 %collective-permute-start.9 = (bf16[16,4096]{1,0:T(8,128)(2,1)S(1)}, bf16[16,4096]{1,0:T(8,128)(2,1)S(1)}, u32[]{:S(2)}, u32[]{:S(2)}) collective-permute-start(bf16[16,4096]{1,0:T(8,128)(2,1)S(1)} %collective-permute-done.3.refs_8_), channel_id=1, source_target_pairs={{0,1},{1,0},{2,3},{3,2},{4,5},{5,4},{6,7},{7,6},{8,9},{9,8},{10,11... | collective-permute-start | bytes 393224 | tf_op jit(solution)/shard_map/ppermute | solution.py:237
  23.0 1.3 %collective-permute-start.10 = (bf16[16,4096]{1,0:T(8,128)(2,1)S(1)}, bf16[16,4096]{1,0:T(8,128)(2,1)S(1)}, u32[]{:S(2)}, u32[]{:S(2)}) collective-permute-start(bf16[16,4096]{1,0:T(8,128)(2,1)S(1)} %collective-permute-done.4.refs_10_), channel_id=1, source_target_pairs={{0,1},{1,0},{2,3},{3,2},{4,5},{5,4},{6,7},{7,6},{8,9},{9,8},{10,11... | collective-permute-start | bytes 393224 | tf_op jit(solution)/shard_map/ppermute | solution.py:237
  23.3 1.3 %collective-permute-start.12 = (bf16[16,4096]{1,0:T(8,128)(2,1)S(1)}, bf16[16,4096]{1,0:T(8,128)(2,1)S(1)}, u32[]{:S(2)}, u32[]{:S(2)}) collective-permute-start(bf16[16,4096]{1,0:T(8,128)(2,1)S(1)} %collective-permute-done.11.refs_12_), channel_id=1, source_target_pairs={{0,1},{1,0},{2,3},{3,2},{4,5},{5,4},{6,7},{7,6},{8,9},{9,8},{10,11... | collective-permute-start | bytes 393224 | tf_op jit(solution)/shard_map/ppermute | solution.py:237
  23.5 1.3 %collective-permute-start.14 = (bf16[16,4096]{1,0:T(8,128)(2,1)S(1)}, bf16[16,4096]{1,0:T(8,128)(2,1)S(1)}, u32[]{:S(2)}, u32[]{:S(2)}) collective-permute-start(bf16[16,4096]{1,0:T(8,128)(2,1)S(1)} %collective-permute-done.13.refs_14_), channel_id=1, source_target_pairs={{0,1},{1,0},{2,3},{3,2},{4,5},{5,4},{6,7},{7,6},{8,9},{9,8},{10,11... | collective-permute-start | bytes 393224 | tf_op jit(solution)/shard_map/ppermute | solution.py:237
  28.0 10.6 %collective-permute-start.17 = (s16[912,128]{1,0:T(8,128)(2,1)S(1)}, s16[912,128]{1,0:T(8,128)(2,1)S(1)}, u32[]{:S(2)}, u32[]{:S(2)}) collective-permute-start(s16[912,128]{1,0:T(8,128)(2,1)S(1)} %get-tuple-element.48), channel_id=1, source_target_pairs={{0,16},{16,0},{1,17},{17,1},{2,18},{18,2},{3,19},{19,3},{4,20},{20... | collective-permute-start | bytes 700424 | tf_op jit(solution)/shard_map/ppermute | solution.py:240
  31.7 9.2 %collective-permute-start.16 = (s16[912,128]{1,0:T(8,128)(2,1)S(1)}, s16[912,128]{1,0:T(8,128)(2,1)S(1)}, u32[]{:S(2)}, u32[]{:S(2)}) collective-permute-start(s16[912,128]{1,0:T(8,128)(2,1)S(1)} %get-tuple-element.46), channel_id=1, source_target_pairs={{0,16},{16,0},{1,17},{17,1},{2,18},{18,2},{3,19},{19,3},{4,20},{20... | collective-permute-start | bytes 700424 | tf_op jit(solution)/shard_map/ppermute | solution.py:240

commit v12 on v11

--- a/solution.py
+++ b/solution.py
@@ -88,13 +88,20 @@
     lax.fori_loop(0, kept.shape[0] // BLOCK, one, 0)
 
 
-def turn_kernel(n_rows, *refs):
-    acts, out = refs[:n_rows], refs[n_rows]
+def pack_kernel(*refs):
+    shards, out = refs[:-1], refs[-1]
+    rows = shards[0].shape[0]
+    for n, shard in enumerate(shards):
+        out[n * rows : (n + 1) * rows, :] = shard[...]
+
+
+def turn_kernel(*refs):
+    acts, out = refs[:-1], refs[-1]
     tokens, hidden = acts[0].shape
-    for k in range(n_rows):
-        place = (n_rows - k) % n_rows
+    for k, act in enumerate(acts):
+        place = (len(acts) - k) % len(acts)
         for c in range(0, hidden, BLOCK):
-            out[c : c + BLOCK, place * tokens : (place + 1) * tokens] = acts[k][:, c : c + BLOCK].T
+            out[c : c + BLOCK, place * tokens : (place + 1) * tokens] = act[:, c : c + BLOCK].T
 
 
 def store_terms(total, own, outs):
@@ -121,9 +128,10 @@
     full, turned, own, *outs, total = refs[n_shards + n_kept :]
     rows = shards[0].shape[0]
     n_cols = table.shape[0]
-    for n, shard in enumerate(shards):
+    slots = [(shard, at) for shard in shards for at in range(0, shard.shape[0], rows)]
+    for n, (shard, at) in enumerate(slots):
         to = lax.rem(table[place[1], n] + n_cols - place[0] * shift, n_cols)
-        full[pl.ds(pl.multiple_of(to * rows, rows), rows), :] = shard[...]
+        full[pl.ds(pl.multiple_of(to * rows, rows), rows), :] = shard[at : at + rows, :]
     for c in range(0, full.shape[1], chunk):
         cols = slice(c, c + chunk)
         turned[cols, :] = full[:, cols].T
@@ -136,8 +144,8 @@
     store_terms(total, own, outs)
 
 
-def more_terms_kernel(n_parts, first, chunk, turned, weight, spread, _, own, *refs):
-    outs, (total,) = refs[:n_parts], refs[n_parts:]
+def more_terms_kernel(n_parts, first, chunk, turned, weight, spread, *refs):
+    acts, (own, *outs, acts_turned, total) = refs[: n_parts + 1], refs[n_parts + 1 :]
     blocks = own.shape[0] // BLOCK
     for c in range(0, weight.shape[1], chunk):
         cols = slice(c, c + chunk)
@@ -149,6 +157,7 @@
         terms = jnp.dot(kept, turned[cols, :], preferred_element_type=jnp.float32)
         total[...] = terms if c == 0 else total[...] + terms
     store_terms(total, own, outs)
+    turn_kernel(*acts, acts_turned)
 
 
 def weight_grad_kernel(chunk, acts, full, spread, out, held, sems):
@@ -242,7 +251,10 @@
     reach = [0]
     for j in range(1, n_chips // 2 + 1):
         reach += [j] if 2 * j == n_chips else [j, -j]
-    steps = [(j, other) for j in reach for other in range(2)]
+    near = [j for j in reach if abs(j) < 3]
+    last = [j for j in reach if abs(j) > 2]
+    steps = [(j, other) for other in range(2) for j in near]
+    steps += [(j, other) for j in last for other in range(2)]
     table = []
     for c in range(n_cols):
         p, core = ring.index(c // 2), c % 2
@@ -320,22 +332,19 @@
             cost_estimate=cost(1 << 34, 2 * piece * width),
             name="fetch",
         )(weight)
-        first = [j for j in reach if abs(j) < 3 or j == 3]
-        rest, *ready = lax.optimization_barrier((rest, *(held[j] for j in first)))
-        held.update(zip(first, ready, strict=True))
-    shards = []
-    for j in reach:
+        rest, *ready = lax.optimization_barrier((rest, *(held[j] for j in last)))
+        held.update(zip(last, ready, strict=True))
+    packed = pl.pallas_call(
+        pack_kernel,
+        in_specs=[in_vmem()] * len(near),
+        out_specs=in_vmem(),
+        out_shape=jax.ShapeDtypeStruct((len(near) * shard_rows, width), bf16),
+        compiler_params=params(),
+        name="pack",
+    )(*(held[j] for j in near))
+    shards = [held[j] for j in near] + [send_core(packed)]
+    for j in last:
         shards += [held[j], send_core(held[j])]
-    acts_turned = pl.pallas_call(
-        functools.partial(turn_kernel, n_rows),
-        in_specs=[in_vmem()] * n_rows,
-        out_specs=in_vmem(),
-        out_shape=jax.ShapeDtypeStruct((hidden, all_tokens), bf16),
-        compiler_params=params(),
-        cost_estimate=cost(all_tokens * hidden, 4 * all_tokens * hidden),
-        name="turn",
-    )(*acts)
-
     n_shards = len(shards)
     code_rows = -(-(piece // BLOCK) // 16) * 16
     sent_shape = jax.ShapeDtypeStruct((piece + code_rows, tokens), jnp.int16)
@@ -361,19 +370,29 @@
     owns = [own]
     parts = [send_row(coded[k], k + 1) for k in range(n_parts)]
 
+    acts_shape = jax.ShapeDtypeStruct((hidden, all_tokens), bf16)
     if n_pieces > 1:
-        own, *coded = pl.pallas_call(
+        own, *coded, acts_turned = pl.pallas_call(
             functools.partial(more_terms_kernel, n_parts, piece_blocks, chunk),
-            in_specs=[in_vmem()] * 3 + [in_hbm()],
-            out_specs=[in_vmem()] * (1 + n_parts),
-            out_shape=[own_shape] + [sent_shape] * n_parts,
+            in_specs=[in_vmem()] * (3 + n_rows),
+            out_specs=[in_vmem()] * (2 + n_parts),
+            out_shape=[own_shape] + [sent_shape] * n_parts + [acts_shape],
             scratch_shapes=[pltpu.VMEM((piece, all_tokens), jnp.float32)],
             compiler_params=params(),
             cost_estimate=small_cost,
             name="more_terms",
-        )(turned, rest, spread, acts_turned)
+        )(turned, rest, spread, *acts)
         owns.append(own)
         parts += [send_row(coded[k], k + 1) for k in range(n_parts)]
+    else:
+        acts_turned = pl.pallas_call(
+            turn_kernel,
+            in_specs=[in_vmem()] * n_rows,
+            out_specs=in_vmem(),
+            out_shape=acts_shape,
+            compiler_params=params(),
+            name="turn",
+        )(*acts)
 
     grad_weight = pl.pallas_call(
         functools.partial(weight_grad_kernel, chunk),

time: 41.9 us -> 41.5 us (level)
    ppermute x8 -> x4, starting transfers between devices: 2.07 us -> 0.8 us  [send_core(): return lax.ppermute(x, 'col', [(c, c ^ 1) for c in range(n_cols)])]
    ppermute x3, starting transfers between devices: 3.68 us -> 4.7 us  [send_row(): lax.ppermute(x, 'row', [(r, (r + by) % n_rows) for r in range(n_rows)])]
    ppermute x8 -> x4, waiting for transfers between devices: 1.38 us -> 1.19 us  [send_core(): return lax.ppermute(x, 'col', [(c, c ^ 1) for c in range(n_cols)])]
  transfers between devices with their start and end apart: 18 -> 14, of which waited for: 7 -> 5; matrix products, arithmetic and copies ran while one was open for 0% -> 0% of each run, Pallas kernels for 49% -> 49%
where the time goes in v12:
time: 41.5 us; the launch traced here: 41.4 us
  Pallas kernels  21 us (51%)
  starting transfers between devices  15.8 us (38%)
  waiting for transfers between devices  3.74 us (9%)
  between operations  0.77 us (2%)
    ppermute x7, starting transfers between devices, send_ring(): return lax.ppermute(x, 'col', perm)  10.3 us
    pallas_call x1, Pallas kernels, per_device(): pl.pallas_call(functools.partial(weight_grad_kernel, chunk), in_specs=[in...  6.04 us
    ppermute x3, starting transfers between devices, send_row(): lax.ppermute(x, 'row', [(r, (r + by) % n_rows) for r in range(n_rows)])  4.7 us
    pallas_call x1, Pallas kernels, per_device(): pl.pallas_call(functools.partial(fetch_kernel, piece_blocks), in_specs=[i...  3.16 us
    pallas_call x1, Pallas kernels, per_device(): pl.pallas_call(functools.partial(first_terms_kernel, n_shards, len(kepts)...  3.07 us
    pallas_call x1, Pallas kernels, per_device(): pl.pallas_call(spread_and_keep_kernel, in_specs=[in_smem(), in_hbm(), in_...  2.53 us
    pallas_call x1, Pallas kernels, per_device(): pl.pallas_call(functools.partial(keep_kernel, early), in_specs=[in_vmem()...  2.29 us
    pallas_call x1, Pallas kernels, per_device(): pl.pallas_call(functools.partial(more_terms_kernel, n_parts, piece_blocks...  2.13 us
  transfers between devices with their start and end apart: 14, of which 5 were waited for; matrix products, arithmetic and copies ran while one was open for 0% of the time, Pallas kernels for 49%

profile of v12, /device:TPU:0, one launch (start us, length us, event | category | flops | bytes accessed | tf_op | source)
XLA Modules:
  0.0 41.4 jit_solution(1794694211633801200)
XLA Ops:
  0.6 4.0 %collective-permute-start.2 = (bf16[16,4096]{1,0:T(8,128)(2,1)}, bf16[16,4096]{1,0:T(8,128)(2,1)S(1)}, u32[]{:S(2)}, u32[]{:S(2)}) collective-permute-start(bf16[16,4096]{1,0:T(8,128)(2,1)} %refs_0_.3), channel_id=1, source_target_pairs={{2,10},{3,5},{6,14},{7,1},{10,12},{11,3},{14,8},{15,7},{12,4},{13,... | collective-permute-start | bytes 393224 | tf_op jit(solution)/shard_map/ppermute | solution.py:243
  4.6 0.2 collective-permute-start.3
  4.8 0.1 pad_add_fusion.place
  4.9 0.0 copy-start
  4.9 2.5 %spread_and_keep.1 = (bf16[384,4096]{1,0:T(8,128)(2,1)S(1)}, f32[14,4096]{1,0:T(8,128)S(1)}) custom-call(s32[2]{0:T(128)S(1)} %pad_add_fusion.place, bf16[1792,4096]{1,0:T(8,128)(2,1)} %weight.4, s32[14,64]{1,0:T(8,128)} %mask.1), custom_call_target="tpu_custom_call" | custom-call | flops 1572864 | bytes 3145728 | tf_op jit(solution)/shard_map/spread_and_keep/pallas_call | solution.py:273
  7.4 0.0 copy-done
  7.4 0.0 copy-start.1
  7.4 1.8 %collective-permute-start = (bf16[16,4096]{1,0:T(8,128)(2,1)S(1)}, bf16[16,4096]{1,0:T(8,128)(2,1)S(1)}, u32[]{:S(2)}, u32[]{:S(2)}) collective-permute-start(bf16[16,4096]{1,0:T(8,128)(2,1)S(1)} %copy-done), channel_id=1, source_target_pairs={{2,6},{3,1},{6,10},{7,3},{10,14},{11,7},{14,12},{15,11},{12,8},{13... | collective-permute-start | bytes 393224 | tf_op jit(solution)/shard_map/ppermute | solution.py:243
  9.2 0.3 collective-permute-start.1
  9.5 2.3 %keep.1.refs_13_ = bf16[512,4096]{1,0:T(8,128)(2,1)S(1)} custom-call(f32[14,4096]{1,0:T(8,128)S(1)} %get-tuple-element.28.spread, bf16[1792,4096]{1,0:T(8,128)(2,1)} %weight.4), custom_call_target="tpu_custom_call" | custom-call | flops 2097152 | bytes 4194304 | tf_op jit(solution)/shard_map/keep/pallas_call | solution.py:301
  11.8 0.0 collective-permute-done.2.refs_3_
  11.8 0.8 %collective-permute-done.3.refs_4_ = bf16[16,4096]{1,0:T(8,128)(2,1)S(1)} collective-permute-done((bf16[16,4096]{1,0:T(8,128)(2,1)}, bf16[16,4096]{1,0:T(8,128)(2,1)S(1)}, u32[]{:S(2)}, u32[]{:S(2)}) %collective-permute-start.3) | collective-permute-done | bytes 131104 | tf_op jit(solution)/shard_map/ppermute | solution.py:243
  12.6 1.0 %collective-permute-start.5 = (bf16[16,4096]{1,0:T(8,128)(2,1)S(1)}, bf16[16,4096]{1,0:T(8,128)(2,1)S(1)}, u32[]{:S(2)}, u32[]{:S(2)}) collective-permute-start(bf16[16,4096]{1,0:T(8,128)(2,1)S(1)} %collective-permute-done.2.refs_3_), channel_id=1, source_target_pairs={{2,6},{3,1},{6,10},{7,3},{10,14},{11,7},{14,12},{15,11},{12,8},{13... | collective-permute-start | bytes 393224 | tf_op jit(solution)/shard_map/ppermute | solution.py:243
  13.6 2.6 %collective-permute-start.7 = (bf16[16,4096]{1,0:T(8,128)(2,1)S(1)}, bf16[16,4096]{1,0:T(8,128)(2,1)S(1)}, u32[]{:S(2)}, u32[]{:S(2)}) collective-permute-start(bf16[16,4096]{1,0:T(8,128)(2,1)S(1)} %collective-permute-done.2.refs_3_), channel_id=1, source_target_pairs={{2,10},{3,5},{6,14},{7,1},{10,12},{11,3},{14,8},{15,7},{12,4},{13,... | collective-permute-start | bytes 393224 | tf_op jit(solution)/shard_map/ppermute | solution.py:243
  16.2 0.0 collective-permute-done.refs_1_
  16.2 0.0 collective-permute-done.1.refs_2_
  16.2 0.5 %collective-permute-start.6 = (bf16[16,4096]{1,0:T(8,128)(2,1)S(1)}, bf16[16,4096]{1,0:T(8,128)(2,1)S(1)}, u32[]{:S(2)}, u32[]{:S(2)}) collective-permute-start(bf16[16,4096]{1,0:T(8,128)(2,1)S(1)} %collective-permute-done.3.refs_4_), channel_id=1, source_target_pairs={{2,0},{3,7},{6,2},{7,11},{10,6},{11,15},{14,10},{15,13},{12,14},{1... | collective-permute-start | bytes 393224 | tf_op jit(solution)/shard_map/ppermute | solution.py:243
  16.7 0.0 copy-start.2
  16.7 0.1 collective-permute-start.4
  16.8 0.0 copy-done.1
  16.8 1.6 %collective-permute-start.11 = (bf16[128,1792]{1,0:T(8,128)(2,1)S(1)}, bf16[128,1792]{1,0:T(8,128)(2,1)S(1)}, u32[]{:S(2)}, u32[]{:S(2)}) collective-permute-start(bf16[128,1792]{1,0:T(8,128)(2,1)S(1)} %copy-done.1), channel_id=1, source_target_pairs={{0,16},{16,0},{1,17},{17,1},{2,18},{18,2},{3,19},{19,3},{4,20},{20... | collective-permute-start | bytes 1376264 | tf_op jit(solution)/shard_map/ppermute | solution.py:249
  18.4 3.2 %fetch.1.weight = bf16[896,4096]{1,0:T(8,128)(2,1)S(1)} custom-call(bf16[1792,4096]{1,0:T(8,128)(2,1)} %weight.4), custom_call_target="tpu_custom_call" | custom-call | flops 17179869184 | bytes 7340032 | tf_op jit(solution)/shard_map/fetch/pallas_call | solution.py:325
  21.6 0.0 collective-permute-done.5.refs_6_
  21.6 0.0 collective-permute-done.7.refs_10_
  21.6 0.0 collective-permute-done.6.refs_8_
  21.6 0.2 collective-permute-start.10
  21.8 0.4 collective-permute-start.8
  22.2 0.2 collective-permute-start.9
  22.4 0.7 %collective-permute-done.10.refs_11_ = bf16[16,4096]{1,0:T(8,128)(2,1)S(1)} collective-permute-done((bf16[16,4096]{1,0:T(8,128)(2,1)S(1)}, bf16[16,4096]{1,0:T(8,128)(2,1)S(1)}, u32[]{:S(2)}, u32[]{:S(2)}) %collective-permute-start.10) | collective-permute-done | bytes 131104 | tf_op jit(solution)/shard_map/ppermute | solution.py:246
  23.0 0.2 collective-permute-done.8.refs_7_
  23.2 0.3 collective-permute-done.9.refs_9_
  23.5 0.0 collective-permute-done.4.refs_5_
  23.6 0.0 copy-done.2
  23.6 3.1 %first_terms.1 = (bf16[256,4096]{1,0:T(8,128)(2,1)S(1)}, bf16[4096,256]{1,0:T(8,128)(2,1)S(1)}, f32[896,128]{1,0:T(8,128)S(1)}, s16[912,128]{1,0:T(8,128)(2,1)S(1)}) custom-call(s32[2]{0:T(128)S(1)} %pad_add_fusion.place, s32[16,16]{1,0:T(8,128)S(1)} %copy-done.2, bf16[16,4096]{1,0:T(8,128)(2,1)S(1)} %copy-done, ...), custom_call_target="tpu_custom_call" | custom-call | flops 3670016 | bytes 458752 | tf_op jit(solution)/shard_map/first_terms/pallas_call | solution.py:353
  26.6 1.6 %collective-permute-start.13 = (s16[912,128]{1,0:T(8,128)(2,1)S(1)}, s16[912,128]{1,0:T(8,128)(2,1)S(1)}, u32[]{:S(2)}, u32[]{:S(2)}) collective-permute-start(s16[912,128]{1,0:T(8,128)(2,1)S(1)} %get-tuple-element.43), channel_id=1, source_target_pairs={{0,16},{16,0},{1,17},{17,1},{2,18},{18,2},{3,19},{19,3},{4,20},{20... | collective-permute-start | bytes 700424 | tf_op jit(solution)/shard_map/ppermute | solution.py:249
  28.3 1.7 %collective-permute-done.11.refs_1_ = bf16[128,1792]{1,0:T(8,128)(2,1)S(1)} collective-permute-done((bf16[128,1792]{1,0:T(8,128)(2,1)S(1)}, bf16[128,1792]{1,0:T(8,128)(2,1)S(1)}, u32[]{:S(2)}, u32[]{:S(2)}) %collective-permute-start.11) | collective-permute-done | bytes 458784 | tf_op jit(solution)/shard_map/ppermute | solution.py:249
  30.0 2.1 %more_terms.1 = (f32[896,128]{1,0:T(8,128)S(1)}, s16[912,128]{1,0:T(8,128)(2,1)S(1)}, bf16[1792,256]{1,0:T(8,128)(2,1)S(1)}) custom-call(bf16[4096,256]{1,0:T(8,128)(2,1)S(1)} %get-tuple-element.37.turned, bf16[896,4096]{1,0:T(8,128)(2,1)S(1)} %fetch.1.weight, f32[14,4096]{1,0:T(8,128)S(1)} %get-tuple-element.28.spread, bf16[128,1792]{1,0:T(8,128)(2,1)S(1)} %copy-done.1, ...), custom_call_target="tpu_custom_call" | custom-call | flops 3670016 | bytes 458752 | tf_op jit(solution)/shard_map/more_terms/pallas_call | solution.py:375
  32.1 1.5 %collective-permute-start.12 = (s16[912,128]{1,0:T(8,128)(2,1)S(1)}, s16[912,128]{1,0:T(8,128)(2,1)S(1)}, u32[]{:S(2)}, u32[]{:S(2)}) collective-permute-start(s16[912,128]{1,0:T(8,128)(2,1)S(1)} %get-tuple-element.41), channel_id=1, source_target_pairs={{0,16},{16,0},{1,17},{17,1},{2,18},{18,2},{3,19},{19,3},{4,20},{20... | collective-permute-start | bytes 700424 | tf_op jit(solution)/shard_map/ppermute | solution.py:249
  33.6 6.0 %weight_grad.1 = bf16[1792,4096]{1,0:T(8,128)(2,1)} custom-call(bf16[1792,256]{1,0:T(8,128)(2,1)S(1)} %get-tuple-element.44.acts, bf16[256,4096]{1,0:T(8,128)(2,1)S(1)} %get-tuple-element.45.full, f32[14,4096]{1,0:T(8,128)S(1)} %get-tuple-element.28.spread), custom_call_target="tpu_custom_call" | custom-call | flops 3670016 | bytes 458752 | tf_op jit(solution)/shard_map/weight_grad/pallas_call | solution.py:397
  39.7 0.0 collective-permute-done.13.refs_0_
  39.7 0.8 %add_terms.2.refs_1_ = bf16[128,1792]{1,0:T(8,128)(2,1)} custom-call(f32[896,128]{1,0:T(8,128)S(1)} %get-tuple-element.42.own, s16[912,128]{1,0:T(8,128)(2,1)S(1)} %collective-permute-done.13.refs_0_), custom_call_target="tpu_custom_call" | custom-call | tf_op jit(solution)/shard_map/add_terms/pallas_call | solution.py:418
  40.5 0.0 collective-permute-done.12.refs_0_
  40.5 0.8 %add_terms.3 = bf16[128,1792]{1,0:T(8,128)(2,1)} custom-call(f32[896,128]{1,0:T(8,128)S(1)} %get-tuple-element.40.own, s16[912,128]{1,0:T(8,128)(2,1)S(1)} %collective-permute-done.12.refs_0_, bf16[128,1792]{1,0:T(8,128)(2,1)} %add_terms.2.refs_1_), custom_call_target="tpu_custom_call", output_to_operand_aliasing={{}: (2, {})} | custom-call | tf_op jit(solution)/shard_map/add_terms/pallas_call | solution.py:418
  (1 shorter events, 0.0 us)
Async XLA Ops:
  0.6 11.2 %collective-permute-start.2 = (bf16[16,4096]{1,0:T(8,128)(2,1)}, bf16[16,4096]{1,0:T(8,128)(2,1)S(1)}, u32[]{:S(2)}, u32[]{:S(2)}) collective-permute-start(bf16[16,4096]{1,0:T(8,128)(2,1)} %refs_0_.3), channel_id=1, source_target_pairs={{2,10},{3,5},{6,14},{7,1},{10,12},{11,3},{14,8},{15,7},{12,4},{13,... | collective-permute-start | bytes 393224 | tf_op jit(solution)/shard_map/ppermute | solution.py:243
  4.6 8.0 %collective-permute-start.3 = (bf16[16,4096]{1,0:T(8,128)(2,1)}, bf16[16,4096]{1,0:T(8,128)(2,1)S(1)}, u32[]{:S(2)}, u32[]{:S(2)}) collective-permute-start(bf16[16,4096]{1,0:T(8,128)(2,1)} %refs_0_.3), channel_id=1, source_target_pairs={{2,4},{3,11},{6,0},{7,15},{10,2},{11,13},{14,6},{15,9},{12,10},{13... | collective-permute-start | bytes 393224 | tf_op jit(solution)/shard_map/ppermute | solution.py:243
  4.9 2.5 %copy-start = (bf16[16,4096]{1,0:T(8,128)(2,1)S(1)}, bf16[16,4096]{1,0:T(8,128)(2,1)}, u32[]{:S(2)}) copy-start(bf16[16,4096]{1,0:T(8,128)(2,1)} %refs_0_.3) | copy-start | bytes 393220
  7.4 9.4 %copy-start.1 = (bf16[128,1792]{1,0:T(8,128)(2,1)S(1)}, bf16[128,1792]{1,0:T(8,128)(2,1)}, u32[]{:S(2)}) copy-start(bf16[128,1792]{1,0:T(8,128)(2,1)} %refs_0_.4) | copy-start | bytes 1376260
  7.4 8.8 %collective-permute-start = (bf16[16,4096]{1,0:T(8,128)(2,1)S(1)}, bf16[16,4096]{1,0:T(8,128)(2,1)S(1)}, u32[]{:S(2)}, u32[]{:S(2)}) collective-permute-start(bf16[16,4096]{1,0:T(8,128)(2,1)S(1)} %copy-done), channel_id=1, source_target_pairs={{2,6},{3,1},{6,10},{7,3},{10,14},{11,7},{14,12},{15,11},{12,8},{13... | collective-permute-start | bytes 393224 | tf_op jit(solution)/shard_map/ppermute | solution.py:243
  9.2 7.0 %collective-permute-start.1 = (bf16[16,4096]{1,0:T(8,128)(2,1)S(1)}, bf16[16,4096]{1,0:T(8,128)(2,1)S(1)}, u32[]{:S(2)}, u32[]{:S(2)}) collective-permute-start(bf16[16,4096]{1,0:T(8,128)(2,1)S(1)} %copy-done), channel_id=1, source_target_pairs={{2,0},{3,7},{6,2},{7,11},{10,6},{11,15},{14,10},{15,13},{12,14},{1... | collective-permute-start | bytes 393224 | tf_op jit(solution)/shard_map/ppermute | solution.py:243
  12.6 9.0 %collective-permute-start.5 = (bf16[16,4096]{1,0:T(8,128)(2,1)S(1)}, bf16[16,4096]{1,0:T(8,128)(2,1)S(1)}, u32[]{:S(2)}, u32[]{:S(2)}) collective-permute-start(bf16[16,4096]{1,0:T(8,128)(2,1)S(1)} %collective-permute-done.2.refs_3_), channel_id=1, source_target_pairs={{2,6},{3,1},{6,10},{7,3},{10,14},{11,7},{14,12},{15,11},{12,8},{13... | collective-permute-start | bytes 393224 | tf_op jit(solution)/shard_map/ppermute | solution.py:243
  13.6 8.0 %collective-permute-start.7 = (bf16[16,4096]{1,0:T(8,128)(2,1)S(1)}, bf16[16,4096]{1,0:T(8,128)(2,1)S(1)}, u32[]{:S(2)}, u32[]{:S(2)}) collective-permute-start(bf16[16,4096]{1,0:T(8,128)(2,1)S(1)} %collective-permute-done.2.refs_3_), channel_id=1, source_target_pairs={{2,10},{3,5},{6,14},{7,1},{10,12},{11,3},{14,8},{15,7},{12,4},{13,... | collective-permute-start | bytes 393224 | tf_op jit(solution)/shard_map/ppermute | solution.py:243
  16.2 5.4 %collective-permute-start.6 = (bf16[16,4096]{1,0:T(8,128)(2,1)S(1)}, bf16[16,4096]{1,0:T(8,128)(2,1)S(1)}, u32[]{:S(2)}, u32[]{:S(2)}) collective-permute-start(bf16[16,4096]{1,0:T(8,128)(2,1)S(1)} %collective-permute-done.3.refs_4_), channel_id=1, source_target_pairs={{2,0},{3,7},{6,2},{7,11},{10,6},{11,15},{14,10},{15,13},{12,14},{1... | collective-permute-start | bytes 393224 | tf_op jit(solution)/shard_map/ppermute | solution.py:243
  16.7 6.8 %copy-start.2 = (s32[16,16]{1,0:T(8,128)S(1)}, s32[16,16]{1,0:T(8,128)}, u32[]{:S(2)}) copy-start(s32[16,16]{1,0:T(8,128)} %constant.11.clone.table) | copy-start | bytes 3076
  16.7 6.8 %collective-permute-start.4 = (bf16[80,4096]{1,0:T(8,128)(2,1)S(1)}, bf16[80,4096]{1,0:T(8,128)(2,1)S(1)}, u32[]{:S(2)}, u32[]{:S(2)}) collective-permute-start(bf16[80,4096]{1,0:T(8,128)(2,1)S(1)} %pack.1), channel_id=1, source_target_pairs={{0,1},{1,0},{2,3},{3,2},{4,5},{5,4},{6,7},{7,6},{8,9},{9,8},{10,11... | collective-permute-start | bytes 1966088 | tf_op jit(solution)/shard_map/ppermute | solution.py:246
  16.8 13.1 %collective-permute-start.11 = (bf16[128,1792]{1,0:T(8,128)(2,1)S(1)}, bf16[128,1792]{1,0:T(8,128)(2,1)S(1)}, u32[]{:S(2)}, u32[]{:S(2)}) collective-permute-start(bf16[128,1792]{1,0:T(8,128)(2,1)S(1)} %copy-done.1), channel_id=1, source_target_pairs={{0,16},{16,0},{1,17},{17,1},{2,18},{18,2},{3,19},{19,3},{4,20},{20... | collective-permute-start | bytes 1376264 | tf_op jit(solution)/shard_map/ppermute | solution.py:249
  21.6 1.4 %collective-permute-start.10 = (bf16[16,4096]{1,0:T(8,128)(2,1)S(1)}, bf16[16,4096]{1,0:T(8,128)(2,1)S(1)}, u32[]{:S(2)}, u32[]{:S(2)}) collective-permute-start(bf16[16,4096]{1,0:T(8,128)(2,1)S(1)} %collective-permute-done.7.refs_10_), channel_id=1, source_target_pairs={{0,1},{1,0},{2,3},{3,2},{4,5},{5,4},{6,7},{7,6},{8,9},{9,8},{10,11... | collective-permute-start | bytes 393224 | tf_op jit(solution)/shard_map/ppermute | solution.py:246
  21.8 1.4 %collective-permute-start.8 = (bf16[16,4096]{1,0:T(8,128)(2,1)S(1)}, bf16[16,4096]{1,0:T(8,128)(2,1)S(1)}, u32[]{:S(2)}, u32[]{:S(2)}) collective-permute-start(bf16[16,4096]{1,0:T(8,128)(2,1)S(1)} %collective-permute-done.5.refs_6_), channel_id=1, source_target_pairs={{0,1},{1,0},{2,3},{3,2},{4,5},{5,4},{6,7},{7,6},{8,9},{9,8},{10,11... | collective-permute-start | bytes 393224 | tf_op jit(solution)/shard_map/ppermute | solution.py:246
  22.2 1.3 %collective-permute-start.9 = (bf16[16,4096]{1,0:T(8,128)(2,1)S(1)}, bf16[16,4096]{1,0:T(8,128)(2,1)S(1)}, u32[]{:S(2)}, u32[]{:S(2)}) collective-permute-start(bf16[16,4096]{1,0:T(8,128)(2,1)S(1)} %collective-permute-done.6.refs_8_), channel_id=1, source_target_pairs={{0,1},{1,0},{2,3},{3,2},{4,5},{5,4},{6,7},{7,6},{8,9},{9,8},{10,11... | collective-permute-start | bytes 393224 | tf_op jit(solution)/shard_map/ppermute | solution.py:246
  26.6 13.0 %collective-permute-start.13 = (s16[912,128]{1,0:T(8,128)(2,1)S(1)}, s16[912,128]{1,0:T(8,128)(2,1)S(1)}, u32[]{:S(2)}, u32[]{:S(2)}) collective-permute-start(s16[912,128]{1,0:T(8,128)(2,1)S(1)} %get-tuple-element.43), channel_id=1, source_target_pairs={{0,16},{16,0},{1,17},{17,1},{2,18},{18,2},{3,19},{19,3},{4,20},{20... | collective-permute-start | bytes 700424 | tf_op jit(solution)/shard_map/ppermute | solution.py:249
  32.1 8.4 %collective-permute-start.12 = (s16[912,128]{1,0:T(8,128)(2,1)S(1)}, s16[912,128]{1,0:T(8,128)(2,1)S(1)}, u32[]{:S(2)}, u32[]{:S(2)}) collective-permute-start(s16[912,128]{1,0:T(8,128)(2,1)S(1)} %get-tuple-element.41), channel_id=1, source_target_pairs={{0,16},{16,0},{1,17},{17,1},{2,18},{18,2},{3,19},{19,3},{4,20},{20... | collective-permute-start | bytes 700424 | tf_op jit(solution)/shard_map/ppermute | solution.py:249

commit v13 on v12

--- a/solution.py
+++ b/solution.py
@@ -284,7 +284,7 @@
             pltpu.SemaphoreType.DMA((early,)),
         ],
         compiler_params=params(),
-        cost_estimate=cost(early * BLOCK * width, 2 * early * BLOCK * width),
+        cost_estimate=cost(1 << 34, BLOCK),
         name="spread_and_keep",
     )(place, weight, block_mask)
 
@@ -305,13 +305,11 @@
             out_shape=pltpu.VMEM((late * BLOCK, width), bf16),
             scratch_shapes=[pltpu.SemaphoreType.DMA((late,))],
             compiler_params=params(),
-            cost_estimate=cost(late * BLOCK * width, 2 * late * BLOCK * width),
+            cost_estimate=cost(BLOCK, BLOCK),
             name="keep",
         )(spread, weight)
         kepts.append(kept_late)
-    kepts[-1], inputs, *ready = lax.optimization_barrier(
-        (kepts[-1], inputs, *(held[j] for j in far))
-    )
+    kepts[-1], *ready = lax.optimization_barrier((kepts[-1], *(held[j] for j in far)))
     held.update(zip(far, ready, strict=True))
     acts = [inputs] + [send_row(inputs, k) for k in range(1, n_rows)]
     for j in range(3, n_chips // 2 + 1):
@@ -321,7 +319,9 @@
             held[-j] = send_ring(held[by - j], -by)
 
     if n_pieces > 1:
-        weight, held[1], held[-1] = lax.optimization_barrier((weight, held[1], held[-1]))
+        weight, held[1], held[-1], *acts = lax.optimization_barrier(
+            (weight, held[1], held[-1], *acts)
+        )
         rest = pl.pallas_call(
             functools.partial(fetch_kernel, piece_blocks),
             in_specs=[in_hbm()],

time: 41.5 us -> 42.5 us (1.024)
  waiting for transfers between devices: 3.74 us -> 5.23 us
  starting transfers between devices: 15.8 us -> 15.3 us
    ppermute x7, waiting for transfers between devices: 0.82 us -> 2.22 us  [send_ring(): return lax.ppermute(x, 'col', perm)]
    ppermute x3, starting transfers between devices: 4.7 us -> 4.01 us  [send_row(): lax.ppermute(x, 'row', [(r, (r + by) % n_rows) for r in range(n_rows)])]
    ppermute x7, starting transfers between devices: 10.3 us -> 10.8 us  [send_ring(): return lax.ppermute(x, 'col', perm)]
  transfers between devices with their start and end apart: 14 -> 14, of which waited for: 5 -> 6; matrix products, arithmetic and copies ran while one was open for 0% -> 0% of each run, Pallas kernels for 49% -> 40%
where the time goes in v13:
time: 42.5 us; the launch traced here: 42.4 us
  Pallas kernels  21 us (49%)
  starting transfers between devices  15.3 us (36%)
  waiting for transfers between devices  5.23 us (12%)
  between operations  0.75 us (2%)
    ppermute x7, starting transfers between devices, send_ring(): return lax.ppermute(x, 'col', perm)  10.8 us
    pallas_call x1, Pallas kernels, per_device(): pl.pallas_call(functools.partial(weight_grad_kernel, chunk), in_specs=[in...  6.04 us
    ppermute x3, starting transfers between devices, send_row(): lax.ppermute(x, 'row', [(r, (r + by) % n_rows) for r in range(n_rows)])  4.01 us
    pallas_call x1, Pallas kernels, per_device(): pl.pallas_call(functools.partial(fetch_kernel, piece_blocks), in_specs=[i...  3.18 us
    pallas_call x1, Pallas kernels, per_device(): pl.pallas_call(functools.partial(first_terms_kernel, n_shards, len(kepts)...  3.09 us
    pallas_call x1, Pallas kernels, per_device(): pl.pallas_call(spread_and_keep_kernel, in_specs=[in_smem(), in_hbm(), in_...  2.53 us
    pallas_call x1, Pallas kernels, per_device(): pl.pallas_call(functools.partial(keep_kernel, early), in_specs=[in_vmem()...  2.29 us
    ppermute x7, waiting for transfers between devices, send_ring(): return lax.ppermute(x, 'col', perm)  2.22 us
  transfers between devices with their start and end apart: 14, of which 6 were waited for; matrix products, arithmetic and copies ran while one was open for 0% of the time, Pallas kernels for 40%

profile of v13, /device:TPU:0, one launch (start us, length us, event | category | flops | bytes accessed | tf_op | source)
XLA Modules:
  0.0 42.4 jit_solution(160520952667847136)
XLA Ops:
  0.6 4.1 %collective-permute-start.4 = (bf16[16,4096]{1,0:T(8,128)(2,1)}, bf16[16,4096]{1,0:T(8,128)(2,1)S(1)}, u32[]{:S(2)}, u32[]{:S(2)}) collective-permute-start(bf16[16,4096]{1,0:T(8,128)(2,1)} %refs_0_.3), channel_id=1, source_target_pairs={{2,4},{3,11},{6,0},{7,15},{10,2},{11,13},{14,6},{15,9},{12,10},{13... | collective-permute-start | bytes 393224 | tf_op jit(solution)/shard_map/ppermute | solution.py:243
  4.7 0.0 collective-permute-start.3
  4.7 1.9 %collective-permute-start.2 = (bf16[128,1792]{1,0:T(8,128)(2,1)}, bf16[128,1792]{1,0:T(8,128)(2,1)S(1)}, u32[]{:S(2)}, u32[]{:S(2)}) collective-permute-start(bf16[128,1792]{1,0:T(8,128)(2,1)} %refs_0_.4), channel_id=1, source_target_pairs={{0,16},{16,0},{1,17},{17,1},{2,18},{18,2},{3,19},{19,3},{4,20},{20... | collective-permute-start | bytes 1376264 | tf_op jit(solution)/shard_map/ppermute | solution.py:249
  6.6 0.1 pad_add_fusion.place
  6.6 0.0 copy-start
  6.7 2.5 %spread_and_keep.1 = (bf16[384,4096]{1,0:T(8,128)(2,1)S(1)}, f32[14,4096]{1,0:T(8,128)S(1)}) custom-call(s32[2]{0:T(128)S(1)} %pad_add_fusion.place, bf16[1792,4096]{1,0:T(8,128)(2,1)} %weight.4, s32[14,64]{1,0:T(8,128)} %mask.1), custom_call_target="tpu_custom_call" | custom-call | flops 17179869184 | bytes 128 | tf_op jit(solution)/shard_map/spread_and_keep/pallas_call | solution.py:273
  9.2 0.0 copy-done
  9.2 1.6 %collective-permute-start.1 = (bf16[16,4096]{1,0:T(8,128)(2,1)S(1)}, bf16[16,4096]{1,0:T(8,128)(2,1)S(1)}, u32[]{:S(2)}, u32[]{:S(2)}) collective-permute-start(bf16[16,4096]{1,0:T(8,128)(2,1)S(1)} %copy-done), channel_id=1, source_target_pairs={{2,0},{3,7},{6,2},{7,11},{10,6},{11,15},{14,10},{15,13},{12,14},{1... | collective-permute-start | bytes 393224 | tf_op jit(solution)/shard_map/ppermute | solution.py:243
  10.8 0.4 %collective-permute-start = (bf16[16,4096]{1,0:T(8,128)(2,1)S(1)}, bf16[16,4096]{1,0:T(8,128)(2,1)S(1)}, u32[]{:S(2)}, u32[]{:S(2)}) collective-permute-start(bf16[16,4096]{1,0:T(8,128)(2,1)S(1)} %copy-done), channel_id=1, source_target_pairs={{2,6},{3,1},{6,10},{7,3},{10,14},{11,7},{14,12},{15,11},{12,8},{13... | collective-permute-start | bytes 393224 | tf_op jit(solution)/shard_map/ppermute | solution.py:243
  11.3 2.3 %keep.1.refs_13_ = bf16[512,4096]{1,0:T(8,128)(2,1)S(1)} custom-call(f32[14,4096]{1,0:T(8,128)S(1)} %get-tuple-element.29.spread, bf16[1792,4096]{1,0:T(8,128)(2,1)} %weight.4), custom_call_target="tpu_custom_call" | custom-call | flops 128 | bytes 128 | tf_op jit(solution)/shard_map/keep/pallas_call | solution.py:301
  13.6 0.0 collective-permute-done.4.refs_4_
  13.6 0.0 collective-permute-done.3.refs_3_
  13.6 2.6 %collective-permute-start.8 = (bf16[16,4096]{1,0:T(8,128)(2,1)S(1)}, bf16[16,4096]{1,0:T(8,128)(2,1)S(1)}, u32[]{:S(2)}, u32[]{:S(2)}) collective-permute-start(bf16[16,4096]{1,0:T(8,128)(2,1)S(1)} %collective-permute-done.3.refs_3_), channel_id=1, source_target_pairs={{2,10},{3,5},{6,14},{7,1},{10,12},{11,3},{14,8},{15,7},{12,4},{13,... | collective-permute-start | bytes 393224 | tf_op jit(solution)/shard_map/ppermute | solution.py:243
  16.2 1.6 %collective-permute-start.6 = (bf16[16,4096]{1,0:T(8,128)(2,1)S(1)}, bf16[16,4096]{1,0:T(8,128)(2,1)S(1)}, u32[]{:S(2)}, u32[]{:S(2)}) collective-permute-start(bf16[16,4096]{1,0:T(8,128)(2,1)S(1)} %collective-permute-done.3.refs_3_), channel_id=1, source_target_pairs={{2,6},{3,1},{6,10},{7,3},{10,14},{11,7},{14,12},{15,11},{12,8},{13... | collective-permute-start | bytes 393224 | tf_op jit(solution)/shard_map/ppermute | solution.py:243
  17.7 0.0 collective-permute-done.1.refs_2_
  17.7 0.4 %collective-permute-start.7 = (bf16[16,4096]{1,0:T(8,128)(2,1)S(1)}, bf16[16,4096]{1,0:T(8,128)(2,1)S(1)}, u32[]{:S(2)}, u32[]{:S(2)}) collective-permute-start(bf16[16,4096]{1,0:T(8,128)(2,1)S(1)} %collective-permute-done.4.refs_4_), channel_id=1, source_target_pairs={{2,0},{3,7},{6,2},{7,11},{10,6},{11,15},{14,10},{15,13},{12,14},{1... | collective-permute-start | bytes 393224 | tf_op jit(solution)/shard_map/ppermute | solution.py:243
  18.2 0.0 collective-permute-done.refs_1_
  18.2 0.0 collective-permute-done.2.refs_1_
  18.2 0.0 copy-start.2
  18.3 0.1 collective-permute-start.5
  18.3 3.2 %fetch.1.weight = bf16[896,4096]{1,0:T(8,128)(2,1)S(1)} custom-call(bf16[1792,4096]{1,0:T(8,128)(2,1)} %weight.4), custom_call_target="tpu_custom_call" | custom-call | flops 17179869184 | bytes 7340032 | tf_op jit(solution)/shard_map/fetch/pallas_call | solution.py:325
  21.5 1.2 %collective-permute-done.7.refs_8_ = bf16[16,4096]{1,0:T(8,128)(2,1)S(1)} collective-permute-done((bf16[16,4096]{1,0:T(8,128)(2,1)S(1)}, bf16[16,4096]{1,0:T(8,128)(2,1)S(1)}, u32[]{:S(2)}, u32[]{:S(2)}) %collective-permute-start.7) | collective-permute-done | bytes 131104 | tf_op jit(solution)/shard_map/ppermute | solution.py:243
  22.7 0.0 collective-permute-done.8.refs_10_
  22.7 1.0 %collective-permute-done.6.refs_6_ = bf16[16,4096]{1,0:T(8,128)(2,1)S(1)} collective-permute-done((bf16[16,4096]{1,0:T(8,128)(2,1)S(1)}, bf16[16,4096]{1,0:T(8,128)(2,1)S(1)}, u32[]{:S(2)}, u32[]{:S(2)}) %collective-permute-start.6) | collective-permute-done | bytes 131104 | tf_op jit(solution)/shard_map/ppermute | solution.py:243
  23.7 0.0 collective-permute-start.9
  23.7 0.5 %collective-permute-start.10 = (bf16[16,4096]{1,0:T(8,128)(2,1)S(1)}, bf16[16,4096]{1,0:T(8,128)(2,1)S(1)}, u32[]{:S(2)}, u32[]{:S(2)}) collective-permute-start(bf16[16,4096]{1,0:T(8,128)(2,1)S(1)} %collective-permute-done.7.refs_8_), channel_id=1, source_target_pairs={{0,1},{1,0},{2,3},{3,2},{4,5},{5,4},{6,7},{7,6},{8,9},{9,8},{10,11... | collective-permute-start | bytes 393224 | tf_op jit(solution)/shard_map/ppermute | solution.py:246
  24.2 0.0 collective-permute-start.11
  24.3 0.8 %collective-permute-done.9.refs_7_ = bf16[16,4096]{1,0:T(8,128)(2,1)S(1)} collective-permute-done((bf16[16,4096]{1,0:T(8,128)(2,1)S(1)}, bf16[16,4096]{1,0:T(8,128)(2,1)S(1)}, u32[]{:S(2)}, u32[]{:S(2)}) %collective-permute-start.9) | collective-permute-done | bytes 131104 | tf_op jit(solution)/shard_map/ppermute | solution.py:246
  25.1 0.2 collective-permute-done.10.refs_9_
  25.3 0.3 collective-permute-done.11.refs_11_
  25.6 0.0 collective-permute-done.5.refs_5_
  25.6 0.0 copy-done.2
  25.6 0.0 copy-start.1
  25.6 3.1 %first_terms.1 = (bf16[256,4096]{1,0:T(8,128)(2,1)S(1)}, bf16[4096,256]{1,0:T(8,128)(2,1)S(1)}, f32[896,128]{1,0:T(8,128)S(1)}, s16[912,128]{1,0:T(8,128)(2,1)S(1)}) custom-call(s32[2]{0:T(128)S(1)} %pad_add_fusion.place, s32[16,16]{1,0:T(8,128)S(1)} %copy-done.2, bf16[16,4096]{1,0:T(8,128)(2,1)S(1)} %copy-done, ...), custom_call_target="tpu_custom_call" | custom-call | flops 3670016 | bytes 458752 | tf_op jit(solution)/shard_map/first_terms/pallas_call | solution.py:353
  28.7 0.2 collective-permute-start.13
  28.9 0.0 copy-done.1
  29.0 2.1 %more_terms.1 = (f32[896,128]{1,0:T(8,128)S(1)}, s16[912,128]{1,0:T(8,128)(2,1)S(1)}, bf16[1792,256]{1,0:T(8,128)(2,1)S(1)}) custom-call(bf16[4096,256]{1,0:T(8,128)(2,1)S(1)} %get-tuple-element.38.turned, bf16[896,4096]{1,0:T(8,128)(2,1)S(1)} %fetch.1.weight, f32[14,4096]{1,0:T(8,128)S(1)} %get-tuple-element.29.spread, bf16[128,1792]{1,0:T(8,128)(2,1)S(1)} %copy-done.1, ...), custom_call_target="tpu_custom_call" | custom-call | flops 3670016 | bytes 458752 | tf_op jit(solution)/shard_map/more_terms/pallas_call | solution.py:375
  31.1 1.9 %collective-permute-start.12 = (s16[912,128]{1,0:T(8,128)(2,1)S(1)}, s16[912,128]{1,0:T(8,128)(2,1)S(1)}, u32[]{:S(2)}, u32[]{:S(2)}) collective-permute-start(s16[912,128]{1,0:T(8,128)(2,1)S(1)} %get-tuple-element.43), channel_id=1, source_target_pairs={{0,16},{16,0},{1,17},{17,1},{2,18},{18,2},{3,19},{19,3},{4,20},{20... | collective-permute-start | bytes 700424 | tf_op jit(solution)/shard_map/ppermute | solution.py:249
  33.0 6.0 %weight_grad.1 = bf16[1792,4096]{1,0:T(8,128)(2,1)} custom-call(bf16[1792,256]{1,0:T(8,128)(2,1)S(1)} %get-tuple-element.46.acts, bf16[256,4096]{1,0:T(8,128)(2,1)S(1)} %get-tuple-element.47.full, f32[14,4096]{1,0:T(8,128)S(1)} %get-tuple-element.29.spread), custom_call_target="tpu_custom_call" | custom-call | flops 3670016 | bytes 458752 | tf_op jit(solution)/shard_map/weight_grad/pallas_call | solution.py:397
  39.0 0.0 collective-permute-done.13.refs_0_
  39.1 0.8 %add_terms.2.refs_1_ = bf16[128,1792]{1,0:T(8,128)(2,1)} custom-call(f32[896,128]{1,0:T(8,128)S(1)} %get-tuple-element.44.own, s16[912,128]{1,0:T(8,128)(2,1)S(1)} %collective-permute-done.13.refs_0_), custom_call_target="tpu_custom_call" | custom-call | tf_op jit(solution)/shard_map/add_terms/pallas_call | solution.py:418
  39.9 1.7 %collective-permute-done.12.refs_0_ = s16[912,128]{1,0:T(8,128)(2,1)S(1)} collective-permute-done((s16[912,128]{1,0:T(8,128)(2,1)S(1)}, s16[912,128]{1,0:T(8,128)(2,1)S(1)}, u32[]{:S(2)}, u32[]{:S(2)}) %collective-permute-start.12) | collective-permute-done | bytes 233504 | tf_op jit(solution)/shard_map/ppermute | solution.py:249
  41.6 0.8 %add_terms.3 = bf16[128,1792]{1,0:T(8,128)(2,1)} custom-call(f32[896,128]{1,0:T(8,128)S(1)} %get-tuple-element.42.own, s16[912,128]{1,0:T(8,128)(2,1)S(1)} %collective-permute-done.12.refs_0_, bf16[128,1792]{1,0:T(8,128)(2,1)} %add_terms.2.refs_1_), custom_call_target="tpu_custom_call", output_to_operand_aliasing={{}: (2, {})} | custom-call | tf_op jit(solution)/shard_map/add_terms/pallas_call | solution.py:418
  (1 shorter events, 0.0 us)
Async XLA Ops:
  0.6 13.0 %collective-permute-start.4 = (bf16[16,4096]{1,0:T(8,128)(2,1)}, bf16[16,4096]{1,0:T(8,128)(2,1)S(1)}, u32[]{:S(2)}, u32[]{:S(2)}) collective-permute-start(bf16[16,4096]{1,0:T(8,128)(2,1)} %refs_0_.3), channel_id=1, source_target_pairs={{2,4},{3,11},{6,0},{7,15},{10,2},{11,13},{14,6},{15,9},{12,10},{13... | collective-permute-start | bytes 393224 | tf_op jit(solution)/shard_map/ppermute | solution.py:243
  4.7 8.9 %collective-permute-start.3 = (bf16[16,4096]{1,0:T(8,128)(2,1)}, bf16[16,4096]{1,0:T(8,128)(2,1)S(1)}, u32[]{:S(2)}, u32[]{:S(2)}) collective-permute-start(bf16[16,4096]{1,0:T(8,128)(2,1)} %refs_0_.3), channel_id=1, source_target_pairs={{2,10},{3,5},{6,14},{7,1},{10,12},{11,3},{14,8},{15,7},{12,4},{13,... | collective-permute-start | bytes 393224 | tf_op jit(solution)/shard_map/ppermute | solution.py:243
  4.7 13.5 %collective-permute-start.2 = (bf16[128,1792]{1,0:T(8,128)(2,1)}, bf16[128,1792]{1,0:T(8,128)(2,1)S(1)}, u32[]{:S(2)}, u32[]{:S(2)}) collective-permute-start(bf16[128,1792]{1,0:T(8,128)(2,1)} %refs_0_.4), channel_id=1, source_target_pairs={{0,16},{16,0},{1,17},{17,1},{2,18},{18,2},{3,19},{19,3},{4,20},{20... | collective-permute-start | bytes 1376264 | tf_op jit(solution)/shard_map/ppermute | solution.py:249
  6.6 2.5 %copy-start = (bf16[16,4096]{1,0:T(8,128)(2,1)S(1)}, bf16[16,4096]{1,0:T(8,128)(2,1)}, u32[]{:S(2)}) copy-start(bf16[16,4096]{1,0:T(8,128)(2,1)} %refs_0_.3) | copy-start | bytes 393220
  9.2 8.5 %collective-permute-start.1 = (bf16[16,4096]{1,0:T(8,128)(2,1)S(1)}, bf16[16,4096]{1,0:T(8,128)(2,1)S(1)}, u32[]{:S(2)}, u32[]{:S(2)}) collective-permute-start(bf16[16,4096]{1,0:T(8,128)(2,1)S(1)} %copy-done), channel_id=1, source_target_pairs={{2,0},{3,7},{6,2},{7,11},{10,6},{11,15},{14,10},{15,13},{12,14},{1... | collective-permute-start | bytes 393224 | tf_op jit(solution)/shard_map/ppermute | solution.py:243
  10.8 7.4 %collective-permute-start = (bf16[16,4096]{1,0:T(8,128)(2,1)S(1)}, bf16[16,4096]{1,0:T(8,128)(2,1)S(1)}, u32[]{:S(2)}, u32[]{:S(2)}) collective-permute-start(bf16[16,4096]{1,0:T(8,128)(2,1)S(1)} %copy-done), channel_id=1, source_target_pairs={{2,6},{3,1},{6,10},{7,3},{10,14},{11,7},{14,12},{15,11},{12,8},{13... | collective-permute-start | bytes 393224 | tf_op jit(solution)/shard_map/ppermute | solution.py:243
  13.6 9.1 %collective-permute-start.8 = (bf16[16,4096]{1,0:T(8,128)(2,1)S(1)}, bf16[16,4096]{1,0:T(8,128)(2,1)S(1)}, u32[]{:S(2)}, u32[]{:S(2)}) collective-permute-start(bf16[16,4096]{1,0:T(8,128)(2,1)S(1)} %collective-permute-done.3.refs_3_), channel_id=1, source_target_pairs={{2,10},{3,5},{6,14},{7,1},{10,12},{11,3},{14,8},{15,7},{12,4},{13,... | collective-permute-start | bytes 393224 | tf_op jit(solution)/shard_map/ppermute | solution.py:243
  16.2 7.6 %collective-permute-start.6 = (bf16[16,4096]{1,0:T(8,128)(2,1)S(1)}, bf16[16,4096]{1,0:T(8,128)(2,1)S(1)}, u32[]{:S(2)}, u32[]{:S(2)}) collective-permute-start(bf16[16,4096]{1,0:T(8,128)(2,1)S(1)} %collective-permute-done.3.refs_3_), channel_id=1, source_target_pairs={{2,6},{3,1},{6,10},{7,3},{10,14},{11,7},{14,12},{15,11},{12,8},{13... | collective-permute-start | bytes 393224 | tf_op jit(solution)/shard_map/ppermute | solution.py:243
  17.7 5.0 %collective-permute-start.7 = (bf16[16,4096]{1,0:T(8,128)(2,1)S(1)}, bf16[16,4096]{1,0:T(8,128)(2,1)S(1)}, u32[]{:S(2)}, u32[]{:S(2)}) collective-permute-start(bf16[16,4096]{1,0:T(8,128)(2,1)S(1)} %collective-permute-done.4.refs_4_), channel_id=1, source_target_pairs={{2,0},{3,7},{6,2},{7,11},{10,6},{11,15},{14,10},{15,13},{12,14},{1... | collective-permute-start | bytes 393224 | tf_op jit(solution)/shard_map/ppermute | solution.py:243
  18.2 7.4 %copy-start.2 = (s32[16,16]{1,0:T(8,128)S(1)}, s32[16,16]{1,0:T(8,128)}, u32[]{:S(2)}) copy-start(s32[16,16]{1,0:T(8,128)} %constant.11.clone.table) | copy-start | bytes 3076
  18.3 7.3 %collective-permute-start.5 = (bf16[80,4096]{1,0:T(8,128)(2,1)S(1)}, bf16[80,4096]{1,0:T(8,128)(2,1)S(1)}, u32[]{:S(2)}, u32[]{:S(2)}) collective-permute-start(bf16[80,4096]{1,0:T(8,128)(2,1)S(1)} %pack.1), channel_id=1, source_target_pairs={{0,1},{1,0},{2,3},{3,2},{4,5},{5,4},{6,7},{7,6},{8,9},{9,8},{10,11... | collective-permute-start | bytes 1966088 | tf_op jit(solution)/shard_map/ppermute | solution.py:246
  23.7 1.3 %collective-permute-start.9 = (bf16[16,4096]{1,0:T(8,128)(2,1)S(1)}, bf16[16,4096]{1,0:T(8,128)(2,1)S(1)}, u32[]{:S(2)}, u32[]{:S(2)}) collective-permute-start(bf16[16,4096]{1,0:T(8,128)(2,1)S(1)} %collective-permute-done.6.refs_6_), channel_id=1, source_target_pairs={{0,1},{1,0},{2,3},{3,2},{4,5},{5,4},{6,7},{7,6},{8,9},{9,8},{10,11... | collective-permute-start | bytes 393224 | tf_op jit(solution)/shard_map/ppermute | solution.py:246
  23.7 1.5 %collective-permute-start.10 = (bf16[16,4096]{1,0:T(8,128)(2,1)S(1)}, bf16[16,4096]{1,0:T(8,128)(2,1)S(1)}, u32[]{:S(2)}, u32[]{:S(2)}) collective-permute-start(bf16[16,4096]{1,0:T(8,128)(2,1)S(1)} %collective-permute-done.7.refs_8_), channel_id=1, source_target_pairs={{0,1},{1,0},{2,3},{3,2},{4,5},{5,4},{6,7},{7,6},{8,9},{9,8},{10,11... | collective-permute-start | bytes 393224 | tf_op jit(solution)/shard_map/ppermute | solution.py:246
  24.2 1.3 %collective-permute-start.11 = (bf16[16,4096]{1,0:T(8,128)(2,1)S(1)}, bf16[16,4096]{1,0:T(8,128)(2,1)S(1)}, u32[]{:S(2)}, u32[]{:S(2)}) collective-permute-start(bf16[16,4096]{1,0:T(8,128)(2,1)S(1)} %collective-permute-done.8.refs_10_), channel_id=1, source_target_pairs={{0,1},{1,0},{2,3},{3,2},{4,5},{5,4},{6,7},{7,6},{8,9},{9,8},{10,11... | collective-permute-start | bytes 393224 | tf_op jit(solution)/shard_map/ppermute | solution.py:246
  25.6 3.3 %copy-start.1 = (bf16[128,1792]{1,0:T(8,128)(2,1)S(1)}, bf16[128,1792]{1,0:T(8,128)(2,1)}, u32[]{:S(2)}) copy-start(bf16[128,1792]{1,0:T(8,128)(2,1)} %refs_0_.4) | copy-start | bytes 1376260
  28.7 10.3 %collective-permute-start.13 = (s16[912,128]{1,0:T(8,128)(2,1)S(1)}, s16[912,128]{1,0:T(8,128)(2,1)S(1)}, u32[]{:S(2)}, u32[]{:S(2)}) collective-permute-start(s16[912,128]{1,0:T(8,128)(2,1)S(1)} %get-tuple-element.45), channel_id=1, source_target_pairs={{0,16},{16,0},{1,17},{17,1},{2,18},{18,2},{3,19},{19,3},{4,20},{20... | collective-permute-start | bytes 700424 | tf_op jit(solution)/shard_map/ppermute | solution.py:249
  31.1 10.5 %collective-permute-start.12 = (s16[912,128]{1,0:T(8,128)(2,1)S(1)}, s16[912,128]{1,0:T(8,128)(2,1)S(1)}, u32[]{:S(2)}, u32[]{:S(2)}) collective-permute-start(s16[912,128]{1,0:T(8,128)(2,1)S(1)} %get-tuple-element.43), channel_id=1, source_target_pairs={{0,16},{16,0},{1,17},{17,1},{2,18},{18,2},{3,19},{19,3},{4,20},{20... | collective-permute-start | bytes 700424 | tf_op jit(solution)/shard_map/ppermute | solution.py:249

commit v14 on v13

--- a/solution.py
+++ b/solution.py
@@ -45,19 +45,12 @@
     )
 
 
-def spread_and_keep_kernel(place, weight, mask, kept, spread, mask_here, mask_sem, sems):
-    rows, width = kept.shape
-    mask_copy = pltpu.make_async_copy(mask, mask_here, mask_sem)
-    mask_copy.start()
-    fetch(weight, 0, kept, sems)
-    mask_copy.wait()
+def spread_kernel(place, mask, spread, mask_here, mask_sem):
+    copy = pltpu.make_async_copy(mask, mask_here, mask_sem)
+    copy.start()
+    copy.wait()
+    width = spread.shape[1]
     spread[...] = wide_mask(mask_here[...], place[0] * (width // BLOCK), width)
-    drop_blocks(weight, 0, kept, spread, sems)
-
-
-def keep_kernel(first, spread, weight, kept, sems):
-    fetch(weight, first, kept, sems)
-    drop_blocks(weight, first, kept, spread, sems)
 
 
 def row_copy(weight, first, here, sems, block):
@@ -76,16 +69,6 @@
 def fetched(weight, first, here, sems):
     blocks = here.shape[0] // BLOCK
     lax.fori_loop(0, blocks, lambda b, _: (row_copy(weight, first, here, sems, b).wait(), 0)[1], 0)
-
-
-def drop_blocks(weight, first, kept, spread, sems):
-    def one(b, _):
-        row_copy(weight, first, kept, sems, b).wait()
-        at = pl.ds(pl.multiple_of(b * BLOCK, BLOCK), BLOCK)
-        kept[at, :] = kept[at, :] * spread[pl.ds(first + b, 1), :].astype(kept.dtype)
-        return 0
-
-    lax.fori_loop(0, kept.shape[0] // BLOCK, one, 0)
 
 
 def pack_kernel(*refs):
@@ -123,9 +106,25 @@
     fetched(weight, first, out, sems)
 
 
-def first_terms_kernel(n_shards, n_kept, n_parts, shift, chunk, place, table, *refs):
-    shards, kepts = refs[:n_shards], refs[n_shards : n_shards + n_kept]
-    full, turned, own, *outs, total = refs[n_shards + n_kept :]
+def kept_blocks(pieces, spread, cols):
+    kept = []
+    for weight, first, end, row in pieces:
+        factors = spread[row : row + end - first, cols].astype(jnp.bfloat16)
+        for b in range(first, end):
+            block = weight[b * BLOCK : (b + 1) * BLOCK, cols]
+            kept.append(block * factors[b - first : b - first + 1, :])
+    return jnp.concatenate(kept, axis=0)
+
+
+def first_terms_kernel(n_shards, n_parts, shift, chunk, blocks, place, table, *refs):
+    shards = refs[:n_shards]
+    *weights, spread, full, turned, own = refs[n_shards : -n_parts - 1]
+    outs, total = refs[-n_parts - 1 : -1], refs[-1]
+    pieces, done = [], 0
+    for weight in weights:
+        end = min(weight.shape[0] // BLOCK, blocks - done)
+        pieces.append((weight, 0, end, done))
+        done += end
     rows = shards[0].shape[0]
     n_cols = table.shape[0]
     slots = [(shard, at) for shard in shards for at in range(0, shard.shape[0], rows)]
@@ -135,25 +134,19 @@
     for c in range(0, full.shape[1], chunk):
         cols = slice(c, c + chunk)
         turned[cols, :] = full[:, cols].T
-        at = 0
-        for kept in kepts:
-            to = slice(at, at + kept.shape[0])
-            terms = jnp.dot(kept[:, cols], turned[cols, :], preferred_element_type=jnp.float32)
-            total[to, :] = terms if c == 0 else total[to, :] + terms
-            at += kept.shape[0]
+        kept = kept_blocks(pieces, spread, cols)
+        terms = jnp.dot(kept, turned[cols, :], preferred_element_type=jnp.float32)
+        total[...] = terms if c == 0 else total[...] + terms
     store_terms(total, own, outs)
 
 
 def more_terms_kernel(n_parts, first, chunk, turned, weight, spread, *refs):
     acts, (own, *outs, acts_turned, total) = refs[: n_parts + 1], refs[n_parts + 1 :]
-    blocks = own.shape[0] // BLOCK
+    end = weight.shape[0] // BLOCK
+    pieces = [(weight, end - own.shape[0] // BLOCK, end, first)]
     for c in range(0, weight.shape[1], chunk):
         cols = slice(c, c + chunk)
-        factors = spread[first : first + blocks, cols].astype(jnp.bfloat16)
-        kept = jnp.concatenate(
-            [weight[b * BLOCK : (b + 1) * BLOCK, cols] * factors[b : b + 1, :] for b in range(blocks)],
-            axis=0,
-        )
+        kept = kept_blocks(pieces, spread, cols)
         terms = jnp.dot(kept, turned[cols, :], preferred_element_type=jnp.float32)
         total[...] = terms if c == 0 else total[...] + terms
     store_terms(total, own, outs)
@@ -269,24 +262,28 @@
     weight = pltpu.with_memory_space_constraint(weight, pltpu.HBM)
     block_mask = pltpu.with_memory_space_constraint(block_mask, pltpu.HBM)
     piece_blocks = piece // BLOCK
-    early = max(1, piece_blocks * 3 // 7)
-    kept_early, spread = pl.pallas_call(
-        spread_and_keep_kernel,
-        in_specs=[in_smem(), in_hbm(), in_hbm()],
-        out_specs=[in_vmem()] * 2,
-        out_shape=[
-            pltpu.VMEM((early * BLOCK, width), bf16),
-            pltpu.VMEM((blocks, width), jnp.float32),
-        ],
-        scratch_shapes=[
-            pltpu.VMEM(block_mask.shape, jnp.int32),
-            pltpu.SemaphoreType.DMA,
-            pltpu.SemaphoreType.DMA((early,)),
-        ],
+    spread = pl.pallas_call(
+        spread_kernel,
+        in_specs=[in_smem(), in_hbm()],
+        out_specs=in_vmem(),
+        out_shape=pltpu.VMEM((blocks, width), jnp.float32),
+        scratch_shapes=[pltpu.VMEM(block_mask.shape, jnp.int32), pltpu.SemaphoreType.DMA],
         compiler_params=params(),
         cost_estimate=cost(1 << 34, BLOCK),
-        name="spread_and_keep",
-    )(place, weight, block_mask)
+        name="spread",
+    )(place, block_mask)
+
+    def fetch_rows(first, count, flops):
+        return pl.pallas_call(
+            functools.partial(fetch_kernel, first),
+            in_specs=[in_hbm()],
+            out_specs=in_vmem(),
+            out_shape=pltpu.VMEM((count * BLOCK, width), bf16),
+            scratch_shapes=[pltpu.SemaphoreType.DMA((count,))],
+            compiler_params=params(),
+            cost_estimate=cost(flops, BLOCK),
+            name="fetch",
+        )(weight)
 
     held = {0: grad_output}
     for j in (2, -2):
@@ -295,21 +292,10 @@
     far = [j for j in held if j]
     spread, again = lax.optimization_barrier((spread, grad_output))
     held[1], held[-1] = send_ring(again, 1), send_ring(again, -1)
-    kepts = [kept_early]
-    if early < piece_blocks:
-        late = piece_blocks - early
-        kept_late = pl.pallas_call(
-            functools.partial(keep_kernel, early),
-            in_specs=[in_vmem(), in_hbm()],
-            out_specs=in_vmem(),
-            out_shape=pltpu.VMEM((late * BLOCK, width), bf16),
-            scratch_shapes=[pltpu.SemaphoreType.DMA((late,))],
-            compiler_params=params(),
-            cost_estimate=cost(BLOCK, BLOCK),
-            name="keep",
-        )(spread, weight)
-        kepts.append(kept_late)
-    kepts[-1], *ready = lax.optimization_barrier((kepts[-1], *(held[j] for j in far)))
+    n_soon = max(1, blocks * 5 // 14)
+    weight, spread = lax.optimization_barrier((weight, spread))
+    soon = fetch_rows(0, n_soon, BLOCK)
+    soon, *ready = lax.optimization_barrier((soon, *(held[j] for j in far)))
     held.update(zip(far, ready, strict=True))
     acts = [inputs] + [send_row(inputs, k) for k in range(1, n_rows)]
     for j in range(3, n_chips // 2 + 1):
@@ -318,22 +304,12 @@
         if 2 * j < n_chips:
             held[-j] = send_ring(held[by - j], -by)
 
-    if n_pieces > 1:
-        weight, held[1], held[-1], *acts = lax.optimization_barrier(
-            (weight, held[1], held[-1], *acts)
-        )
-        rest = pl.pallas_call(
-            functools.partial(fetch_kernel, piece_blocks),
-            in_specs=[in_hbm()],
-            out_specs=in_vmem(),
-            out_shape=pltpu.VMEM((piece, width), bf16),
-            scratch_shapes=[pltpu.SemaphoreType.DMA((piece_blocks,))],
-            compiler_params=params(),
-            cost_estimate=cost(1 << 34, 2 * piece * width),
-            name="fetch",
-        )(weight)
-        rest, *ready = lax.optimization_barrier((rest, *(held[j] for j in last)))
-        held.update(zip(last, ready, strict=True))
+    weight, held[1], held[-1], *acts = lax.optimization_barrier(
+        (weight, held[1], held[-1], *acts)
+    )
+    rest = fetch_rows(n_soon, blocks - n_soon, 1 << 34)
+    rest, *ready = lax.optimization_barrier((rest, *(held[j] for j in last)))
+    held.update(zip(last, ready, strict=True))
     packed = pl.pallas_call(
         pack_kernel,
         in_specs=[in_vmem()] * len(near),
@@ -352,9 +328,9 @@
     small_cost = cost(piece * width, piece * width // 8)
     full, turned, own, *coded = pl.pallas_call(
         functools.partial(
-            first_terms_kernel, n_shards, len(kepts), n_parts, tokens // shard_rows, chunk
+            first_terms_kernel, n_shards, n_parts, tokens // shard_rows, chunk, piece_blocks
         ),
-        in_specs=[in_smem()] * 2 + [in_vmem()] * (n_shards + len(kepts)),
+        in_specs=[in_smem()] * 2 + [in_vmem()] * (n_shards + 3),
         out_specs=[in_vmem()] * (3 + n_parts),
         out_shape=[
             jax.ShapeDtypeStruct((all_tokens, width), bf16),
@@ -366,7 +342,7 @@
         compiler_params=params(),
         cost_estimate=small_cost,
         name="first_terms",
-    )(place, jnp.array(table, jnp.int32), *shards, *kepts)
+    )(place, jnp.array(table, jnp.int32), *shards, soon, rest, spread)
     owns = [own]
     parts = [send_row(coded[k], k + 1) for k in range(n_parts)]
 

time: 42.5 us -> 41.8 us (0.984)
  waiting for transfers between devices: 5.23 us -> 4.6 us
    ppermute x7, waiting for transfers between devices: 2.22 us -> 1.59 us  [send_ring(): return lax.ppermute(x, 'col', perm)]
where the time goes in v14:
time: 41.8 us; the launch traced here: 41.6 us
  Pallas kernels  20.8 us (50%)
  starting transfers between devices  15.3 us (37%)
  waiting for transfers between devices  4.6 us (11%)
  between operations  0.75 us (2%)
    ppermute x7, starting transfers between devices, send_ring(): return lax.ppermute(x, 'col', perm)  10.8 us
    pallas_call x2, Pallas kernels, fetch_rows(): pl.pallas_call(functools.partial(fetch_kernel, first), in_specs=[in_hbm()...  6.33 us
    pallas_call x1, Pallas kernels, per_device(): pl.pallas_call(functools.partial(weight_grad_kernel, chunk), in_specs=[in...  6.05 us
    ppermute x3, starting transfers between devices, send_row(): lax.ppermute(x, 'row', [(r, (r + by) % n_rows) for r in range(n_rows)])  4.01 us
    pallas_call x1, Pallas kernels, per_device(): pl.pallas_call(functools.partial(first_terms_kernel, n_shards, n_parts, t...  3.17 us
    pallas_call x1, Pallas kernels, per_device(): pl.pallas_call(functools.partial(more_terms_kernel, n_parts, piece_blocks...  2.12 us
    pallas_call x2, Pallas kernels, per_device(): pl.pallas_call(functools.partial(finish_kernel, n_parts), grid=(1,), in_s...  1.68 us
    ppermute x3, waiting for transfers between devices, send_row(): lax.ppermute(x, 'row', [(r, (r + by) % n_rows) for r in range(n_rows)])  1.66 us
  transfers between devices with their start and end apart: 14, of which 6 were waited for; matrix products, arithmetic and copies ran while one was open for 0% of the time, Pallas kernels for 40%

profile of v14, /device:TPU:0, one launch (start us, length us, event | category | flops | bytes accessed | tf_op | source)
XLA Modules:
  0.0 41.6 jit_solution(5697832424264326220)
XLA Ops:
  0.6 4.1 %collective-permute-start.4 = (bf16[16,4096]{1,0:T(8,128)(2,1)}, bf16[16,4096]{1,0:T(8,128)(2,1)S(1)}, u32[]{:S(2)}, u32[]{:S(2)}) collective-permute-start(bf16[16,4096]{1,0:T(8,128)(2,1)} %refs_0_.3), channel_id=1, source_target_pairs={{2,4},{3,11},{6,0},{7,15},{10,2},{11,13},{14,6},{15,9},{12,10},{13... | collective-permute-start | bytes 393224 | tf_op jit(solution)/shard_map/ppermute | solution.py:236
  4.7 0.0 collective-permute-start.3
  4.7 1.9 %collective-permute-start.2 = (bf16[128,1792]{1,0:T(8,128)(2,1)}, bf16[128,1792]{1,0:T(8,128)(2,1)S(1)}, u32[]{:S(2)}, u32[]{:S(2)}) collective-permute-start(bf16[128,1792]{1,0:T(8,128)(2,1)} %refs_0_.4), channel_id=1, source_target_pairs={{0,16},{16,0},{1,17},{17,1},{2,18},{18,2},{3,19},{19,3},{4,20},{20... | collective-permute-start | bytes 1376264 | tf_op jit(solution)/shard_map/ppermute | solution.py:242
  6.6 0.1 pad_add_fusion.place
  6.6 0.0 copy-start
  6.7 1.4 %spread.1.refs_14_ = f32[14,4096]{1,0:T(8,128)S(1)} custom-call(s32[2]{0:T(128)S(1)} %pad_add_fusion.place, s32[14,64]{1,0:T(8,128)} %mask.1), custom_call_target="tpu_custom_call" | custom-call | flops 17179869184 | bytes 128 | tf_op jit(solution)/shard_map/spread/pallas_call | solution.py:265
  8.1 0.0 copy-done
  8.1 1.6 %collective-permute-start.1 = (bf16[16,4096]{1,0:T(8,128)(2,1)S(1)}, bf16[16,4096]{1,0:T(8,128)(2,1)S(1)}, u32[]{:S(2)}, u32[]{:S(2)}) collective-permute-start(bf16[16,4096]{1,0:T(8,128)(2,1)S(1)} %copy-done), channel_id=1, source_target_pairs={{2,0},{3,7},{6,2},{7,11},{10,6},{11,15},{14,10},{15,13},{12,14},{1... | collective-permute-start | bytes 393224 | tf_op jit(solution)/shard_map/ppermute | solution.py:236
  9.7 0.4 %collective-permute-start = (bf16[16,4096]{1,0:T(8,128)(2,1)S(1)}, bf16[16,4096]{1,0:T(8,128)(2,1)S(1)}, u32[]{:S(2)}, u32[]{:S(2)}) collective-permute-start(bf16[16,4096]{1,0:T(8,128)(2,1)S(1)} %copy-done), channel_id=1, source_target_pairs={{2,6},{3,1},{6,10},{7,3},{10,14},{11,7},{14,12},{15,11},{12,8},{13... | collective-permute-start | bytes 393224 | tf_op jit(solution)/shard_map/ppermute | solution.py:236
  10.2 2.5 %fetch.2.refs_12_ = bf16[640,4096]{1,0:T(8,128)(2,1)S(1)} custom-call(bf16[1792,4096]{1,0:T(8,128)(2,1)} %weight.1), custom_call_target="tpu_custom_call" | custom-call | flops 128 | bytes 128 | tf_op jit(solution)/shard_map/fetch/pallas_call | solution.py:277
  12.7 0.0 collective-permute-done.4.refs_4_
  12.7 0.0 collective-permute-done.3.refs_3_
  12.7 2.6 %collective-permute-start.8 = (bf16[16,4096]{1,0:T(8,128)(2,1)S(1)}, bf16[16,4096]{1,0:T(8,128)(2,1)S(1)}, u32[]{:S(2)}, u32[]{:S(2)}) collective-permute-start(bf16[16,4096]{1,0:T(8,128)(2,1)S(1)} %collective-permute-done.3.refs_3_), channel_id=1, source_target_pairs={{2,10},{3,5},{6,14},{7,1},{10,12},{11,3},{14,8},{15,7},{12,4},{13,... | collective-permute-start | bytes 393224 | tf_op jit(solution)/shard_map/ppermute | solution.py:236
  15.3 1.6 %collective-permute-start.6 = (bf16[16,4096]{1,0:T(8,128)(2,1)S(1)}, bf16[16,4096]{1,0:T(8,128)(2,1)S(1)}, u32[]{:S(2)}, u32[]{:S(2)}) collective-permute-start(bf16[16,4096]{1,0:T(8,128)(2,1)S(1)} %collective-permute-done.3.refs_3_), channel_id=1, source_target_pairs={{2,6},{3,1},{6,10},{7,3},{10,14},{11,7},{14,12},{15,11},{12,8},{13... | collective-permute-start | bytes 393224 | tf_op jit(solution)/shard_map/ppermute | solution.py:236
  16.9 0.0 collective-permute-done.1.refs_2_
  16.9 0.4 %collective-permute-start.7 = (bf16[16,4096]{1,0:T(8,128)(2,1)S(1)}, bf16[16,4096]{1,0:T(8,128)(2,1)S(1)}, u32[]{:S(2)}, u32[]{:S(2)}) collective-permute-start(bf16[16,4096]{1,0:T(8,128)(2,1)S(1)} %collective-permute-done.4.refs_4_), channel_id=1, source_target_pairs={{2,0},{3,7},{6,2},{7,11},{10,6},{11,15},{14,10},{15,13},{12,14},{1... | collective-permute-start | bytes 393224 | tf_op jit(solution)/shard_map/ppermute | solution.py:236
  17.3 0.0 collective-permute-done.refs_1_
  17.3 0.0 collective-permute-done.2.refs_1_
  17.4 0.0 copy-start.2
  17.4 0.1 collective-permute-start.5
  17.5 3.8 %fetch.3.refs_13_.weight = bf16[1152,4096]{1,0:T(8,128)(2,1)S(1)} custom-call(bf16[1792,4096]{1,0:T(8,128)(2,1)} %weight.1), custom_call_target="tpu_custom_call" | custom-call | flops 17179869184 | bytes 128 | tf_op jit(solution)/shard_map/fetch/pallas_call | solution.py:277
  21.3 0.0 copy-start.1
  21.3 0.6 %collective-permute-done.7.refs_8_ = bf16[16,4096]{1,0:T(8,128)(2,1)S(1)} collective-permute-done((bf16[16,4096]{1,0:T(8,128)(2,1)S(1)}, bf16[16,4096]{1,0:T(8,128)(2,1)S(1)}, u32[]{:S(2)}, u32[]{:S(2)}) %collective-permute-start.7) | collective-permute-done | bytes 131104 | tf_op jit(solution)/shard_map/ppermute | solution.py:236
  21.9 0.0 collective-permute-done.8.refs_10_
  21.9 1.0 %collective-permute-done.6.refs_6_ = bf16[16,4096]{1,0:T(8,128)(2,1)S(1)} collective-permute-done((bf16[16,4096]{1,0:T(8,128)(2,1)S(1)}, bf16[16,4096]{1,0:T(8,128)(2,1)S(1)}, u32[]{:S(2)}, u32[]{:S(2)}) %collective-permute-start.6) | collective-permute-done | bytes 131104 | tf_op jit(solution)/shard_map/ppermute | solution.py:236
  22.9 0.0 collective-permute-start.9
  22.9 0.5 %collective-permute-start.10 = (bf16[16,4096]{1,0:T(8,128)(2,1)S(1)}, bf16[16,4096]{1,0:T(8,128)(2,1)S(1)}, u32[]{:S(2)}, u32[]{:S(2)}) collective-permute-start(bf16[16,4096]{1,0:T(8,128)(2,1)S(1)} %collective-permute-done.7.refs_8_), channel_id=1, source_target_pairs={{0,1},{1,0},{2,3},{3,2},{4,5},{5,4},{6,7},{7,6},{8,9},{9,8},{10,11... | collective-permute-start | bytes 393224 | tf_op jit(solution)/shard_map/ppermute | solution.py:239
  23.4 0.0 collective-permute-start.11
  23.4 0.8 %collective-permute-done.9.refs_7_ = bf16[16,4096]{1,0:T(8,128)(2,1)S(1)} collective-permute-done((bf16[16,4096]{1,0:T(8,128)(2,1)S(1)}, bf16[16,4096]{1,0:T(8,128)(2,1)S(1)}, u32[]{:S(2)}, u32[]{:S(2)}) %collective-permute-start.9) | collective-permute-done | bytes 131104 | tf_op jit(solution)/shard_map/ppermute | solution.py:239
  24.2 0.2 collective-permute-done.10.refs_9_
  24.4 0.3 collective-permute-done.11.refs_11_
  24.7 0.0 collective-permute-done.5.refs_5_
  24.7 0.0 copy-done.2
  24.7 3.2 %first_terms.1 = (bf16[256,4096]{1,0:T(8,128)(2,1)S(1)}, bf16[4096,256]{1,0:T(8,128)(2,1)S(1)}, f32[896,128]{1,0:T(8,128)S(1)}, s16[912,128]{1,0:T(8,128)(2,1)S(1)}) custom-call(s32[2]{0:T(128)S(1)} %pad_add_fusion.place, s32[16,16]{1,0:T(8,128)S(1)} %copy-done.2, bf16[16,4096]{1,0:T(8,128)(2,1)S(1)} %copy-done, ...), custom_call_target="tpu_custom_call" | custom-call | flops 3670016 | bytes 458752 | tf_op jit(solution)/shard_map/first_terms/pallas_call | solution.py:329
  27.9 1.0 %collective-permute-start.13 = (s16[912,128]{1,0:T(8,128)(2,1)S(1)}, s16[912,128]{1,0:T(8,128)(2,1)S(1)}, u32[]{:S(2)}, u32[]{:S(2)}) collective-permute-start(s16[912,128]{1,0:T(8,128)(2,1)S(1)} %get-tuple-element.45), channel_id=1, source_target_pairs={{0,16},{16,0},{1,17},{17,1},{2,18},{18,2},{3,19},{19,3},{4,20},{20... | collective-permute-start | bytes 700424 | tf_op jit(solution)/shard_map/ppermute | solution.py:242
  28.9 0.0 copy-done.1
  28.9 2.1 %more_terms.1 = (f32[896,128]{1,0:T(8,128)S(1)}, s16[912,128]{1,0:T(8,128)(2,1)S(1)}, bf16[1792,256]{1,0:T(8,128)(2,1)S(1)}) custom-call(bf16[4096,256]{1,0:T(8,128)(2,1)S(1)} %get-tuple-element.39.turned, bf16[1152,4096]{1,0:T(8,128)(2,1)S(1)} %fetch.3.refs_13_.weight, f32[14,4096]{1,0:T(8,128)S(1)} %spread.1.refs_14_, bf16[128,1792]{1,0:T(8,128)(2,1)S(1)} %copy-done.1, ...), custom_call_target="tpu_custom_call" | custom-call | flops 3670016 | bytes 458752 | tf_op jit(solution)/shard_map/more_terms/pallas_call | solution.py:351
  31.0 1.2 %collective-permute-start.12 = (s16[912,128]{1,0:T(8,128)(2,1)S(1)}, s16[912,128]{1,0:T(8,128)(2,1)S(1)}, u32[]{:S(2)}, u32[]{:S(2)}) collective-permute-start(s16[912,128]{1,0:T(8,128)(2,1)S(1)} %get-tuple-element.43), channel_id=1, source_target_pairs={{0,16},{16,0},{1,17},{17,1},{2,18},{18,2},{3,19},{19,3},{4,20},{20... | collective-permute-start | bytes 700424 | tf_op jit(solution)/shard_map/ppermute | solution.py:242
  32.2 6.1 %weight_grad.1 = bf16[1792,4096]{1,0:T(8,128)(2,1)} custom-call(bf16[1792,256]{1,0:T(8,128)(2,1)S(1)} %get-tuple-element.46.acts, bf16[256,4096]{1,0:T(8,128)(2,1)S(1)} %get-tuple-element.47.full, f32[14,4096]{1,0:T(8,128)S(1)} %spread.1.refs_14_), custom_call_target="tpu_custom_call" | custom-call | flops 3670016 | bytes 458752 | tf_op jit(solution)/shard_map/weight_grad/pallas_call | solution.py:373
  38.3 0.0 collective-permute-done.13.refs_0_
  38.3 0.8 %add_terms.2.refs_1_ = bf16[128,1792]{1,0:T(8,128)(2,1)} custom-call(f32[896,128]{1,0:T(8,128)S(1)} %get-tuple-element.44.own, s16[912,128]{1,0:T(8,128)(2,1)S(1)} %collective-permute-done.13.refs_0_), custom_call_target="tpu_custom_call" | custom-call | tf_op jit(solution)/shard_map/add_terms/pallas_call | solution.py:394
  39.1 1.7 %collective-permute-done.12.refs_0_ = s16[912,128]{1,0:T(8,128)(2,1)S(1)} collective-permute-done((s16[912,128]{1,0:T(8,128)(2,1)S(1)}, s16[912,128]{1,0:T(8,128)(2,1)S(1)}, u32[]{:S(2)}, u32[]{:S(2)}) %collective-permute-start.12) | collective-permute-done | bytes 233504 | tf_op jit(solution)/shard_map/ppermute | solution.py:242
  40.8 0.8 %add_terms.3 = bf16[128,1792]{1,0:T(8,128)(2,1)} custom-call(f32[896,128]{1,0:T(8,128)S(1)} %get-tuple-element.42.own, s16[912,128]{1,0:T(8,128)(2,1)S(1)} %collective-permute-done.12.refs_0_, bf16[128,1792]{1,0:T(8,128)(2,1)} %add_terms.2.refs_1_), custom_call_target="tpu_custom_call", output_to_operand_aliasing={{}: (2, {})} | custom-call | tf_op jit(solution)/shard_map/add_terms/pallas_call | solution.py:394
  (1 shorter events, 0.0 us)
Async XLA Ops:
  0.6 12.1 %collective-permute-start.4 = (bf16[16,4096]{1,0:T(8,128)(2,1)}, bf16[16,4096]{1,0:T(8,128)(2,1)S(1)}, u32[]{:S(2)}, u32[]{:S(2)}) collective-permute-start(bf16[16,4096]{1,0:T(8,128)(2,1)} %refs_0_.3), channel_id=1, source_target_pairs={{2,4},{3,11},{6,0},{7,15},{10,2},{11,13},{14,6},{15,9},{12,10},{13... | collective-permute-start | bytes 393224 | tf_op jit(solution)/shard_map/ppermute | solution.py:236
  4.7 8.0 %collective-permute-start.3 = (bf16[16,4096]{1,0:T(8,128)(2,1)}, bf16[16,4096]{1,0:T(8,128)(2,1)S(1)}, u32[]{:S(2)}, u32[]{:S(2)}) collective-permute-start(bf16[16,4096]{1,0:T(8,128)(2,1)} %refs_0_.3), channel_id=1, source_target_pairs={{2,10},{3,5},{6,14},{7,1},{10,12},{11,3},{14,8},{15,7},{12,4},{13,... | collective-permute-start | bytes 393224 | tf_op jit(solution)/shard_map/ppermute | solution.py:236
  4.7 12.6 %collective-permute-start.2 = (bf16[128,1792]{1,0:T(8,128)(2,1)}, bf16[128,1792]{1,0:T(8,128)(2,1)S(1)}, u32[]{:S(2)}, u32[]{:S(2)}) collective-permute-start(bf16[128,1792]{1,0:T(8,128)(2,1)} %refs_0_.4), channel_id=1, source_target_pairs={{0,16},{16,0},{1,17},{17,1},{2,18},{18,2},{3,19},{19,3},{4,20},{20... | collective-permute-start | bytes 1376264 | tf_op jit(solution)/shard_map/ppermute | solution.py:242
  6.6 1.5 %copy-start = (bf16[16,4096]{1,0:T(8,128)(2,1)S(1)}, bf16[16,4096]{1,0:T(8,128)(2,1)}, u32[]{:S(2)}) copy-start(bf16[16,4096]{1,0:T(8,128)(2,1)} %refs_0_.3) | copy-start | bytes 393220
  8.1 8.8 %collective-permute-start.1 = (bf16[16,4096]{1,0:T(8,128)(2,1)S(1)}, bf16[16,4096]{1,0:T(8,128)(2,1)S(1)}, u32[]{:S(2)}, u32[]{:S(2)}) collective-permute-start(bf16[16,4096]{1,0:T(8,128)(2,1)S(1)} %copy-done), channel_id=1, source_target_pairs={{2,0},{3,7},{6,2},{7,11},{10,6},{11,15},{14,10},{15,13},{12,14},{1... | collective-permute-start | bytes 393224 | tf_op jit(solution)/shard_map/ppermute | solution.py:236
  9.7 7.6 %collective-permute-start = (bf16[16,4096]{1,0:T(8,128)(2,1)S(1)}, bf16[16,4096]{1,0:T(8,128)(2,1)S(1)}, u32[]{:S(2)}, u32[]{:S(2)}) collective-permute-start(bf16[16,4096]{1,0:T(8,128)(2,1)S(1)} %copy-done), channel_id=1, source_target_pairs={{2,6},{3,1},{6,10},{7,3},{10,14},{11,7},{14,12},{15,11},{12,8},{13... | collective-permute-start | bytes 393224 | tf_op jit(solution)/shard_map/ppermute | solution.py:236
  12.7 9.1 %collective-permute-start.8 = (bf16[16,4096]{1,0:T(8,128)(2,1)S(1)}, bf16[16,4096]{1,0:T(8,128)(2,1)S(1)}, u32[]{:S(2)}, u32[]{:S(2)}) collective-permute-start(bf16[16,4096]{1,0:T(8,128)(2,1)S(1)} %collective-permute-done.3.refs_3_), channel_id=1, source_target_pairs={{2,10},{3,5},{6,14},{7,1},{10,12},{11,3},{14,8},{15,7},{12,4},{13,... | collective-permute-start | bytes 393224 | tf_op jit(solution)/shard_map/ppermute | solution.py:236
  15.3 7.6 %collective-permute-start.6 = (bf16[16,4096]{1,0:T(8,128)(2,1)S(1)}, bf16[16,4096]{1,0:T(8,128)(2,1)S(1)}, u32[]{:S(2)}, u32[]{:S(2)}) collective-permute-start(bf16[16,4096]{1,0:T(8,128)(2,1)S(1)} %collective-permute-done.3.refs_3_), channel_id=1, source_target_pairs={{2,6},{3,1},{6,10},{7,3},{10,14},{11,7},{14,12},{15,11},{12,8},{13... | collective-permute-start | bytes 393224 | tf_op jit(solution)/shard_map/ppermute | solution.py:236
  16.9 5.0 %collective-permute-start.7 = (bf16[16,4096]{1,0:T(8,128)(2,1)S(1)}, bf16[16,4096]{1,0:T(8,128)(2,1)S(1)}, u32[]{:S(2)}, u32[]{:S(2)}) collective-permute-start(bf16[16,4096]{1,0:T(8,128)(2,1)S(1)} %collective-permute-done.4.refs_4_), channel_id=1, source_target_pairs={{2,0},{3,7},{6,2},{7,11},{10,6},{11,15},{14,10},{15,13},{12,14},{1... | collective-permute-start | bytes 393224 | tf_op jit(solution)/shard_map/ppermute | solution.py:236
  17.4 7.4 %copy-start.2 = (s32[16,16]{1,0:T(8,128)S(1)}, s32[16,16]{1,0:T(8,128)}, u32[]{:S(2)}) copy-start(s32[16,16]{1,0:T(8,128)} %constant.11.clone.table) | copy-start | bytes 3076
  17.4 7.3 %collective-permute-start.5 = (bf16[80,4096]{1,0:T(8,128)(2,1)S(1)}, bf16[80,4096]{1,0:T(8,128)(2,1)S(1)}, u32[]{:S(2)}, u32[]{:S(2)}) collective-permute-start(bf16[80,4096]{1,0:T(8,128)(2,1)S(1)} %pack.1), channel_id=1, source_target_pairs={{0,1},{1,0},{2,3},{3,2},{4,5},{5,4},{6,7},{7,6},{8,9},{9,8},{10,11... | collective-permute-start | bytes 1966088 | tf_op jit(solution)/shard_map/ppermute | solution.py:239
  21.3 7.6 %copy-start.1 = (bf16[128,1792]{1,0:T(8,128)(2,1)S(1)}, bf16[128,1792]{1,0:T(8,128)(2,1)}, u32[]{:S(2)}) copy-start(bf16[128,1792]{1,0:T(8,128)(2,1)} %refs_0_.4) | copy-start | bytes 1376260
  22.9 1.3 %collective-permute-start.9 = (bf16[16,4096]{1,0:T(8,128)(2,1)S(1)}, bf16[16,4096]{1,0:T(8,128)(2,1)S(1)}, u32[]{:S(2)}, u32[]{:S(2)}) collective-permute-start(bf16[16,4096]{1,0:T(8,128)(2,1)S(1)} %collective-permute-done.6.refs_6_), channel_id=1, source_target_pairs={{0,1},{1,0},{2,3},{3,2},{4,5},{5,4},{6,7},{7,6},{8,9},{9,8},{10,11... | collective-permute-start | bytes 393224 | tf_op jit(solution)/shard_map/ppermute | solution.py:239
  22.9 1.5 %collective-permute-start.10 = (bf16[16,4096]{1,0:T(8,128)(2,1)S(1)}, bf16[16,4096]{1,0:T(8,128)(2,1)S(1)}, u32[]{:S(2)}, u32[]{:S(2)}) collective-permute-start(bf16[16,4096]{1,0:T(8,128)(2,1)S(1)} %collective-permute-done.7.refs_8_), channel_id=1, source_target_pairs={{0,1},{1,0},{2,3},{3,2},{4,5},{5,4},{6,7},{7,6},{8,9},{9,8},{10,11... | collective-permute-start | bytes 393224 | tf_op jit(solution)/shard_map/ppermute | solution.py:239
  23.4 1.3 %collective-permute-start.11 = (bf16[16,4096]{1,0:T(8,128)(2,1)S(1)}, bf16[16,4096]{1,0:T(8,128)(2,1)S(1)}, u32[]{:S(2)}, u32[]{:S(2)}) collective-permute-start(bf16[16,4096]{1,0:T(8,128)(2,1)S(1)} %collective-permute-done.8.refs_10_), channel_id=1, source_target_pairs={{0,1},{1,0},{2,3},{3,2},{4,5},{5,4},{6,7},{7,6},{8,9},{9,8},{10,11... | collective-permute-start | bytes 393224 | tf_op jit(solution)/shard_map/ppermute | solution.py:239
  27.9 10.3 %collective-permute-start.13 = (s16[912,128]{1,0:T(8,128)(2,1)S(1)}, s16[912,128]{1,0:T(8,128)(2,1)S(1)}, u32[]{:S(2)}, u32[]{:S(2)}) collective-permute-start(s16[912,128]{1,0:T(8,128)(2,1)S(1)} %get-tuple-element.45), channel_id=1, source_target_pairs={{0,16},{16,0},{1,17},{17,1},{2,18},{18,2},{3,19},{19,3},{4,20},{20... | collective-permute-start | bytes 700424 | tf_op jit(solution)/shard_map/ppermute | solution.py:242
  31.0 9.8 %collective-permute-start.12 = (s16[912,128]{1,0:T(8,128)(2,1)S(1)}, s16[912,128]{1,0:T(8,128)(2,1)S(1)}, u32[]{:S(2)}, u32[]{:S(2)}) collective-permute-start(s16[912,128]{1,0:T(8,128)(2,1)S(1)} %get-tuple-element.43), channel_id=1, source_target_pairs={{0,16},{16,0},{1,17},{17,1},{2,18},{18,2},{3,19},{19,3},{4,20},{20... | collective-permute-start | bytes 700424 | tf_op jit(solution)/shard_map/ppermute | solution.py:242

commit v15 on v14

--- a/solution.py
+++ b/solution.py
@@ -123,7 +123,8 @@
     pieces, done = [], 0
     for weight in weights:
         end = min(weight.shape[0] // BLOCK, blocks - done)
-        pieces.append((weight, 0, end, done))
+        if end:
+            pieces.append((weight, 0, end, done))
         done += end
     rows = shards[0].shape[0]
     n_cols = table.shape[0]
@@ -269,7 +270,7 @@
         out_shape=pltpu.VMEM((blocks, width), jnp.float32),
         scratch_shapes=[pltpu.VMEM(block_mask.shape, jnp.int32), pltpu.SemaphoreType.DMA],
         compiler_params=params(),
-        cost_estimate=cost(1 << 34, BLOCK),
+        cost_estimate=cost(BLOCK, BLOCK),
         name="spread",
     )(place, block_mask)
 
@@ -292,10 +293,10 @@
     far = [j for j in held if j]
     spread, again = lax.optimization_barrier((spread, grad_output))
     held[1], held[-1] = send_ring(again, 1), send_ring(again, -1)
-    n_soon = max(1, blocks * 5 // 14)
+    n_soon = piece_blocks if n_pieces > 1 else max(1, blocks * 5 // 14)
     weight, spread = lax.optimization_barrier((weight, spread))
     soon = fetch_rows(0, n_soon, BLOCK)
-    soon, *ready = lax.optimization_barrier((soon, *(held[j] for j in far)))
+    soon, inputs, *ready = lax.optimization_barrier((soon, inputs, *(held[j] for j in far)))
     held.update(zip(far, ready, strict=True))
     acts = [inputs] + [send_row(inputs, k) for k in range(1, n_rows)]
     for j in range(3, n_chips // 2 + 1):
@@ -304,9 +305,7 @@
         if 2 * j < n_chips:
             held[-j] = send_ring(held[by - j], -by)
 
-    weight, held[1], held[-1], *acts = lax.optimization_barrier(
-        (weight, held[1], held[-1], *acts)
-    )
+    weight, held[1], held[-1] = lax.optimization_barrier((weight, held[1], held[-1]))
     rest = fetch_rows(n_soon, blocks - n_soon, 1 << 34)
     rest, *ready = lax.optimization_barrier((rest, *(held[j] for j in last)))
     held.update(zip(last, ready, strict=True))

time: 41.8 us -> 41.9 us (level)
    ppermute x7, waiting for transfers between devices: 1.59 us -> 2.78 us  [send_ring(): return lax.ppermute(x, 'col', perm)]
    ppermute x3, waiting for transfers between devices: 1.66 us -> 0.64 us  [send_row(): lax.ppermute(x, 'row', [(r, (r + by) % n_rows) for r in range(n_rows)])]
    ppermute x7, starting transfers between devices: 10.8 us -> 9.88 us  [send_ring(): return lax.ppermute(x, 'col', perm)]
    ppermute x3, starting transfers between devices: 4.01 us -> 4.76 us  [send_row(): lax.ppermute(x, 'row', [(r, (r + by) % n_rows) for r in range(n_rows)])]
  transfers between devices with their start and end apart: 14 -> 14, of which waited for: 6 -> 7; matrix products, arithmetic and copies ran while one was open for 0% -> 0% of each run, Pallas kernels for 40% -> 48%
where the time goes in v15:
time: 41.9 us; the launch traced here: 41.7 us
  Pallas kernels  20.8 us (50%)
  starting transfers between devices  15.2 us (36%)
  waiting for transfers between devices  4.76 us (11%)
  between operations  0.76 us (2%)
    ppermute x7, starting transfers between devices, send_ring(): return lax.ppermute(x, 'col', perm)  9.88 us
    pallas_call x2, Pallas kernels, fetch_rows(): pl.pallas_call(functools.partial(fetch_kernel, first), in_specs=[in_hbm()...  6.33 us
    pallas_call x1, Pallas kernels, per_device(): pl.pallas_call(functools.partial(weight_grad_kernel, chunk), in_specs=[in...  6.05 us
    ppermute x3, starting transfers between devices, send_row(): lax.ppermute(x, 'row', [(r, (r + by) % n_rows) for r in range(n_rows)])  4.76 us
    pallas_call x1, Pallas kernels, per_device(): pl.pallas_call(functools.partial(first_terms_kernel, n_shards, n_parts, t...  3.16 us
    ppermute x7, waiting for transfers between devices, send_ring(): return lax.ppermute(x, 'col', perm)  2.78 us
    pallas_call x1, Pallas kernels, per_device(): pl.pallas_call(functools.partial(more_terms_kernel, n_parts, piece_blocks...  2.12 us
    pallas_call x2, Pallas kernels, per_device(): pl.pallas_call(functools.partial(finish_kernel, n_parts), grid=(1,), in_s...  1.68 us
  transfers between devices with their start and end apart: 14, of which 7 were waited for; matrix products, arithmetic and copies ran while one was open for 0% of the time, Pallas kernels for 48%

profile of v15, /device:TPU:0, one launch (start us, length us, event | category | flops | bytes accessed | tf_op | source)
XLA Modules:
  0.0 41.7 jit_solution(7870084986833602435)
XLA Ops:
  0.6 4.0 %collective-permute-start.2 = (bf16[16,4096]{1,0:T(8,128)(2,1)}, bf16[16,4096]{1,0:T(8,128)(2,1)S(1)}, u32[]{:S(2)}, u32[]{:S(2)}) collective-permute-start(bf16[16,4096]{1,0:T(8,128)(2,1)} %refs_0_.3), channel_id=1, source_target_pairs={{2,10},{3,5},{6,14},{7,1},{10,12},{11,3},{14,8},{15,7},{12,4},{13,... | collective-permute-start | bytes 393224 | tf_op jit(solution)/shard_map/ppermute | solution.py:237
  4.6 0.2 collective-permute-start.3
  4.8 0.1 pad_add_fusion.place
  4.9 1.4 %spread.1.refs_14_ = f32[14,4096]{1,0:T(8,128)S(1)} custom-call(s32[2]{0:T(128)S(1)} %pad_add_fusion.place, s32[14,64]{1,0:T(8,128)} %mask.1), custom_call_target="tpu_custom_call" | custom-call | flops 128 | bytes 128 | tf_op jit(solution)/shard_map/spread/pallas_call | solution.py:266
  6.3 0.0 copy-start
  6.3 0.0 copy-start.1
  6.3 1.8 %collective-permute-start = (bf16[16,4096]{1,0:T(8,128)(2,1)}, bf16[16,4096]{1,0:T(8,128)(2,1)S(1)}, u32[]{:S(2)}, u32[]{:S(2)}) collective-permute-start(bf16[16,4096]{1,0:T(8,128)(2,1)} %refs_0_.3), channel_id=1, source_target_pairs={{2,6},{3,1},{6,10},{7,3},{10,14},{11,7},{14,12},{15,11},{12,8},{13... | collective-permute-start | bytes 393224 | tf_op jit(solution)/shard_map/ppermute | solution.py:237
  8.1 0.3 collective-permute-start.1
  8.4 3.2 %fetch.2.refs_12_ = bf16[896,4096]{1,0:T(8,128)(2,1)S(1)} custom-call(bf16[1792,4096]{1,0:T(8,128)(2,1)} %weight.1), custom_call_target="tpu_custom_call" | custom-call | flops 128 | bytes 128 | tf_op jit(solution)/shard_map/fetch/pallas_call | solution.py:278
  11.6 0.0 collective-permute-done.2.refs_3_
  11.6 1.5 %collective-permute-done.3.refs_4_ = bf16[16,4096]{1,0:T(8,128)(2,1)S(1)} collective-permute-done((bf16[16,4096]{1,0:T(8,128)(2,1)}, bf16[16,4096]{1,0:T(8,128)(2,1)S(1)}, u32[]{:S(2)}, u32[]{:S(2)}) %collective-permute-start.3) | collective-permute-done | bytes 131104 | tf_op jit(solution)/shard_map/ppermute | solution.py:237
  13.1 1.7 %collective-permute-start.5 = (bf16[16,4096]{1,0:T(8,128)(2,1)S(1)}, bf16[16,4096]{1,0:T(8,128)(2,1)S(1)}, u32[]{:S(2)}, u32[]{:S(2)}) collective-permute-start(bf16[16,4096]{1,0:T(8,128)(2,1)S(1)} %collective-permute-done.2.refs_3_), channel_id=1, source_target_pairs={{2,6},{3,1},{6,10},{7,3},{10,14},{11,7},{14,12},{15,11},{12,8},{13... | collective-permute-start | bytes 393224 | tf_op jit(solution)/shard_map/ppermute | solution.py:237
  14.8 1.2 %collective-permute-start.7 = (bf16[16,4096]{1,0:T(8,128)(2,1)S(1)}, bf16[16,4096]{1,0:T(8,128)(2,1)S(1)}, u32[]{:S(2)}, u32[]{:S(2)}) collective-permute-start(bf16[16,4096]{1,0:T(8,128)(2,1)S(1)} %collective-permute-done.2.refs_3_), channel_id=1, source_target_pairs={{2,10},{3,5},{6,14},{7,1},{10,12},{11,3},{14,8},{15,7},{12,4},{13,... | collective-permute-start | bytes 393224 | tf_op jit(solution)/shard_map/ppermute | solution.py:237
  16.0 0.0 collective-permute-done.refs_1_
  16.0 0.0 collective-permute-done.1.refs_2_
  16.0 0.8 %collective-permute-start.6 = (bf16[16,4096]{1,0:T(8,128)(2,1)S(1)}, bf16[16,4096]{1,0:T(8,128)(2,1)S(1)}, u32[]{:S(2)}, u32[]{:S(2)}) collective-permute-start(bf16[16,4096]{1,0:T(8,128)(2,1)S(1)} %collective-permute-done.3.refs_4_), channel_id=1, source_target_pairs={{2,0},{3,7},{6,2},{7,11},{10,6},{11,15},{14,10},{15,13},{12,14},{1... | collective-permute-start | bytes 393224 | tf_op jit(solution)/shard_map/ppermute | solution.py:237
  16.8 0.0 copy-done
  16.8 0.0 copy-start.2
  16.9 0.1 collective-permute-start.4
  16.9 0.0 copy-done.1
  16.9 1.6 %collective-permute-start.11 = (bf16[128,1792]{1,0:T(8,128)(2,1)S(1)}, bf16[128,1792]{1,0:T(8,128)(2,1)S(1)}, u32[]{:S(2)}, u32[]{:S(2)}) collective-permute-start(bf16[128,1792]{1,0:T(8,128)(2,1)S(1)} %copy-done.1), channel_id=1, source_target_pairs={{0,16},{16,0},{1,17},{17,1},{2,18},{18,2},{3,19},{19,3},{4,20},{20... | collective-permute-start | bytes 1376264 | tf_op jit(solution)/shard_map/ppermute | solution.py:243
  18.5 3.2 %fetch.3.refs_13_.weight = bf16[896,4096]{1,0:T(8,128)(2,1)S(1)} custom-call(bf16[1792,4096]{1,0:T(8,128)(2,1)} %weight.1), custom_call_target="tpu_custom_call" | custom-call | flops 17179869184 | bytes 128 | tf_op jit(solution)/shard_map/fetch/pallas_call | solution.py:278
  21.7 0.0 collective-permute-done.5.refs_6_
  21.7 1.2 %collective-permute-done.7.refs_10_ = bf16[16,4096]{1,0:T(8,128)(2,1)S(1)} collective-permute-done((bf16[16,4096]{1,0:T(8,128)(2,1)S(1)}, bf16[16,4096]{1,0:T(8,128)(2,1)S(1)}, u32[]{:S(2)}, u32[]{:S(2)}) %collective-permute-start.7) | collective-permute-done | bytes 131104 | tf_op jit(solution)/shard_map/ppermute | solution.py:237
  22.9 0.0 collective-permute-done.6.refs_8_
  22.9 0.0 collective-permute-start.10
  22.9 0.5 %collective-permute-start.8 = (bf16[16,4096]{1,0:T(8,128)(2,1)S(1)}, bf16[16,4096]{1,0:T(8,128)(2,1)S(1)}, u32[]{:S(2)}, u32[]{:S(2)}) collective-permute-start(bf16[16,4096]{1,0:T(8,128)(2,1)S(1)} %collective-permute-done.5.refs_6_), channel_id=1, source_target_pairs={{0,1},{1,0},{2,3},{3,2},{4,5},{5,4},{6,7},{7,6},{8,9},{9,8},{10,11... | collective-permute-start | bytes 393224 | tf_op jit(solution)/shard_map/ppermute | solution.py:240
  23.4 0.0 collective-permute-start.9
  23.4 0.8 %collective-permute-done.10.refs_11_ = bf16[16,4096]{1,0:T(8,128)(2,1)S(1)} collective-permute-done((bf16[16,4096]{1,0:T(8,128)(2,1)S(1)}, bf16[16,4096]{1,0:T(8,128)(2,1)S(1)}, u32[]{:S(2)}, u32[]{:S(2)}) %collective-permute-start.10) | collective-permute-done | bytes 131104 | tf_op jit(solution)/shard_map/ppermute | solution.py:240
  24.3 0.2 collective-permute-done.8.refs_7_
  24.5 0.3 collective-permute-done.9.refs_9_
  24.8 0.0 collective-permute-done.4.refs_5_
  24.8 0.0 copy-done.2
  24.8 3.2 %first_terms.1 = (bf16[256,4096]{1,0:T(8,128)(2,1)S(1)}, bf16[4096,256]{1,0:T(8,128)(2,1)S(1)}, f32[896,128]{1,0:T(8,128)S(1)}, s16[912,128]{1,0:T(8,128)(2,1)S(1)}) custom-call(s32[2]{0:T(128)S(1)} %pad_add_fusion.place, s32[16,16]{1,0:T(8,128)S(1)} %copy-done.2, bf16[16,4096]{1,0:T(8,128)(2,1)S(1)} %copy-done, ...), custom_call_target="tpu_custom_call" | custom-call | flops 3670016 | bytes 458752 | tf_op jit(solution)/shard_map/first_terms/pallas_call | solution.py:328
  28.0 1.6 %collective-permute-start.13 = (s16[912,128]{1,0:T(8,128)(2,1)S(1)}, s16[912,128]{1,0:T(8,128)(2,1)S(1)}, u32[]{:S(2)}, u32[]{:S(2)}) collective-permute-start(s16[912,128]{1,0:T(8,128)(2,1)S(1)} %get-tuple-element.43), channel_id=1, source_target_pairs={{0,16},{16,0},{1,17},{17,1},{2,18},{18,2},{3,19},{19,3},{4,20},{20... | collective-permute-start | bytes 700424 | tf_op jit(solution)/shard_map/ppermute | solution.py:243
  29.6 0.3 collective-permute-done.11.refs_1_
  29.9 2.1 %more_terms.1 = (f32[896,128]{1,0:T(8,128)S(1)}, s16[912,128]{1,0:T(8,128)(2,1)S(1)}, bf16[1792,256]{1,0:T(8,128)(2,1)S(1)}) custom-call(bf16[4096,256]{1,0:T(8,128)(2,1)S(1)} %get-tuple-element.38.turned, bf16[896,4096]{1,0:T(8,128)(2,1)S(1)} %fetch.3.refs_13_.weight, f32[14,4096]{1,0:T(8,128)S(1)} %spread.1.refs_14_, bf16[128,1792]{1,0:T(8,128)(2,1)S(1)} %copy-done.1, ...), custom_call_target="tpu_custom_call" | custom-call | flops 3670016 | bytes 458752 | tf_op jit(solution)/shard_map/more_terms/pallas_call | solution.py:350
  32.0 1.6 %collective-permute-start.12 = (s16[912,128]{1,0:T(8,128)(2,1)S(1)}, s16[912,128]{1,0:T(8,128)(2,1)S(1)}, u32[]{:S(2)}, u32[]{:S(2)}) collective-permute-start(s16[912,128]{1,0:T(8,128)(2,1)S(1)} %get-tuple-element.41), channel_id=1, source_target_pairs={{0,16},{16,0},{1,17},{17,1},{2,18},{18,2},{3,19},{19,3},{4,20},{20... | collective-permute-start | bytes 700424 | tf_op jit(solution)/shard_map/ppermute | solution.py:243
  33.6 6.1 %weight_grad.1 = bf16[1792,4096]{1,0:T(8,128)(2,1)} custom-call(bf16[1792,256]{1,0:T(8,128)(2,1)S(1)} %get-tuple-element.44.acts, bf16[256,4096]{1,0:T(8,128)(2,1)S(1)} %get-tuple-element.45.full, f32[14,4096]{1,0:T(8,128)S(1)} %spread.1.refs_14_), custom_call_target="tpu_custom_call" | custom-call | flops 3670016 | bytes 458752 | tf_op jit(solution)/shard_map/weight_grad/pallas_call | solution.py:372
  39.7 0.0 collective-permute-done.13.refs_0_
  39.7 0.8 %add_terms.2.refs_1_ = bf16[128,1792]{1,0:T(8,128)(2,1)} custom-call(f32[896,128]{1,0:T(8,128)S(1)} %get-tuple-element.42.own, s16[912,128]{1,0:T(8,128)(2,1)S(1)} %collective-permute-done.13.refs_0_), custom_call_target="tpu_custom_call" | custom-call | tf_op jit(solution)/shard_map/add_terms/pallas_call | solution.py:393
  40.5 0.3 collective-permute-done.12.refs_0_
  40.8 0.8 %add_terms.3 = bf16[128,1792]{1,0:T(8,128)(2,1)} custom-call(f32[896,128]{1,0:T(8,128)S(1)} %get-tuple-element.40.own, s16[912,128]{1,0:T(8,128)(2,1)S(1)} %collective-permute-done.12.refs_0_, bf16[128,1792]{1,0:T(8,128)(2,1)} %add_terms.2.refs_1_), custom_call_target="tpu_custom_call", output_to_operand_aliasing={{}: (2, {})} | custom-call | tf_op jit(solution)/shard_map/add_terms/pallas_call | solution.py:393
  (1 shorter events, 0.0 us)
Async XLA Ops:
  0.6 11.0 %collective-permute-start.2 = (bf16[16,4096]{1,0:T(8,128)(2,1)}, bf16[16,4096]{1,0:T(8,128)(2,1)S(1)}, u32[]{:S(2)}, u32[]{:S(2)}) collective-permute-start(bf16[16,4096]{1,0:T(8,128)(2,1)} %refs_0_.3), channel_id=1, source_target_pairs={{2,10},{3,5},{6,14},{7,1},{10,12},{11,3},{14,8},{15,7},{12,4},{13,... | collective-permute-start | bytes 393224 | tf_op jit(solution)/shard_map/ppermute | solution.py:237
  4.6 8.5 %collective-permute-start.3 = (bf16[16,4096]{1,0:T(8,128)(2,1)}, bf16[16,4096]{1,0:T(8,128)(2,1)S(1)}, u32[]{:S(2)}, u32[]{:S(2)}) collective-permute-start(bf16[16,4096]{1,0:T(8,128)(2,1)} %refs_0_.3), channel_id=1, source_target_pairs={{2,4},{3,11},{6,0},{7,15},{10,2},{11,13},{14,6},{15,9},{12,10},{13... | collective-permute-start | bytes 393224 | tf_op jit(solution)/shard_map/ppermute | solution.py:237
  6.3 10.5 %copy-start = (bf16[16,4096]{1,0:T(8,128)(2,1)S(1)}, bf16[16,4096]{1,0:T(8,128)(2,1)}, u32[]{:S(2)}) copy-start(bf16[16,4096]{1,0:T(8,128)(2,1)} %refs_0_.3) | copy-start | bytes 393220
  6.3 10.6 %copy-start.1 = (bf16[128,1792]{1,0:T(8,128)(2,1)S(1)}, bf16[128,1792]{1,0:T(8,128)(2,1)}, u32[]{:S(2)}) copy-start(bf16[128,1792]{1,0:T(8,128)(2,1)} %refs_0_.4) | copy-start | bytes 1376260
  6.3 9.7 %collective-permute-start = (bf16[16,4096]{1,0:T(8,128)(2,1)}, bf16[16,4096]{1,0:T(8,128)(2,1)S(1)}, u32[]{:S(2)}, u32[]{:S(2)}) collective-permute-start(bf16[16,4096]{1,0:T(8,128)(2,1)} %refs_0_.3), channel_id=1, source_target_pairs={{2,6},{3,1},{6,10},{7,3},{10,14},{11,7},{14,12},{15,11},{12,8},{13... | collective-permute-start | bytes 393224 | tf_op jit(solution)/shard_map/ppermute | solution.py:237
  8.1 7.9 %collective-permute-start.1 = (bf16[16,4096]{1,0:T(8,128)(2,1)}, bf16[16,4096]{1,0:T(8,128)(2,1)S(1)}, u32[]{:S(2)}, u32[]{:S(2)}) collective-permute-start(bf16[16,4096]{1,0:T(8,128)(2,1)} %refs_0_.3), channel_id=1, source_target_pairs={{2,0},{3,7},{6,2},{7,11},{10,6},{11,15},{14,10},{15,13},{12,14},{1... | collective-permute-start | bytes 393224 | tf_op jit(solution)/shard_map/ppermute | solution.py:237
  13.1 8.6 %collective-permute-start.5 = (bf16[16,4096]{1,0:T(8,128)(2,1)S(1)}, bf16[16,4096]{1,0:T(8,128)(2,1)S(1)}, u32[]{:S(2)}, u32[]{:S(2)}) collective-permute-start(bf16[16,4096]{1,0:T(8,128)(2,1)S(1)} %collective-permute-done.2.refs_3_), channel_id=1, source_target_pairs={{2,6},{3,1},{6,10},{7,3},{10,14},{11,7},{14,12},{15,11},{12,8},{13... | collective-permute-start | bytes 393224 | tf_op jit(solution)/shard_map/ppermute | solution.py:237
  14.8 8.1 %collective-permute-start.7 = (bf16[16,4096]{1,0:T(8,128)(2,1)S(1)}, bf16[16,4096]{1,0:T(8,128)(2,1)S(1)}, u32[]{:S(2)}, u32[]{:S(2)}) collective-permute-start(bf16[16,4096]{1,0:T(8,128)(2,1)S(1)} %collective-permute-done.2.refs_3_), channel_id=1, source_target_pairs={{2,10},{3,5},{6,14},{7,1},{10,12},{11,3},{14,8},{15,7},{12,4},{13,... | collective-permute-start | bytes 393224 | tf_op jit(solution)/shard_map/ppermute | solution.py:237
  16.0 6.9 %collective-permute-start.6 = (bf16[16,4096]{1,0:T(8,128)(2,1)S(1)}, bf16[16,4096]{1,0:T(8,128)(2,1)S(1)}, u32[]{:S(2)}, u32[]{:S(2)}) collective-permute-start(bf16[16,4096]{1,0:T(8,128)(2,1)S(1)} %collective-permute-done.3.refs_4_), channel_id=1, source_target_pairs={{2,0},{3,7},{6,2},{7,11},{10,6},{11,15},{14,10},{15,13},{12,14},{1... | collective-permute-start | bytes 393224 | tf_op jit(solution)/shard_map/ppermute | solution.py:237
  16.8 8.0 %copy-start.2 = (s32[16,16]{1,0:T(8,128)S(1)}, s32[16,16]{1,0:T(8,128)}, u32[]{:S(2)}) copy-start(s32[16,16]{1,0:T(8,128)} %constant.11.clone.table) | copy-start | bytes 3076
  16.9 7.9 %collective-permute-start.4 = (bf16[80,4096]{1,0:T(8,128)(2,1)S(1)}, bf16[80,4096]{1,0:T(8,128)(2,1)S(1)}, u32[]{:S(2)}, u32[]{:S(2)}) collective-permute-start(bf16[80,4096]{1,0:T(8,128)(2,1)S(1)} %pack.1), channel_id=1, source_target_pairs={{0,1},{1,0},{2,3},{3,2},{4,5},{5,4},{6,7},{7,6},{8,9},{9,8},{10,11... | collective-permute-start | bytes 1966088 | tf_op jit(solution)/shard_map/ppermute | solution.py:240
  16.9 12.9 %collective-permute-start.11 = (bf16[128,1792]{1,0:T(8,128)(2,1)S(1)}, bf16[128,1792]{1,0:T(8,128)(2,1)S(1)}, u32[]{:S(2)}, u32[]{:S(2)}) collective-permute-start(bf16[128,1792]{1,0:T(8,128)(2,1)S(1)} %copy-done.1), channel_id=1, source_target_pairs={{0,16},{16,0},{1,17},{17,1},{2,18},{18,2},{3,19},{19,3},{4,20},{20... | collective-permute-start | bytes 1376264 | tf_op jit(solution)/shard_map/ppermute | solution.py:243
  22.9 1.3 %collective-permute-start.10 = (bf16[16,4096]{1,0:T(8,128)(2,1)S(1)}, bf16[16,4096]{1,0:T(8,128)(2,1)S(1)}, u32[]{:S(2)}, u32[]{:S(2)}) collective-permute-start(bf16[16,4096]{1,0:T(8,128)(2,1)S(1)} %collective-permute-done.7.refs_10_), channel_id=1, source_target_pairs={{0,1},{1,0},{2,3},{3,2},{4,5},{5,4},{6,7},{7,6},{8,9},{9,8},{10,11... | collective-permute-start | bytes 393224 | tf_op jit(solution)/shard_map/ppermute | solution.py:240
  22.9 1.5 %collective-permute-start.8 = (bf16[16,4096]{1,0:T(8,128)(2,1)S(1)}, bf16[16,4096]{1,0:T(8,128)(2,1)S(1)}, u32[]{:S(2)}, u32[]{:S(2)}) collective-permute-start(bf16[16,4096]{1,0:T(8,128)(2,1)S(1)} %collective-permute-done.5.refs_6_), channel_id=1, source_target_pairs={{0,1},{1,0},{2,3},{3,2},{4,5},{5,4},{6,7},{7,6},{8,9},{9,8},{10,11... | collective-permute-start | bytes 393224 | tf_op jit(solution)/shard_map/ppermute | solution.py:240
  23.4 1.3 %collective-permute-start.9 = (bf16[16,4096]{1,0:T(8,128)(2,1)S(1)}, bf16[16,4096]{1,0:T(8,128)(2,1)S(1)}, u32[]{:S(2)}, u32[]{:S(2)}) collective-permute-start(bf16[16,4096]{1,0:T(8,128)(2,1)S(1)} %collective-permute-done.6.refs_8_), channel_id=1, source_target_pairs={{0,1},{1,0},{2,3},{3,2},{4,5},{5,4},{6,7},{7,6},{8,9},{9,8},{10,11... | collective-permute-start | bytes 393224 | tf_op jit(solution)/shard_map/ppermute | solution.py:240
  28.0 11.7 %collective-permute-start.13 = (s16[912,128]{1,0:T(8,128)(2,1)S(1)}, s16[912,128]{1,0:T(8,128)(2,1)S(1)}, u32[]{:S(2)}, u32[]{:S(2)}) collective-permute-start(s16[912,128]{1,0:T(8,128)(2,1)S(1)} %get-tuple-element.43), channel_id=1, source_target_pairs={{0,16},{16,0},{1,17},{17,1},{2,18},{18,2},{3,19},{19,3},{4,20},{20... | collective-permute-start | bytes 700424 | tf_op jit(solution)/shard_map/ppermute | solution.py:243
  32.0 8.8 %collective-permute-start.12 = (s16[912,128]{1,0:T(8,128)(2,1)S(1)}, s16[912,128]{1,0:T(8,128)(2,1)S(1)}, u32[]{:S(2)}, u32[]{:S(2)}) collective-permute-start(s16[912,128]{1,0:T(8,128)(2,1)S(1)} %get-tuple-element.41), channel_id=1, source_target_pairs={{0,16},{16,0},{1,17},{17,1},{2,18},{18,2},{3,19},{19,3},{4,20},{20... | collective-permute-start | bytes 700424 | tf_op jit(solution)/shard_map/ppermute | solution.py:243

commit v16 on v14

--- a/solution.py
+++ b/solution.py
@@ -175,8 +175,8 @@
         copy.wait()
 
 
-def finish_kernel(n_parts, own, *refs):
-    parts, out = refs[:n_parts], refs[-1]
+def finish_kernel(first, n_parts, own, *refs):
+    parts, (*_, out, held, sem) = refs[:n_parts], refs[n_parts:]
     rows = own.shape[0]
     scales = []
     for part in parts:
@@ -188,7 +188,10 @@
         for part, scale in zip(parts, scales, strict=True):
             got = part[at, :].astype(jnp.int32).astype(jnp.float32)
             total = total + got * scale[b : b + 1, :]
-        out[:, at] = total.T.astype(out.dtype)
+        held[:, at] = total.T.astype(out.dtype)
+    copy = pltpu.make_async_copy(held, out.at[:, pl.ds(first, rows)], sem)
+    copy.start()
+    copy.wait()
 
 
 def in_vmem():
@@ -215,8 +218,9 @@
     row, col = lax.axis_index("row"), lax.axis_index("col")
     hidden, width = weight.shape
     blocks = hidden // BLOCK
-    n_pieces = 2 if blocks % 2 == 0 else 1
-    piece = hidden // n_pieces
+    n_pieces = 2 if blocks > 7 else 1
+    piece = blocks * 5 // 14 * BLOCK if n_pieces > 1 else hidden
+    sizes = [piece, hidden - piece][:n_pieces]
     n_parts = n_rows - 1
     tokens = inputs.shape[0]
     shard_rows = grad_output.shape[0]
@@ -292,7 +296,7 @@
     far = [j for j in held if j]
     spread, again = lax.optimization_barrier((spread, grad_output))
     held[1], held[-1] = send_ring(again, 1), send_ring(again, -1)
-    n_soon = max(1, blocks * 5 // 14)
+    n_soon = max(1, blocks // 7)
     weight, spread = lax.optimization_barrier((weight, spread))
     soon = fetch_rows(0, n_soon, BLOCK)
     soon, *ready = lax.optimization_barrier((soon, *(held[j] for j in far)))
@@ -322,9 +326,11 @@
     for j in last:
         shards += [held[j], send_core(held[j])]
     n_shards = len(shards)
-    code_rows = -(-(piece // BLOCK) // 16) * 16
-    sent_shape = jax.ShapeDtypeStruct((piece + code_rows, tokens), jnp.int16)
-    own_shape = jax.ShapeDtypeStruct((piece, tokens), jnp.float32)
+    def out_shapes(rows):
+        code_rows = -(-(rows // BLOCK) // 16) * 16
+        sent_shape = jax.ShapeDtypeStruct((rows + code_rows, tokens), jnp.int16)
+        return [jax.ShapeDtypeStruct((rows, tokens), jnp.float32)] + [sent_shape] * n_parts
+
     small_cost = cost(piece * width, piece * width // 8)
     full, turned, own, *coded = pl.pallas_call(
         functools.partial(
@@ -335,9 +341,8 @@
         out_shape=[
             jax.ShapeDtypeStruct((all_tokens, width), bf16),
             jax.ShapeDtypeStruct((width, all_tokens), bf16),
-            own_shape,
         ]
-        + [sent_shape] * n_parts,
+        + out_shapes(piece),
         scratch_shapes=[pltpu.VMEM((piece, all_tokens), jnp.float32)],
         compiler_params=params(),
         cost_estimate=small_cost,
@@ -352,8 +357,8 @@
             functools.partial(more_terms_kernel, n_parts, piece_blocks, chunk),
             in_specs=[in_vmem()] * (3 + n_rows),
             out_specs=[in_vmem()] * (2 + n_parts),
-            out_shape=[own_shape] + [sent_shape] * n_parts + [acts_shape],
-            scratch_shapes=[pltpu.VMEM((piece, all_tokens), jnp.float32)],
+            out_shape=out_shapes(sizes[1]) + [acts_shape],
+            scratch_shapes=[pltpu.VMEM((sizes[1], all_tokens), jnp.float32)],
             compiler_params=params(),
             cost_estimate=small_cost,
             name="more_terms",
@@ -385,20 +390,21 @@
     )(acts_turned, full, spread)
 
     grad_input = None
-    for p in range(n_pieces):
+    for p, rows in enumerate(sizes):
         operands = [owns[p], *parts[p * n_parts : (p + 1) * n_parts]]
         specs = [in_vmem()] * len(operands)
         if p:
             operands.append(grad_input)
             specs.append(in_hbm())
         grad_input = pl.pallas_call(
-            functools.partial(finish_kernel, n_parts),
-            grid=(1,),
+            functools.partial(finish_kernel, sum(sizes[:p]), n_parts),
             in_specs=specs,
-            out_specs=pl.BlockSpec((tokens, piece), lambda i, p=p: (0, p)),
+            out_specs=in_hbm(),
             out_shape=jax.ShapeDtypeStruct((tokens, hidden), bf16),
+            scratch_shapes=[pltpu.VMEM((tokens, rows), bf16), pltpu.SemaphoreType.DMA],
             input_output_aliases={len(operands) - 1: 0} if p else {},
             compiler_params=params(),
+            cost_estimate=cost(BLOCK if p else 1 << 34, BLOCK),
             name="add_terms",
         )(*operands)
     return (grad_input, grad_weight)

time: 41.8 us -> 41.1 us (0.983)
  waiting for transfers between devices: 4.6 us -> 2.74 us
  starting transfers between devices: 15.3 us -> 16.6 us
    ppermute x7, waiting for transfers between devices: 1.59 us -> 0.06 us  [send_ring(): return lax.ppermute(x, 'col', perm)]
    ppermute x7, starting transfers between devices: 10.8 us -> 11.5 us  [send_ring(): return lax.ppermute(x, 'col', perm)]
    pallas_call x1, Pallas kernels: 3.17 us -> 2.47 us  [per_device(): pl.pallas_call(functools.partial(first_terms_kernel, n_shards, n_parts, t...]
    pallas_call x1, Pallas kernels: 2.12 us -> 2.75 us  [per_device(): pl.pallas_call(functools.partial(more_terms_kernel, n_parts, piece_blocks...]
    ppermute x4, starting transfers between devices: 0.58 us -> 1.12 us  [send_core(): return lax.ppermute(x, 'col', [(c, c ^ 1) for c in range(n_cols)])]
  transfers between devices with their start and end apart: 14 -> 14, of which waited for: 6 -> 4; matrix products, arithmetic and copies ran while one was open for 0% -> 0% of each run, Pallas kernels for 40% -> 42%
where the time goes in v16:
time: 41.1 us; the launch traced here: 41 us
  Pallas kernels  20.8 us (51%)
  starting transfers between devices  16.6 us (40%)
  waiting for transfers between devices  2.74 us (7%)
  between operations  0.77 us (2%)
    ppermute x7, starting transfers between devices, send_ring(): return lax.ppermute(x, 'col', perm)  11.5 us
    pallas_call x2, Pallas kernels, fetch_rows(): pl.pallas_call(functools.partial(fetch_kernel, first), in_specs=[in_hbm()...  6.28 us
    pallas_call x1, Pallas kernels, per_device(): pl.pallas_call(functools.partial(weight_grad_kernel, chunk), in_specs=[in...  6.04 us
    ppermute x3, starting transfers between devices, send_row(): lax.ppermute(x, 'row', [(r, (r + by) % n_rows) for r in range(n_rows)])  4.01 us
    pallas_call x1, Pallas kernels, per_device(): pl.pallas_call(functools.partial(more_terms_kernel, n_parts, piece_blocks...  2.75 us
    pallas_call x1, Pallas kernels, per_device(): pl.pallas_call(functools.partial(first_terms_kernel, n_shards, n_parts, t...  2.47 us
    pallas_call x2, Pallas kernels, per_device(): pl.pallas_call(functools.partial(finish_kernel, sum(sizes[:p]), n_parts),...  1.73 us
    ppermute x3, waiting for transfers between devices, send_row(): lax.ppermute(x, 'row', [(r, (r + by) % n_rows) for r in range(n_rows)])  1.65 us
  transfers between devices with their start and end apart: 14, of which 4 were waited for; matrix products, arithmetic and copies ran while one was open for 0% of the time, Pallas kernels for 42%

profile of v16, /device:TPU:0, one launch (start us, length us, event | category | flops | bytes accessed | tf_op | source)
XLA Modules:
  0.0 41.0 jit_solution(2826399671680085111)
XLA Ops:
  0.6 4.1 %collective-permute-start.4 = (bf16[16,4096]{1,0:T(8,128)(2,1)}, bf16[16,4096]{1,0:T(8,128)(2,1)S(1)}, u32[]{:S(2)}, u32[]{:S(2)}) collective-permute-start(bf16[16,4096]{1,0:T(8,128)(2,1)} %refs_0_.3), channel_id=1, source_target_pairs={{2,4},{3,11},{6,0},{7,15},{10,2},{11,13},{14,6},{15,9},{12,10},{13... | collective-permute-start | bytes 393224 | tf_op jit(solution)/shard_map/ppermute | solution.py:240
  4.7 0.0 collective-permute-start.3
  4.7 1.9 %collective-permute-start.2 = (bf16[128,1792]{1,0:T(8,128)(2,1)}, bf16[128,1792]{1,0:T(8,128)(2,1)S(1)}, u32[]{:S(2)}, u32[]{:S(2)}) collective-permute-start(bf16[128,1792]{1,0:T(8,128)(2,1)} %refs_0_.4), channel_id=1, source_target_pairs={{0,16},{16,0},{1,17},{17,1},{2,18},{18,2},{3,19},{19,3},{4,20},{20... | collective-permute-start | bytes 1376264 | tf_op jit(solution)/shard_map/ppermute | solution.py:246
  6.6 0.1 pad_add_fusion.place
  6.6 0.0 copy-start
  6.7 1.4 %spread.1.refs_14_ = f32[14,4096]{1,0:T(8,128)S(1)} custom-call(s32[2]{0:T(128)S(1)} %pad_add_fusion.place, s32[14,64]{1,0:T(8,128)} %mask.1), custom_call_target="tpu_custom_call" | custom-call | flops 17179869184 | bytes 128 | tf_op jit(solution)/shard_map/spread/pallas_call | solution.py:269
  8.1 0.0 copy-done
  8.1 1.6 %collective-permute-start.1 = (bf16[16,4096]{1,0:T(8,128)(2,1)S(1)}, bf16[16,4096]{1,0:T(8,128)(2,1)S(1)}, u32[]{:S(2)}, u32[]{:S(2)}) collective-permute-start(bf16[16,4096]{1,0:T(8,128)(2,1)S(1)} %copy-done), channel_id=1, source_target_pairs={{2,0},{3,7},{6,2},{7,11},{10,6},{11,15},{14,10},{15,13},{12,14},{1... | collective-permute-start | bytes 393224 | tf_op jit(solution)/shard_map/ppermute | solution.py:240
  9.7 0.4 %collective-permute-start = (bf16[16,4096]{1,0:T(8,128)(2,1)S(1)}, bf16[16,4096]{1,0:T(8,128)(2,1)S(1)}, u32[]{:S(2)}, u32[]{:S(2)}) collective-permute-start(bf16[16,4096]{1,0:T(8,128)(2,1)S(1)} %copy-done), channel_id=1, source_target_pairs={{2,6},{3,1},{6,10},{7,3},{10,14},{11,7},{14,12},{15,11},{12,8},{13... | collective-permute-start | bytes 393224 | tf_op jit(solution)/shard_map/ppermute | solution.py:240
  10.2 1.6 %fetch.2.refs_12_ = bf16[256,4096]{1,0:T(8,128)(2,1)S(1)} custom-call(bf16[1792,4096]{1,0:T(8,128)(2,1)} %weight.1), custom_call_target="tpu_custom_call" | custom-call | flops 128 | bytes 128 | tf_op jit(solution)/shard_map/fetch/pallas_call | solution.py:281
  11.8 0.0 collective-permute-done.4.refs_4_
  11.8 0.0 collective-permute-done.3.refs_3_
  11.8 3.3 %collective-permute-start.8 = (bf16[16,4096]{1,0:T(8,128)(2,1)S(1)}, bf16[16,4096]{1,0:T(8,128)(2,1)S(1)}, u32[]{:S(2)}, u32[]{:S(2)}) collective-permute-start(bf16[16,4096]{1,0:T(8,128)(2,1)S(1)} %collective-permute-done.3.refs_3_), channel_id=1, source_target_pairs={{2,10},{3,5},{6,14},{7,1},{10,12},{11,3},{14,8},{15,7},{12,4},{13,... | collective-permute-start | bytes 393224 | tf_op jit(solution)/shard_map/ppermute | solution.py:240
  15.1 0.8 %collective-permute-start.6 = (bf16[16,4096]{1,0:T(8,128)(2,1)S(1)}, bf16[16,4096]{1,0:T(8,128)(2,1)S(1)}, u32[]{:S(2)}, u32[]{:S(2)}) collective-permute-start(bf16[16,4096]{1,0:T(8,128)(2,1)S(1)} %collective-permute-done.3.refs_3_), channel_id=1, source_target_pairs={{2,6},{3,1},{6,10},{7,3},{10,14},{11,7},{14,12},{15,11},{12,8},{13... | collective-permute-start | bytes 393224 | tf_op jit(solution)/shard_map/ppermute | solution.py:240
  15.9 0.0 collective-permute-done.1.refs_2_
  15.9 1.2 %collective-permute-start.7 = (bf16[16,4096]{1,0:T(8,128)(2,1)S(1)}, bf16[16,4096]{1,0:T(8,128)(2,1)S(1)}, u32[]{:S(2)}, u32[]{:S(2)}) collective-permute-start(bf16[16,4096]{1,0:T(8,128)(2,1)S(1)} %collective-permute-done.4.refs_4_), channel_id=1, source_target_pairs={{2,0},{3,7},{6,2},{7,11},{10,6},{11,15},{14,10},{15,13},{12,14},{1... | collective-permute-start | bytes 393224 | tf_op jit(solution)/shard_map/ppermute | solution.py:240
  17.1 0.0 collective-permute-done.refs_1_
  17.1 0.0 collective-permute-done.2.refs_1_
  17.2 0.0 copy-start.2
  17.2 0.1 collective-permute-start.5
  17.3 4.7 %fetch.3.refs_13_.weight = bf16[1536,4096]{1,0:T(8,128)(2,1)S(1)} custom-call(bf16[1792,4096]{1,0:T(8,128)(2,1)} %weight.1), custom_call_target="tpu_custom_call" | custom-call | flops 17179869184 | bytes 128 | tf_op jit(solution)/shard_map/fetch/pallas_call | solution.py:281
  22.0 0.0 copy-start.1
  22.0 0.0 collective-permute-done.7.refs_8_
  22.0 0.0 collective-permute-done.8.refs_10_
  22.0 0.0 collective-permute-done.6.refs_6_
  22.0 0.5 %collective-permute-start.9 = (bf16[16,4096]{1,0:T(8,128)(2,1)S(1)}, bf16[16,4096]{1,0:T(8,128)(2,1)S(1)}, u32[]{:S(2)}, u32[]{:S(2)}) collective-permute-start(bf16[16,4096]{1,0:T(8,128)(2,1)S(1)} %collective-permute-done.6.refs_6_), channel_id=1, source_target_pairs={{0,1},{1,0},{2,3},{3,2},{4,5},{5,4},{6,7},{7,6},{8,9},{9,8},{10,11... | collective-permute-start | bytes 393224 | tf_op jit(solution)/shard_map/ppermute | solution.py:243
  22.6 0.1 collective-permute-start.10
  22.7 0.4 %collective-permute-start.11 = (bf16[16,4096]{1,0:T(8,128)(2,1)S(1)}, bf16[16,4096]{1,0:T(8,128)(2,1)S(1)}, u32[]{:S(2)}, u32[]{:S(2)}) collective-permute-start(bf16[16,4096]{1,0:T(8,128)(2,1)S(1)} %collective-permute-done.8.refs_10_), channel_id=1, source_target_pairs={{0,1},{1,0},{2,3},{3,2},{4,5},{5,4},{6,7},{7,6},{8,9},{9,8},{10,11... | collective-permute-start | bytes 393224 | tf_op jit(solution)/shard_map/ppermute | solution.py:243
  23.1 0.5 %collective-permute-done.9.refs_7_ = bf16[16,4096]{1,0:T(8,128)(2,1)S(1)} collective-permute-done((bf16[16,4096]{1,0:T(8,128)(2,1)S(1)}, bf16[16,4096]{1,0:T(8,128)(2,1)S(1)}, u32[]{:S(2)}, u32[]{:S(2)}) %collective-permute-start.9) | collective-permute-done | bytes 131104 | tf_op jit(solution)/shard_map/ppermute | solution.py:243
  23.6 0.4 collective-permute-done.10.refs_9_
  23.9 0.2 collective-permute-done.11.refs_11_
  24.1 0.0 collective-permute-done.5.refs_5_
  24.1 0.0 copy-done.2
  24.1 2.5 %first_terms.1 = (bf16[256,4096]{1,0:T(8,128)(2,1)S(1)}, bf16[4096,256]{1,0:T(8,128)(2,1)S(1)}, f32[640,128]{1,0:T(8,128)S(1)}, s16[656,128]{1,0:T(8,128)(2,1)S(1)}) custom-call(s32[2]{0:T(128)S(1)} %pad_add_fusion.place, s32[16,16]{1,0:T(8,128)S(1)} %copy-done.2, bf16[16,4096]{1,0:T(8,128)(2,1)S(1)} %copy-done, ...), custom_call_target="tpu_custom_call" | custom-call | flops 2621440 | bytes 327680 | tf_op jit(solution)/shard_map/first_terms/pallas_call | solution.py:335
  26.6 1.6 %collective-permute-start.13 = (s16[656,128]{1,0:T(8,128)(2,1)S(1)}, s16[656,128]{1,0:T(8,128)(2,1)S(1)}, u32[]{:S(2)}, u32[]{:S(2)}) collective-permute-start(s16[656,128]{1,0:T(8,128)(2,1)S(1)} %get-tuple-element.45), channel_id=1, source_target_pairs={{0,16},{16,0},{1,17},{17,1},{2,18},{18,2},{3,19},{19,3},{4,20},{20... | collective-permute-start | bytes 503816 | tf_op jit(solution)/shard_map/ppermute | solution.py:246
  28.2 0.0 copy-done.1
  28.2 2.7 %more_terms.1 = (f32[1152,128]{1,0:T(8,128)S(1)}, s16[1168,128]{1,0:T(8,128)(2,1)S(1)}, bf16[1792,256]{1,0:T(8,128)(2,1)S(1)}) custom-call(bf16[4096,256]{1,0:T(8,128)(2,1)S(1)} %get-tuple-element.39.turned, bf16[1536,4096]{1,0:T(8,128)(2,1)S(1)} %fetch.3.refs_13_.weight, f32[14,4096]{1,0:T(8,128)S(1)} %spread.1.refs_14_, bf16[128,1792]{1,0:T(8,128)(2,1)S(1)} %copy-done.1, ...), custom_call_target="tpu_custom_call" | custom-call | flops 2621440 | bytes 327680 | tf_op jit(solution)/shard_map/more_terms/pallas_call | solution.py:356
  30.9 0.6 %collective-permute-start.12 = (s16[1168,128]{1,0:T(8,128)(2,1)S(1)}, s16[1168,128]{1,0:T(8,128)(2,1)S(1)}, u32[]{:S(2)}, u32[]{:S(2)}) collective-permute-start(s16[1168,128]{1,0:T(8,128)(2,1)S(1)} %get-tuple-element.43), channel_id=1, source_target_pairs={{0,16},{16,0},{1,17},{17,1},{2,18},{18,2},{3,19},{19,3},{4,20},{20... | collective-permute-start | bytes 897032 | tf_op jit(solution)/shard_map/ppermute | solution.py:246
  31.5 6.0 %weight_grad.1 = bf16[1792,4096]{1,0:T(8,128)(2,1)} custom-call(bf16[1792,256]{1,0:T(8,128)(2,1)S(1)} %get-tuple-element.46.acts, bf16[256,4096]{1,0:T(8,128)(2,1)S(1)} %get-tuple-element.47.full, f32[14,4096]{1,0:T(8,128)S(1)} %spread.1.refs_14_), custom_call_target="tpu_custom_call" | custom-call | flops 2621440 | bytes 327680 | tf_op jit(solution)/shard_map/weight_grad/pallas_call | solution.py:378
  37.6 0.0 collective-permute-done.13.refs_0_
  37.6 0.8 %add_terms.2.refs_1_ = bf16[128,1792]{1,0:T(8,128)(2,1)} custom-call(f32[640,128]{1,0:T(8,128)S(1)} %get-tuple-element.44.own, s16[656,128]{1,0:T(8,128)(2,1)S(1)} %collective-permute-done.13.refs_0_), custom_call_target="tpu_custom_call" | custom-call | flops 17179869184 | bytes 128 | tf_op jit(solution)/shard_map/add_terms/pallas_call | solution.py:399
  38.4 1.6 %collective-permute-done.12.refs_0_ = s16[1168,128]{1,0:T(8,128)(2,1)S(1)} collective-permute-done((s16[1168,128]{1,0:T(8,128)(2,1)S(1)}, s16[1168,128]{1,0:T(8,128)(2,1)S(1)}, u32[]{:S(2)}, u32[]{:S(2)}) %collective-permute-start.12) | collective-permute-done | bytes 299040 | tf_op jit(solution)/shard_map/ppermute | solution.py:246
  40.0 0.9 %add_terms.3 = bf16[128,1792]{1,0:T(8,128)(2,1)} custom-call(f32[1152,128]{1,0:T(8,128)S(1)} %get-tuple-element.42.own, s16[1168,128]{1,0:T(8,128)(2,1)S(1)} %collective-permute-done.12.refs_0_, bf16[128,1792]{1,0:T(8,128)(2,1)} %add_terms.2.refs_1_), custom_call_target="tpu_custom_call", output_to_operand_aliasing={{}: (2, {})} | custom-call | flops 128 | bytes 128 | tf_op jit(solution)/shard_map/add_terms/pallas_call | solution.py:399
  (1 shorter events, 0.0 us)
Async XLA Ops:
  0.6 11.1 %collective-permute-start.4 = (bf16[16,4096]{1,0:T(8,128)(2,1)}, bf16[16,4096]{1,0:T(8,128)(2,1)S(1)}, u32[]{:S(2)}, u32[]{:S(2)}) collective-permute-start(bf16[16,4096]{1,0:T(8,128)(2,1)} %refs_0_.3), channel_id=1, source_target_pairs={{2,4},{3,11},{6,0},{7,15},{10,2},{11,13},{14,6},{15,9},{12,10},{13... | collective-permute-start | bytes 393224 | tf_op jit(solution)/shard_map/ppermute | solution.py:240
  4.7 7.1 %collective-permute-start.3 = (bf16[16,4096]{1,0:T(8,128)(2,1)}, bf16[16,4096]{1,0:T(8,128)(2,1)S(1)}, u32[]{:S(2)}, u32[]{:S(2)}) collective-permute-start(bf16[16,4096]{1,0:T(8,128)(2,1)} %refs_0_.3), channel_id=1, source_target_pairs={{2,10},{3,5},{6,14},{7,1},{10,12},{11,3},{14,8},{15,7},{12,4},{13,... | collective-permute-start | bytes 393224 | tf_op jit(solution)/shard_map/ppermute | solution.py:240
  4.7 12.4 %collective-permute-start.2 = (bf16[128,1792]{1,0:T(8,128)(2,1)}, bf16[128,1792]{1,0:T(8,128)(2,1)S(1)}, u32[]{:S(2)}, u32[]{:S(2)}) collective-permute-start(bf16[128,1792]{1,0:T(8,128)(2,1)} %refs_0_.4), channel_id=1, source_target_pairs={{0,16},{16,0},{1,17},{17,1},{2,18},{18,2},{3,19},{19,3},{4,20},{20... | collective-permute-start | bytes 1376264 | tf_op jit(solution)/shard_map/ppermute | solution.py:246
  6.6 1.5 %copy-start = (bf16[16,4096]{1,0:T(8,128)(2,1)S(1)}, bf16[16,4096]{1,0:T(8,128)(2,1)}, u32[]{:S(2)}) copy-start(bf16[16,4096]{1,0:T(8,128)(2,1)} %refs_0_.3) | copy-start | bytes 393220
  8.1 7.8 %collective-permute-start.1 = (bf16[16,4096]{1,0:T(8,128)(2,1)S(1)}, bf16[16,4096]{1,0:T(8,128)(2,1)S(1)}, u32[]{:S(2)}, u32[]{:S(2)}) collective-permute-start(bf16[16,4096]{1,0:T(8,128)(2,1)S(1)} %copy-done), channel_id=1, source_target_pairs={{2,0},{3,7},{6,2},{7,11},{10,6},{11,15},{14,10},{15,13},{12,14},{1... | collective-permute-start | bytes 393224 | tf_op jit(solution)/shard_map/ppermute | solution.py:240
  9.7 7.4 %collective-permute-start = (bf16[16,4096]{1,0:T(8,128)(2,1)S(1)}, bf16[16,4096]{1,0:T(8,128)(2,1)S(1)}, u32[]{:S(2)}, u32[]{:S(2)}) collective-permute-start(bf16[16,4096]{1,0:T(8,128)(2,1)S(1)} %copy-done), channel_id=1, source_target_pairs={{2,6},{3,1},{6,10},{7,3},{10,14},{11,7},{14,12},{15,11},{12,8},{13... | collective-permute-start | bytes 393224 | tf_op jit(solution)/shard_map/ppermute | solution.py:240
  11.8 10.2 %collective-permute-start.8 = (bf16[16,4096]{1,0:T(8,128)(2,1)S(1)}, bf16[16,4096]{1,0:T(8,128)(2,1)S(1)}, u32[]{:S(2)}, u32[]{:S(2)}) collective-permute-start(bf16[16,4096]{1,0:T(8,128)(2,1)S(1)} %collective-permute-done.3.refs_3_), channel_id=1, source_target_pairs={{2,10},{3,5},{6,14},{7,1},{10,12},{11,3},{14,8},{15,7},{12,4},{13,... | collective-permute-start | bytes 393224 | tf_op jit(solution)/shard_map/ppermute | solution.py:240
  15.1 6.9 %collective-permute-start.6 = (bf16[16,4096]{1,0:T(8,128)(2,1)S(1)}, bf16[16,4096]{1,0:T(8,128)(2,1)S(1)}, u32[]{:S(2)}, u32[]{:S(2)}) collective-permute-start(bf16[16,4096]{1,0:T(8,128)(2,1)S(1)} %collective-permute-done.3.refs_3_), channel_id=1, source_target_pairs={{2,6},{3,1},{6,10},{7,3},{10,14},{11,7},{14,12},{15,11},{12,8},{13... | collective-permute-start | bytes 393224 | tf_op jit(solution)/shard_map/ppermute | solution.py:240
  15.9 6.1 %collective-permute-start.7 = (bf16[16,4096]{1,0:T(8,128)(2,1)S(1)}, bf16[16,4096]{1,0:T(8,128)(2,1)S(1)}, u32[]{:S(2)}, u32[]{:S(2)}) collective-permute-start(bf16[16,4096]{1,0:T(8,128)(2,1)S(1)} %collective-permute-done.4.refs_4_), channel_id=1, source_target_pairs={{2,0},{3,7},{6,2},{7,11},{10,6},{11,15},{14,10},{15,13},{12,14},{1... | collective-permute-start | bytes 393224 | tf_op jit(solution)/shard_map/ppermute | solution.py:240
  17.2 6.9 %copy-start.2 = (s32[16,16]{1,0:T(8,128)S(1)}, s32[16,16]{1,0:T(8,128)}, u32[]{:S(2)}) copy-start(s32[16,16]{1,0:T(8,128)} %constant.11.clone.table) | copy-start | bytes 3076
  17.2 6.9 %collective-permute-start.5 = (bf16[80,4096]{1,0:T(8,128)(2,1)S(1)}, bf16[80,4096]{1,0:T(8,128)(2,1)S(1)}, u32[]{:S(2)}, u32[]{:S(2)}) collective-permute-start(bf16[80,4096]{1,0:T(8,128)(2,1)S(1)} %pack.1), channel_id=1, source_target_pairs={{0,1},{1,0},{2,3},{3,2},{4,5},{5,4},{6,7},{7,6},{8,9},{9,8},{10,11... | collective-permute-start | bytes 1966088 | tf_op jit(solution)/shard_map/ppermute | solution.py:243
  22.0 6.2 %copy-start.1 = (bf16[128,1792]{1,0:T(8,128)(2,1)S(1)}, bf16[128,1792]{1,0:T(8,128)(2,1)}, u32[]{:S(2)}) copy-start(bf16[128,1792]{1,0:T(8,128)(2,1)} %refs_0_.4) | copy-start | bytes 1376260
  22.0 1.5 %collective-permute-start.9 = (bf16[16,4096]{1,0:T(8,128)(2,1)S(1)}, bf16[16,4096]{1,0:T(8,128)(2,1)S(1)}, u32[]{:S(2)}, u32[]{:S(2)}) collective-permute-start(bf16[16,4096]{1,0:T(8,128)(2,1)S(1)} %collective-permute-done.6.refs_6_), channel_id=1, source_target_pairs={{0,1},{1,0},{2,3},{3,2},{4,5},{5,4},{6,7},{7,6},{8,9},{9,8},{10,11... | collective-permute-start | bytes 393224 | tf_op jit(solution)/shard_map/ppermute | solution.py:243
  22.6 1.3 %collective-permute-start.10 = (bf16[16,4096]{1,0:T(8,128)(2,1)S(1)}, bf16[16,4096]{1,0:T(8,128)(2,1)S(1)}, u32[]{:S(2)}, u32[]{:S(2)}) collective-permute-start(bf16[16,4096]{1,0:T(8,128)(2,1)S(1)} %collective-permute-done.7.refs_8_), channel_id=1, source_target_pairs={{0,1},{1,0},{2,3},{3,2},{4,5},{5,4},{6,7},{7,6},{8,9},{9,8},{10,11... | collective-permute-start | bytes 393224 | tf_op jit(solution)/shard_map/ppermute | solution.py:243
  22.7 1.5 %collective-permute-start.11 = (bf16[16,4096]{1,0:T(8,128)(2,1)S(1)}, bf16[16,4096]{1,0:T(8,128)(2,1)S(1)}, u32[]{:S(2)}, u32[]{:S(2)}) collective-permute-start(bf16[16,4096]{1,0:T(8,128)(2,1)S(1)} %collective-permute-done.8.refs_10_), channel_id=1, source_target_pairs={{0,1},{1,0},{2,3},{3,2},{4,5},{5,4},{6,7},{7,6},{8,9},{9,8},{10,11... | collective-permute-start | bytes 393224 | tf_op jit(solution)/shard_map/ppermute | solution.py:243
  26.6 11.0 %collective-permute-start.13 = (s16[656,128]{1,0:T(8,128)(2,1)S(1)}, s16[656,128]{1,0:T(8,128)(2,1)S(1)}, u32[]{:S(2)}, u32[]{:S(2)}) collective-permute-start(s16[656,128]{1,0:T(8,128)(2,1)S(1)} %get-tuple-element.45), channel_id=1, source_target_pairs={{0,16},{16,0},{1,17},{17,1},{2,18},{18,2},{3,19},{19,3},{4,20},{20... | collective-permute-start | bytes 503816 | tf_op jit(solution)/shard_map/ppermute | solution.py:246
  30.9 9.1 %collective-permute-start.12 = (s16[1168,128]{1,0:T(8,128)(2,1)S(1)}, s16[1168,128]{1,0:T(8,128)(2,1)S(1)}, u32[]{:S(2)}, u32[]{:S(2)}) collective-permute-start(s16[1168,128]{1,0:T(8,128)(2,1)S(1)} %get-tuple-element.43), channel_id=1, source_target_pairs={{0,16},{16,0},{1,17},{17,1},{2,18},{18,2},{3,19},{19,3},{4,20},{20... | collective-permute-start | bytes 897032 | tf_op jit(solution)/shard_map/ppermute | solution.py:246

commit v17 on v16

--- a/solution.py
+++ b/solution.py
@@ -296,7 +296,7 @@
     far = [j for j in held if j]
     spread, again = lax.optimization_barrier((spread, grad_output))
     held[1], held[-1] = send_ring(again, 1), send_ring(again, -1)
-    n_soon = max(1, blocks // 7)
+    n_soon = max(1, blocks * 2 // 7)
     weight, spread = lax.optimization_barrier((weight, spread))
     soon = fetch_rows(0, n_soon, BLOCK)
     soon, *ready = lax.optimization_barrier((soon, *(held[j] for j in far)))

time: 41.1 us -> 41 us (level)
  starting transfers between devices: 16.6 us -> 15.4 us
  waiting for transfers between devices: 2.74 us -> 3.73 us
    ppermute x7, waiting for transfers between devices: 0.06 us -> 1.18 us  [send_ring(): return lax.ppermute(x, 'col', perm)]
    ppermute x7, starting transfers between devices: 11.5 us -> 10.9 us  [send_ring(): return lax.ppermute(x, 'col', perm)]
    ppermute x4, starting transfers between devices: 1.12 us -> 0.58 us  [send_core(): return lax.ppermute(x, 'col', [(c, c ^ 1) for c in range(n_cols)])]
    ppermute x3, waiting for transfers between devices: 1.65 us -> 1.2 us  [send_row(): lax.ppermute(x, 'row', [(r, (r + by) % n_rows) for r in range(n_rows)])]
  transfers between devices with their start and end apart: 14 -> 14, of which waited for: 4 -> 6; matrix products, arithmetic and copies ran while one was open for 0% -> 0% of each run, Pallas kernels for 42% -> 43%
where the time goes in v17:
time: 41 us; the launch traced here: 40.8 us
  Pallas kernels  20.8 us (51%)
  starting transfers between devices  15.4 us (38%)
  waiting for transfers between devices  3.73 us (9%)
  between operations  0.76 us (2%)
    ppermute x7, starting transfers between devices, send_ring(): return lax.ppermute(x, 'col', perm)  10.9 us
    pallas_call x2, Pallas kernels, fetch_rows(): pl.pallas_call(functools.partial(fetch_kernel, first), in_specs=[in_hbm()...  6.31 us
    pallas_call x1, Pallas kernels, per_device(): pl.pallas_call(functools.partial(weight_grad_kernel, chunk), in_specs=[in...  6.05 us
    ppermute x3, starting transfers between devices, send_row(): lax.ppermute(x, 'row', [(r, (r + by) % n_rows) for r in range(n_rows)])  4.01 us
    pallas_call x1, Pallas kernels, per_device(): pl.pallas_call(functools.partial(more_terms_kernel, n_parts, piece_blocks...  2.74 us
    pallas_call x1, Pallas kernels, per_device(): pl.pallas_call(functools.partial(first_terms_kernel, n_shards, n_parts, t...  2.49 us
    pallas_call x2, Pallas kernels, per_device(): pl.pallas_call(functools.partial(finish_kernel, sum(sizes[:p]), n_parts),...  1.73 us
    pallas_call x1, Pallas kernels, per_device(): pl.pallas_call(spread_kernel, in_specs=[in_smem(), in_hbm()], out_specs=i...  1.44 us
  transfers between devices with their start and end apart: 14, of which 6 were waited for; matrix products, arithmetic and copies ran while one was open for 0% of the time, Pallas kernels for 43%

profile of v17, /device:TPU:0, one launch (start us, length us, event | category | flops | bytes accessed | tf_op | source)
XLA Modules:
  0.0 40.8 jit_solution(2302435543239592455)
XLA Ops:
  0.6 4.1 %collective-permute-start.4 = (bf16[16,4096]{1,0:T(8,128)(2,1)}, bf16[16,4096]{1,0:T(8,128)(2,1)S(1)}, u32[]{:S(2)}, u32[]{:S(2)}) collective-permute-start(bf16[16,4096]{1,0:T(8,128)(2,1)} %refs_0_.3), channel_id=1, source_target_pairs={{2,4},{3,11},{6,0},{7,15},{10,2},{11,13},{14,6},{15,9},{12,10},{13... | collective-permute-start | bytes 393224 | tf_op jit(solution)/shard_map/ppermute | solution.py:240
  4.7 0.0 collective-permute-start.3
  4.7 1.9 %collective-permute-start.2 = (bf16[128,1792]{1,0:T(8,128)(2,1)}, bf16[128,1792]{1,0:T(8,128)(2,1)S(1)}, u32[]{:S(2)}, u32[]{:S(2)}) collective-permute-start(bf16[128,1792]{1,0:T(8,128)(2,1)} %refs_0_.4), channel_id=1, source_target_pairs={{0,16},{16,0},{1,17},{17,1},{2,18},{18,2},{3,19},{19,3},{4,20},{20... | collective-permute-start | bytes 1376264 | tf_op jit(solution)/shard_map/ppermute | solution.py:246
  6.6 0.1 pad_add_fusion.place
  6.6 0.0 copy-start
  6.7 1.4 %spread.1.refs_14_ = f32[14,4096]{1,0:T(8,128)S(1)} custom-call(s32[2]{0:T(128)S(1)} %pad_add_fusion.place, s32[14,64]{1,0:T(8,128)} %mask.1), custom_call_target="tpu_custom_call" | custom-call | flops 17179869184 | bytes 128 | tf_op jit(solution)/shard_map/spread/pallas_call | solution.py:269
  8.1 0.0 copy-done
  8.1 1.6 %collective-permute-start.1 = (bf16[16,4096]{1,0:T(8,128)(2,1)S(1)}, bf16[16,4096]{1,0:T(8,128)(2,1)S(1)}, u32[]{:S(2)}, u32[]{:S(2)}) collective-permute-start(bf16[16,4096]{1,0:T(8,128)(2,1)S(1)} %copy-done), channel_id=1, source_target_pairs={{2,0},{3,7},{6,2},{7,11},{10,6},{11,15},{14,10},{15,13},{12,14},{1... | collective-permute-start | bytes 393224 | tf_op jit(solution)/shard_map/ppermute | solution.py:240
  9.7 0.4 %collective-permute-start = (bf16[16,4096]{1,0:T(8,128)(2,1)S(1)}, bf16[16,4096]{1,0:T(8,128)(2,1)S(1)}, u32[]{:S(2)}, u32[]{:S(2)}) collective-permute-start(bf16[16,4096]{1,0:T(8,128)(2,1)S(1)} %copy-done), channel_id=1, source_target_pairs={{2,6},{3,1},{6,10},{7,3},{10,14},{11,7},{14,12},{15,11},{12,8},{13... | collective-permute-start | bytes 393224 | tf_op jit(solution)/shard_map/ppermute | solution.py:240
  10.2 2.2 %fetch.2.refs_12_ = bf16[512,4096]{1,0:T(8,128)(2,1)S(1)} custom-call(bf16[1792,4096]{1,0:T(8,128)(2,1)} %weight.1), custom_call_target="tpu_custom_call" | custom-call | flops 128 | bytes 128 | tf_op jit(solution)/shard_map/fetch/pallas_call | solution.py:281
  12.4 0.0 collective-permute-done.4.refs_4_
  12.4 0.0 collective-permute-done.3.refs_3_
  12.4 2.7 %collective-permute-start.8 = (bf16[16,4096]{1,0:T(8,128)(2,1)S(1)}, bf16[16,4096]{1,0:T(8,128)(2,1)S(1)}, u32[]{:S(2)}, u32[]{:S(2)}) collective-permute-start(bf16[16,4096]{1,0:T(8,128)(2,1)S(1)} %collective-permute-done.3.refs_3_), channel_id=1, source_target_pairs={{2,10},{3,5},{6,14},{7,1},{10,12},{11,3},{14,8},{15,7},{12,4},{13,... | collective-permute-start | bytes 393224 | tf_op jit(solution)/shard_map/ppermute | solution.py:240
  15.1 1.5 %collective-permute-start.6 = (bf16[16,4096]{1,0:T(8,128)(2,1)S(1)}, bf16[16,4096]{1,0:T(8,128)(2,1)S(1)}, u32[]{:S(2)}, u32[]{:S(2)}) collective-permute-start(bf16[16,4096]{1,0:T(8,128)(2,1)S(1)} %collective-permute-done.3.refs_3_), channel_id=1, source_target_pairs={{2,6},{3,1},{6,10},{7,3},{10,14},{11,7},{14,12},{15,11},{12,8},{13... | collective-permute-start | bytes 393224 | tf_op jit(solution)/shard_map/ppermute | solution.py:240
  16.6 0.0 collective-permute-done.1.refs_2_
  16.6 0.6 %collective-permute-start.7 = (bf16[16,4096]{1,0:T(8,128)(2,1)S(1)}, bf16[16,4096]{1,0:T(8,128)(2,1)S(1)}, u32[]{:S(2)}, u32[]{:S(2)}) collective-permute-start(bf16[16,4096]{1,0:T(8,128)(2,1)S(1)} %collective-permute-done.4.refs_4_), channel_id=1, source_target_pairs={{2,0},{3,7},{6,2},{7,11},{10,6},{11,15},{14,10},{15,13},{12,14},{1... | collective-permute-start | bytes 393224 | tf_op jit(solution)/shard_map/ppermute | solution.py:240
  17.1 0.0 collective-permute-done.refs_1_
  17.1 0.0 collective-permute-done.2.refs_1_
  17.2 0.0 copy-start.2
  17.2 0.1 collective-permute-start.5
  17.3 4.1 %fetch.3.refs_13_.weight = bf16[1280,4096]{1,0:T(8,128)(2,1)S(1)} custom-call(bf16[1792,4096]{1,0:T(8,128)(2,1)} %weight.1), custom_call_target="tpu_custom_call" | custom-call | flops 17179869184 | bytes 128 | tf_op jit(solution)/shard_map/fetch/pallas_call | solution.py:281
  21.4 0.0 copy-start.1
  21.4 0.1 collective-permute-done.7.refs_8_
  21.5 0.0 collective-permute-done.8.refs_10_
  21.5 1.0 %collective-permute-done.6.refs_6_ = bf16[16,4096]{1,0:T(8,128)(2,1)S(1)} collective-permute-done((bf16[16,4096]{1,0:T(8,128)(2,1)S(1)}, bf16[16,4096]{1,0:T(8,128)(2,1)S(1)}, u32[]{:S(2)}, u32[]{:S(2)}) %collective-permute-start.6) | collective-permute-done | bytes 131104 | tf_op jit(solution)/shard_map/ppermute | solution.py:240
  22.6 0.0 collective-permute-start.9
  22.6 0.5 %collective-permute-start.10 = (bf16[16,4096]{1,0:T(8,128)(2,1)S(1)}, bf16[16,4096]{1,0:T(8,128)(2,1)S(1)}, u32[]{:S(2)}, u32[]{:S(2)}) collective-permute-start(bf16[16,4096]{1,0:T(8,128)(2,1)S(1)} %collective-permute-done.7.refs_8_), channel_id=1, source_target_pairs={{0,1},{1,0},{2,3},{3,2},{4,5},{5,4},{6,7},{7,6},{8,9},{9,8},{10,11... | collective-permute-start | bytes 393224 | tf_op jit(solution)/shard_map/ppermute | solution.py:243
  23.1 0.0 collective-permute-start.11
  23.1 0.8 %collective-permute-done.9.refs_7_ = bf16[16,4096]{1,0:T(8,128)(2,1)S(1)} collective-permute-done((bf16[16,4096]{1,0:T(8,128)(2,1)S(1)}, bf16[16,4096]{1,0:T(8,128)(2,1)S(1)}, u32[]{:S(2)}, u32[]{:S(2)}) %collective-permute-start.9) | collective-permute-done | bytes 131104 | tf_op jit(solution)/shard_map/ppermute | solution.py:243
  23.9 0.2 collective-permute-done.10.refs_9_
  24.1 0.3 collective-permute-done.11.refs_11_
  24.4 0.0 collective-permute-done.5.refs_5_
  24.4 0.0 copy-done.2
  24.4 2.5 %first_terms.1 = (bf16[256,4096]{1,0:T(8,128)(2,1)S(1)}, bf16[4096,256]{1,0:T(8,128)(2,1)S(1)}, f32[640,128]{1,0:T(8,128)S(1)}, s16[656,128]{1,0:T(8,128)(2,1)S(1)}) custom-call(s32[2]{0:T(128)S(1)} %pad_add_fusion.place, s32[16,16]{1,0:T(8,128)S(1)} %copy-done.2, bf16[16,4096]{1,0:T(8,128)(2,1)S(1)} %copy-done, ...), custom_call_target="tpu_custom_call" | custom-call | flops 2621440 | bytes 327680 | tf_op jit(solution)/shard_map/first_terms/pallas_call | solution.py:335
  26.9 1.3 %collective-permute-start.13 = (s16[656,128]{1,0:T(8,128)(2,1)S(1)}, s16[656,128]{1,0:T(8,128)(2,1)S(1)}, u32[]{:S(2)}, u32[]{:S(2)}) collective-permute-start(s16[656,128]{1,0:T(8,128)(2,1)S(1)} %get-tuple-element.45), channel_id=1, source_target_pairs={{0,16},{16,0},{1,17},{17,1},{2,18},{18,2},{3,19},{19,3},{4,20},{20... | collective-permute-start | bytes 503816 | tf_op jit(solution)/shard_map/ppermute | solution.py:246
  28.2 0.0 copy-done.1
  28.2 2.7 %more_terms.1 = (f32[1152,128]{1,0:T(8,128)S(1)}, s16[1168,128]{1,0:T(8,128)(2,1)S(1)}, bf16[1792,256]{1,0:T(8,128)(2,1)S(1)}) custom-call(bf16[4096,256]{1,0:T(8,128)(2,1)S(1)} %get-tuple-element.39.turned, bf16[1280,4096]{1,0:T(8,128)(2,1)S(1)} %fetch.3.refs_13_.weight, f32[14,4096]{1,0:T(8,128)S(1)} %spread.1.refs_14_, bf16[128,1792]{1,0:T(8,128)(2,1)S(1)} %copy-done.1, ...), custom_call_target="tpu_custom_call" | custom-call | flops 2621440 | bytes 327680 | tf_op jit(solution)/shard_map/more_terms/pallas_call | solution.py:356
  31.0 0.9 %collective-permute-start.12 = (s16[1168,128]{1,0:T(8,128)(2,1)S(1)}, s16[1168,128]{1,0:T(8,128)(2,1)S(1)}, u32[]{:S(2)}, u32[]{:S(2)}) collective-permute-start(s16[1168,128]{1,0:T(8,128)(2,1)S(1)} %get-tuple-element.43), channel_id=1, source_target_pairs={{0,16},{16,0},{1,17},{17,1},{2,18},{18,2},{3,19},{19,3},{4,20},{20... | collective-permute-start | bytes 897032 | tf_op jit(solution)/shard_map/ppermute | solution.py:246
  31.8 6.1 %weight_grad.1 = bf16[1792,4096]{1,0:T(8,128)(2,1)} custom-call(bf16[1792,256]{1,0:T(8,128)(2,1)S(1)} %get-tuple-element.46.acts, bf16[256,4096]{1,0:T(8,128)(2,1)S(1)} %get-tuple-element.47.full, f32[14,4096]{1,0:T(8,128)S(1)} %spread.1.refs_14_), custom_call_target="tpu_custom_call" | custom-call | flops 2621440 | bytes 327680 | tf_op jit(solution)/shard_map/weight_grad/pallas_call | solution.py:378
  37.9 0.0 collective-permute-done.13.refs_0_
  37.9 0.8 %add_terms.2.refs_1_ = bf16[128,1792]{1,0:T(8,128)(2,1)} custom-call(f32[640,128]{1,0:T(8,128)S(1)} %get-tuple-element.44.own, s16[656,128]{1,0:T(8,128)(2,1)S(1)} %collective-permute-done.13.refs_0_), custom_call_target="tpu_custom_call" | custom-call | flops 17179869184 | bytes 128 | tf_op jit(solution)/shard_map/add_terms/pallas_call | solution.py:399
  38.7 1.2 %collective-permute-done.12.refs_0_ = s16[1168,128]{1,0:T(8,128)(2,1)S(1)} collective-permute-done((s16[1168,128]{1,0:T(8,128)(2,1)S(1)}, s16[1168,128]{1,0:T(8,128)(2,1)S(1)}, u32[]{:S(2)}, u32[]{:S(2)}) %collective-permute-start.12) | collective-permute-done | bytes 299040 | tf_op jit(solution)/shard_map/ppermute | solution.py:246
  39.9 0.9 %add_terms.3 = bf16[128,1792]{1,0:T(8,128)(2,1)} custom-call(f32[1152,128]{1,0:T(8,128)S(1)} %get-tuple-element.42.own, s16[1168,128]{1,0:T(8,128)(2,1)S(1)} %collective-permute-done.12.refs_0_, bf16[128,1792]{1,0:T(8,128)(2,1)} %add_terms.2.refs_1_), custom_call_target="tpu_custom_call", output_to_operand_aliasing={{}: (2, {})} | custom-call | flops 128 | bytes 128 | tf_op jit(solution)/shard_map/add_terms/pallas_call | solution.py:399
  (1 shorter events, 0.0 us)
Async XLA Ops:
  0.6 11.8 %collective-permute-start.4 = (bf16[16,4096]{1,0:T(8,128)(2,1)}, bf16[16,4096]{1,0:T(8,128)(2,1)S(1)}, u32[]{:S(2)}, u32[]{:S(2)}) collective-permute-start(bf16[16,4096]{1,0:T(8,128)(2,1)} %refs_0_.3), channel_id=1, source_target_pairs={{2,4},{3,11},{6,0},{7,15},{10,2},{11,13},{14,6},{15,9},{12,10},{13... | collective-permute-start | bytes 393224 | tf_op jit(solution)/shard_map/ppermute | solution.py:240
  4.7 7.7 %collective-permute-start.3 = (bf16[16,4096]{1,0:T(8,128)(2,1)}, bf16[16,4096]{1,0:T(8,128)(2,1)S(1)}, u32[]{:S(2)}, u32[]{:S(2)}) collective-permute-start(bf16[16,4096]{1,0:T(8,128)(2,1)} %refs_0_.3), channel_id=1, source_target_pairs={{2,10},{3,5},{6,14},{7,1},{10,12},{11,3},{14,8},{15,7},{12,4},{13,... | collective-permute-start | bytes 393224 | tf_op jit(solution)/shard_map/ppermute | solution.py:240
  4.7 12.4 %collective-permute-start.2 = (bf16[128,1792]{1,0:T(8,128)(2,1)}, bf16[128,1792]{1,0:T(8,128)(2,1)S(1)}, u32[]{:S(2)}, u32[]{:S(2)}) collective-permute-start(bf16[128,1792]{1,0:T(8,128)(2,1)} %refs_0_.4), channel_id=1, source_target_pairs={{0,16},{16,0},{1,17},{17,1},{2,18},{18,2},{3,19},{19,3},{4,20},{20... | collective-permute-start | bytes 1376264 | tf_op jit(solution)/shard_map/ppermute | solution.py:246
  6.6 1.5 %copy-start = (bf16[16,4096]{1,0:T(8,128)(2,1)S(1)}, bf16[16,4096]{1,0:T(8,128)(2,1)}, u32[]{:S(2)}) copy-start(bf16[16,4096]{1,0:T(8,128)(2,1)} %refs_0_.3) | copy-start | bytes 393220
  8.1 8.4 %collective-permute-start.1 = (bf16[16,4096]{1,0:T(8,128)(2,1)S(1)}, bf16[16,4096]{1,0:T(8,128)(2,1)S(1)}, u32[]{:S(2)}, u32[]{:S(2)}) collective-permute-start(bf16[16,4096]{1,0:T(8,128)(2,1)S(1)} %copy-done), channel_id=1, source_target_pairs={{2,0},{3,7},{6,2},{7,11},{10,6},{11,15},{14,10},{15,13},{12,14},{1... | collective-permute-start | bytes 393224 | tf_op jit(solution)/shard_map/ppermute | solution.py:240
  9.7 7.4 %collective-permute-start = (bf16[16,4096]{1,0:T(8,128)(2,1)S(1)}, bf16[16,4096]{1,0:T(8,128)(2,1)S(1)}, u32[]{:S(2)}, u32[]{:S(2)}) collective-permute-start(bf16[16,4096]{1,0:T(8,128)(2,1)S(1)} %copy-done), channel_id=1, source_target_pairs={{2,6},{3,1},{6,10},{7,3},{10,14},{11,7},{14,12},{15,11},{12,8},{13... | collective-permute-start | bytes 393224 | tf_op jit(solution)/shard_map/ppermute | solution.py:240
  12.4 9.1 %collective-permute-start.8 = (bf16[16,4096]{1,0:T(8,128)(2,1)S(1)}, bf16[16,4096]{1,0:T(8,128)(2,1)S(1)}, u32[]{:S(2)}, u32[]{:S(2)}) collective-permute-start(bf16[16,4096]{1,0:T(8,128)(2,1)S(1)} %collective-permute-done.3.refs_3_), channel_id=1, source_target_pairs={{2,10},{3,5},{6,14},{7,1},{10,12},{11,3},{14,8},{15,7},{12,4},{13,... | collective-permute-start | bytes 393224 | tf_op jit(solution)/shard_map/ppermute | solution.py:240
  15.1 7.5 %collective-permute-start.6 = (bf16[16,4096]{1,0:T(8,128)(2,1)S(1)}, bf16[16,4096]{1,0:T(8,128)(2,1)S(1)}, u32[]{:S(2)}, u32[]{:S(2)}) collective-permute-start(bf16[16,4096]{1,0:T(8,128)(2,1)S(1)} %collective-permute-done.3.refs_3_), channel_id=1, source_target_pairs={{2,6},{3,1},{6,10},{7,3},{10,14},{11,7},{14,12},{15,11},{12,8},{13... | collective-permute-start | bytes 393224 | tf_op jit(solution)/shard_map/ppermute | solution.py:240
  16.6 5.0 %collective-permute-start.7 = (bf16[16,4096]{1,0:T(8,128)(2,1)S(1)}, bf16[16,4096]{1,0:T(8,128)(2,1)S(1)}, u32[]{:S(2)}, u32[]{:S(2)}) collective-permute-start(bf16[16,4096]{1,0:T(8,128)(2,1)S(1)} %collective-permute-done.4.refs_4_), channel_id=1, source_target_pairs={{2,0},{3,7},{6,2},{7,11},{10,6},{11,15},{14,10},{15,13},{12,14},{1... | collective-permute-start | bytes 393224 | tf_op jit(solution)/shard_map/ppermute | solution.py:240
  17.2 7.3 %copy-start.2 = (s32[16,16]{1,0:T(8,128)S(1)}, s32[16,16]{1,0:T(8,128)}, u32[]{:S(2)}) copy-start(s32[16,16]{1,0:T(8,128)} %constant.11.clone.table) | copy-start | bytes 3076
  17.2 7.2 %collective-permute-start.5 = (bf16[80,4096]{1,0:T(8,128)(2,1)S(1)}, bf16[80,4096]{1,0:T(8,128)(2,1)S(1)}, u32[]{:S(2)}, u32[]{:S(2)}) collective-permute-start(bf16[80,4096]{1,0:T(8,128)(2,1)S(1)} %pack.1), channel_id=1, source_target_pairs={{0,1},{1,0},{2,3},{3,2},{4,5},{5,4},{6,7},{7,6},{8,9},{9,8},{10,11... | collective-permute-start | bytes 1966088 | tf_op jit(solution)/shard_map/ppermute | solution.py:243
  21.4 6.8 %copy-start.1 = (bf16[128,1792]{1,0:T(8,128)(2,1)S(1)}, bf16[128,1792]{1,0:T(8,128)(2,1)}, u32[]{:S(2)}) copy-start(bf16[128,1792]{1,0:T(8,128)(2,1)} %refs_0_.4) | copy-start | bytes 1376260
  22.6 1.3 %collective-permute-start.9 = (bf16[16,4096]{1,0:T(8,128)(2,1)S(1)}, bf16[16,4096]{1,0:T(8,128)(2,1)S(1)}, u32[]{:S(2)}, u32[]{:S(2)}) collective-permute-start(bf16[16,4096]{1,0:T(8,128)(2,1)S(1)} %collective-permute-done.6.refs_6_), channel_id=1, source_target_pairs={{0,1},{1,0},{2,3},{3,2},{4,5},{5,4},{6,7},{7,6},{8,9},{9,8},{10,11... | collective-permute-start | bytes 393224 | tf_op jit(solution)/shard_map/ppermute | solution.py:243
  22.6 1.5 %collective-permute-start.10 = (bf16[16,4096]{1,0:T(8,128)(2,1)S(1)}, bf16[16,4096]{1,0:T(8,128)(2,1)S(1)}, u32[]{:S(2)}, u32[]{:S(2)}) collective-permute-start(bf16[16,4096]{1,0:T(8,128)(2,1)S(1)} %collective-permute-done.7.refs_8_), channel_id=1, source_target_pairs={{0,1},{1,0},{2,3},{3,2},{4,5},{5,4},{6,7},{7,6},{8,9},{9,8},{10,11... | collective-permute-start | bytes 393224 | tf_op jit(solution)/shard_map/ppermute | solution.py:243
  23.1 1.3 %collective-permute-start.11 = (bf16[16,4096]{1,0:T(8,128)(2,1)S(1)}, bf16[16,4096]{1,0:T(8,128)(2,1)S(1)}, u32[]{:S(2)}, u32[]{:S(2)}) collective-permute-start(bf16[16,4096]{1,0:T(8,128)(2,1)S(1)} %collective-permute-done.8.refs_10_), channel_id=1, source_target_pairs={{0,1},{1,0},{2,3},{3,2},{4,5},{5,4},{6,7},{7,6},{8,9},{9,8},{10,11... | collective-permute-start | bytes 393224 | tf_op jit(solution)/shard_map/ppermute | solution.py:243
  26.9 11.0 %collective-permute-start.13 = (s16[656,128]{1,0:T(8,128)(2,1)S(1)}, s16[656,128]{1,0:T(8,128)(2,1)S(1)}, u32[]{:S(2)}, u32[]{:S(2)}) collective-permute-start(s16[656,128]{1,0:T(8,128)(2,1)S(1)} %get-tuple-element.45), channel_id=1, source_target_pairs={{0,16},{16,0},{1,17},{17,1},{2,18},{18,2},{3,19},{19,3},{4,20},{20... | collective-permute-start | bytes 503816 | tf_op jit(solution)/shard_map/ppermute | solution.py:246
  31.0 9.0 %collective-permute-start.12 = (s16[1168,128]{1,0:T(8,128)(2,1)S(1)}, s16[1168,128]{1,0:T(8,128)(2,1)S(1)}, u32[]{:S(2)}, u32[]{:S(2)}) collective-permute-start(s16[1168,128]{1,0:T(8,128)(2,1)S(1)} %get-tuple-element.43), channel_id=1, source_target_pairs={{0,16},{16,0},{1,17},{17,1},{2,18},{18,2},{3,19},{19,3},{4,20},{20... | collective-permute-start | bytes 897032 | tf_op jit(solution)/shard_map/ppermute | solution.py:246

commit v18 on v17

--- a/solution.py
+++ b/solution.py
@@ -312,8 +312,9 @@
         (weight, held[1], held[-1], *acts)
     )
     rest = fetch_rows(n_soon, blocks - n_soon, 1 << 34)
-    rest, *ready = lax.optimization_barrier((rest, *(held[j] for j in last)))
-    held.update(zip(last, ready, strict=True))
+    order = sorted(last, reverse=True)
+    rest, *ready = lax.optimization_barrier((rest, *(held[j] for j in order)))
+    held.update(zip(order, ready, strict=True))
     packed = pl.pallas_call(
         pack_kernel,
         in_specs=[in_vmem()] * len(near),

time: 41 us -> 41.8 us (1.020)
  waiting for transfers between devices: 3.73 us -> 4.53 us
    ppermute x7, waiting for transfers between devices: 1.18 us -> 2.14 us  [send_ring(): return lax.ppermute(x, 'col', perm)]
  transfers between devices with their start and end apart: 14 -> 14, of which waited for: 6 -> 6; matrix products, arithmetic and copies ran while one was open for 0% -> 0% of each run, Pallas kernels for 43% -> 42%
where the time goes in v18:
time: 41.8 us; the launch traced here: 41.6 us
  Pallas kernels  20.8 us (50%)
  starting transfers between devices  15.4 us (37%)
  waiting for transfers between devices  4.53 us (11%)
  between operations  0.76 us (2%)
    ppermute x7, starting transfers between devices, send_ring(): return lax.ppermute(x, 'col', perm)  10.9 us
    pallas_call x2, Pallas kernels, fetch_rows(): pl.pallas_call(functools.partial(fetch_kernel, first), in_specs=[in_hbm()...  6.31 us
    pallas_call x1, Pallas kernels, per_device(): pl.pallas_call(functools.partial(weight_grad_kernel, chunk), in_specs=[in...  6.05 us
    ppermute x3, starting transfers between devices, send_row(): lax.ppermute(x, 'row', [(r, (r + by) % n_rows) for r in range(n_rows)])  4.01 us
    pallas_call x1, Pallas kernels, per_device(): pl.pallas_call(functools.partial(more_terms_kernel, n_parts, piece_blocks...  2.74 us
    pallas_call x1, Pallas kernels, per_device(): pl.pallas_call(functools.partial(first_terms_kernel, n_shards, n_parts, t...  2.49 us
    ppermute x7, waiting for transfers between devices, send_ring(): return lax.ppermute(x, 'col', perm)  2.14 us
    pallas_call x2, Pallas kernels, per_device(): pl.pallas_call(functools.partial(finish_kernel, sum(sizes[:p]), n_parts),...  1.73 us
  transfers between devices with their start and end apart: 14, of which 6 were waited for; matrix products, arithmetic and copies ran while one was open for 0% of the time, Pallas kernels for 42%

profile of v18, /device:TPU:0, one launch (start us, length us, event | category | flops | bytes accessed | tf_op | source)
XLA Modules:
  0.0 41.6 jit_solution(17750589730006001493)
XLA Ops:
  0.6 4.1 %collective-permute-start.4 = (bf16[16,4096]{1,0:T(8,128)(2,1)}, bf16[16,4096]{1,0:T(8,128)(2,1)S(1)}, u32[]{:S(2)}, u32[]{:S(2)}) collective-permute-start(bf16[16,4096]{1,0:T(8,128)(2,1)} %refs_0_.3), channel_id=1, source_target_pairs={{2,4},{3,11},{6,0},{7,15},{10,2},{11,13},{14,6},{15,9},{12,10},{13... | collective-permute-start | bytes 393224 | tf_op jit(solution)/shard_map/ppermute | solution.py:240
  4.7 0.0 collective-permute-start.3
  4.7 1.9 %collective-permute-start.2 = (bf16[128,1792]{1,0:T(8,128)(2,1)}, bf16[128,1792]{1,0:T(8,128)(2,1)S(1)}, u32[]{:S(2)}, u32[]{:S(2)}) collective-permute-start(bf16[128,1792]{1,0:T(8,128)(2,1)} %refs_0_.4), channel_id=1, source_target_pairs={{0,16},{16,0},{1,17},{17,1},{2,18},{18,2},{3,19},{19,3},{4,20},{20... | collective-permute-start | bytes 1376264 | tf_op jit(solution)/shard_map/ppermute | solution.py:246
  6.6 0.1 pad_add_fusion.place
  6.6 0.0 copy-start
  6.7 1.4 %spread.1.refs_14_ = f32[14,4096]{1,0:T(8,128)S(1)} custom-call(s32[2]{0:T(128)S(1)} %pad_add_fusion.place, s32[14,64]{1,0:T(8,128)} %mask.1), custom_call_target="tpu_custom_call" | custom-call | flops 17179869184 | bytes 128 | tf_op jit(solution)/shard_map/spread/pallas_call | solution.py:269
  8.1 0.0 copy-done
  8.1 1.6 %collective-permute-start.1 = (bf16[16,4096]{1,0:T(8,128)(2,1)S(1)}, bf16[16,4096]{1,0:T(8,128)(2,1)S(1)}, u32[]{:S(2)}, u32[]{:S(2)}) collective-permute-start(bf16[16,4096]{1,0:T(8,128)(2,1)S(1)} %copy-done), channel_id=1, source_target_pairs={{2,0},{3,7},{6,2},{7,11},{10,6},{11,15},{14,10},{15,13},{12,14},{1... | collective-permute-start | bytes 393224 | tf_op jit(solution)/shard_map/ppermute | solution.py:240
  9.7 0.4 %collective-permute-start = (bf16[16,4096]{1,0:T(8,128)(2,1)S(1)}, bf16[16,4096]{1,0:T(8,128)(2,1)S(1)}, u32[]{:S(2)}, u32[]{:S(2)}) collective-permute-start(bf16[16,4096]{1,0:T(8,128)(2,1)S(1)} %copy-done), channel_id=1, source_target_pairs={{2,6},{3,1},{6,10},{7,3},{10,14},{11,7},{14,12},{15,11},{12,8},{13... | collective-permute-start | bytes 393224 | tf_op jit(solution)/shard_map/ppermute | solution.py:240
  10.2 2.2 %fetch.2.refs_12_ = bf16[512,4096]{1,0:T(8,128)(2,1)S(1)} custom-call(bf16[1792,4096]{1,0:T(8,128)(2,1)} %weight.1), custom_call_target="tpu_custom_call" | custom-call | flops 128 | bytes 128 | tf_op jit(solution)/shard_map/fetch/pallas_call | solution.py:281
  12.4 0.0 collective-permute-done.4.refs_4_
  12.4 0.0 collective-permute-done.3.refs_3_
  12.4 1.5 %collective-permute-start.7 = (bf16[16,4096]{1,0:T(8,128)(2,1)S(1)}, bf16[16,4096]{1,0:T(8,128)(2,1)S(1)}, u32[]{:S(2)}, u32[]{:S(2)}) collective-permute-start(bf16[16,4096]{1,0:T(8,128)(2,1)S(1)} %collective-permute-done.3.refs_3_), channel_id=1, source_target_pairs={{2,6},{3,1},{6,10},{7,3},{10,14},{11,7},{14,12},{15,11},{12,8},{13... | collective-permute-start | bytes 393224 | tf_op jit(solution)/shard_map/ppermute | solution.py:240
  14.0 2.6 %collective-permute-start.6 = (bf16[16,4096]{1,0:T(8,128)(2,1)S(1)}, bf16[16,4096]{1,0:T(8,128)(2,1)S(1)}, u32[]{:S(2)}, u32[]{:S(2)}) collective-permute-start(bf16[16,4096]{1,0:T(8,128)(2,1)S(1)} %collective-permute-done.3.refs_3_), channel_id=1, source_target_pairs={{2,10},{3,5},{6,14},{7,1},{10,12},{11,3},{14,8},{15,7},{12,4},{13,... | collective-permute-start | bytes 393224 | tf_op jit(solution)/shard_map/ppermute | solution.py:240
  16.6 0.0 collective-permute-done.1.refs_2_
  16.6 0.6 %collective-permute-start.8 = (bf16[16,4096]{1,0:T(8,128)(2,1)S(1)}, bf16[16,4096]{1,0:T(8,128)(2,1)S(1)}, u32[]{:S(2)}, u32[]{:S(2)}) collective-permute-start(bf16[16,4096]{1,0:T(8,128)(2,1)S(1)} %collective-permute-done.4.refs_4_), channel_id=1, source_target_pairs={{2,0},{3,7},{6,2},{7,11},{10,6},{11,15},{14,10},{15,13},{12,14},{1... | collective-permute-start | bytes 393224 | tf_op jit(solution)/shard_map/ppermute | solution.py:240
  17.1 0.0 collective-permute-done.refs_1_
  17.1 0.0 collective-permute-done.2.refs_1_
  17.2 0.0 copy-start.2
  17.2 0.1 collective-permute-start.5
  17.3 4.1 %fetch.3.refs_13_.weight = bf16[1280,4096]{1,0:T(8,128)(2,1)S(1)} custom-call(bf16[1792,4096]{1,0:T(8,128)(2,1)} %weight.1), custom_call_target="tpu_custom_call" | custom-call | flops 17179869184 | bytes 128 | tf_op jit(solution)/shard_map/fetch/pallas_call | solution.py:281
  21.4 0.0 copy-start.1
  21.4 0.1 collective-permute-done.8.refs_8_
  21.5 0.0 collective-permute-done.7.refs_6_
  21.5 2.0 %collective-permute-done.6.refs_10_ = bf16[16,4096]{1,0:T(8,128)(2,1)S(1)} collective-permute-done((bf16[16,4096]{1,0:T(8,128)(2,1)S(1)}, bf16[16,4096]{1,0:T(8,128)(2,1)S(1)}, u32[]{:S(2)}, u32[]{:S(2)}) %collective-permute-start.6) | collective-permute-done | bytes 131104 | tf_op jit(solution)/shard_map/ppermute | solution.py:240
  23.5 0.0 collective-permute-start.9
  23.5 0.5 %collective-permute-start.10 = (bf16[16,4096]{1,0:T(8,128)(2,1)S(1)}, bf16[16,4096]{1,0:T(8,128)(2,1)S(1)}, u32[]{:S(2)}, u32[]{:S(2)}) collective-permute-start(bf16[16,4096]{1,0:T(8,128)(2,1)S(1)} %collective-permute-done.8.refs_8_), channel_id=1, source_target_pairs={{0,1},{1,0},{2,3},{3,2},{4,5},{5,4},{6,7},{7,6},{8,9},{9,8},{10,11... | collective-permute-start | bytes 393224 | tf_op jit(solution)/shard_map/ppermute | solution.py:243
  24.0 0.0 collective-permute-start.11
  24.0 0.8 %collective-permute-done.9.refs_7_ = bf16[16,4096]{1,0:T(8,128)(2,1)S(1)} collective-permute-done((bf16[16,4096]{1,0:T(8,128)(2,1)S(1)}, bf16[16,4096]{1,0:T(8,128)(2,1)S(1)}, u32[]{:S(2)}, u32[]{:S(2)}) %collective-permute-start.9) | collective-permute-done | bytes 131104 | tf_op jit(solution)/shard_map/ppermute | solution.py:243
  24.9 0.2 collective-permute-done.10.refs_9_
  25.1 0.3 collective-permute-done.11.refs_11_
  25.4 0.0 collective-permute-done.5.refs_5_
  25.4 0.0 copy-done.2
  25.4 2.5 %first_terms.1 = (bf16[256,4096]{1,0:T(8,128)(2,1)S(1)}, bf16[4096,256]{1,0:T(8,128)(2,1)S(1)}, f32[640,128]{1,0:T(8,128)S(1)}, s16[656,128]{1,0:T(8,128)(2,1)S(1)}) custom-call(s32[2]{0:T(128)S(1)} %pad_add_fusion.place, s32[16,16]{1,0:T(8,128)S(1)} %copy-done.2, bf16[16,4096]{1,0:T(8,128)(2,1)S(1)} %copy-done, ...), custom_call_target="tpu_custom_call" | custom-call | flops 2621440 | bytes 327680 | tf_op jit(solution)/shard_map/first_terms/pallas_call | solution.py:336
  27.9 0.7 %collective-permute-start.13 = (s16[656,128]{1,0:T(8,128)(2,1)S(1)}, s16[656,128]{1,0:T(8,128)(2,1)S(1)}, u32[]{:S(2)}, u32[]{:S(2)}) collective-permute-start(s16[656,128]{1,0:T(8,128)(2,1)S(1)} %get-tuple-element.45), channel_id=1, source_target_pairs={{0,16},{16,0},{1,17},{17,1},{2,18},{18,2},{3,19},{19,3},{4,20},{20... | collective-permute-start | bytes 503816 | tf_op jit(solution)/shard_map/ppermute | solution.py:246
  28.6 0.0 copy-done.1
  28.6 2.7 %more_terms.1 = (f32[1152,128]{1,0:T(8,128)S(1)}, s16[1168,128]{1,0:T(8,128)(2,1)S(1)}, bf16[1792,256]{1,0:T(8,128)(2,1)S(1)}) custom-call(bf16[4096,256]{1,0:T(8,128)(2,1)S(1)} %get-tuple-element.39.turned, bf16[1280,4096]{1,0:T(8,128)(2,1)S(1)} %fetch.3.refs_13_.weight, f32[14,4096]{1,0:T(8,128)S(1)} %spread.1.refs_14_, bf16[128,1792]{1,0:T(8,128)(2,1)S(1)} %copy-done.1, ...), custom_call_target="tpu_custom_call" | custom-call | flops 2621440 | bytes 327680 | tf_op jit(solution)/shard_map/more_terms/pallas_call | solution.py:357
  31.3 1.4 %collective-permute-start.12 = (s16[1168,128]{1,0:T(8,128)(2,1)S(1)}, s16[1168,128]{1,0:T(8,128)(2,1)S(1)}, u32[]{:S(2)}, u32[]{:S(2)}) collective-permute-start(s16[1168,128]{1,0:T(8,128)(2,1)S(1)} %get-tuple-element.43), channel_id=1, source_target_pairs={{0,16},{16,0},{1,17},{17,1},{2,18},{18,2},{3,19},{19,3},{4,20},{20... | collective-permute-start | bytes 897032 | tf_op jit(solution)/shard_map/ppermute | solution.py:246
  32.8 6.1 %weight_grad.1 = bf16[1792,4096]{1,0:T(8,128)(2,1)} custom-call(bf16[1792,256]{1,0:T(8,128)(2,1)S(1)} %get-tuple-element.46.acts, bf16[256,4096]{1,0:T(8,128)(2,1)S(1)} %get-tuple-element.47.full, f32[14,4096]{1,0:T(8,128)S(1)} %spread.1.refs_14_), custom_call_target="tpu_custom_call" | custom-call | flops 2621440 | bytes 327680 | tf_op jit(solution)/shard_map/weight_grad/pallas_call | solution.py:379
  38.8 0.0 collective-permute-done.13.refs_0_
  38.9 0.8 %add_terms.2.refs_1_ = bf16[128,1792]{1,0:T(8,128)(2,1)} custom-call(f32[640,128]{1,0:T(8,128)S(1)} %get-tuple-element.44.own, s16[656,128]{1,0:T(8,128)(2,1)S(1)} %collective-permute-done.13.refs_0_), custom_call_target="tpu_custom_call" | custom-call | flops 17179869184 | bytes 128 | tf_op jit(solution)/shard_map/add_terms/pallas_call | solution.py:400
  39.7 1.0 %collective-permute-done.12.refs_0_ = s16[1168,128]{1,0:T(8,128)(2,1)S(1)} collective-permute-done((s16[1168,128]{1,0:T(8,128)(2,1)S(1)}, s16[1168,128]{1,0:T(8,128)(2,1)S(1)}, u32[]{:S(2)}, u32[]{:S(2)}) %collective-permute-start.12) | collective-permute-done | bytes 299040 | tf_op jit(solution)/shard_map/ppermute | solution.py:246
  40.7 0.9 %add_terms.3 = bf16[128,1792]{1,0:T(8,128)(2,1)} custom-call(f32[1152,128]{1,0:T(8,128)S(1)} %get-tuple-element.42.own, s16[1168,128]{1,0:T(8,128)(2,1)S(1)} %collective-permute-done.12.refs_0_, bf16[128,1792]{1,0:T(8,128)(2,1)} %add_terms.2.refs_1_), custom_call_target="tpu_custom_call", output_to_operand_aliasing={{}: (2, {})} | custom-call | flops 128 | bytes 128 | tf_op jit(solution)/shard_map/add_terms/pallas_call | solution.py:400
  (1 shorter events, 0.0 us)
Async XLA Ops:
  0.6 11.8 %collective-permute-start.4 = (bf16[16,4096]{1,0:T(8,128)(2,1)}, bf16[16,4096]{1,0:T(8,128)(2,1)S(1)}, u32[]{:S(2)}, u32[]{:S(2)}) collective-permute-start(bf16[16,4096]{1,0:T(8,128)(2,1)} %refs_0_.3), channel_id=1, source_target_pairs={{2,4},{3,11},{6,0},{7,15},{10,2},{11,13},{14,6},{15,9},{12,10},{13... | collective-permute-start | bytes 393224 | tf_op jit(solution)/shard_map/ppermute | solution.py:240
  4.7 7.7 %collective-permute-start.3 = (bf16[16,4096]{1,0:T(8,128)(2,1)}, bf16[16,4096]{1,0:T(8,128)(2,1)S(1)}, u32[]{:S(2)}, u32[]{:S(2)}) collective-permute-start(bf16[16,4096]{1,0:T(8,128)(2,1)} %refs_0_.3), channel_id=1, source_target_pairs={{2,10},{3,5},{6,14},{7,1},{10,12},{11,3},{14,8},{15,7},{12,4},{13,... | collective-permute-start | bytes 393224 | tf_op jit(solution)/shard_map/ppermute | solution.py:240
  4.7 12.4 %collective-permute-start.2 = (bf16[128,1792]{1,0:T(8,128)(2,1)}, bf16[128,1792]{1,0:T(8,128)(2,1)S(1)}, u32[]{:S(2)}, u32[]{:S(2)}) collective-permute-start(bf16[128,1792]{1,0:T(8,128)(2,1)} %refs_0_.4), channel_id=1, source_target_pairs={{0,16},{16,0},{1,17},{17,1},{2,18},{18,2},{3,19},{19,3},{4,20},{20... | collective-permute-start | bytes 1376264 | tf_op jit(solution)/shard_map/ppermute | solution.py:246
  6.6 1.5 %copy-start = (bf16[16,4096]{1,0:T(8,128)(2,1)S(1)}, bf16[16,4096]{1,0:T(8,128)(2,1)}, u32[]{:S(2)}) copy-start(bf16[16,4096]{1,0:T(8,128)(2,1)} %refs_0_.3) | copy-start | bytes 393220
  8.1 8.4 %collective-permute-start.1 = (bf16[16,4096]{1,0:T(8,128)(2,1)S(1)}, bf16[16,4096]{1,0:T(8,128)(2,1)S(1)}, u32[]{:S(2)}, u32[]{:S(2)}) collective-permute-start(bf16[16,4096]{1,0:T(8,128)(2,1)S(1)} %copy-done), channel_id=1, source_target_pairs={{2,0},{3,7},{6,2},{7,11},{10,6},{11,15},{14,10},{15,13},{12,14},{1... | collective-permute-start | bytes 393224 | tf_op jit(solution)/shard_map/ppermute | solution.py:240
  9.7 7.4 %collective-permute-start = (bf16[16,4096]{1,0:T(8,128)(2,1)S(1)}, bf16[16,4096]{1,0:T(8,128)(2,1)S(1)}, u32[]{:S(2)}, u32[]{:S(2)}) collective-permute-start(bf16[16,4096]{1,0:T(8,128)(2,1)S(1)} %copy-done), channel_id=1, source_target_pairs={{2,6},{3,1},{6,10},{7,3},{10,14},{11,7},{14,12},{15,11},{12,8},{13... | collective-permute-start | bytes 393224 | tf_op jit(solution)/shard_map/ppermute | solution.py:240
  12.4 9.1 %collective-permute-start.7 = (bf16[16,4096]{1,0:T(8,128)(2,1)S(1)}, bf16[16,4096]{1,0:T(8,128)(2,1)S(1)}, u32[]{:S(2)}, u32[]{:S(2)}) collective-permute-start(bf16[16,4096]{1,0:T(8,128)(2,1)S(1)} %collective-permute-done.3.refs_3_), channel_id=1, source_target_pairs={{2,6},{3,1},{6,10},{7,3},{10,14},{11,7},{14,12},{15,11},{12,8},{13... | collective-permute-start | bytes 393224 | tf_op jit(solution)/shard_map/ppermute | solution.py:240
  14.0 9.6 %collective-permute-start.6 = (bf16[16,4096]{1,0:T(8,128)(2,1)S(1)}, bf16[16,4096]{1,0:T(8,128)(2,1)S(1)}, u32[]{:S(2)}, u32[]{:S(2)}) collective-permute-start(bf16[16,4096]{1,0:T(8,128)(2,1)S(1)} %collective-permute-done.3.refs_3_), channel_id=1, source_target_pairs={{2,10},{3,5},{6,14},{7,1},{10,12},{11,3},{14,8},{15,7},{12,4},{13,... | collective-permute-start | bytes 393224 | tf_op jit(solution)/shard_map/ppermute | solution.py:240
  16.6 5.0 %collective-permute-start.8 = (bf16[16,4096]{1,0:T(8,128)(2,1)S(1)}, bf16[16,4096]{1,0:T(8,128)(2,1)S(1)}, u32[]{:S(2)}, u32[]{:S(2)}) collective-permute-start(bf16[16,4096]{1,0:T(8,128)(2,1)S(1)} %collective-permute-done.4.refs_4_), channel_id=1, source_target_pairs={{2,0},{3,7},{6,2},{7,11},{10,6},{11,15},{14,10},{15,13},{12,14},{1... | collective-permute-start | bytes 393224 | tf_op jit(solution)/shard_map/ppermute | solution.py:240
  17.2 8.2 %copy-start.2 = (s32[16,16]{1,0:T(8,128)S(1)}, s32[16,16]{1,0:T(8,128)}, u32[]{:S(2)}) copy-start(s32[16,16]{1,0:T(8,128)} %constant.11.clone.table) | copy-start | bytes 3076
  17.2 8.2 %collective-permute-start.5 = (bf16[80,4096]{1,0:T(8,128)(2,1)S(1)}, bf16[80,4096]{1,0:T(8,128)(2,1)S(1)}, u32[]{:S(2)}, u32[]{:S(2)}) collective-permute-start(bf16[80,4096]{1,0:T(8,128)(2,1)S(1)} %pack.1), channel_id=1, source_target_pairs={{0,1},{1,0},{2,3},{3,2},{4,5},{5,4},{6,7},{7,6},{8,9},{9,8},{10,11... | collective-permute-start | bytes 1966088 | tf_op jit(solution)/shard_map/ppermute | solution.py:243
  21.4 7.2 %copy-start.1 = (bf16[128,1792]{1,0:T(8,128)(2,1)S(1)}, bf16[128,1792]{1,0:T(8,128)(2,1)}, u32[]{:S(2)}) copy-start(bf16[128,1792]{1,0:T(8,128)(2,1)} %refs_0_.4) | copy-start | bytes 1376260
  23.5 1.3 %collective-permute-start.9 = (bf16[16,4096]{1,0:T(8,128)(2,1)S(1)}, bf16[16,4096]{1,0:T(8,128)(2,1)S(1)}, u32[]{:S(2)}, u32[]{:S(2)}) collective-permute-start(bf16[16,4096]{1,0:T(8,128)(2,1)S(1)} %collective-permute-done.7.refs_6_), channel_id=1, source_target_pairs={{0,1},{1,0},{2,3},{3,2},{4,5},{5,4},{6,7},{7,6},{8,9},{9,8},{10,11... | collective-permute-start | bytes 393224 | tf_op jit(solution)/shard_map/ppermute | solution.py:243
  23.5 1.5 %collective-permute-start.10 = (bf16[16,4096]{1,0:T(8,128)(2,1)S(1)}, bf16[16,4096]{1,0:T(8,128)(2,1)S(1)}, u32[]{:S(2)}, u32[]{:S(2)}) collective-permute-start(bf16[16,4096]{1,0:T(8,128)(2,1)S(1)} %collective-permute-done.8.refs_8_), channel_id=1, source_target_pairs={{0,1},{1,0},{2,3},{3,2},{4,5},{5,4},{6,7},{7,6},{8,9},{9,8},{10,11... | collective-permute-start | bytes 393224 | tf_op jit(solution)/shard_map/ppermute | solution.py:243
  24.0 1.3 %collective-permute-start.11 = (bf16[16,4096]{1,0:T(8,128)(2,1)S(1)}, bf16[16,4096]{1,0:T(8,128)(2,1)S(1)}, u32[]{:S(2)}, u32[]{:S(2)}) collective-permute-start(bf16[16,4096]{1,0:T(8,128)(2,1)S(1)} %collective-permute-done.6.refs_10_), channel_id=1, source_target_pairs={{0,1},{1,0},{2,3},{3,2},{4,5},{5,4},{6,7},{7,6},{8,9},{9,8},{10,11... | collective-permute-start | bytes 393224 | tf_op jit(solution)/shard_map/ppermute | solution.py:243
  27.9 11.0 %collective-permute-start.13 = (s16[656,128]{1,0:T(8,128)(2,1)S(1)}, s16[656,128]{1,0:T(8,128)(2,1)S(1)}, u32[]{:S(2)}, u32[]{:S(2)}) collective-permute-start(s16[656,128]{1,0:T(8,128)(2,1)S(1)} %get-tuple-element.45), channel_id=1, source_target_pairs={{0,16},{16,0},{1,17},{17,1},{2,18},{18,2},{3,19},{19,3},{4,20},{20... | collective-permute-start | bytes 503816 | tf_op jit(solution)/shard_map/ppermute | solution.py:246
  31.3 9.4 %collective-permute-start.12 = (s16[1168,128]{1,0:T(8,128)(2,1)S(1)}, s16[1168,128]{1,0:T(8,128)(2,1)S(1)}, u32[]{:S(2)}, u32[]{:S(2)}) collective-permute-start(s16[1168,128]{1,0:T(8,128)(2,1)S(1)} %get-tuple-element.43), channel_id=1, source_target_pairs={{0,16},{16,0},{1,17},{17,1},{2,18},{18,2},{3,19},{19,3},{4,20},{20... | collective-permute-start | bytes 897032 | tf_op jit(solution)/shard_map/ppermute | solution.py:246

commit v19 on v17

--- a/solution.py
+++ b/solution.py
@@ -312,8 +312,14 @@
         (weight, held[1], held[-1], *acts)
     )
     rest = fetch_rows(n_soon, blocks - n_soon, 1 << 34)
-    rest, *ready = lax.optimization_barrier((rest, *(held[j] for j in last)))
-    held.update(zip(last, ready, strict=True))
+    across, late = {}, [j for j in last if j != 3]
+    rest, *ready = lax.optimization_barrier((rest, *(held[j] for j in late)))
+    held.update(zip(late, ready, strict=True))
+    for j in late:
+        across[j] = send_core(held[j])
+    if 3 in last:
+        held[3], *ready = lax.optimization_barrier((held[3], *(across[j] for j in late)))
+        across = dict(zip(late, ready, strict=True))
     packed = pl.pallas_call(
         pack_kernel,
         in_specs=[in_vmem()] * len(near),
@@ -324,7 +330,7 @@
     )(*(held[j] for j in near))
     shards = [held[j] for j in near] + [send_core(packed)]
     for j in last:
-        shards += [held[j], send_core(held[j])]
+        shards += [held[j], across[j] if j in across else send_core(held[j])]
     n_shards = len(shards)
     def out_shapes(rows):
         code_rows = -(-(rows // BLOCK) // 16) * 16

time: 41 us -> 41.6 us (1.015)
    ppermute x4, waiting for transfers between devices: 1.35 us -> 1.9 us  [send_core(): return lax.ppermute(x, 'col', [(c, c ^ 1) for c in range(n_cols)])]
    ppermute x7, waiting for transfers between devices: 1.18 us -> 0.66 us  [send_ring(): return lax.ppermute(x, 'col', perm)]
  transfers between devices with their start and end apart: 14 -> 14, of which waited for: 6 -> 6; matrix products, arithmetic and copies ran while one was open for 0% -> 0% of each run, Pallas kernels for 43% -> 42%
where the time goes in v19:
time: 41.6 us; the launch traced here: 41.4 us
  Pallas kernels  20.8 us (50%)
  starting transfers between devices  15.6 us (38%)
  waiting for transfers between devices  4.07 us (10%)
  between operations  0.76 us (2%)
    ppermute x7, starting transfers between devices, send_ring(): return lax.ppermute(x, 'col', perm)  10.9 us
    pallas_call x2, Pallas kernels, fetch_rows(): pl.pallas_call(functools.partial(fetch_kernel, first), in_specs=[in_hbm()...  6.31 us
    pallas_call x1, Pallas kernels, per_device(): pl.pallas_call(functools.partial(weight_grad_kernel, chunk), in_specs=[in...  6.05 us
    ppermute x3, starting transfers between devices, send_row(): lax.ppermute(x, 'row', [(r, (r + by) % n_rows) for r in range(n_rows)])  4.01 us
    pallas_call x1, Pallas kernels, per_device(): pl.pallas_call(functools.partial(more_terms_kernel, n_parts, piece_blocks...  2.74 us
    pallas_call x1, Pallas kernels, per_device(): pl.pallas_call(functools.partial(first_terms_kernel, n_shards, n_parts, t...  2.49 us
    ppermute x4, waiting for transfers between devices, send_core(): return lax.ppermute(x, 'col', [(c, c ^ 1) for c in range(n_cols)])  1.9 us
    pallas_call x2, Pallas kernels, per_device(): pl.pallas_call(functools.partial(finish_kernel, sum(sizes[:p]), n_parts),...  1.73 us
  transfers between devices with their start and end apart: 14, of which 6 were waited for; matrix products, arithmetic and copies ran while one was open for 0% of the time, Pallas kernels for 42%

profile of v19, /device:TPU:0, one launch (start us, length us, event | category | flops | bytes accessed | tf_op | source)
XLA Modules:
  0.0 41.4 jit_solution(4947034289097942551)
XLA Ops:
  0.6 4.1 %collective-permute-start.4 = (bf16[16,4096]{1,0:T(8,128)(2,1)}, bf16[16,4096]{1,0:T(8,128)(2,1)S(1)}, u32[]{:S(2)}, u32[]{:S(2)}) collective-permute-start(bf16[16,4096]{1,0:T(8,128)(2,1)} %refs_0_.3), channel_id=1, source_target_pairs={{2,4},{3,11},{6,0},{7,15},{10,2},{11,13},{14,6},{15,9},{12,10},{13... | collective-permute-start | bytes 393224 | tf_op jit(solution)/shard_map/ppermute | solution.py:240
  4.7 0.0 collective-permute-start.3
  4.7 1.9 %collective-permute-start.2 = (bf16[128,1792]{1,0:T(8,128)(2,1)}, bf16[128,1792]{1,0:T(8,128)(2,1)S(1)}, u32[]{:S(2)}, u32[]{:S(2)}) collective-permute-start(bf16[128,1792]{1,0:T(8,128)(2,1)} %refs_0_.4), channel_id=1, source_target_pairs={{0,16},{16,0},{1,17},{17,1},{2,18},{18,2},{3,19},{19,3},{4,20},{20... | collective-permute-start | bytes 1376264 | tf_op jit(solution)/shard_map/ppermute | solution.py:246
  6.6 0.1 pad_add_fusion.place
  6.6 0.0 copy-start
  6.7 1.4 %spread.1.refs_14_ = f32[14,4096]{1,0:T(8,128)S(1)} custom-call(s32[2]{0:T(128)S(1)} %pad_add_fusion.place, s32[14,64]{1,0:T(8,128)} %mask.1), custom_call_target="tpu_custom_call" | custom-call | flops 17179869184 | bytes 128 | tf_op jit(solution)/shard_map/spread/pallas_call | solution.py:269
  8.1 0.0 copy-done
  8.1 1.6 %collective-permute-start.1 = (bf16[16,4096]{1,0:T(8,128)(2,1)S(1)}, bf16[16,4096]{1,0:T(8,128)(2,1)S(1)}, u32[]{:S(2)}, u32[]{:S(2)}) collective-permute-start(bf16[16,4096]{1,0:T(8,128)(2,1)S(1)} %copy-done), channel_id=1, source_target_pairs={{2,0},{3,7},{6,2},{7,11},{10,6},{11,15},{14,10},{15,13},{12,14},{1... | collective-permute-start | bytes 393224 | tf_op jit(solution)/shard_map/ppermute | solution.py:240
  9.7 0.4 %collective-permute-start = (bf16[16,4096]{1,0:T(8,128)(2,1)S(1)}, bf16[16,4096]{1,0:T(8,128)(2,1)S(1)}, u32[]{:S(2)}, u32[]{:S(2)}) collective-permute-start(bf16[16,4096]{1,0:T(8,128)(2,1)S(1)} %copy-done), channel_id=1, source_target_pairs={{2,6},{3,1},{6,10},{7,3},{10,14},{11,7},{14,12},{15,11},{12,8},{13... | collective-permute-start | bytes 393224 | tf_op jit(solution)/shard_map/ppermute | solution.py:240
  10.2 2.2 %fetch.2.refs_12_ = bf16[512,4096]{1,0:T(8,128)(2,1)S(1)} custom-call(bf16[1792,4096]{1,0:T(8,128)(2,1)} %weight.1), custom_call_target="tpu_custom_call" | custom-call | flops 128 | bytes 128 | tf_op jit(solution)/shard_map/fetch/pallas_call | solution.py:281
  12.4 0.0 collective-permute-done.4.refs_4_
  12.4 0.0 collective-permute-done.3.refs_3_
  12.4 2.7 %collective-permute-start.8 = (bf16[16,4096]{1,0:T(8,128)(2,1)S(1)}, bf16[16,4096]{1,0:T(8,128)(2,1)S(1)}, u32[]{:S(2)}, u32[]{:S(2)}) collective-permute-start(bf16[16,4096]{1,0:T(8,128)(2,1)S(1)} %collective-permute-done.3.refs_3_), channel_id=1, source_target_pairs={{2,10},{3,5},{6,14},{7,1},{10,12},{11,3},{14,8},{15,7},{12,4},{13,... | collective-permute-start | bytes 393224 | tf_op jit(solution)/shard_map/ppermute | solution.py:240
  15.1 1.5 %collective-permute-start.6 = (bf16[16,4096]{1,0:T(8,128)(2,1)S(1)}, bf16[16,4096]{1,0:T(8,128)(2,1)S(1)}, u32[]{:S(2)}, u32[]{:S(2)}) collective-permute-start(bf16[16,4096]{1,0:T(8,128)(2,1)S(1)} %collective-permute-done.3.refs_3_), channel_id=1, source_target_pairs={{2,6},{3,1},{6,10},{7,3},{10,14},{11,7},{14,12},{15,11},{12,8},{13... | collective-permute-start | bytes 393224 | tf_op jit(solution)/shard_map/ppermute | solution.py:240
  16.6 0.0 collective-permute-done.1.refs_2_
  16.6 0.6 %collective-permute-start.7 = (bf16[16,4096]{1,0:T(8,128)(2,1)S(1)}, bf16[16,4096]{1,0:T(8,128)(2,1)S(1)}, u32[]{:S(2)}, u32[]{:S(2)}) collective-permute-start(bf16[16,4096]{1,0:T(8,128)(2,1)S(1)} %collective-permute-done.4.refs_4_), channel_id=1, source_target_pairs={{2,0},{3,7},{6,2},{7,11},{10,6},{11,15},{14,10},{15,13},{12,14},{1... | collective-permute-start | bytes 393224 | tf_op jit(solution)/shard_map/ppermute | solution.py:240
  17.1 0.0 collective-permute-done.refs_1_
  17.1 0.0 collective-permute-done.2.refs_1_
  17.2 0.0 copy-start.2
  17.2 0.1 collective-permute-start.5
  17.3 4.1 %fetch.3.refs_13_.weight = bf16[1280,4096]{1,0:T(8,128)(2,1)S(1)} custom-call(bf16[1792,4096]{1,0:T(8,128)(2,1)} %weight.1), custom_call_target="tpu_custom_call" | custom-call | flops 17179869184 | bytes 128 | tf_op jit(solution)/shard_map/fetch/pallas_call | solution.py:281
  21.4 0.0 copy-start.1
  21.4 0.1 collective-permute-done.7.refs_8_
  21.5 0.0 collective-permute-done.8.refs_10_
  21.5 0.4 %collective-permute-start.9 = (bf16[16,4096]{1,0:T(8,128)(2,1)S(1)}, bf16[16,4096]{1,0:T(8,128)(2,1)S(1)}, u32[]{:S(2)}, u32[]{:S(2)}) collective-permute-start(bf16[16,4096]{1,0:T(8,128)(2,1)S(1)} %collective-permute-done.7.refs_8_), channel_id=1, source_target_pairs={{0,1},{1,0},{2,3},{3,2},{4,5},{5,4},{6,7},{7,6},{8,9},{9,8},{10,11... | collective-permute-start | bytes 393224 | tf_op jit(solution)/shard_map/ppermute | solution.py:243
  21.9 0.1 collective-permute-start.10
  22.0 0.5 %collective-permute-done.6.refs_6_ = bf16[16,4096]{1,0:T(8,128)(2,1)S(1)} collective-permute-done((bf16[16,4096]{1,0:T(8,128)(2,1)S(1)}, bf16[16,4096]{1,0:T(8,128)(2,1)S(1)}, u32[]{:S(2)}, u32[]{:S(2)}) %collective-permute-start.6) | collective-permute-done | bytes 131104 | tf_op jit(solution)/shard_map/ppermute | solution.py:240
  22.6 0.4 collective-permute-done.9.refs_9_
  22.9 0.4 collective-permute-done.10.refs_11_
  23.3 0.2 collective-permute-start.11
  23.5 1.2 %collective-permute-done.11.refs_7_ = bf16[16,4096]{1,0:T(8,128)(2,1)S(1)} collective-permute-done((bf16[16,4096]{1,0:T(8,128)(2,1)S(1)}, bf16[16,4096]{1,0:T(8,128)(2,1)S(1)}, u32[]{:S(2)}, u32[]{:S(2)}) %collective-permute-start.11) | collective-permute-done | bytes 131104 | tf_op jit(solution)/shard_map/ppermute | solution.py:243
  24.6 0.0 collective-permute-done.5.refs_5_
  24.6 0.0 copy-done.2
  24.7 2.5 %first_terms.1 = (bf16[256,4096]{1,0:T(8,128)(2,1)S(1)}, bf16[4096,256]{1,0:T(8,128)(2,1)S(1)}, f32[640,128]{1,0:T(8,128)S(1)}, s16[656,128]{1,0:T(8,128)(2,1)S(1)}) custom-call(s32[2]{0:T(128)S(1)} %pad_add_fusion.place, s32[16,16]{1,0:T(8,128)S(1)} %copy-done.2, bf16[16,4096]{1,0:T(8,128)(2,1)S(1)} %copy-done, ...), custom_call_target="tpu_custom_call" | custom-call | flops 2621440 | bytes 327680 | tf_op jit(solution)/shard_map/first_terms/pallas_call | solution.py:341
  27.2 1.6 %collective-permute-start.13 = (s16[656,128]{1,0:T(8,128)(2,1)S(1)}, s16[656,128]{1,0:T(8,128)(2,1)S(1)}, u32[]{:S(2)}, u32[]{:S(2)}) collective-permute-start(s16[656,128]{1,0:T(8,128)(2,1)S(1)} %get-tuple-element.49), channel_id=1, source_target_pairs={{0,16},{16,0},{1,17},{17,1},{2,18},{18,2},{3,19},{19,3},{4,20},{20... | collective-permute-start | bytes 503816 | tf_op jit(solution)/shard_map/ppermute | solution.py:246
  28.7 0.0 copy-done.1
  28.7 2.7 %more_terms.1 = (f32[1152,128]{1,0:T(8,128)S(1)}, s16[1168,128]{1,0:T(8,128)(2,1)S(1)}, bf16[1792,256]{1,0:T(8,128)(2,1)S(1)}) custom-call(bf16[4096,256]{1,0:T(8,128)(2,1)S(1)} %get-tuple-element.43.turned, bf16[1280,4096]{1,0:T(8,128)(2,1)S(1)} %fetch.3.refs_13_.weight, f32[14,4096]{1,0:T(8,128)S(1)} %spread.1.refs_14_, bf16[128,1792]{1,0:T(8,128)(2,1)S(1)} %copy-done.1, ...), custom_call_target="tpu_custom_call" | custom-call | flops 2621440 | bytes 327680 | tf_op jit(solution)/shard_map/more_terms/pallas_call | solution.py:362
  31.5 0.6 %collective-permute-start.12 = (s16[1168,128]{1,0:T(8,128)(2,1)S(1)}, s16[1168,128]{1,0:T(8,128)(2,1)S(1)}, u32[]{:S(2)}, u32[]{:S(2)}) collective-permute-start(s16[1168,128]{1,0:T(8,128)(2,1)S(1)} %get-tuple-element.47), channel_id=1, source_target_pairs={{0,16},{16,0},{1,17},{17,1},{2,18},{18,2},{3,19},{19,3},{4,20},{20... | collective-permute-start | bytes 897032 | tf_op jit(solution)/shard_map/ppermute | solution.py:246
  32.1 6.1 %weight_grad.1 = bf16[1792,4096]{1,0:T(8,128)(2,1)} custom-call(bf16[1792,256]{1,0:T(8,128)(2,1)S(1)} %get-tuple-element.50.acts, bf16[256,4096]{1,0:T(8,128)(2,1)S(1)} %get-tuple-element.51.full, f32[14,4096]{1,0:T(8,128)S(1)} %spread.1.refs_14_), custom_call_target="tpu_custom_call" | custom-call | flops 2621440 | bytes 327680 | tf_op jit(solution)/shard_map/weight_grad/pallas_call | solution.py:384
  38.1 0.0 collective-permute-done.13.refs_0_
  38.1 0.8 %add_terms.2.refs_1_ = bf16[128,1792]{1,0:T(8,128)(2,1)} custom-call(f32[640,128]{1,0:T(8,128)S(1)} %get-tuple-element.48.own, s16[656,128]{1,0:T(8,128)(2,1)S(1)} %collective-permute-done.13.refs_0_), custom_call_target="tpu_custom_call" | custom-call | flops 17179869184 | bytes 128 | tf_op jit(solution)/shard_map/add_terms/pallas_call | solution.py:405
  39.0 1.5 %collective-permute-done.12.refs_0_ = s16[1168,128]{1,0:T(8,128)(2,1)S(1)} collective-permute-done((s16[1168,128]{1,0:T(8,128)(2,1)S(1)}, s16[1168,128]{1,0:T(8,128)(2,1)S(1)}, u32[]{:S(2)}, u32[]{:S(2)}) %collective-permute-start.12) | collective-permute-done | bytes 299040 | tf_op jit(solution)/shard_map/ppermute | solution.py:246
  40.5 0.9 %add_terms.3 = bf16[128,1792]{1,0:T(8,128)(2,1)} custom-call(f32[1152,128]{1,0:T(8,128)S(1)} %get-tuple-element.46.own, s16[1168,128]{1,0:T(8,128)(2,1)S(1)} %collective-permute-done.12.refs_0_, bf16[128,1792]{1,0:T(8,128)(2,1)} %add_terms.2.refs_1_), custom_call_target="tpu_custom_call", output_to_operand_aliasing={{}: (2, {})} | custom-call | flops 128 | bytes 128 | tf_op jit(solution)/shard_map/add_terms/pallas_call | solution.py:405
  (1 shorter events, 0.0 us)
Async XLA Ops:
  0.6 11.8 %collective-permute-start.4 = (bf16[16,4096]{1,0:T(8,128)(2,1)}, bf16[16,4096]{1,0:T(8,128)(2,1)S(1)}, u32[]{:S(2)}, u32[]{:S(2)}) collective-permute-start(bf16[16,4096]{1,0:T(8,128)(2,1)} %refs_0_.3), channel_id=1, source_target_pairs={{2,4},{3,11},{6,0},{7,15},{10,2},{11,13},{14,6},{15,9},{12,10},{13... | collective-permute-start | bytes 393224 | tf_op jit(solution)/shard_map/ppermute | solution.py:240
  4.7 7.7 %collective-permute-start.3 = (bf16[16,4096]{1,0:T(8,128)(2,1)}, bf16[16,4096]{1,0:T(8,128)(2,1)S(1)}, u32[]{:S(2)}, u32[]{:S(2)}) collective-permute-start(bf16[16,4096]{1,0:T(8,128)(2,1)} %refs_0_.3), channel_id=1, source_target_pairs={{2,10},{3,5},{6,14},{7,1},{10,12},{11,3},{14,8},{15,7},{12,4},{13,... | collective-permute-start | bytes 393224 | tf_op jit(solution)/shard_map/ppermute | solution.py:240
  4.7 12.4 %collective-permute-start.2 = (bf16[128,1792]{1,0:T(8,128)(2,1)}, bf16[128,1792]{1,0:T(8,128)(2,1)S(1)}, u32[]{:S(2)}, u32[]{:S(2)}) collective-permute-start(bf16[128,1792]{1,0:T(8,128)(2,1)} %refs_0_.4), channel_id=1, source_target_pairs={{0,16},{16,0},{1,17},{17,1},{2,18},{18,2},{3,19},{19,3},{4,20},{20... | collective-permute-start | bytes 1376264 | tf_op jit(solution)/shard_map/ppermute | solution.py:246
  6.6 1.5 %copy-start = (bf16[16,4096]{1,0:T(8,128)(2,1)S(1)}, bf16[16,4096]{1,0:T(8,128)(2,1)}, u32[]{:S(2)}) copy-start(bf16[16,4096]{1,0:T(8,128)(2,1)} %refs_0_.3) | copy-start | bytes 393220
  8.1 8.4 %collective-permute-start.1 = (bf16[16,4096]{1,0:T(8,128)(2,1)S(1)}, bf16[16,4096]{1,0:T(8,128)(2,1)S(1)}, u32[]{:S(2)}, u32[]{:S(2)}) collective-permute-start(bf16[16,4096]{1,0:T(8,128)(2,1)S(1)} %copy-done), channel_id=1, source_target_pairs={{2,0},{3,7},{6,2},{7,11},{10,6},{11,15},{14,10},{15,13},{12,14},{1... | collective-permute-start | bytes 393224 | tf_op jit(solution)/shard_map/ppermute | solution.py:240
  9.7 7.4 %collective-permute-start = (bf16[16,4096]{1,0:T(8,128)(2,1)S(1)}, bf16[16,4096]{1,0:T(8,128)(2,1)S(1)}, u32[]{:S(2)}, u32[]{:S(2)}) collective-permute-start(bf16[16,4096]{1,0:T(8,128)(2,1)S(1)} %copy-done), channel_id=1, source_target_pairs={{2,6},{3,1},{6,10},{7,3},{10,14},{11,7},{14,12},{15,11},{12,8},{13... | collective-permute-start | bytes 393224 | tf_op jit(solution)/shard_map/ppermute | solution.py:240
  12.4 9.1 %collective-permute-start.8 = (bf16[16,4096]{1,0:T(8,128)(2,1)S(1)}, bf16[16,4096]{1,0:T(8,128)(2,1)S(1)}, u32[]{:S(2)}, u32[]{:S(2)}) collective-permute-start(bf16[16,4096]{1,0:T(8,128)(2,1)S(1)} %collective-permute-done.3.refs_3_), channel_id=1, source_target_pairs={{2,10},{3,5},{6,14},{7,1},{10,12},{11,3},{14,8},{15,7},{12,4},{13,... | collective-permute-start | bytes 393224 | tf_op jit(solution)/shard_map/ppermute | solution.py:240
  15.1 7.5 %collective-permute-start.6 = (bf16[16,4096]{1,0:T(8,128)(2,1)S(1)}, bf16[16,4096]{1,0:T(8,128)(2,1)S(1)}, u32[]{:S(2)}, u32[]{:S(2)}) collective-permute-start(bf16[16,4096]{1,0:T(8,128)(2,1)S(1)} %collective-permute-done.3.refs_3_), channel_id=1, source_target_pairs={{2,6},{3,1},{6,10},{7,3},{10,14},{11,7},{14,12},{15,11},{12,8},{13... | collective-permute-start | bytes 393224 | tf_op jit(solution)/shard_map/ppermute | solution.py:240
  16.6 5.0 %collective-permute-start.7 = (bf16[16,4096]{1,0:T(8,128)(2,1)S(1)}, bf16[16,4096]{1,0:T(8,128)(2,1)S(1)}, u32[]{:S(2)}, u32[]{:S(2)}) collective-permute-start(bf16[16,4096]{1,0:T(8,128)(2,1)S(1)} %collective-permute-done.4.refs_4_), channel_id=1, source_target_pairs={{2,0},{3,7},{6,2},{7,11},{10,6},{11,15},{14,10},{15,13},{12,14},{1... | collective-permute-start | bytes 393224 | tf_op jit(solution)/shard_map/ppermute | solution.py:240
  17.2 7.5 %copy-start.2 = (s32[16,16]{1,0:T(8,128)S(1)}, s32[16,16]{1,0:T(8,128)}, u32[]{:S(2)}) copy-start(s32[16,16]{1,0:T(8,128)} %constant.11.clone.table) | copy-start | bytes 3076
  17.2 7.5 %collective-permute-start.5 = (bf16[80,4096]{1,0:T(8,128)(2,1)S(1)}, bf16[80,4096]{1,0:T(8,128)(2,1)S(1)}, u32[]{:S(2)}, u32[]{:S(2)}) collective-permute-start(bf16[80,4096]{1,0:T(8,128)(2,1)S(1)} %pack.1), channel_id=1, source_target_pairs={{0,1},{1,0},{2,3},{3,2},{4,5},{5,4},{6,7},{7,6},{8,9},{9,8},{10,11... | collective-permute-start | bytes 1966088 | tf_op jit(solution)/shard_map/ppermute | solution.py:243
  21.4 7.4 %copy-start.1 = (bf16[128,1792]{1,0:T(8,128)(2,1)S(1)}, bf16[128,1792]{1,0:T(8,128)(2,1)}, u32[]{:S(2)}) copy-start(bf16[128,1792]{1,0:T(8,128)(2,1)} %refs_0_.4) | copy-start | bytes 1376260
  21.5 1.4 %collective-permute-start.9 = (bf16[16,4096]{1,0:T(8,128)(2,1)S(1)}, bf16[16,4096]{1,0:T(8,128)(2,1)S(1)}, u32[]{:S(2)}, u32[]{:S(2)}) collective-permute-start(bf16[16,4096]{1,0:T(8,128)(2,1)S(1)} %collective-permute-done.7.refs_8_), channel_id=1, source_target_pairs={{0,1},{1,0},{2,3},{3,2},{4,5},{5,4},{6,7},{7,6},{8,9},{9,8},{10,11... | collective-permute-start | bytes 393224 | tf_op jit(solution)/shard_map/ppermute | solution.py:243
  21.9 1.3 %collective-permute-start.10 = (bf16[16,4096]{1,0:T(8,128)(2,1)S(1)}, bf16[16,4096]{1,0:T(8,128)(2,1)S(1)}, u32[]{:S(2)}, u32[]{:S(2)}) collective-permute-start(bf16[16,4096]{1,0:T(8,128)(2,1)S(1)} %collective-permute-done.8.refs_10_), channel_id=1, source_target_pairs={{0,1},{1,0},{2,3},{3,2},{4,5},{5,4},{6,7},{7,6},{8,9},{9,8},{10,11... | collective-permute-start | bytes 393224 | tf_op jit(solution)/shard_map/ppermute | solution.py:243
  23.3 1.3 %collective-permute-start.11 = (bf16[16,4096]{1,0:T(8,128)(2,1)S(1)}, bf16[16,4096]{1,0:T(8,128)(2,1)S(1)}, u32[]{:S(2)}, u32[]{:S(2)}) collective-permute-start(bf16[16,4096]{1,0:T(8,128)(2,1)S(1)} %collective-permute-done.6.refs_6_), channel_id=1, source_target_pairs={{0,1},{1,0},{2,3},{3,2},{4,5},{5,4},{6,7},{7,6},{8,9},{9,8},{10,11... | collective-permute-start | bytes 393224 | tf_op jit(solution)/shard_map/ppermute | solution.py:243
  27.2 11.0 %collective-permute-start.13 = (s16[656,128]{1,0:T(8,128)(2,1)S(1)}, s16[656,128]{1,0:T(8,128)(2,1)S(1)}, u32[]{:S(2)}, u32[]{:S(2)}) collective-permute-start(s16[656,128]{1,0:T(8,128)(2,1)S(1)} %get-tuple-element.49), channel_id=1, source_target_pairs={{0,16},{16,0},{1,17},{17,1},{2,18},{18,2},{3,19},{19,3},{4,20},{20... | collective-permute-start | bytes 503816 | tf_op jit(solution)/shard_map/ppermute | solution.py:246
  31.5 9.0 %collective-permute-start.12 = (s16[1168,128]{1,0:T(8,128)(2,1)S(1)}, s16[1168,128]{1,0:T(8,128)(2,1)S(1)}, u32[]{:S(2)}, u32[]{:S(2)}) collective-permute-start(s16[1168,128]{1,0:T(8,128)(2,1)S(1)} %get-tuple-element.47), channel_id=1, source_target_pairs={{0,16},{16,0},{1,17},{17,1},{2,18},{18,2},{3,19},{19,3},{4,20},{20... | collective-permute-start | bytes 897032 | tf_op jit(solution)/shard_map/ppermute | solution.py:246
